TPU v7x, 32 devices: a whole 2x2x4 slice. The times are simulated.
32 devices in a mesh: dp: 8 (over y, x, core), owner: 4 (over z).
Axes of the slice: x: 2, y: 2, z: 4, core: 2. Of those that a mesh axis runs over, the one named last changes fastest.
Arguments:
- gradients: bfloat16 [32, 704, 1024], P(None, 'dp', 'owner')
- momentum: float32 [32, 704, 1024], P(None, 'dp', 'owner'), may hold values from -6 to 6
- owner_table: int32 [32], replicated, may hold values from 0 to 31, as said below
Outputs:
- new_momentum: float32 [32, 704, 1024], P(None, 'dp', 'owner')
- update: bfloat16 [32, 704, 1024], P(None, 'dp', 'owner')
- owned: bfloat16 [64, 704, 1024], P(('dp', 'owner'))
Inputs may be any that keep to these rules, and one draw needn't show every extreme that they name: owner_table[i] numbers a device as 4 times its dp index plus its owner index; exactly half of the devices own 2 matrices each and the others own none; the first and the last device are always among the owners.
All inputs are finite; a program needn't handle non-finite values.
Results may differ from a plain program's by a relative error of at most 0.0083.
Values may be sent and summed in bfloat16 or wider, within the bound.
No kernel may reach another device: no remote copies, remote signals or barrier semaphores. Data moves between devices by JAX's collectives and lax.ppermute only.
A program may use at most 128 MiB of HBM per device.

v0:
```python
import math

import jax
import jax.numpy as jnp
from jax import lax
from jax.sharding import PartitionSpec as P

D = 1024
FF = 704
ITERS = 2
CAP = 2


coef_a = 3.4445
coef_b = -4.775
coef_c = 2.0315
momentum_beta = 0.95
epsilon = 1e-07


def orthogonalize(matrices):
    magnitude = jnp.sqrt(jnp.sum(jnp.square(matrices.astype(jnp.float32)), axis=(1, 2)))
    current = (matrices.astype(jnp.float32) / (magnitude[:, None, None] + epsilon)).astype(
        jnp.bfloat16
    )
    update_scale = 0.2 * math.sqrt(max(FF, D))
    result = current
    for iteration in range(ITERS):
        gram_matrix = jnp.einsum(
            "sik,sjk->sij", current, current, preferred_element_type=jnp.float32
        ).astype(jnp.bfloat16)
        square = jnp.einsum(
            "sij,sjk->sik", gram_matrix, gram_matrix, preferred_element_type=jnp.float32
        )
        mixing = (coef_b * gram_matrix.astype(jnp.float32) + coef_c * square).astype(jnp.bfloat16)
        combined = coef_a * current.astype(jnp.float32) + jnp.einsum(
            "sij,sjk->sik", mixing, current, preferred_element_type=jnp.float32
        )
        if iteration + 1 < ITERS:
            current = combined.astype(jnp.bfloat16)
        else:
            result = (update_scale * combined).astype(jnp.bfloat16)
    return result


def on_device(gradients, momentum, owner_table):
    matrix_count, row_shard, col_shard = gradients.shape
    dp_size = lax.axis_size("dp")
    owner_size = lax.axis_size("owner")
    devices = dp_size * owner_size
    new_momentum = momentum_beta * momentum + gradients.astype(jnp.float32)
    nesterov = (gradients.astype(jnp.float32) + momentum_beta * new_momentum).astype(jnp.bfloat16)
    positions = jnp.arange(matrix_count, dtype=jnp.int32)
    same_owner = (owner_table[None, :] == owner_table[:, None]) & (
        positions[None, :] < positions[:, None]
    )
    slot_rank = jnp.sum(same_owner.astype(jnp.int32), axis=1)
    slot_index = owner_table * CAP + slot_rank
    slots = jnp.arange(devices * CAP, dtype=jnp.int32)
    slot_hits = slot_index[None, :] == slots[:, None]
    source_matrix = jnp.sum(jnp.where(slot_hits, positions[None, :], 0), axis=1)
    filled = jnp.any(slot_hits, axis=1)
    outgoing = jnp.where(
        filled[:, None, None],
        jnp.take(nesterov, source_matrix, axis=0),
        jnp.zeros((), jnp.bfloat16),
    )
    outgoing = outgoing.reshape(dp_size, owner_size, CAP, row_shard, col_shard)
    arrived = lax.all_to_all(
        lax.all_to_all(outgoing, "dp", split_axis=0, concat_axis=3, tiled=True),
        "owner",
        split_axis=1,
        concat_axis=4,
        tiled=True,
    )
    owned_stack = orthogonalize(arrived.reshape(CAP, FF, D))
    returned = lax.all_to_all(
        lax.all_to_all(
            owned_stack.reshape(1, 1, CAP, FF, D), "dp", split_axis=3, concat_axis=0, tiled=True
        ),
        "owner",
        split_axis=4,
        concat_axis=1,
        tiled=True,
    )
    update = jnp.take(returned.reshape(devices * CAP, row_shard, col_shard), slot_index, axis=0)
    return (new_momentum, update, owned_stack)


def solution(mesh):
    return jax.shard_map(
        on_device,
        mesh=mesh,
        in_specs=(P(None, "dp", "owner"), P(None, "dp", "owner"), P()),
        out_specs=(P(None, "dp", "owner"), P(None, "dp", "owner"), P(("dp", "owner"), None, None)),
        check_vma=False,
    )
```

profile of v0, /device:TPU:0, one launch (start us, length us, event | category | flops | bytes accessed | tf_op | source)
XLA Modules:
  0.0 336.4 jit_solution(9378040447552604695)
XLA Ops:
  0.6 0.9 convert_reduce_fusion
  1.5 0.7 compare_and_fusion.1
  2.2 0.1 select_reduce_fusion
  2.3 0.1 fusion.8
  2.4 0.1 reduce_sum.33
  2.5 0.1 broadcast_in_dim.58
  2.7 4.4 %fusion.1 = (bf16[32,88,256]{2,1,0:T(8,128)(2,1)S(1)}, f32[32,88,256]{2,1,0:T(8,128)}) fusion(bf16[32,88,256]{2,1,0:T(8,128)(2,1)} %param.3, f32[32,88,256]{2,1,0:T(8,128)} %param.4), kind=kLoop, calls=%fused_computation.12 | loop fusion | flops 4325376 | bytes 8650752 | tf_op jit(solution)/shard_map/convert_element_type | solution.py:52
  7.1 2.3 gather_fusion
  9.4 2.2 select_select_fusion
  11.6 40.0 %all_to_all.60 = bf16[8,4,2,88,256]{4,3,2,1,0:T(8,128)(2,1)S(1)} all-to-all(bf16[8,4,2,88,256]{4,3,2,1,0:T(8,128)(2,1)S(1)} %select_select_fusion), channel_id=1, replica_groups=mesh['dp'=8,'owner'=4] {'dp'}, dimensions={0} | all-to-all | bytes 5767168 | tf_op jit(solution)/shard_map/all_to_all | solution.py:70
  51.6 0.2 copy.31
  51.8 69.1 %all_to_all.61 = bf16[1,4,2,704,256]{4,3,2,0,1:T(8,128)(2,1)S(1)} all-to-all(bf16[1,4,2,704,256]{4,3,2,0,1:T(8,128)(2,1)S(1)} %bitcast.38), channel_id=1, replica_groups=mesh['dp'=8,'owner'=4] {'owner'}, dimensions={1} | all-to-all | bytes 5767168 | tf_op jit(solution)/shard_map/all_to_all | solution.py:69
  120.9 0.9 fusion
  121.8 0.5 convert_bitcast_fusion
  122.3 6.2 %copy.33 = f32[1,1,2,704,4,256]{5,4,3,2,1,0:T(4,128)} copy(f32[1,1,2,704,4,256]{5,3,2,4,1,0:T(8,128)S(1)} %convert_bitcast_fusion) | data formatting | bytes 11534336 | tf_op jit(solution)/shard_map/convert_element_type | solution.py:23
  128.5 7.8 %reshape.61 = f32[2,704,1024]{2,1,0:T(8,128)} reshape(f32[1,1,2,704,4,256]{5,4,3,2,1,0:T(4,128)} %copy.33) | data formatting | bytes 11534336 | tf_op jit(solution)/shard_map/convert_element_type | solution.py:23
  136.4 3.5 %divide_convert_fusion = bf16[2,704,1024]{2,1,0:T(8,128)(2,1)S(1)} fusion(f32[2,704,1024]{2,1,0:T(8,128)} %reshape.61, f32[2]{0:T(128)S(1)} %sqrt_add_fusion), kind=kLoop, calls=%fused_computation.7 | loop fusion | flops 2883584 | bytes 8650760 | tf_op jit(solution)/shard_map/convert_element_type | solution.py:23
  139.9 3.8 %fusion.15 = bf16[2,704,704]{2,1,0:T(8,128)(2,1)} fusion(bf16[2,704,1024]{2,1,0:T(8,128)(2,1)S(1)} %divide_convert_fusion), kind=kOutput, calls=%fused_computation.37 | convolution fusion | flops 2030043136 | bytes 4866048 | tf_op jit(solution)/shard_map/sik,sjk->sij/dot_general | solution.py:29
  143.7 8.5 %add_convert_fusion = bf16[2,704,1024]{2,1,0:T(8,128)(2,1)} fusion(bf16[2,704,1024]{2,1,0:T(8,128)(2,1)S(1)} %divide_convert_fusion, bf16[2,704,704]{2,1,0:T(8,128)(2,1)} %fusion.15), kind=kOutput, calls=%fused_computation.6 | convolution fusion | flops 3436421120 | bytes 7749632 | tf_op jit(solution)/shard_map/sij,sjk->sik/dot_general | solution.py:36
  152.1 6.5 %fusion.16 = bf16[2,704,704]{2,1,0:T(8,128)(2,1)} fusion(bf16[2,704,1024]{2,1,0:T(8,128)(2,1)} %add_convert_fusion), kind=kOutput, calls=%fused_computation.38 | convolution fusion | flops 2030043136 | bytes 4866048 | tf_op jit(solution)/shard_map/sik,sjk->sij/dot_general | solution.py:29
  158.6 9.0 %multiply_convert_fusion = bf16[2,704,1024]{2,1,0:T(8,128)(2,1)S(1)} fusion(bf16[2,704,1024]{2,1,0:T(8,128)(2,1)} %add_convert_fusion, bf16[2,704,704]{2,1,0:T(8,128)(2,1)} %fusion.16), kind=kOutput, calls=%fused_computation.5 | convolution fusion | flops 3437862912 | bytes 7749632 | tf_op jit(solution)/shard_map/sij,sjk->sik/dot_general | solution.py:36
  167.6 0.0 copy-start
  167.6 1.6 copy-done
  169.2 3.0 copy.34
  172.1 37.5 %all_to_all.62 = bf16[1,1,2,704,1024]{4,2,1,0,3:T(2,128)(2,1)S(1)} all-to-all(bf16[1,1,2,704,1024]{4,2,1,0,3:T(2,128)(2,1)S(1)} %copy.34), channel_id=1, replica_groups=mesh['dp'=8,'owner'=4] {'dp'}, dimensions={3} | all-to-all | bytes 5767168 | tf_op jit(solution)/shard_map/all_to_all | solution.py:78
  209.6 13.1 %copy.35 = bf16[1,1,2,8,88,1024]{4,2,3,5,1,0:T(2,128)(2,1)} copy(bf16[1,1,2,8,88,1024]{5,2,4,3,1,0:T(2,128)(2,1)S(1)} %bitcast.35) | data formatting | bytes 5767168 | tf_op jit(solution)/shard_map/all_to_all | solution.py:78
  222.7 4.9 %all-to-all-start.3 = ((bf16[8,1,2,88,1024]{3,2,0,1,4:T(2,128)(2,1)}), bf16[8,1,2,88,1024]{3,2,0,1,4:T(2,128)(2,1)}, u32[]{:S(2)}, u32[]{:S(2)}) async-start(bf16[8,1,2,88,1024]{3,2,0,1,4:T(2,128)(2,1)} %bitcast.34), calls=%async_computation.3 | async-start | bytes 8388608 | tf_op jit(solution)/shard_map/all_to_all | solution.py:77
  227.6 92.8 %all-to-all-done.3 = bf16[8,1,2,88,1024]{3,2,0,1,4:T(2,128)(2,1)} async-done(((bf16[8,1,2,88,1024]{3,2,0,1,4:T(2,128)(2,1)}), bf16[8,1,2,88,1024]{3,2,0,1,4:T(2,128)(2,1)}, u32[]{:S(2)}, u32[]{:S(2)}) %all-to-all-start.3) | async-done | bytes 2883616 | tf_op jit(solution)/shard_map/all_to_all | solution.py:77
  320.4 10.2 %copy.38 = bf16[8,1,2,88,4,256]{5,4,3,2,0,1:T(4,128)(2,1)S(1)} copy(bf16[8,1,2,88,4,256]{3,2,0,5,4,1:T(2,128)(2,1)} %bitcast.13) | data formatting | bytes 5767168 | tf_op jit(solution)/shard_map/all_to_all | solution.py:77
  330.6 2.0 copy.37
  332.6 2.5 gather_fusion.1
  335.1 1.3 broadcast_select_fusion
  (6 shorter events, 0.0 us)
Async XLA Ops:
  167.6 1.6 copy-start
  222.7 97.7 %all-to-all-start.3 = ((bf16[8,1,2,88,1024]{3,2,0,1,4:T(2,128)(2,1)}), bf16[8,1,2,88,1024]{3,2,0,1,4:T(2,128)(2,1)}, u32[]{:S(2)}, u32[]{:S(2)}) async-start(bf16[8,1,2,88,1024]{3,2,0,1,4:T(2,128)(2,1)} %bitcast.34), calls=%async_computation.3 | async-start | bytes 8388608 | tf_op jit(solution)/shard_map/all_to_all | solution.py:77
where the time goes:
time: 337 us; the launch traced here: 336 us
  blocking collectives  147 us (44%)
  waiting for transfers between devices  92.8 us (28%)
  local copies, waits for them, and re-layouts  49.1 us (15%)
  matrix products  27.7 us (8%)
  other arithmetic  14.6 us (4%)
  starting transfers between devices  4.86 us (1%)
    all_to_all x1, waiting for transfers between devices, on_device(): lax.all_to_all(lax.all_to_all(owned_stack.reshape(1, 1, CAP, FF, D), 'dp'...  92.8 us
    all_to_all x1, blocking collectives, on_device(): lax.all_to_all(lax.all_to_all(outgoing, 'dp', split_axis=0, concat_axis=3...  69.1 us
    all_to_all x1, blocking collectives, on_device(): lax.all_to_all(outgoing, 'dp', split_axis=0, concat_axis=3, tiled=True)  40 us
    all_to_all x1, blocking collectives, on_device(): lax.all_to_all(owned_stack.reshape(1, 1, CAP, FF, D), 'dp', split_axis=3,...  37.5 us
    dot_general x2, matrix products, orthogonalize(): jnp.einsum('sij,sjk->sik', mixing, current, preferred_element_type=jnp.fl...  17.4 us
    convert_element_type x2, local copies, waits for them, and re-layouts, orthogonalize(): matrices.astype(jnp.float32) / (magnitude[:, None, None] + epsilon)  14 us
    all_to_all x1, local copies, waits for them, and re-layouts, on_device(): lax.all_to_all(owned_stack.reshape(1, 1, CAP, FF, D), 'dp', split_axis=3,...  13.1 us
    all_to_all x2, local copies, waits for them, and re-layouts, on_device(): lax.all_to_all(lax.all_to_all(owned_stack.reshape(1, 1, CAP, FF, D), 'dp'...  12.2 us
  transfers between devices with their start and end apart: 1, of which 1 were waited for; matrix products, arithmetic and copies ran while one was open for 0% of the time, Pallas kernels for 0%

commit v1 on v0

v1 whole, which is shorter than its diff:
```python
import functools
import math

import jax
import jax.numpy as jnp
from jax import lax
from jax.experimental import pallas as pl
from jax.experimental.pallas import tpu as pltpu
from jax.sharding import PartitionSpec as P

ITERS = 2
CAP = 2

coef_a = 3.4445
coef_b = -4.775
coef_c = 2.0315
momentum_beta = 0.95
epsilon = 1e-07

AXES = ("dp", "owner")
VMEM_BYTES = 56 * 1024 * 1024


def round_up(value, multiple):
    return -(-value // multiple) * multiple


def pack_kernel(chunk, owner_ref, g_ref, m_ref, nm_ref, first_ref, second_ref, count_ref):
    step = pl.program_id(0)
    devices = first_ref.shape[0]

    @pl.when(step == 0)
    def _():
        first_ref[...] = jnp.zeros_like(first_ref)
        second_ref[...] = jnp.zeros_like(second_ref)

        @pl.loop(0, devices)
        def _(d):
            count_ref[d] = 0

    for j in range(chunk):
        owner = owner_ref[step * chunk + j]
        rank = count_ref[owner]
        count_ref[owner] = rank + 1
        grad = g_ref[j].astype(jnp.float32)
        new = momentum_beta * m_ref[j] + grad
        nm_ref[j] = new
        nesterov = (grad + momentum_beta * new).astype(jnp.bfloat16)

        @pl.when(rank == 0)
        def _():
            first_ref[owner] = nesterov

        @pl.when(rank == 1)
        def _():
            second_ref[owner] = nesterov


def pack(gradients, momentum, owner_table, devices):
    mats, rows, cols = gradients.shape
    chunk = 8
    block = pl.BlockSpec((chunk, rows, cols), lambda i, table: (i, 0, 0))
    slots = pl.BlockSpec((devices, rows, cols), lambda i, table: (0, 0, 0))
    slot_shape = jax.ShapeDtypeStruct((devices, rows, cols), jnp.bfloat16)
    return pl.pallas_call(
        functools.partial(pack_kernel, chunk),
        grid_spec=pltpu.PrefetchScalarGridSpec(
            num_scalar_prefetch=1,
            grid=(mats // chunk,),
            in_specs=[block, block],
            out_specs=[block, slots, slots],
            scratch_shapes=[pltpu.SMEM((devices,), jnp.int32)],
        ),
        out_shape=[jax.ShapeDtypeStruct(momentum.shape, jnp.float32), slot_shape, slot_shape],
        compiler_params=pltpu.CompilerParams(vmem_limit_bytes=VMEM_BYTES),
        cost_estimate=pl.CostEstimate(
            flops=4 * mats * rows * cols, bytes_accessed=14 * mats * rows * cols, transcendentals=0
        ),
        name="pack",
    )(owner_table, gradients, momentum)


def matmul(lhs, rhs, rhs_dim):
    return lax.dot_general(
        lhs, rhs, (((1,), (rhs_dim,)), ((), ())), preferred_element_type=jnp.float32
    )


def ortho_kernel(row_size, col_size, tile_blocks, *refs):
    x_ref, owned_ref, back_ref, x_s, y_s, gram_s, mix_s = refs[0], *refs[-6:]
    _, rows, cols = x_ref.shape
    padded = round_up(rows, 16)
    tile = padded * tile_blocks
    tiles = row_size // tile_blocks

    total = jnp.zeros((1, cols), jnp.float32)
    for r in range(row_size):
        if padded > rows:
            x_s[r * padded + rows : (r + 1) * padded, :] = jnp.zeros(
                (padded - rows, x_s.shape[1]), x_s.dtype
            )
        for c in range(col_size):
            block = x_ref[r * col_size + c]
            x_s[r * padded : r * padded + rows, c * cols : (c + 1) * cols] = block
            wide = block.astype(jnp.float32)
            total += jnp.sum(wide * wide, axis=0, keepdims=True)
    magnitude = jnp.sqrt(jnp.sum(total, axis=1, keepdims=True))
    inverse = 1.0 / (magnitude + epsilon)
    update_scale = 0.2 * math.sqrt(max(rows * row_size, cols * col_size))

    for iteration in range(ITERS):
        src = x_s if iteration == 0 else y_s
        for t in range(tiles):
            span = slice(t * tile, (t + 1) * tile)
            gram = matmul(src[span, :], src[...], 1)
            if iteration == 0:
                gram = gram * (inverse * inverse)
            gram_s[span, :] = gram.astype(jnp.bfloat16)
        for t in range(tiles):
            span = slice(t * tile, (t + 1) * tile)
            square = matmul(gram_s[span, :], gram_s[...], 0)
            mix_s[span, :] = (
                coef_b * gram_s[span, :].astype(jnp.float32) + coef_c * square
            ).astype(jnp.bfloat16)
        for t in range(tiles):
            span = slice(t * tile, (t + 1) * tile)
            combined = coef_a * src[span, :].astype(jnp.float32) + matmul(
                mix_s[span, :], src[...], 0
            )
            if iteration == 0:
                combined = combined * inverse
            if iteration + 1 < ITERS:
                y_s[span, :] = combined.astype(jnp.bfloat16)
            else:
                result = (update_scale * combined).astype(jnp.bfloat16)
                for j in range(tile_blocks):
                    r = t * tile_blocks + j
                    block = result[j * padded : j * padded + rows, :]
                    owned_ref[0, r * rows : (r + 1) * rows, :] = block
                    for c in range(col_size):
                        back_ref[r * col_size + c] = block[:, c * cols : (c + 1) * cols]


def orthogonalize(arrived, slot, row_size, col_size, owned):
    devices, rows, cols = arrived.shape
    height, width = rows * row_size, cols * col_size
    padded = round_up(rows, 16) * row_size
    tile_blocks = max(row_size // 2, 1)
    whole = pl.BlockSpec((devices, rows, cols), lambda i: (0, 0, 0))
    in_specs, operands, aliases = [whole], [arrived], {}
    if owned is not None:
        in_specs.append(pl.BlockSpec(memory_space=pl.ANY))
        operands.append(owned)
        aliases = {1: 0}
    return pl.pallas_call(
        functools.partial(ortho_kernel, row_size, col_size, tile_blocks),
        grid=(1,),
        in_specs=in_specs,
        out_specs=[pl.BlockSpec((1, height, width), lambda i: (slot, 0, 0)), whole],
        out_shape=[
            jax.ShapeDtypeStruct((CAP, height, width), jnp.bfloat16),
            jax.ShapeDtypeStruct((devices, rows, cols), jnp.bfloat16),
        ],
        scratch_shapes=[
            pltpu.VMEM((padded, width), jnp.bfloat16),
            pltpu.VMEM((padded, width), jnp.bfloat16),
            pltpu.VMEM((padded, padded), jnp.bfloat16),
            pltpu.VMEM((padded, padded), jnp.bfloat16),
        ],
        input_output_aliases=aliases,
        compiler_params=pltpu.CompilerParams(vmem_limit_bytes=VMEM_BYTES),
        cost_estimate=pl.CostEstimate(
            flops=2 * ITERS * padded * padded * (2 * width + padded),
            bytes_accessed=6 * height * width,
            transcendentals=0,
        ),
        name="orthogonalize",
    )(*operands)


def unpack_kernel(owner_ref, first_ref, second_ref, update_ref, count_ref):
    mats = update_ref.shape[0]
    devices = first_ref.shape[0]

    @pl.loop(0, devices)
    def _(d):
        count_ref[d] = 0

    for i in range(mats):
        owner = owner_ref[i]
        rank = count_ref[owner]
        count_ref[owner] = rank + 1

        @pl.when(rank == 0)
        def _():
            update_ref[i] = first_ref[owner]

        @pl.when(rank == 1)
        def _():
            update_ref[i] = second_ref[owner]


def unpack(first, second, owner_table):
    devices, rows, cols = first.shape
    mats = owner_table.shape[0]
    slots = pl.BlockSpec((devices, rows, cols), lambda i, table: (0, 0, 0))
    return pl.pallas_call(
        unpack_kernel,
        grid_spec=pltpu.PrefetchScalarGridSpec(
            num_scalar_prefetch=1,
            grid=(1,),
            in_specs=[slots, slots],
            out_specs=pl.BlockSpec((mats, rows, cols), lambda i, table: (0, 0, 0)),
            scratch_shapes=[pltpu.SMEM((devices,), jnp.int32)],
        ),
        out_shape=jax.ShapeDtypeStruct((mats, rows, cols), jnp.bfloat16),
        compiler_params=pltpu.CompilerParams(vmem_limit_bytes=VMEM_BYTES),
        cost_estimate=pl.CostEstimate(
            flops=0, bytes_accessed=6 * devices * rows * cols, transcendentals=0
        ),
        name="unpack",
    )(owner_table, first, second)


def exchange(blocks):
    return lax.all_to_all(blocks, AXES, split_axis=0, concat_axis=0, tiled=True)


def on_device(gradients, momentum, owner_table):
    row_size = lax.axis_size("dp")
    col_size = lax.axis_size("owner")
    devices = row_size * col_size
    new_momentum, first, second = pack(gradients, momentum, owner_table, devices)
    owned, back_first = orthogonalize(exchange(first), 0, row_size, col_size, None)
    owned, back_second = orthogonalize(exchange(second), 1, row_size, col_size, owned)
    update = unpack(exchange(back_first), exchange(back_second), owner_table)
    return (new_momentum, update, owned)


def solution(mesh):
    return jax.shard_map(
        on_device,
        mesh=mesh,
        in_specs=(P(None, "dp", "owner"), P(None, "dp", "owner"), P()),
        out_specs=(P(None, "dp", "owner"), P(None, "dp", "owner"), P(("dp", "owner"), None, None)),
        check_vma=False,
    )
```

time: 337 us -> 169 us (0.50)
  blocking collectives: 147 us -> 80.7 us
  local copies, waits for them, and re-layouts: 49.1 us -> 1.11 us
  waiting for transfers between devices: 92.8 us -> 46.4 us
  Pallas kernels: 0 us -> 30.5 us
  matrix products: 27.7 us -> 0 us
  other arithmetic: 14.6 us -> 0 us
  starting transfers between devices: 4.86 us -> 8.6 us
    all_to_all x3 -> x2, blocking collectives: 147 us -> 80.7 us  [exchange(): return lax.all_to_all(blocks, AXES, split_axis=0, concat_axis=0, tiled=True)]
    all_to_all x1 -> x2, waiting for transfers between devices: 92.8 us -> 46.4 us  [exchange(): return lax.all_to_all(blocks, AXES, split_axis=0, concat_axis=0, tiled=True)]
    pallas_call x0 -> x4, Pallas kernels: none -> 30.5 us  [the longest x2 19.8 us: orthogonalize(): pl.pallas_call(functools.partial(ortho_kernel, row_size, col_size, tile_b...]
    dot_general x4 -> x0, matrix products: 27.7 us -> none  [the longest x2 17.4 us: orthogonalize(): jnp.einsum('sij,sjk->sik', mixing, current, preferred_element_type=jnp.fl...]
    all_to_all x4 -> x0, local copies, waits for them, and re-layouts: 25.5 us -> none  [the longest x1 13.1 us: on_device(): lax.all_to_all(owned_stack.reshape(1, 1, CAP, FF, D), 'dp', split_axis=3,...]
    convert_element_type x2 -> x0, local copies, waits for them, and re-layouts: 14 us -> none  [orthogonalize(): matrices.astype(jnp.float32) / (magnitude[:, None, None] + epsilon)]
    convert_element_type x3 -> x0, other arithmetic: 8.42 us -> none  [the longest x1 4.39 us: on_device(): (gradients.astype(jnp.float32) + momentum_beta * new_momentum).astype(jnp...]
    gather x2 -> x0, local copies, waits for them, and re-layouts: 4.76 us -> none  [the longest x1 2.46 us: on_device(): jnp.take(returned.reshape(devices * CAP, row_shard, col_shard), slot_inde...]
  transfers between devices with their start and end apart: 1 -> 2, of which waited for: 1 -> 2; matrix products, arithmetic and copies ran while one was open for 0% -> 0% of each run, Pallas kernels for 0% -> 12%
where the time goes in v1:
time: 169 us; the launch traced here: 168 us
  blocking collectives  80.7 us (48%)
  waiting for transfers between devices  46.4 us (27%)
  Pallas kernels  30.5 us (18%)
  starting transfers between devices  8.6 us (5%)
    all_to_all x2, blocking collectives, exchange(): return lax.all_to_all(blocks, AXES, split_axis=0, concat_axis=0, tiled=True)  80.7 us
    all_to_all x2, waiting for transfers between devices, exchange(): return lax.all_to_all(blocks, AXES, split_axis=0, concat_axis=0, tiled=True)  46.4 us
    pallas_call x2, Pallas kernels, orthogonalize(): pl.pallas_call(functools.partial(ortho_kernel, row_size, col_size, tile_b...  19.8 us
    all_to_all x2, starting transfers between devices, exchange(): return lax.all_to_all(blocks, AXES, split_axis=0, concat_axis=0, tiled=True)  8.6 us
    pallas_call x1, Pallas kernels, pack(): pl.pallas_call(functools.partial(pack_kernel, chunk), grid_spec=pltpu.Pre...  6.63 us
    pallas_call x1, Pallas kernels, unpack(): pl.pallas_call(unpack_kernel, grid_spec=pltpu.PrefetchScalarGridSpec(num_...  4.09 us
  transfers between devices with their start and end apart: 2, of which 2 were waited for; matrix products, arithmetic and copies ran while one was open for 0% of the time, Pallas kernels for 12%

profile of v1, /device:TPU:0, one launch (start us, length us, event | category | flops | bytes accessed | tf_op | source)
XLA Modules:
  0.0 168.0 jit_solution(2533063089145605214)
XLA Ops:
  0.6 6.6 %pack.1 = (f32[32,88,256]{2,1,0:T(8,128)}, bf16[32,88,256]{2,1,0:T(8,128)(2,1)}, bf16[32,88,256]{2,1,0:T(8,128)(2,1)}) custom-call(s32[32]{0:T(128)} %owner_ref.3, bf16[32,88,256]{2,1,0:T(8,128)(2,1)} %g_ref.1, f32[32,88,256]{2,1,0:T(8,128)} %m_ref.1), custom_call_target="tpu_custom_call" | custom-call | flops 2883584 | bytes 10092544 | tf_op jit(solution)/shard_map/pack/pallas_call | solution.py:65
  7.3 41.7 %all_to_all.20.refs_0_ = bf16[32,88,256]{2,1,0:T(8,128)(2,1)} all-to-all(bf16[32,88,256]{2,1,0:T(8,128)(2,1)} %get-tuple-element.11), channel_id=1, replica_groups=mesh['dp'=8,'owner'=4] {'dp','owner'}, dimensions={0} | all-to-all | bytes 2883584 | tf_op jit(solution)/shard_map/all_to_all | solution.py:226
  49.0 3.9 %all-to-all-start.2 = ((bf16[32,88,256]{2,1,0:T(8,128)(2,1)}), bf16[32,88,256]{2,1,0:T(8,128)(2,1)S(1)}, u32[]{:S(2)}, u32[]{:S(2)}) async-start(bf16[32,88,256]{2,1,0:T(8,128)(2,1)} %get-tuple-element.13), calls=%async_computation.2 | async-start | bytes 2883584 | tf_op jit(solution)/shard_map/all_to_all | solution.py:226
  52.8 9.9 %orthogonalize.2 = (bf16[2,704,1024]{2,1,0:T(8,128)(2,1)}, bf16[32,88,256]{2,1,0:T(8,128)(2,1)}) custom-call(bf16[32,88,256]{2,1,0:T(8,128)(2,1)} %all_to_all.20.refs_0_), custom_call_target="tpu_custom_call" | custom-call | flops 6643777536 | bytes 4325376 | tf_op jit(solution)/shard_map/orthogonalize/pallas_call | solution.py:155
  62.7 23.3 %all-to-all-done.2.refs_0_ = bf16[32,88,256]{2,1,0:T(8,128)(2,1)S(1)} async-done(((bf16[32,88,256]{2,1,0:T(8,128)(2,1)}), bf16[32,88,256]{2,1,0:T(8,128)(2,1)S(1)}, u32[]{:S(2)}, u32[]{:S(2)}) %all-to-all-start.2) | async-done | bytes 1441824 | tf_op jit(solution)/shard_map/all_to_all | solution.py:226
  86.1 0.0 copy-start.1
  86.1 1.1 copy-done.1
  87.2 4.7 %all-to-all-start.1 = ((bf16[32,88,256]{2,1,0:T(8,128)(2,1)}), bf16[32,88,256]{2,1,0:T(8,128)(2,1)S(1)}, u32[]{:S(2)}, u32[]{:S(2)}) async-start(bf16[32,88,256]{2,1,0:T(8,128)(2,1)} %get-tuple-element.12), calls=%async_computation.1 | async-start | bytes 2883584 | tf_op jit(solution)/shard_map/all_to_all | solution.py:226
  91.9 9.9 %orthogonalize.3 = (bf16[2,704,1024]{2,1,0:T(8,128)(2,1)}, bf16[32,88,256]{2,1,0:T(8,128)(2,1)}) custom-call(bf16[32,88,256]{2,1,0:T(8,128)(2,1)} %copy-done.1, bf16[2,704,1024]{2,1,0:T(8,128)(2,1)} %get-tuple-element.14.refs_1_), custom_call_target="tpu_custom_call", output_to_operand_aliasing={{0}: (1, {})} | custom-call | flops 6643777536 | bytes 4325376 | tf_op jit(solution)/shard_map/orthogonalize/pallas_call | solution.py:155
  101.8 23.1 %all-to-all-done.1.first_ref = bf16[32,88,256]{2,1,0:T(8,128)(2,1)S(1)} async-done(((bf16[32,88,256]{2,1,0:T(8,128)(2,1)}), bf16[32,88,256]{2,1,0:T(8,128)(2,1)S(1)}, u32[]{:S(2)}, u32[]{:S(2)}) %all-to-all-start.1) | async-done | bytes 1441824 | tf_op jit(solution)/shard_map/all_to_all | solution.py:226
  125.0 0.0 copy-start
  125.0 39.0 %all_to_all.21.second_ref = bf16[32,88,256]{2,1,0:T(8,128)(2,1)} all-to-all(bf16[32,88,256]{2,1,0:T(8,128)(2,1)} %get-tuple-element.15), channel_id=1, replica_groups=mesh['dp'=8,'owner'=4] {'dp','owner'}, dimensions={0} | all-to-all | bytes 2883584 | tf_op jit(solution)/shard_map/all_to_all | solution.py:226
  163.9 0.0 copy-done
  163.9 4.1 %unpack.1 = bf16[32,88,256]{2,1,0:T(8,128)(2,1)} custom-call(s32[32]{0:T(128)} %owner_ref.3, bf16[32,88,256]{2,1,0:T(8,128)(2,1)} %copy-done, bf16[32,88,256]{2,1,0:T(8,128)(2,1)} %all_to_all.21.second_ref), custom_call_target="tpu_custom_call" | custom-call | bytes 4325376 | tf_op jit(solution)/shard_map/unpack/pallas_call | solution.py:207
Async XLA Ops:
  49.0 37.1 %all-to-all-start.2 = ((bf16[32,88,256]{2,1,0:T(8,128)(2,1)}), bf16[32,88,256]{2,1,0:T(8,128)(2,1)S(1)}, u32[]{:S(2)}, u32[]{:S(2)}) async-start(bf16[32,88,256]{2,1,0:T(8,128)(2,1)} %get-tuple-element.13), calls=%async_computation.2 | async-start | bytes 2883584 | tf_op jit(solution)/shard_map/all_to_all | solution.py:226
  86.1 1.1 copy-start.1
  87.2 37.8 %all-to-all-start.1 = ((bf16[32,88,256]{2,1,0:T(8,128)(2,1)}), bf16[32,88,256]{2,1,0:T(8,128)(2,1)S(1)}, u32[]{:S(2)}, u32[]{:S(2)}) async-start(bf16[32,88,256]{2,1,0:T(8,128)(2,1)} %get-tuple-element.12), calls=%async_computation.1 | async-start | bytes 2883584 | tf_op jit(solution)/shard_map/all_to_all | solution.py:226
  125.0 39.0 %copy-start = (bf16[32,88,256]{2,1,0:T(8,128)(2,1)}, bf16[32,88,256]{2,1,0:T(8,128)(2,1)S(1)}, u32[]{:S(2)}) copy-start(bf16[32,88,256]{2,1,0:T(8,128)(2,1)S(1)} %all-to-all-done.1.first_ref) | copy-start | bytes 4325380

commit v2 on v1

--- a/solution.py
+++ b/solution.py
@@ -25,33 +25,62 @@
     return -(-value // multiple) * multiple
 
 
-def pack_kernel(chunk, owner_ref, g_ref, m_ref, nm_ref, first_ref, second_ref, count_ref):
+def pack_kernel(
+    chunk, owner_ref, g_ref, m_ref, nm_ref, first_ref, second_ref, host_ref, count_ref, helper_ref
+):
     step = pl.program_id(0)
     devices = first_ref.shape[0]
+    mats = host_ref.shape[0]
 
     @pl.when(step == 0)
     def _():
-        first_ref[...] = jnp.zeros_like(first_ref)
         second_ref[...] = jnp.zeros_like(second_ref)
 
         @pl.loop(0, devices)
         def _(d):
             count_ref[d] = 0
 
+        @pl.loop(0, mats)
+        def _(i):
+            count_ref[owner_ref[i]] = 1
+
+        def list_idle(d, found):
+            helper_ref[found] = d
+            return found + 1 - count_ref[d]
+
+        lax.fori_loop(0, devices, list_idle, 0)
+
+        def list_owners(d, found):
+            owns = count_ref[d]
+            count_ref[d] = found
+            return found + owns
+
+        lax.fori_loop(0, devices, list_owners, 0)
+
+        @pl.loop(0, mats)
+        def _(i):
+            host_ref[i] = -1
+
+        def place(i, _):
+            owner = owner_ref[i]
+            found = count_ref[owner]
+            again = found < 0
+            host_ref[i] = jnp.where(again, helper_ref[jnp.where(again, -1 - found, 0)], owner)
+            count_ref[owner] = jnp.where(again, found, -1 - found)
+            return 0
+
+        lax.fori_loop(0, mats, place, 0)
+
     for j in range(chunk):
         owner = owner_ref[step * chunk + j]
-        rank = count_ref[owner]
-        count_ref[owner] = rank + 1
+        host = host_ref[step * chunk + j]
         grad = g_ref[j].astype(jnp.float32)
         new = momentum_beta * m_ref[j] + grad
         nm_ref[j] = new
         nesterov = (grad + momentum_beta * new).astype(jnp.bfloat16)
-
-        @pl.when(rank == 0)
-        def _():
-            first_ref[owner] = nesterov
-
-        @pl.when(rank == 1)
+        first_ref[host] = nesterov
+
+        @pl.when(host != owner)
         def _():
             second_ref[owner] = nesterov
 
@@ -68,10 +97,18 @@
             num_scalar_prefetch=1,
             grid=(mats // chunk,),
             in_specs=[block, block],
-            out_specs=[block, slots, slots],
-            scratch_shapes=[pltpu.SMEM((devices,), jnp.int32)],
-        ),
-        out_shape=[jax.ShapeDtypeStruct(momentum.shape, jnp.float32), slot_shape, slot_shape],
+            out_specs=[block, slots, slots, pl.BlockSpec(memory_space=pltpu.SMEM)],
+            scratch_shapes=[
+                pltpu.SMEM((devices,), jnp.int32),
+                pltpu.SMEM((devices + 1,), jnp.int32),
+            ],
+        ),
+        out_shape=[
+            jax.ShapeDtypeStruct(momentum.shape, jnp.float32),
+            slot_shape,
+            slot_shape,
+            jax.ShapeDtypeStruct((mats,), jnp.int32),
+        ],
         compiler_params=pltpu.CompilerParams(vmem_limit_bytes=VMEM_BYTES),
         cost_estimate=pl.CostEstimate(
             flops=4 * mats * rows * cols, bytes_accessed=14 * mats * rows * cols, transcendentals=0
@@ -86,8 +123,14 @@
     )
 
 
-def ortho_kernel(row_size, col_size, tile_blocks, *refs):
-    x_ref, owned_ref, back_ref, x_s, y_s, gram_s, mix_s = refs[0], *refs[-6:]
+def ortho_kernel(row_size, col_size, tile_blocks, slot, *refs):
+    owns_ref, x_ref = refs[:2]
+    x_s, y_s, gram_s, mix_s = refs[-4:]
+    if slot == 0:
+        owned_ref, back_ref = refs[2:4]
+    else:
+        owned_ref, back_ref = refs[3], None
+    owns = owns_ref[0] != 0
     _, rows, cols = x_ref.shape
     padded = round_up(rows, 16)
     tile = padded * tile_blocks
@@ -136,31 +179,36 @@
                 for j in range(tile_blocks):
                     r = t * tile_blocks + j
                     block = result[j * padded : j * padded + rows, :]
-                    owned_ref[0, r * rows : (r + 1) * rows, :] = block
-                    for c in range(col_size):
-                        back_ref[r * col_size + c] = block[:, c * cols : (c + 1) * cols]
-
-
-def orthogonalize(arrived, slot, row_size, col_size, owned):
+                    owned_ref[0, r * rows : (r + 1) * rows, :] = jnp.where(
+                        owns, block, jnp.zeros_like(block)
+                    )
+                    if back_ref is not None:
+                        for c in range(col_size):
+                            back_ref[r * col_size + c] = block[:, c * cols : (c + 1) * cols]
+
+
+def orthogonalize(owns, arrived, slot, row_size, col_size, owned=None):
     devices, rows, cols = arrived.shape
     height, width = rows * row_size, cols * col_size
     padded = round_up(rows, 16) * row_size
     tile_blocks = max(row_size // 2, 1)
     whole = pl.BlockSpec((devices, rows, cols), lambda i: (0, 0, 0))
-    in_specs, operands, aliases = [whole], [arrived], {}
-    if owned is not None:
+    in_specs, operands, aliases = [pl.BlockSpec(memory_space=pltpu.SMEM), whole], [owns, arrived], {}
+    out_specs = [pl.BlockSpec((1, height, width), lambda i: (slot, 0, 0))]
+    out_shape = [jax.ShapeDtypeStruct((CAP, height, width), jnp.bfloat16)]
+    if slot == 0:
+        out_specs.append(whole)
+        out_shape.append(jax.ShapeDtypeStruct((devices, rows, cols), jnp.bfloat16))
+    else:
         in_specs.append(pl.BlockSpec(memory_space=pl.ANY))
         operands.append(owned)
-        aliases = {1: 0}
+        aliases = {2: 0}
     return pl.pallas_call(
-        functools.partial(ortho_kernel, row_size, col_size, tile_blocks),
+        functools.partial(ortho_kernel, row_size, col_size, tile_blocks, slot),
         grid=(1,),
         in_specs=in_specs,
-        out_specs=[pl.BlockSpec((1, height, width), lambda i: (slot, 0, 0)), whole],
-        out_shape=[
-            jax.ShapeDtypeStruct((CAP, height, width), jnp.bfloat16),
-            jax.ShapeDtypeStruct((devices, rows, cols), jnp.bfloat16),
-        ],
+        out_specs=out_specs,
+        out_shape=out_shape,
         scratch_shapes=[
             pltpu.VMEM((padded, width), jnp.bfloat16),
             pltpu.VMEM((padded, width), jnp.bfloat16),
@@ -178,48 +226,29 @@
     )(*operands)
 
 
-def unpack_kernel(owner_ref, first_ref, second_ref, update_ref, count_ref):
-    mats = update_ref.shape[0]
-    devices = first_ref.shape[0]
-
-    @pl.loop(0, devices)
-    def _(d):
-        count_ref[d] = 0
-
-    for i in range(mats):
-        owner = owner_ref[i]
-        rank = count_ref[owner]
-        count_ref[owner] = rank + 1
-
-        @pl.when(rank == 0)
-        def _():
-            update_ref[i] = first_ref[owner]
-
-        @pl.when(rank == 1)
-        def _():
-            update_ref[i] = second_ref[owner]
-
-
-def unpack(first, second, owner_table):
-    devices, rows, cols = first.shape
-    mats = owner_table.shape[0]
-    slots = pl.BlockSpec((devices, rows, cols), lambda i, table: (0, 0, 0))
+def unpack_kernel(host_ref, back_ref, update_ref):
+    for i in range(update_ref.shape[0]):
+        update_ref[i] = back_ref[host_ref[i]]
+
+
+def unpack(back, host):
+    devices, rows, cols = back.shape
+    mats = host.shape[0]
     return pl.pallas_call(
         unpack_kernel,
         grid_spec=pltpu.PrefetchScalarGridSpec(
             num_scalar_prefetch=1,
             grid=(1,),
-            in_specs=[slots, slots],
+            in_specs=[pl.BlockSpec((devices, rows, cols), lambda i, table: (0, 0, 0))],
             out_specs=pl.BlockSpec((mats, rows, cols), lambda i, table: (0, 0, 0)),
-            scratch_shapes=[pltpu.SMEM((devices,), jnp.int32)],
         ),
         out_shape=jax.ShapeDtypeStruct((mats, rows, cols), jnp.bfloat16),
         compiler_params=pltpu.CompilerParams(vmem_limit_bytes=VMEM_BYTES),
         cost_estimate=pl.CostEstimate(
-            flops=0, bytes_accessed=6 * devices * rows * cols, transcendentals=0
+            flops=0, bytes_accessed=4 * devices * rows * cols, transcendentals=0
         ),
         name="unpack",
-    )(owner_table, first, second)
+    )(host, back)
 
 
 def exchange(blocks):
@@ -230,10 +259,12 @@
     row_size = lax.axis_size("dp")
     col_size = lax.axis_size("owner")
     devices = row_size * col_size
-    new_momentum, first, second = pack(gradients, momentum, owner_table, devices)
-    owned, back_first = orthogonalize(exchange(first), 0, row_size, col_size, None)
-    owned, back_second = orthogonalize(exchange(second), 1, row_size, col_size, owned)
-    update = unpack(exchange(back_first), exchange(back_second), owner_table)
+    me = lax.axis_index("dp") * col_size + lax.axis_index("owner")
+    owns = jnp.any(owner_table == me).astype(jnp.int32).reshape(1)
+    new_momentum, first, second, host = pack(gradients, momentum, owner_table, devices)
+    owned, back = orthogonalize(owns, exchange(first), 0, row_size, col_size)
+    (owned,) = orthogonalize(owns, exchange(second), 1, row_size, col_size, owned)
+    update = unpack(exchange(back), host)
     return (new_momentum, update, owned)
 
 

time: 169 us -> 132 us (0.78)
  blocking collectives: 80.7 us -> 41.7 us
    all_to_all x2 -> x1, blocking collectives: 80.7 us -> 41.7 us  [exchange(): return lax.all_to_all(blocks, AXES, split_axis=0, concat_axis=0, tiled=True)]
  transfers between devices with their start and end apart: 2 -> 2, of which waited for: 2 -> 2; matrix products, arithmetic and copies ran while one was open for 0% -> 0% of each run, Pallas kernels for 12% -> 15%
where the time goes in v2:
time: 132 us; the launch traced here: 130 us
  waiting for transfers between devices  45.6 us (35%)
  blocking collectives  41.7 us (32%)
  Pallas kernels  30.4 us (23%)
  starting transfers between devices  8.6 us (7%)
  local copies, waits for them, and re-layouts  2.24 us (2%)
  between operations  1.32 us (1%)
    all_to_all x2, waiting for transfers between devices, exchange(): return lax.all_to_all(blocks, AXES, split_axis=0, concat_axis=0, tiled=True)  45.6 us
    all_to_all x1, blocking collectives, exchange(): return lax.all_to_all(blocks, AXES, split_axis=0, concat_axis=0, tiled=True)  41.7 us
    pallas_call x2, Pallas kernels, orthogonalize(): pl.pallas_call(functools.partial(ortho_kernel, row_size, col_size, tile_b...  19.4 us
    all_to_all x2, starting transfers between devices, exchange(): return lax.all_to_all(blocks, AXES, split_axis=0, concat_axis=0, tiled=True)  8.6 us
    pallas_call x1, Pallas kernels, pack(): pl.pallas_call(functools.partial(pack_kernel, chunk), grid_spec=pltpu.Pre...  7.76 us
    pallas_call x1, Pallas kernels, unpack(): pl.pallas_call(unpack_kernel, grid_spec=pltpu.PrefetchScalarGridSpec(num_...  3.22 us
  transfers between devices with their start and end apart: 2, of which 2 were waited for; matrix products, arithmetic and copies ran while one was open for 0% of the time, Pallas kernels for 15%

profile of v2, /device:TPU:0, one launch (start us, length us, event | category | flops | bytes accessed | tf_op | source)
XLA Modules:
  0.0 130.5 jit_solution(4225825494962380268)
XLA Ops:
  0.6 7.8 %pack.1 = (f32[32,88,256]{2,1,0:T(8,128)}, bf16[32,88,256]{2,1,0:T(8,128)(2,1)}, bf16[32,88,256]{2,1,0:T(8,128)(2,1)}, s32[32]{0:T(128)}) custom-call(s32[32]{0:T(128)} %owner_ref.1, bf16[32,88,256]{2,1,0:T(8,128)(2,1)} %g_ref.1, f32[32,88,256]{2,1,0:T(8,128)} %m_ref.1), custom_call_target="tpu_custom_call" | custom-call | flops 2883584 | bytes 10092544 | tf_op jit(solution)/shard_map/pack/pallas_call | solution.py:94
  8.4 41.7 %all_to_all.15.refs_1_ = bf16[32,88,256]{2,1,0:T(8,128)(2,1)} all-to-all(bf16[32,88,256]{2,1,0:T(8,128)(2,1)} %get-tuple-element.11), channel_id=1, replica_groups=mesh['dp'=8,'owner'=4] {'dp','owner'}, dimensions={0} | all-to-all | bytes 2883584 | tf_op jit(solution)/shard_map/all_to_all | solution.py:255
  50.1 0.0 copy-start.2
  50.1 3.9 %all-to-all-start.2 = ((bf16[32,88,256]{2,1,0:T(8,128)(2,1)}), bf16[32,88,256]{2,1,0:T(8,128)(2,1)S(1)}, u32[]{:S(2)}, u32[]{:S(2)}) async-start(bf16[32,88,256]{2,1,0:T(8,128)(2,1)} %get-tuple-element.13), calls=%async_computation.2 | async-start | bytes 2883584 | tf_op jit(solution)/shard_map/all_to_all | solution.py:255
  54.0 0.0 copy-done.2
  54.0 0.6 compare_reduce_fusion
  55.3 9.9 %orthogonalize.2 = (bf16[2,704,1024]{2,1,0:T(8,128)(2,1)}, bf16[32,88,256]{2,1,0:T(8,128)(2,1)}) custom-call(s32[1]{0:T(128)} %bitcast.refs_0_, bf16[32,88,256]{2,1,0:T(8,128)(2,1)} %all_to_all.15.refs_1_), custom_call_target="tpu_custom_call" | custom-call | flops 6643777536 | bytes 4325376 | tf_op jit(solution)/shard_map/orthogonalize/pallas_call | solution.py:206
  65.2 22.0 %all-to-all-done.2.refs_1_ = bf16[32,88,256]{2,1,0:T(8,128)(2,1)S(1)} async-done(((bf16[32,88,256]{2,1,0:T(8,128)(2,1)}), bf16[32,88,256]{2,1,0:T(8,128)(2,1)S(1)}, u32[]{:S(2)}, u32[]{:S(2)}) %all-to-all-start.2) | async-done | bytes 1441824 | tf_op jit(solution)/shard_map/all_to_all | solution.py:255
  87.2 0.0 copy-start.1
  87.2 1.1 copy-done.1
  88.3 4.7 %all-to-all-start.1 = ((bf16[32,88,256]{2,1,0:T(8,128)(2,1)}), bf16[32,88,256]{2,1,0:T(8,128)(2,1)S(1)}, u32[]{:S(2)}, u32[]{:S(2)}) async-start(bf16[32,88,256]{2,1,0:T(8,128)(2,1)} %get-tuple-element.12), calls=%async_computation.1 | async-start | bytes 2883584 | tf_op jit(solution)/shard_map/all_to_all | solution.py:255
  93.1 9.4 %orthogonalize.3 = bf16[2,704,1024]{2,1,0:T(8,128)(2,1)} custom-call(s32[1]{0:T(128)} %bitcast.refs_0_, bf16[32,88,256]{2,1,0:T(8,128)(2,1)} %copy-done.1, bf16[2,704,1024]{2,1,0:T(8,128)(2,1)} %get-tuple-element.14.refs_2_), custom_call_target="tpu_custom_call", output_to_operand_aliasing={{}: (2, {})} | custom-call | flops 6643777536 | bytes 4325376 | tf_op jit(solution)/shard_map/orthogonalize/pallas_call | solution.py:206
  102.5 23.6 %all-to-all-done.1.back_ref = bf16[32,88,256]{2,1,0:T(8,128)(2,1)S(1)} async-done(((bf16[32,88,256]{2,1,0:T(8,128)(2,1)}), bf16[32,88,256]{2,1,0:T(8,128)(2,1)S(1)}, u32[]{:S(2)}, u32[]{:S(2)}) %all-to-all-start.1) | async-done | bytes 1441824 | tf_op jit(solution)/shard_map/all_to_all | solution.py:255
  126.1 0.0 copy-start
  126.1 1.1 copy-done
  127.2 3.2 %unpack.1 = bf16[32,88,256]{2,1,0:T(8,128)(2,1)} custom-call(s32[32]{0:T(128)} %get-tuple-element.10.host_ref, bf16[32,88,256]{2,1,0:T(8,128)(2,1)} %copy-done), custom_call_target="tpu_custom_call" | custom-call | bytes 2883584 | tf_op jit(solution)/shard_map/unpack/pallas_call | solution.py:237
Async XLA Ops:
  50.1 3.9 %copy-start.2 = (s32[32]{0:T(128)S(1)}, s32[32]{0:T(128)}, u32[]{:S(2)}) copy-start(s32[32]{0:T(128)} %owner_ref.1) | copy-start | bytes 388
  50.1 37.1 %all-to-all-start.2 = ((bf16[32,88,256]{2,1,0:T(8,128)(2,1)}), bf16[32,88,256]{2,1,0:T(8,128)(2,1)S(1)}, u32[]{:S(2)}, u32[]{:S(2)}) async-start(bf16[32,88,256]{2,1,0:T(8,128)(2,1)} %get-tuple-element.13), calls=%async_computation.2 | async-start | bytes 2883584 | tf_op jit(solution)/shard_map/all_to_all | solution.py:255
  87.2 1.1 copy-start.1
  88.3 37.8 %all-to-all-start.1 = ((bf16[32,88,256]{2,1,0:T(8,128)(2,1)}), bf16[32,88,256]{2,1,0:T(8,128)(2,1)S(1)}, u32[]{:S(2)}, u32[]{:S(2)}) async-start(bf16[32,88,256]{2,1,0:T(8,128)(2,1)} %get-tuple-element.12), calls=%async_computation.1 | async-start | bytes 2883584 | tf_op jit(solution)/shard_map/all_to_all | solution.py:255
  126.1 1.1 copy-start

commit v3 on v2

v3 whole, which is shorter than its diff:
```python
import functools
import math

import jax
import jax.numpy as jnp
from jax import lax
from jax.experimental import pallas as pl
from jax.experimental.pallas import tpu as pltpu
from jax.sharding import PartitionSpec as P

ITERS = 2
CAP = 2

coef_a = 3.4445
coef_b = -4.775
coef_c = 2.0315
momentum_beta = 0.95
epsilon = 1e-07

AXES = ("dp", "owner")
VMEM_BYTES = 56 * 1024 * 1024
PARAMS = pltpu.CompilerParams(vmem_limit_bytes=VMEM_BYTES)
SMEM = pl.BlockSpec(memory_space=pltpu.SMEM)

NOTHING, SINGLE, PAIRED = 0, 1, 2


def round_up(value, multiple):
    return -(-value // multiple) * multiple


def whole(shape):
    return pl.BlockSpec(shape, lambda *_: (0,) * len(shape))


def nesterov_of(grad_ref, momentum_ref, j):
    grad = grad_ref[j].astype(jnp.float32)
    new = momentum_beta * momentum_ref[j] + grad
    return new, (grad + momentum_beta * new).astype(jnp.bfloat16)


def pack_kernel(
    chunk, col_size, owner_ref, g_ref, m_ref, first_ref, host_ref, kind_ref, most_ref,
    idle_ref, helper_ref, layer_ref,
):
    step = pl.program_id(0)
    devices = first_ref.shape[0]
    mats = host_ref.shape[0]

    @pl.when(step == 0)
    def _():
        @pl.loop(0, devices)
        def _(d):
            kind_ref[d] = 0

        @pl.loop(0, col_size)
        def _(z):
            layer_ref[z] = 0

        @pl.loop(0, mats)
        def _(i):
            kind_ref[owner_ref[i]] = 1

        def list_idle(d, found):
            idle_ref[found] = d
            taken = kind_ref[d] + kind_ref[d ^ col_size]
            return found + jnp.where(taken == 0, 1, 0)

        lax.fori_loop(0, devices, list_idle, 0)

        def plan_chip(k, carry):
            found, most = carry
            low = (k // col_size) * 2 * col_size + k % col_size
            high = low + col_size
            owns_low, owns_high = kind_ref[low], kind_ref[high]
            paired = owns_low + owns_high == 2
            z = k % col_size
            place = layer_ref[z]
            layer_ref[z] = jnp.where(paired, place + 2, place)
            kind_ref[low] = jnp.where(paired, PAIRED + place, owns_low)
            kind_ref[high] = jnp.where(paired, PAIRED + place + 1, owns_high)
            helper_ref[low] = jnp.where(paired, idle_ref[found], high)
            helper_ref[high] = jnp.where(paired, idle_ref[found + 1], low)
            return jnp.where(paired, found + 2, found), jnp.maximum(most, layer_ref[z])

        _, most = lax.fori_loop(0, devices // 2, plan_chip, (0, 0))
        most_ref[0] = most

        def place_matrix(i, _):
            owner = owner_ref[i]
            helper = helper_ref[owner]
            again = helper < 0
            host_ref[i] = jnp.where(again, -1 - helper, owner)
            helper_ref[owner] = -1 - helper
            return 0

        lax.fori_loop(0, mats, place_matrix, 0)

    for j in range(chunk):
        _, nesterov = nesterov_of(g_ref, m_ref, j)
        first_ref[host_ref[step * chunk + j]] = nesterov


def pack(gradients, momentum, owner_table, devices, col_size):
    mats, rows, cols = gradients.shape
    chunk = 8
    block = pl.BlockSpec((chunk, rows, cols), lambda i, *_: (i, 0, 0))
    return pl.pallas_call(
        functools.partial(pack_kernel, chunk, col_size),
        grid_spec=pltpu.PrefetchScalarGridSpec(
            num_scalar_prefetch=1,
            grid=(mats // chunk,),
            in_specs=[block, block],
            out_specs=[whole((devices, rows, cols)), SMEM, SMEM, SMEM],
            scratch_shapes=[
                pltpu.SMEM((devices + 1,), jnp.int32),
                pltpu.SMEM((devices,), jnp.int32),
                pltpu.SMEM((col_size,), jnp.int32),
            ],
        ),
        out_shape=[
            jax.ShapeDtypeStruct((devices, rows, cols), jnp.bfloat16),
            jax.ShapeDtypeStruct((mats,), jnp.int32),
            jax.ShapeDtypeStruct((devices,), jnp.int32),
            jax.ShapeDtypeStruct((1,), jnp.int32),
        ],
        compiler_params=PARAMS,
        cost_estimate=pl.CostEstimate(
            flops=4 * mats * rows * cols, bytes_accessed=8 * mats * rows * cols, transcendentals=0
        ),
        name="pack",
    )(owner_table, gradients, momentum)


def momentum_kernel(
    chunk, col_size, room, owner_ref, host_ref, kind_ref, g_ref, m_ref, nm_ref, *refs
):
    near_refs, far_ref, held = refs[:col_size], refs[col_size], refs[col_size + 1]
    step = pl.program_id(0)
    here = lax.axis_index("owner")
    for j in range(chunk):
        new, nesterov = nesterov_of(g_ref, m_ref, j)
        nm_ref[j] = new
        owner = owner_ref[step * chunk + j]
        place = kind_ref[owner] - PAIRED
        second = (host_ref[step * chunk + j] != owner) & (place >= 0)
        layer = owner % col_size

        @pl.when(second & (place < room))
        def _():
            held[(layer ^ here) * room + place] = nesterov

        @pl.when(second & (place >= room))
        def _():
            far_ref[layer * room + place - room] = nesterov

    @pl.when(step == pl.num_programs(0) - 1)
    def _():
        for offset in range(col_size):
            near_refs[offset][...] = held[offset * room : (offset + 1) * room]


def update_momentum(gradients, momentum, owner_table, host, kind, col_size, room):
    mats, rows, cols = gradients.shape
    chunk = 8
    block = pl.BlockSpec((chunk, rows, cols), lambda i, *_: (i, 0, 0))
    near = jax.ShapeDtypeStruct((room, rows, cols), jnp.bfloat16)
    far = jax.ShapeDtypeStruct((col_size * room, rows, cols), jnp.bfloat16)
    new_momentum, *near, far = pl.pallas_call(
        functools.partial(momentum_kernel, chunk, col_size, room),
        grid_spec=pltpu.PrefetchScalarGridSpec(
            num_scalar_prefetch=3,
            grid=(mats // chunk,),
            in_specs=[block, block],
            out_specs=[block] + [whole(near.shape)] * col_size + [whole(far.shape)],
            scratch_shapes=[pltpu.VMEM(far.shape, jnp.bfloat16)],
        ),
        out_shape=[jax.ShapeDtypeStruct(momentum.shape, jnp.float32)] + [near] * col_size + [far],
        compiler_params=PARAMS,
        cost_estimate=pl.CostEstimate(
            flops=4 * mats * rows * cols, bytes_accessed=12 * mats * rows * cols, transcendentals=0
        ),
        name="update_momentum",
    )(owner_table, host, kind, gradients, momentum)
    return new_momentum, near, far


def forward_kernel(col_size, row_size, room, kind_ref, *refs):
    near_refs, far_ref, out_refs = refs[:col_size], refs[col_size], refs[col_size + 1 :]
    row, col = lax.axis_index("dp"), lax.axis_index("owner")
    for offset in range(row_size):
        place = jnp.maximum(kind_ref[(row ^ offset) * col_size + col] - PAIRED, 0)

        @pl.when(place < room)
        def _():
            for z in range(col_size):
                out_refs[offset][col ^ z] = near_refs[z][place]

        @pl.when(place >= room)
        def _():
            for z in range(col_size):
                out_refs[offset][z] = far_ref[z * room + place - room]


def forward(kind, near, far, row_size, col_size, room):
    _, rows, cols = far.shape
    out = jax.ShapeDtypeStruct((col_size, rows, cols), jnp.bfloat16)
    return pl.pallas_call(
        functools.partial(forward_kernel, col_size, row_size, room),
        grid=(1,),
        in_specs=[SMEM] + [whole(near[0].shape)] * col_size + [whole(far.shape)],
        out_specs=[whole(out.shape)] * row_size,
        out_shape=[out] * row_size,
        compiler_params=PARAMS,
        cost_estimate=pl.CostEstimate(
            flops=0, bytes_accessed=8 * col_size * room * rows * cols, transcendentals=0
        ),
        name="forward",
    )(kind, *near, far)


def matmul(lhs, rhs, rhs_dim):
    return lax.dot_general(
        lhs, rhs, (((1,), (rhs_dim,)), ((), ())), preferred_element_type=jnp.float32
    )


def newton_schulz(rows, cols, row_size, col_size, x_s, y_s, gram_s, mix_s, write):
    padded = round_up(rows, 16)
    tile_blocks = max(row_size // 2, 1)
    tile = padded * tile_blocks
    tiles = row_size // tile_blocks

    total = jnp.zeros((1, cols), jnp.float32)
    for r in range(row_size):
        for c in range(col_size):
            wide = x_s[r * padded : (r + 1) * padded, c * cols : (c + 1) * cols]
            wide = wide.astype(jnp.float32)
            total += jnp.sum(wide * wide, axis=0, keepdims=True)
    magnitude = jnp.sqrt(jnp.sum(total, axis=1, keepdims=True))
    inverse = 1.0 / (magnitude + epsilon)
    update_scale = 0.2 * math.sqrt(max(rows * row_size, cols * col_size))

    for iteration in range(ITERS):
        src = x_s if iteration == 0 else y_s
        for t in range(tiles):
            span = slice(t * tile, (t + 1) * tile)
            gram = matmul(src[span, :], src[...], 1)
            if iteration == 0:
                gram = gram * (inverse * inverse)
            gram_s[span, :] = gram.astype(jnp.bfloat16)
        for t in range(tiles):
            span = slice(t * tile, (t + 1) * tile)
            square = matmul(gram_s[span, :], gram_s[...], 0)
            mix_s[span, :] = (
                coef_b * gram_s[span, :].astype(jnp.float32) + coef_c * square
            ).astype(jnp.bfloat16)
        for t in range(tiles):
            span = slice(t * tile, (t + 1) * tile)
            combined = coef_a * src[span, :].astype(jnp.float32) + matmul(
                mix_s[span, :], src[...], 0
            )
            if iteration == 0:
                combined = combined * inverse
            if iteration + 1 < ITERS:
                y_s[span, :] = combined.astype(jnp.bfloat16)
            else:
                result = (update_scale * combined).astype(jnp.bfloat16)
                for j in range(tile_blocks):
                    write(t * tile_blocks + j, result[j * padded : j * padded + rows, :])


def clear_padding(x_s, rows, row_size):
    padded = round_up(rows, 16)
    if padded > rows:
        for r in range(row_size):
            x_s[r * padded + rows : (r + 1) * padded, :] = jnp.zeros(
                (padded - rows, x_s.shape[1]), x_s.dtype
            )


def gather_blocks(x_ref, x_s, row_size, col_size):
    _, rows, cols = x_ref.shape
    padded = round_up(rows, 16)
    for r in range(row_size):
        for c in range(col_size):
            x_s[r * padded : r * padded + rows, c * cols : (c + 1) * cols] = x_ref[
                r * col_size + c
            ]


def hosted_kernel(row_size, col_size, kind_ref, x_ref, owned_ref, back_ref, *scratch):
    _, rows, cols = x_ref.shape
    me = lax.axis_index("dp") * col_size + lax.axis_index("owner")
    owns = kind_ref[me] != NOTHING
    clear_padding(scratch[0], rows, row_size)
    gather_blocks(x_ref, scratch[0], row_size, col_size)

    def write(r, block):
        owned_ref[0, r * rows : (r + 1) * rows, :] = jnp.where(owns, block, jnp.zeros_like(block))
        for c in range(col_size):
            back_ref[r * col_size + c] = block[:, c * cols : (c + 1) * cols]

    newton_schulz(rows, cols, row_size, col_size, *scratch, write)


def second_kernel(row_size, col_size, kind_ref, shared_ref, *refs):
    row_refs, owned_ref, scratch = refs[:row_size], refs[row_size + 1], refs[row_size + 2 :]
    x_s = scratch[0]
    _, rows, cols = shared_ref.shape
    padded = round_up(rows, 16)
    row = lax.axis_index("dp")
    kind = kind_ref[row * col_size + lax.axis_index("owner")]
    clear_padding(x_s, rows, row_size)

    @pl.when(kind < PAIRED)
    def _():
        gather_blocks(shared_ref, x_s, row_size, col_size)

    @pl.when(kind >= PAIRED)
    def _():
        for offset in range(row_size):
            start = pl.multiple_of((row ^ offset) * padded, 16)
            for c in range(col_size):
                x_s[pl.ds(start, rows), c * cols : (c + 1) * cols] = row_refs[offset][c]

    def write(r, block):
        owned_ref[0, r * rows : (r + 1) * rows, :] = jnp.where(
            kind != NOTHING, block, jnp.zeros_like(block)
        )

    newton_schulz(rows, cols, row_size, col_size, *scratch, write)


def ortho_scratch(rows, cols, row_size, col_size):
    padded, width = round_up(rows, 16) * row_size, cols * col_size
    return [
        pltpu.VMEM((padded, width), jnp.bfloat16),
        pltpu.VMEM((padded, width), jnp.bfloat16),
        pltpu.VMEM((padded, padded), jnp.bfloat16),
        pltpu.VMEM((padded, padded), jnp.bfloat16),
    ]


def ortho_cost(rows, cols, row_size, col_size):
    padded, width = round_up(rows, 16) * row_size, cols * col_size
    return pl.CostEstimate(
        flops=2 * ITERS * padded * padded * (2 * width + padded),
        bytes_accessed=6 * padded * width,
        transcendentals=0,
    )


def orthogonalize_hosted(kind, arrived, row_size, col_size):
    devices, rows, cols = arrived.shape
    height, width = rows * row_size, cols * col_size
    return pl.pallas_call(
        functools.partial(hosted_kernel, row_size, col_size),
        grid=(1,),
        in_specs=[SMEM, whole(arrived.shape)],
        out_specs=[whole((1, height, width)), whole(arrived.shape)],
        out_shape=[
            jax.ShapeDtypeStruct((CAP, height, width), jnp.bfloat16),
            jax.ShapeDtypeStruct(arrived.shape, jnp.bfloat16),
        ],
        scratch_shapes=ortho_scratch(rows, cols, row_size, col_size),
        compiler_params=PARAMS,
        cost_estimate=ortho_cost(rows, cols, row_size, col_size),
        name="orthogonalize_hosted",
    )(kind, arrived)


def orthogonalize_second(kind, shared, by_row, owned, row_size, col_size):
    devices, rows, cols = shared.shape
    height, width = rows * row_size, cols * col_size
    return pl.pallas_call(
        functools.partial(second_kernel, row_size, col_size),
        grid=(1,),
        in_specs=[SMEM, whole(shared.shape)]
        + [whole(by_row[0].shape)] * row_size
        + [pl.BlockSpec(memory_space=pl.ANY)],
        out_specs=pl.BlockSpec((1, height, width), lambda i: (1, 0, 0)),
        out_shape=jax.ShapeDtypeStruct((CAP, height, width), jnp.bfloat16),
        scratch_shapes=ortho_scratch(rows, cols, row_size, col_size),
        input_output_aliases={2 + row_size: 0},
        compiler_params=PARAMS,
        cost_estimate=ortho_cost(rows, cols, row_size, col_size),
        name="orthogonalize_second",
    )(kind, shared, *by_row, owned)


def unpack_kernel(host_ref, back_ref, update_ref, sems):
    mats = update_ref.shape[0]

    def copy(i):
        return pltpu.make_async_copy(back_ref.at[host_ref[i]], update_ref.at[i], sems.at[i])

    @pl.loop(0, mats)
    def _(i):
        copy(i).start()

    @pl.loop(0, mats)
    def _(i):
        copy(i).wait()


def unpack(back, host):
    devices, rows, cols = back.shape
    mats = host.shape[0]
    return pl.pallas_call(
        unpack_kernel,
        grid_spec=pltpu.PrefetchScalarGridSpec(
            num_scalar_prefetch=1,
            grid=(1,),
            in_specs=[pl.BlockSpec(memory_space=pl.ANY)],
            out_specs=pl.BlockSpec(memory_space=pl.ANY),
            scratch_shapes=[pltpu.SemaphoreType.DMA((mats,))],
        ),
        out_shape=jax.ShapeDtypeStruct((mats, rows, cols), jnp.bfloat16),
        compiler_params=PARAMS,
        cost_estimate=pl.CostEstimate(
            flops=0, bytes_accessed=4 * mats * rows * cols, transcendentals=0
        ),
        name="unpack",
    )(host, back)


def exchange(blocks):
    return lax.all_to_all(blocks, AXES, split_axis=0, concat_axis=0, tiled=True)


def swap(block, axis, offset):
    size = lax.axis_size(axis)
    return lax.ppermute(block, axis, [(i, i ^ offset) for i in range(size)])


def on_device(gradients, momentum, owner_table):
    row_size = lax.axis_size("dp")
    col_size = lax.axis_size("owner")
    devices = row_size * col_size
    room = max(row_size // 2, 1)

    first, host, kind, most = pack(gradients, momentum, owner_table, devices, col_size)
    arrived = exchange(first)
    new_momentum, near, far = update_momentum(
        gradients, momentum, owner_table, host, kind, col_size, room
    )
    far = lax.cond(
        most[0] > room,
        lambda blocks: lax.all_to_all(blocks, "owner", split_axis=0, concat_axis=0, tiled=True),
        lambda blocks: blocks,
        far,
    )

    arrived, near = lax.optimization_barrier((arrived, near))
    near = [near[0]] + [swap(near[z], "owner", z) for z in range(1, col_size)]
    shared = swap(arrived, "dp", 1)
    owned, back = orthogonalize_hosted(kind, arrived, row_size, col_size)
    returned = exchange(back)
    by_row = forward(kind, near, far, row_size, col_size, room)
    by_row = [by_row[0]] + [swap(by_row[r], "dp", r) for r in range(1, row_size)]
    owned = orthogonalize_second(kind, shared, by_row, owned, row_size, col_size)
    update = unpack(returned, host)
    return (new_momentum, update, owned)


def solution(mesh):
    return jax.shard_map(
        on_device,
        mesh=mesh,
        in_specs=(P(None, "dp", "owner"), P(None, "dp", "owner"), P()),
        out_specs=(P(None, "dp", "owner"), P(None, "dp", "owner"), P(("dp", "owner"), None, None)),
        check_vma=False,
    )
```

time: 132 us -> 198 us (1.50)
  Pallas kernels: 30.4 us -> 79.1 us
  starting transfers between devices: 8.6 us -> 17.5 us
  waiting for transfers between devices: 45.6 us -> 52.9 us
    ppermute x0 -> x11, waiting for transfers between devices: none -> 52.9 us  [swap(): return lax.ppermute(block, axis, [(i, i ^ offset) for i in range(size)])]
    all_to_all x2 -> x1, waiting for transfers between devices: 45.6 us -> 0.01 us  [exchange(): return lax.all_to_all(blocks, AXES, split_axis=0, concat_axis=0, tiled=True)]
    pallas_call x1, Pallas kernels: 3.22 us -> 45.7 us  [unpack(): pl.pallas_call(unpack_kernel, grid_spec=pltpu.PrefetchScalarGridSpec(num_...]
    ppermute x0 -> x11, starting transfers between devices: none -> 13.6 us  [swap(): return lax.ppermute(block, axis, [(i, i ^ offset) for i in range(size)])]
    pallas_call x3 -> x5, Pallas kernels: 27.1 us -> 33.4 us  [the longest x1 10.3 us: orthogonalize_second(): pl.pallas_call(functools.partial(second_kernel, row_size, col_size), grid...]
    all_to_all x2 -> x1, starting transfers between devices: 8.6 us -> 3.87 us  [exchange(): return lax.all_to_all(blocks, AXES, split_axis=0, concat_axis=0, tiled=True)]
  transfers between devices with their start and end apart: 2 -> 12, of which waited for: 2 -> 5; matrix products, arithmetic and copies ran while one was open for 0% -> 0% of each run, Pallas kernels for 15% -> 7%
where the time goes in v3:
time: 198 us; the launch traced here: 197 us
  Pallas kernels  79.1 us (40%)
  waiting for transfers between devices  52.9 us (27%)
  blocking collectives  41.7 us (21%)
  starting transfers between devices  17.5 us (9%)
  local copies, waits for them, and re-layouts  3.68 us (2%)
    ppermute x11, waiting for transfers between devices, swap(): return lax.ppermute(block, axis, [(i, i ^ offset) for i in range(size)])  52.9 us
    pallas_call x1, Pallas kernels, unpack(): pl.pallas_call(unpack_kernel, grid_spec=pltpu.PrefetchScalarGridSpec(num_...  45.7 us
    all_to_all x1, blocking collectives, exchange(): return lax.all_to_all(blocks, AXES, split_axis=0, concat_axis=0, tiled=True)  41.7 us
    ppermute x11, starting transfers between devices, swap(): return lax.ppermute(block, axis, [(i, i ^ offset) for i in range(size)])  13.6 us
    pallas_call x1, Pallas kernels, orthogonalize_second(): pl.pallas_call(functools.partial(second_kernel, row_size, col_size), grid...  10.3 us
    pallas_call x1, Pallas kernels, orthogonalize_hosted(): pl.pallas_call(functools.partial(hosted_kernel, row_size, col_size), grid...  9.93 us
    pallas_call x1, Pallas kernels, update_momentum(): pl.pallas_call(functools.partial(momentum_kernel, chunk, col_size, room),...  5.6 us
    pallas_call x1, Pallas kernels, pack(): pl.pallas_call(functools.partial(pack_kernel, chunk, col_size), grid_spec...  4.99 us
  transfers between devices with their start and end apart: 12, of which 5 were waited for; matrix products, arithmetic and copies ran while one was open for 0% of the time, Pallas kernels for 7%

profile of v3, /device:TPU:0, one launch (start us, length us, event | category | flops | bytes accessed | tf_op | source)
XLA Modules:
  0.0 196.5 jit_solution(4797884223917644040)
XLA Ops:
  0.6 5.0 %pack.1 = (bf16[32,88,256]{2,1,0:T(8,128)(2,1)}, s32[32]{0:T(128)}, s32[32]{0:T(128)}, s32[1]{0:T(128)}) custom-call(s32[32]{0:T(128)} %owner_ref.3, bf16[32,88,256]{2,1,0:T(8,128)(2,1)} %g_ref.3, f32[32,88,256]{2,1,0:T(8,128)} %m_ref.3), custom_call_target="tpu_custom_call" | custom-call | flops 2883584 | bytes 5767168 | tf_op jit(solution)/shard_map/pack/pallas_call | solution.py:108
  6.3 5.6 %update_momentum.1 = (f32[32,88,256]{2,1,0:T(8,128)}, bf16[4,88,256]{2,1,0:T(8,128)(2,1)}, bf16[4,88,256]{2,1,0:T(8,128)(2,1)}, bf16[4,88,256]{2,1,0:T(8,128)(2,...) custom-call(s32[32]{0:T(128)} %owner_ref.3, s32[32]{0:T(128)} %get-tuple-element.33.host_ref, ...), custom_call_target="tpu_custom_call" | custom-call | flops 2883584 | bytes 8650752 | tf_op jit(solution)/shard_map/update_momentum/pallas_call | solution.py:169
  11.9 41.7 %all_to_all.15.x_ref = bf16[32,88,256]{2,1,0:T(8,128)(2,1)} all-to-all(bf16[32,88,256]{2,1,0:T(8,128)(2,1)} %get-tuple-element.36), channel_id=1, replica_groups=mesh['dp'=8,'owner'=4] {'dp','owner'}, dimensions={0} | all-to-all | bytes 2883584 | tf_op jit(solution)/shard_map/all_to_all | solution.py:429
  53.6 9.9 %orthogonalize_hosted.1 = (bf16[2,704,1024]{2,1,0:T(8,128)(2,1)}, bf16[32,88,256]{2,1,0:T(8,128)(2,1)}) custom-call(s32[32]{0:T(128)} %get-tuple-element.34.kind_ref, bf16[32,88,256]{2,1,0:T(8,128)(2,1)} %all_to_all.15.x_ref), custom_call_target="tpu_custom_call" | custom-call | flops 6643777536 | bytes 4718592 | tf_op jit(solution)/shard_map/orthogonalize_hosted/pallas_call | solution.py:357
  63.5 3.9 %all-to-all-start.2 = ((bf16[32,88,256]{2,1,0:T(8,128)(2,1)}), bf16[32,88,256]{2,1,0:T(8,128)(2,1)S(1)}, u32[]{:S(2)}, u32[]{:S(2)}) async-start(bf16[32,88,256]{2,1,0:T(8,128)(2,1)} %get-tuple-element.42), calls=%async_computation.2 | async-start | bytes 2883584 | tf_op jit(solution)/shard_map/all_to_all | solution.py:429
  67.4 0.3 collective-permute-start
  67.7 0.0 copy-done.12
  67.7 1.7 collective-permute-start.1
  69.4 0.0 copy-done.10
  69.4 2.4 %collective-permute-start.2 = (bf16[4,88,256]{2,1,0:T(8,128)(2,1)S(1)}, bf16[4,88,256]{2,1,0:T(8,128)(2,1)S(1)}, u32[]{:S(2)}, u32[]{:S(2)}) collective-permute-start(bf16[4,88,256]{2,1,0:T(8,128)(2,1)S(1)} %copy-done.10), channel_id=1, source_target_pairs={{0,2},{1,3},{2,0},{3,1},{4,6},{5,7},{6,4},{7,5},{8,10},{9,11},{10,... | collective-permute-start | bytes 540680 | tf_op jit(solution)/shard_map/ppermute | solution.py:434
  71.8 0.0 copy-done.9
  71.8 0.3 collective-permute-start.3
  72.1 23.4 %collective-permute-done.1.refs_1_ = bf16[4,88,256]{2,1,0:T(8,128)(2,1)S(1)} collective-permute-done((bf16[4,88,256]{2,1,0:T(8,128)(2,1)S(1)}, bf16[4,88,256]{2,1,0:T(8,128)(2,1)S(1)}, u32[]{:S(2)}, u32[]{:S(2)}) %collective-permute-start.1) | collective-permute-done | bytes 180256 | tf_op jit(solution)/shard_map/ppermute | solution.py:434
  95.5 18.6 %collective-permute-done.2.refs_2_ = bf16[4,88,256]{2,1,0:T(8,128)(2,1)S(1)} collective-permute-done((bf16[4,88,256]{2,1,0:T(8,128)(2,1)S(1)}, bf16[4,88,256]{2,1,0:T(8,128)(2,1)S(1)}, u32[]{:S(2)}, u32[]{:S(2)}) %collective-permute-start.2) | collective-permute-done | bytes 180256 | tf_op jit(solution)/shard_map/ppermute | solution.py:434
  114.1 0.0 collective-permute-done.3.refs_3_
  114.1 0.0 copy-done.1
  114.1 0.6 copy-done.2
  114.8 0.7 copy-done.3
  115.4 2.6 %forward.1 = (bf16[4,88,256]{2,1,0:T(8,128)(2,1)}, bf16[4,88,256]{2,1,0:T(8,128)(2,1)}, bf16[4,88,256]{2,1,0:T(8,128)(2,1)}, bf16[4,88,256]{2,1,0:T(8,128)(2,1)}...) custom-call(s32[32]{0:T(128)} %get-tuple-element.34.kind_ref, ...), custom_call_target="tpu_custom_call" | custom-call | bytes 2883584 | tf_op jit(solution)/shard_map/forward/pallas_call | solution.py:208
  118.0 0.0 collective-permute-start.4
  118.0 1.5 collective-permute-start.5
  119.5 0.3 collective-permute-start.6
  119.9 1.5 collective-permute-start.7
  121.4 0.0 collective-permute-done.4.refs_1_
  121.4 0.2 collective-permute-start.8
  121.6 4.1 %collective-permute-done.5.refs_2_ = bf16[4,88,256]{2,1,0:T(8,128)(2,1)S(1)} collective-permute-done((bf16[4,88,256]{2,1,0:T(8,128)(2,1)}, bf16[4,88,256]{2,1,0:T(8,128)(2,1)S(1)}, u32[]{:S(2)}, u32[]{:S(2)}) %collective-permute-start.5) | collective-permute-done | bytes 180256 | tf_op jit(solution)/shard_map/ppermute | solution.py:434
  125.6 2.4 %collective-permute-start.9 = (bf16[4,88,256]{2,1,0:T(8,128)(2,1)}, bf16[4,88,256]{2,1,0:T(8,128)(2,1)S(1)}, u32[]{:S(2)}, u32[]{:S(2)}) collective-permute-start(bf16[4,88,256]{2,1,0:T(8,128)(2,1)} %get-tuple-element.55), channel_id=1, source_target_pairs={{0,24},{4,28},{8,16},{12,20},{16,8},{20,12},{24,0},{28,4},{1,25},{... | collective-permute-start | bytes 540680 | tf_op jit(solution)/shard_map/ppermute | solution.py:434
  128.0 0.6 collective-permute-done.6.refs_3_
  128.6 3.0 %collective-permute-start.10 = (bf16[4,88,256]{2,1,0:T(8,128)(2,1)}, bf16[4,88,256]{2,1,0:T(8,128)(2,1)S(1)}, u32[]{:S(2)}, u32[]{:S(2)}) collective-permute-start(bf16[4,88,256]{2,1,0:T(8,128)(2,1)} %get-tuple-element.56), channel_id=1, source_target_pairs={{0,28},{4,24},{8,20},{12,16},{16,12},{20,8},{24,4},{28,0},{1,29},{... | collective-permute-start | bytes 540680 | tf_op jit(solution)/shard_map/ppermute | solution.py:434
  131.6 0.0 collective-permute-done.7.refs_4_
  131.6 6.3 %collective-permute-done.8.refs_5_ = bf16[4,88,256]{2,1,0:T(8,128)(2,1)S(1)} collective-permute-done((bf16[4,88,256]{2,1,0:T(8,128)(2,1)}, bf16[4,88,256]{2,1,0:T(8,128)(2,1)S(1)}, u32[]{:S(2)}, u32[]{:S(2)}) %collective-permute-start.8) | collective-permute-done | bytes 180256 | tf_op jit(solution)/shard_map/ppermute | solution.py:434
  137.9 0.0 collective-permute-done.9.refs_6_
  137.9 0.0 collective-permute-done.10.refs_7_
  137.9 0.0 copy-start.14
  137.9 0.0 collective-permute-done.shared_ref
  137.9 0.0 copy-start.4
  137.9 0.0 copy-done.5
  137.9 0.0 copy-done.6
  137.9 0.0 copy-done.7
  137.9 0.0 copy-done.8
  138.0 0.6 copy-done.11
  138.6 0.1 copy-done.13
  138.6 0.1 copy-done.14
  138.7 0.5 copy-done.4
  139.2 10.3 %orthogonalize_second.1 = bf16[2,704,1024]{2,1,0:T(8,128)(2,1)} custom-call(s32[32]{0:T(128)} %get-tuple-element.34.kind_ref, bf16[32,88,256]{2,1,0:T(8,128)(2,1)} %copy-done.4, bf16[4,88,256]{2,1,0:T(8,128)(2,1)} %get-tuple-element.49.refs_0_, bf16[4,88,256]{2,1,0:T(8,128)(2,1)} %copy-done.5, ...), custom_call_target="tpu_custom_call", output_to_operand_aliasing={{}: (10, {})} | custom-call | flops 6643777536 | bytes 4718592 | tf_op jit(solution)/shard_map/orthogonalize_second/pallas_call | solution.py:376
  149.5 0.0 all-to-all-done.2.back_ref
  149.5 1.1 copy-done
  150.6 45.7 %unpack.1 = bf16[32,88,256]{2,1,0:T(8,128)(2,1)} custom-call(s32[32]{0:T(128)} %get-tuple-element.33.host_ref, bf16[32,88,256]{2,1,0:T(8,128)(2,1)} %copy-done), custom_call_target="tpu_custom_call" | custom-call | bytes 2883584 | tf_op jit(solution)/shard_map/unpack/pallas_call | solution.py:410
  (14 shorter events, 0.0 us)
Async XLA Ops:
  63.5 4.2 %copy-start.12 = (bf16[4,88,256]{2,1,0:T(8,128)(2,1)S(1)}, bf16[4,88,256]{2,1,0:T(8,128)(2,1)}, u32[]{:S(2)}) copy-start(bf16[4,88,256]{2,1,0:T(8,128)(2,1)} %get-tuple-element.44) | copy-start | bytes 540676
  63.5 5.9 %copy-start.10 = (bf16[4,88,256]{2,1,0:T(8,128)(2,1)S(1)}, bf16[4,88,256]{2,1,0:T(8,128)(2,1)}, u32[]{:S(2)}) copy-start(bf16[4,88,256]{2,1,0:T(8,128)(2,1)} %get-tuple-element.45) | copy-start | bytes 540676
  63.5 8.3 %copy-start.9 = (bf16[4,88,256]{2,1,0:T(8,128)(2,1)S(1)}, bf16[4,88,256]{2,1,0:T(8,128)(2,1)}, u32[]{:S(2)}) copy-start(bf16[4,88,256]{2,1,0:T(8,128)(2,1)} %get-tuple-element.46) | copy-start | bytes 540676
  63.5 86.0 %all-to-all-start.2 = ((bf16[32,88,256]{2,1,0:T(8,128)(2,1)}), bf16[32,88,256]{2,1,0:T(8,128)(2,1)S(1)}, u32[]{:S(2)}, u32[]{:S(2)}) async-start(bf16[32,88,256]{2,1,0:T(8,128)(2,1)} %get-tuple-element.42), calls=%async_computation.2 | async-start | bytes 2883584 | tf_op jit(solution)/shard_map/all_to_all | solution.py:429
  67.4 70.5 %collective-permute-start = (bf16[32,88,256]{2,1,0:T(8,128)(2,1)}, bf16[32,88,256]{2,1,0:T(8,128)(2,1)S(1)}, u32[]{:S(2)}, u32[]{:S(2)}) collective-permute-start(bf16[32,88,256]{2,1,0:T(8,128)(2,1)} %all_to_all.15.x_ref), channel_id=1, source_target_pairs={{0,4},{4,0},{8,12},{12,8},{16,20},{20,16},{24,28},{28,24},{1,5},{5... | collective-permute-start | bytes 4325384 | tf_op jit(solution)/shard_map/ppermute | solution.py:434
  67.7 27.8 %collective-permute-start.1 = (bf16[4,88,256]{2,1,0:T(8,128)(2,1)S(1)}, bf16[4,88,256]{2,1,0:T(8,128)(2,1)S(1)}, u32[]{:S(2)}, u32[]{:S(2)}) collective-permute-start(bf16[4,88,256]{2,1,0:T(8,128)(2,1)S(1)} %copy-done.12), channel_id=1, source_target_pairs={{0,1},{1,0},{2,3},{3,2},{4,5},{5,4},{6,7},{7,6},{8,9},{9,8},{10,11... | collective-permute-start | bytes 540680 | tf_op jit(solution)/shard_map/ppermute | solution.py:434
  69.4 44.7 %collective-permute-start.2 = (bf16[4,88,256]{2,1,0:T(8,128)(2,1)S(1)}, bf16[4,88,256]{2,1,0:T(8,128)(2,1)S(1)}, u32[]{:S(2)}, u32[]{:S(2)}) collective-permute-start(bf16[4,88,256]{2,1,0:T(8,128)(2,1)S(1)} %copy-done.10), channel_id=1, source_target_pairs={{0,2},{1,3},{2,0},{3,1},{4,6},{5,7},{6,4},{7,5},{8,10},{9,11},{10,... | collective-permute-start | bytes 540680 | tf_op jit(solution)/shard_map/ppermute | solution.py:434
  71.8 42.3 %collective-permute-start.3 = (bf16[4,88,256]{2,1,0:T(8,128)(2,1)S(1)}, bf16[4,88,256]{2,1,0:T(8,128)(2,1)S(1)}, u32[]{:S(2)}, u32[]{:S(2)}) collective-permute-start(bf16[4,88,256]{2,1,0:T(8,128)(2,1)S(1)} %copy-done.9), channel_id=1, source_target_pairs={{0,3},{1,2},{2,1},{3,0},{4,7},{5,6},{6,5},{7,4},{8,11},{9,10},{10,... | collective-permute-start | bytes 540680 | tf_op jit(solution)/shard_map/ppermute | solution.py:434
  95.5 18.6 %copy-start.1 = (bf16[4,88,256]{2,1,0:T(8,128)(2,1)}, bf16[4,88,256]{2,1,0:T(8,128)(2,1)S(1)}, u32[]{:S(2)}) copy-start(bf16[4,88,256]{2,1,0:T(8,128)(2,1)S(1)} %collective-permute-done.1.refs_1_) | copy-start | bytes 540676
  114.1 0.7 copy-start.2
  114.8 0.7 copy-start.3
  118.0 3.3 %collective-permute-start.4 = (bf16[4,88,256]{2,1,0:T(8,128)(2,1)}, bf16[4,88,256]{2,1,0:T(8,128)(2,1)S(1)}, u32[]{:S(2)}, u32[]{:S(2)}) collective-permute-start(bf16[4,88,256]{2,1,0:T(8,128)(2,1)} %get-tuple-element.50), channel_id=1, source_target_pairs={{0,4},{4,0},{8,12},{12,8},{16,20},{20,16},{24,28},{28,24},{1,5},{5... | collective-permute-start | bytes 540680 | tf_op jit(solution)/shard_map/ppermute | solution.py:434
  118.0 7.6 %collective-permute-start.5 = (bf16[4,88,256]{2,1,0:T(8,128)(2,1)}, bf16[4,88,256]{2,1,0:T(8,128)(2,1)S(1)}, u32[]{:S(2)}, u32[]{:S(2)}) collective-permute-start(bf16[4,88,256]{2,1,0:T(8,128)(2,1)} %get-tuple-element.51), channel_id=1, source_target_pairs={{0,8},{4,12},{8,0},{12,4},{16,24},{20,28},{24,16},{28,20},{1,9},{5... | collective-permute-start | bytes 540680 | tf_op jit(solution)/shard_map/ppermute | solution.py:434
  119.5 9.1 %collective-permute-start.6 = (bf16[4,88,256]{2,1,0:T(8,128)(2,1)}, bf16[4,88,256]{2,1,0:T(8,128)(2,1)S(1)}, u32[]{:S(2)}, u32[]{:S(2)}) collective-permute-start(bf16[4,88,256]{2,1,0:T(8,128)(2,1)} %get-tuple-element.52), channel_id=1, source_target_pairs={{0,12},{4,8},{8,4},{12,0},{16,28},{20,24},{24,20},{28,16},{1,13},{... | collective-permute-start | bytes 540680 | tf_op jit(solution)/shard_map/ppermute | solution.py:434
  119.9 11.7 %collective-permute-start.7 = (bf16[4,88,256]{2,1,0:T(8,128)(2,1)}, bf16[4,88,256]{2,1,0:T(8,128)(2,1)S(1)}, u32[]{:S(2)}, u32[]{:S(2)}) collective-permute-start(bf16[4,88,256]{2,1,0:T(8,128)(2,1)} %get-tuple-element.53), channel_id=1, source_target_pairs={{0,16},{4,20},{8,24},{12,28},{16,0},{20,4},{24,8},{28,12},{1,17},{... | collective-permute-start | bytes 540680 | tf_op jit(solution)/shard_map/ppermute | solution.py:434
  121.4 16.6 %copy-start.5 = (bf16[4,88,256]{2,1,0:T(8,128)(2,1)}, bf16[4,88,256]{2,1,0:T(8,128)(2,1)S(1)}, u32[]{:S(2)}) copy-start(bf16[4,88,256]{2,1,0:T(8,128)(2,1)S(1)} %collective-permute-done.4.refs_1_) | copy-start | bytes 540676
  121.4 16.5 %collective-permute-start.8 = (bf16[4,88,256]{2,1,0:T(8,128)(2,1)}, bf16[4,88,256]{2,1,0:T(8,128)(2,1)S(1)}, u32[]{:S(2)}, u32[]{:S(2)}) collective-permute-start(bf16[4,88,256]{2,1,0:T(8,128)(2,1)} %get-tuple-element.54), channel_id=1, source_target_pairs={{0,20},{4,16},{8,28},{12,24},{16,4},{20,0},{24,12},{28,8},{1,21},{... | collective-permute-start | bytes 540680 | tf_op jit(solution)/shard_map/ppermute | solution.py:434
  125.6 12.3 %copy-start.6 = (bf16[4,88,256]{2,1,0:T(8,128)(2,1)}, bf16[4,88,256]{2,1,0:T(8,128)(2,1)S(1)}, u32[]{:S(2)}) copy-start(bf16[4,88,256]{2,1,0:T(8,128)(2,1)S(1)} %collective-permute-done.5.refs_2_) | copy-start | bytes 540676
  125.6 12.3 %collective-permute-start.9 = (bf16[4,88,256]{2,1,0:T(8,128)(2,1)}, bf16[4,88,256]{2,1,0:T(8,128)(2,1)S(1)}, u32[]{:S(2)}, u32[]{:S(2)}) collective-permute-start(bf16[4,88,256]{2,1,0:T(8,128)(2,1)} %get-tuple-element.55), channel_id=1, source_target_pairs={{0,24},{4,28},{8,16},{12,20},{16,8},{20,12},{24,0},{28,4},{1,25},{... | collective-permute-start | bytes 540680 | tf_op jit(solution)/shard_map/ppermute | solution.py:434
  128.6 9.3 %copy-start.7 = (bf16[4,88,256]{2,1,0:T(8,128)(2,1)}, bf16[4,88,256]{2,1,0:T(8,128)(2,1)S(1)}, u32[]{:S(2)}) copy-start(bf16[4,88,256]{2,1,0:T(8,128)(2,1)S(1)} %collective-permute-done.6.refs_3_) | copy-start | bytes 540676
  128.6 9.3 %collective-permute-start.10 = (bf16[4,88,256]{2,1,0:T(8,128)(2,1)}, bf16[4,88,256]{2,1,0:T(8,128)(2,1)S(1)}, u32[]{:S(2)}, u32[]{:S(2)}) collective-permute-start(bf16[4,88,256]{2,1,0:T(8,128)(2,1)} %get-tuple-element.56), channel_id=1, source_target_pairs={{0,28},{4,24},{8,20},{12,16},{16,12},{20,8},{24,4},{28,0},{1,29},{... | collective-permute-start | bytes 540680 | tf_op jit(solution)/shard_map/ppermute | solution.py:434
  131.6 6.3 %copy-start.8 = (bf16[4,88,256]{2,1,0:T(8,128)(2,1)}, bf16[4,88,256]{2,1,0:T(8,128)(2,1)S(1)}, u32[]{:S(2)}) copy-start(bf16[4,88,256]{2,1,0:T(8,128)(2,1)S(1)} %collective-permute-done.7.refs_4_) | copy-start | bytes 540676
  137.9 0.7 copy-start.11
  137.9 0.8 copy-start.13
  137.9 0.8 copy-start.14
  137.9 1.3 copy-start.4
  149.5 1.1 copy-start

commit v4 on v3

--- a/solution.py
+++ b/solution.py
@@ -18,7 +18,7 @@
 epsilon = 1e-07
 
 AXES = ("dp", "owner")
-VMEM_BYTES = 56 * 1024 * 1024
+VMEM_BYTES = 60 * 1024 * 1024
 PARAMS = pltpu.CompilerParams(vmem_limit_bytes=VMEM_BYTES)
 SMEM = pl.BlockSpec(memory_space=pltpu.SMEM)
 
@@ -133,11 +133,9 @@
 
 
 def momentum_kernel(
-    chunk, col_size, room, owner_ref, host_ref, kind_ref, g_ref, m_ref, nm_ref, *refs
+    chunk, col_size, room, owner_ref, host_ref, kind_ref, g_ref, m_ref, nm_ref, near_ref, far_ref
 ):
-    near_refs, far_ref, held = refs[:col_size], refs[col_size], refs[col_size + 1]
     step = pl.program_id(0)
-    here = lax.axis_index("owner")
     for j in range(chunk):
         new, nesterov = nesterov_of(g_ref, m_ref, j)
         nm_ref[j] = new
@@ -148,45 +146,36 @@
 
         @pl.when(second & (place < room))
         def _():
-            held[(layer ^ here) * room + place] = nesterov
+            near_ref[layer * room + place] = nesterov
 
         @pl.when(second & (place >= room))
         def _():
             far_ref[layer * room + place - room] = nesterov
-
-    @pl.when(step == pl.num_programs(0) - 1)
-    def _():
-        for offset in range(col_size):
-            near_refs[offset][...] = held[offset * room : (offset + 1) * room]
 
 
 def update_momentum(gradients, momentum, owner_table, host, kind, col_size, room):
     mats, rows, cols = gradients.shape
     chunk = 8
     block = pl.BlockSpec((chunk, rows, cols), lambda i, *_: (i, 0, 0))
-    near = jax.ShapeDtypeStruct((room, rows, cols), jnp.bfloat16)
-    far = jax.ShapeDtypeStruct((col_size * room, rows, cols), jnp.bfloat16)
-    new_momentum, *near, far = pl.pallas_call(
+    part = jax.ShapeDtypeStruct((col_size * room, rows, cols), jnp.bfloat16)
+    return pl.pallas_call(
         functools.partial(momentum_kernel, chunk, col_size, room),
         grid_spec=pltpu.PrefetchScalarGridSpec(
             num_scalar_prefetch=3,
             grid=(mats // chunk,),
             in_specs=[block, block],
-            out_specs=[block] + [whole(near.shape)] * col_size + [whole(far.shape)],
-            scratch_shapes=[pltpu.VMEM(far.shape, jnp.bfloat16)],
-        ),
-        out_shape=[jax.ShapeDtypeStruct(momentum.shape, jnp.float32)] + [near] * col_size + [far],
+            out_specs=[block, whole(part.shape), whole(part.shape)],
+        ),
+        out_shape=[jax.ShapeDtypeStruct(momentum.shape, jnp.float32), part, part],
         compiler_params=PARAMS,
         cost_estimate=pl.CostEstimate(
             flops=4 * mats * rows * cols, bytes_accessed=12 * mats * rows * cols, transcendentals=0
         ),
         name="update_momentum",
     )(owner_table, host, kind, gradients, momentum)
-    return new_momentum, near, far
-
-
-def forward_kernel(col_size, row_size, room, kind_ref, *refs):
-    near_refs, far_ref, out_refs = refs[:col_size], refs[col_size], refs[col_size + 1 :]
+
+
+def forward_kernel(col_size, row_size, room, kind_ref, near_ref, far_ref, *out_refs):
     row, col = lax.axis_index("dp"), lax.axis_index("owner")
     for offset in range(row_size):
         place = jnp.maximum(kind_ref[(row ^ offset) * col_size + col] - PAIRED, 0)
@@ -194,7 +183,7 @@
         @pl.when(place < room)
         def _():
             for z in range(col_size):
-                out_refs[offset][col ^ z] = near_refs[z][place]
+                out_refs[offset][z] = near_ref[z * room + place]
 
         @pl.when(place >= room)
         def _():
@@ -208,7 +197,7 @@
     return pl.pallas_call(
         functools.partial(forward_kernel, col_size, row_size, room),
         grid=(1,),
-        in_specs=[SMEM] + [whole(near[0].shape)] * col_size + [whole(far.shape)],
+        in_specs=[SMEM, whole(near.shape), whole(far.shape)],
         out_specs=[whole(out.shape)] * row_size,
         out_shape=[out] * row_size,
         compiler_params=PARAMS,
@@ -216,7 +205,7 @@
             flops=0, bytes_accessed=8 * col_size * room * rows * cols, transcendentals=0
         ),
         name="forward",
-    )(kind, *near, far)
+    )(kind, near, far)
 
 
 def matmul(lhs, rhs, rhs_dim):
@@ -389,32 +378,23 @@
     )(kind, shared, *by_row, owned)
 
 
-def unpack_kernel(host_ref, back_ref, update_ref, sems):
-    mats = update_ref.shape[0]
-
-    def copy(i):
-        return pltpu.make_async_copy(back_ref.at[host_ref[i]], update_ref.at[i], sems.at[i])
-
-    @pl.loop(0, mats)
-    def _(i):
-        copy(i).start()
-
-    @pl.loop(0, mats)
-    def _(i):
-        copy(i).wait()
+def unpack_kernel(chunk, host_ref, back_ref, update_ref):
+    step = pl.program_id(0)
+    for j in range(chunk):
+        update_ref[j] = back_ref[host_ref[step * chunk + j]]
 
 
 def unpack(back, host):
     devices, rows, cols = back.shape
     mats = host.shape[0]
-    return pl.pallas_call(
-        unpack_kernel,
+    chunk = 8
+    return pl.pallas_call(
+        functools.partial(unpack_kernel, chunk),
         grid_spec=pltpu.PrefetchScalarGridSpec(
             num_scalar_prefetch=1,
-            grid=(1,),
-            in_specs=[pl.BlockSpec(memory_space=pl.ANY)],
-            out_specs=pl.BlockSpec(memory_space=pl.ANY),
-            scratch_shapes=[pltpu.SemaphoreType.DMA((mats,))],
+            grid=(mats // chunk,),
+            in_specs=[whole(back.shape)],
+            out_specs=pl.BlockSpec((chunk, rows, cols), lambda i, *_: (i, 0, 0)),
         ),
         out_shape=jax.ShapeDtypeStruct((mats, rows, cols), jnp.bfloat16),
         compiler_params=PARAMS,
@@ -425,8 +405,8 @@
     )(host, back)
 
 
-def exchange(blocks):
-    return lax.all_to_all(blocks, AXES, split_axis=0, concat_axis=0, tiled=True)
+def exchange(blocks, axes):
+    return lax.all_to_all(blocks, axes, split_axis=0, concat_axis=0, tiled=True)
 
 
 def swap(block, axis, offset):
@@ -441,22 +421,16 @@
     room = max(row_size // 2, 1)
 
     first, host, kind, most = pack(gradients, momentum, owner_table, devices, col_size)
-    arrived = exchange(first)
+    arrived = exchange(first, AXES)
     new_momentum, near, far = update_momentum(
         gradients, momentum, owner_table, host, kind, col_size, room
     )
-    far = lax.cond(
-        most[0] > room,
-        lambda blocks: lax.all_to_all(blocks, "owner", split_axis=0, concat_axis=0, tiled=True),
-        lambda blocks: blocks,
-        far,
-    )
-
-    arrived, near = lax.optimization_barrier((arrived, near))
-    near = [near[0]] + [swap(near[z], "owner", z) for z in range(1, col_size)]
+    arrived, near, far = lax.optimization_barrier((arrived, near, far))
+    near = exchange(near, "owner")
     shared = swap(arrived, "dp", 1)
     owned, back = orthogonalize_hosted(kind, arrived, row_size, col_size)
-    returned = exchange(back)
+    far = lax.cond(most[0] > room, lambda part: exchange(part, "owner"), lambda part: part, far)
+    returned = exchange(back, AXES)
     by_row = forward(kind, near, far, row_size, col_size, room)
     by_row = [by_row[0]] + [swap(by_row[r], "dp", r) for r in range(1, row_size)]
     owned = orthogonalize_second(kind, shared, by_row, owned, row_size, col_size)

time: 198 us -> 126 us (0.64)
  Pallas kernels: 79.1 us -> 36.9 us
  blocking collectives: 41.7 us -> 0 us
  waiting for transfers between devices: 52.9 us -> 60.5 us
  starting transfers between devices: 17.5 us -> 23.2 us
    pallas_call x1, Pallas kernels: 45.7 us -> 3.68 us  [unpack(): pl.pallas_call(functools.partial(unpack_kernel, chunk), grid_spec=pltpu.P...]
    all_to_all x1 -> x0, blocking collectives: 41.7 us -> none  [exchange(): return lax.all_to_all(blocks, AXES, split_axis=0, concat_axis=0, tiled=True)]
    all_to_all x1 -> x3, waiting for transfers between devices: 0.01 us -> 36.7 us  [exchange(): return lax.all_to_all(blocks, axes, split_axis=0, concat_axis=0, tiled=True)]
    ppermute x11 -> x8, waiting for transfers between devices: 52.9 us -> 23.8 us  [swap(): return lax.ppermute(block, axis, [(i, i ^ offset) for i in range(size)])]
    all_to_all x1 -> x3, starting transfers between devices: 3.87 us -> 14.7 us  [exchange(): return lax.all_to_all(blocks, axes, split_axis=0, concat_axis=0, tiled=True)]
    ppermute x11 -> x8, starting transfers between devices: 13.6 us -> 8.52 us  [swap(): return lax.ppermute(block, axis, [(i, i ^ offset) for i in range(size)])]
  transfers between devices with their start and end apart: 12 -> 11, of which waited for: 5 -> 6; matrix products, arithmetic and copies ran while one was open for 0% -> 0% of each run, Pallas kernels for 7% -> 22%
where the time goes in v4:
time: 126 us
  waiting for transfers between devices  60.5 us (48%)
  Pallas kernels  36.9 us (29%)
  starting transfers between devices  23.2 us (18%)
  local copies, waits for them, and re-layouts  3.73 us (3%)
  between operations  1.38 us (1%)
    all_to_all x3, waiting for transfers between devices, exchange(): return lax.all_to_all(blocks, axes, split_axis=0, concat_axis=0, tiled=True)  36.7 us
    ppermute x8, waiting for transfers between devices, swap(): return lax.ppermute(block, axis, [(i, i ^ offset) for i in range(size)])  23.8 us
    all_to_all x3, starting transfers between devices, exchange(): return lax.all_to_all(blocks, axes, split_axis=0, concat_axis=0, tiled=True)  14.7 us
    pallas_call x1, Pallas kernels, orthogonalize_second(): pl.pallas_call(functools.partial(second_kernel, row_size, col_size), grid...  10.3 us
    pallas_call x1, Pallas kernels, orthogonalize_hosted(): pl.pallas_call(functools.partial(hosted_kernel, row_size, col_size), grid...  9.94 us
    ppermute x8, starting transfers between devices, swap(): return lax.ppermute(block, axis, [(i, i ^ offset) for i in range(size)])  8.52 us
    pallas_call x1, Pallas kernels, update_momentum(): pl.pallas_call(functools.partial(momentum_kernel, chunk, col_size, room),...  5.55 us
    pallas_call x1, Pallas kernels, pack(): pl.pallas_call(functools.partial(pack_kernel, chunk, col_size), grid_spec...  4.99 us
  transfers between devices with their start and end apart: 11, of which 6 were waited for; matrix products, arithmetic and copies ran while one was open for 0% of the time, Pallas kernels for 22%

profile of v4, /device:TPU:0, one launch (start us, length us, event | category | flops | bytes accessed | tf_op | source)
XLA Modules:
  0.0 125.8 jit_solution(13840327997320597489)
XLA Ops:
  0.6 5.0 %pack.1 = (bf16[32,88,256]{2,1,0:T(8,128)(2,1)}, s32[32]{0:T(128)}, s32[32]{0:T(128)}, s32[1]{0:T(128)}) custom-call(s32[32]{0:T(128)} %owner_ref.3, bf16[32,88,256]{2,1,0:T(8,128)(2,1)} %g_ref.3, f32[32,88,256]{2,1,0:T(8,128)} %m_ref.3), custom_call_target="tpu_custom_call" | custom-call | flops 2883584 | bytes 5767168 | tf_op jit(solution)/shard_map/pack/pallas_call | solution.py:108
  5.6 7.3 %all-to-all-start.1 = ((bf16[32,88,256]{2,1,0:T(8,128)(2,1)}), bf16[32,88,256]{2,1,0:T(8,128)(2,1)S(1)}, u32[]{:S(2)}, u32[]{:S(2)}) async-start(bf16[32,88,256]{2,1,0:T(8,128)(2,1)} %get-tuple-element.31), calls=%async_computation.1 | async-start | bytes 2883584 | tf_op jit(solution)/shard_map/all_to_all | solution.py:409
  13.6 5.6 %update_momentum.1 = (f32[32,88,256]{2,1,0:T(8,128)}, bf16[16,88,256]{2,1,0:T(8,128)(2,1)}, bf16[16,88,256]{2,1,0:T(8,128)(2,1)S(1)}) custom-call(s32[32]{0:T(128)} %owner_ref.3, s32[32]{0:T(128)} %get-tuple-element.28.host_ref, s32[32]{0:T(128)} %get-tuple-element.29.kind_ref, bf16[32,88,256]{2,1,0:T(8,128)(2,1)} %g_ref.3, f32[32,88,256]{2,1,0:T(8,128)} %m_ref.3), custom_call_target="tpu_custom_call" | custom-call | flops 2883584 | bytes 8650752 | tf_op jit(solution)/shard_map/update_momentum/pallas_call | solution.py:161
  19.1 27.0 %all-to-all-done.1.x_ref = bf16[32,88,256]{2,1,0:T(8,128)(2,1)S(1)} async-done(((bf16[32,88,256]{2,1,0:T(8,128)(2,1)}), bf16[32,88,256]{2,1,0:T(8,128)(2,1)S(1)}, u32[]{:S(2)}, u32[]{:S(2)}) %all-to-all-start.1) | async-done | bytes 1441824 | tf_op jit(solution)/shard_map/all_to_all | solution.py:409
  46.2 0.0 copy-start.2
  46.2 1.1 copy-done.2
  47.3 4.6 %all-to-all-start.3 = ((bf16[16,88,256]{2,1,0:T(8,128)(2,1)}), bf16[16,88,256]{2,1,0:T(8,128)(2,1)S(1)}, u32[]{:S(2)}, u32[]{:S(2)}) async-start(bf16[16,88,256]{2,1,0:T(8,128)(2,1)} %get-tuple-element.36), calls=%async_computation.3 | async-start | bytes 1441792 | tf_op jit(solution)/shard_map/all_to_all | solution.py:409
  51.9 9.9 %orthogonalize_hosted.1 = (bf16[2,704,1024]{2,1,0:T(8,128)(2,1)}, bf16[32,88,256]{2,1,0:T(8,128)(2,1)}) custom-call(s32[32]{0:T(128)} %get-tuple-element.29.kind_ref, bf16[32,88,256]{2,1,0:T(8,128)(2,1)} %copy-done.2), custom_call_target="tpu_custom_call" | custom-call | flops 6643777536 | bytes 4718592 | tf_op jit(solution)/shard_map/orthogonalize_hosted/pallas_call | solution.py:346
  61.8 9.7 %all-to-all-done.3.near_ref = bf16[16,88,256]{2,1,0:T(8,128)(2,1)S(1)} async-done(((bf16[16,88,256]{2,1,0:T(8,128)(2,1)}), bf16[16,88,256]{2,1,0:T(8,128)(2,1)S(1)}, u32[]{:S(2)}, u32[]{:S(2)}) %all-to-all-start.3) | async-done | bytes 720928 | tf_op jit(solution)/shard_map/all_to_all | solution.py:409
  71.5 0.0 copy-start.1
  71.5 0.9 copy-done.1
  72.4 2.8 %all-to-all-start.2 = ((bf16[32,88,256]{2,1,0:T(8,128)(2,1)}), bf16[32,88,256]{2,1,0:T(8,128)(2,1)S(1)}, u32[]{:S(2)}, u32[]{:S(2)}) async-start(bf16[32,88,256]{2,1,0:T(8,128)(2,1)} %get-tuple-element.35), calls=%async_computation.2 | async-start | bytes 2883584 | tf_op jit(solution)/shard_map/all_to_all | solution.py:409
  75.2 0.3 collective-permute-start
  75.5 2.5 %forward.1 = (bf16[4,88,256]{2,1,0:T(8,128)(2,1)}, bf16[4,88,256]{2,1,0:T(8,128)(2,1)}, bf16[4,88,256]{2,1,0:T(8,128)(2,1)}, bf16[4,88,256]{2,1,0:T(8,128)(2,1)}...) custom-call(s32[32]{0:T(128)} %get-tuple-element.29.kind_ref, ...), custom_call_target="tpu_custom_call" | custom-call | bytes 2883584 | tf_op jit(solution)/shard_map/forward/pallas_call | solution.py:197
  78.0 0.3 collective-permute-start.1
  78.2 1.8 %collective-permute-start.2 = (bf16[4,88,256]{2,1,0:T(8,128)(2,1)}, bf16[4,88,256]{2,1,0:T(8,128)(2,1)S(1)}, u32[]{:S(2)}, u32[]{:S(2)}) collective-permute-start(bf16[4,88,256]{2,1,0:T(8,128)(2,1)} %get-tuple-element.41), channel_id=1, source_target_pairs={{0,8},{4,12},{8,0},{12,4},{16,24},{20,28},{24,16},{28,20},{1,9},{5... | collective-permute-start | bytes 540680 | tf_op jit(solution)/shard_map/ppermute | solution.py:414
  80.0 0.0 collective-permute-start.3
  80.0 1.5 %collective-permute-start.4 = (bf16[4,88,256]{2,1,0:T(8,128)(2,1)}, bf16[4,88,256]{2,1,0:T(8,128)(2,1)S(1)}, u32[]{:S(2)}, u32[]{:S(2)}) collective-permute-start(bf16[4,88,256]{2,1,0:T(8,128)(2,1)} %get-tuple-element.43), channel_id=1, source_target_pairs={{0,16},{4,20},{8,24},{12,28},{16,0},{20,4},{24,8},{28,12},{1,17},{... | collective-permute-start | bytes 540680 | tf_op jit(solution)/shard_map/ppermute | solution.py:414
  81.5 0.0 collective-permute-done.1.refs_1_
  81.5 0.0 copy-start.3
  81.5 0.3 collective-permute-start.5
  81.8 11.2 %collective-permute-done.2.refs_2_ = bf16[4,88,256]{2,1,0:T(8,128)(2,1)S(1)} collective-permute-done((bf16[4,88,256]{2,1,0:T(8,128)(2,1)}, bf16[4,88,256]{2,1,0:T(8,128)(2,1)S(1)}, u32[]{:S(2)}, u32[]{:S(2)}) %collective-permute-start.2) | collective-permute-done | bytes 180256 | tf_op jit(solution)/shard_map/ppermute | solution.py:414
  93.0 0.0 copy-start.4
  93.0 1.4 %collective-permute-start.6 = (bf16[4,88,256]{2,1,0:T(8,128)(2,1)}, bf16[4,88,256]{2,1,0:T(8,128)(2,1)S(1)}, u32[]{:S(2)}, u32[]{:S(2)}) collective-permute-start(bf16[4,88,256]{2,1,0:T(8,128)(2,1)} %get-tuple-element.45), channel_id=1, source_target_pairs={{0,24},{4,28},{8,16},{12,20},{16,8},{20,12},{24,0},{28,4},{1,25},{... | collective-permute-start | bytes 540680 | tf_op jit(solution)/shard_map/ppermute | solution.py:414
  94.4 2.6 %collective-permute-done.3.refs_3_ = bf16[4,88,256]{2,1,0:T(8,128)(2,1)S(1)} collective-permute-done((bf16[4,88,256]{2,1,0:T(8,128)(2,1)}, bf16[4,88,256]{2,1,0:T(8,128)(2,1)S(1)}, u32[]{:S(2)}, u32[]{:S(2)}) %collective-permute-start.3) | collective-permute-done | bytes 180256 | tf_op jit(solution)/shard_map/ppermute | solution.py:414
  97.0 0.0 copy-start.5
  97.0 3.0 %collective-permute-start.7 = (bf16[4,88,256]{2,1,0:T(8,128)(2,1)}, bf16[4,88,256]{2,1,0:T(8,128)(2,1)S(1)}, u32[]{:S(2)}, u32[]{:S(2)}) collective-permute-start(bf16[4,88,256]{2,1,0:T(8,128)(2,1)} %get-tuple-element.46), channel_id=1, source_target_pairs={{0,28},{4,24},{8,20},{12,16},{16,12},{20,8},{24,4},{28,0},{1,29},{... | collective-permute-start | bytes 540680 | tf_op jit(solution)/shard_map/ppermute | solution.py:414
  100.0 0.0 collective-permute-done.4.refs_4_
  100.0 0.0 copy-start.6
  100.0 0.0 collective-permute-done.5.refs_5_
  100.0 0.0 copy-start.7
  100.0 6.1 %collective-permute-done.6.refs_6_ = bf16[4,88,256]{2,1,0:T(8,128)(2,1)S(1)} collective-permute-done((bf16[4,88,256]{2,1,0:T(8,128)(2,1)}, bf16[4,88,256]{2,1,0:T(8,128)(2,1)S(1)}, u32[]{:S(2)}, u32[]{:S(2)}) %collective-permute-start.6) | collective-permute-done | bytes 180256 | tf_op jit(solution)/shard_map/ppermute | solution.py:414
  106.1 0.0 copy-start.8
  106.1 3.9 %collective-permute-done.7.refs_7_ = bf16[4,88,256]{2,1,0:T(8,128)(2,1)S(1)} collective-permute-done((bf16[4,88,256]{2,1,0:T(8,128)(2,1)}, bf16[4,88,256]{2,1,0:T(8,128)(2,1)S(1)}, u32[]{:S(2)}, u32[]{:S(2)}) %collective-permute-start.7) | collective-permute-done | bytes 180256 | tf_op jit(solution)/shard_map/ppermute | solution.py:414
  110.0 0.0 copy-start.9
  110.0 0.0 collective-permute-done.shared_ref
  110.0 0.0 copy-done.3
  110.0 0.0 copy-done.4
  110.0 0.0 copy-done.5
  110.0 0.0 copy-done.6
  110.0 0.0 copy-done.7
  110.0 0.0 copy-done.8
  110.0 0.6 copy-done.9
  110.6 10.3 %orthogonalize_second.1 = bf16[2,704,1024]{2,1,0:T(8,128)(2,1)} custom-call(s32[32]{0:T(128)} %get-tuple-element.29.kind_ref, bf16[32,88,256]{2,1,0:T(8,128)(2,1)} %collective-permute-done.shared_ref, bf16[4,88,256]{2,1,0:T(8,128)(2,1)} %get-tuple-element.39.refs_0_, bf16[4,88,256]{2,1,0:T(8,128)(2,1)} %copy-done.3, ...), custom_call_target="tpu_custom_call", output_to_operand_aliasing={{}: (10, {})} | custom-call | flops 6643777536 | bytes 4718592 | tf_op jit(solution)/shard_map/orthogonalize_second/pallas_call | solution.py:365
  120.9 0.0 all-to-all-done.2.back_ref
  120.9 0.0 copy-start
  120.9 1.1 copy-done
  122.1 3.7 %unpack.1 = bf16[32,88,256]{2,1,0:T(8,128)(2,1)} custom-call(s32[32]{0:T(128)} %get-tuple-element.28.host_ref, bf16[32,88,256]{2,1,0:T(8,128)(2,1)} %copy-done), custom_call_target="tpu_custom_call" | custom-call | bytes 2883584 | tf_op jit(solution)/shard_map/unpack/pallas_call | solution.py:391
  (1 shorter events, 0.0 us)
Async XLA Ops:
  5.6 40.5 %all-to-all-start.1 = ((bf16[32,88,256]{2,1,0:T(8,128)(2,1)}), bf16[32,88,256]{2,1,0:T(8,128)(2,1)S(1)}, u32[]{:S(2)}, u32[]{:S(2)}) async-start(bf16[32,88,256]{2,1,0:T(8,128)(2,1)} %get-tuple-element.31), calls=%async_computation.1 | async-start | bytes 2883584 | tf_op jit(solution)/shard_map/all_to_all | solution.py:409
  46.2 1.1 copy-start.2
  47.3 24.3 %all-to-all-start.3 = ((bf16[16,88,256]{2,1,0:T(8,128)(2,1)}), bf16[16,88,256]{2,1,0:T(8,128)(2,1)S(1)}, u32[]{:S(2)}, u32[]{:S(2)}) async-start(bf16[16,88,256]{2,1,0:T(8,128)(2,1)} %get-tuple-element.36), calls=%async_computation.3 | async-start | bytes 1441792 | tf_op jit(solution)/shard_map/all_to_all | solution.py:409
  71.5 0.9 copy-start.1
  72.4 48.5 %all-to-all-start.2 = ((bf16[32,88,256]{2,1,0:T(8,128)(2,1)}), bf16[32,88,256]{2,1,0:T(8,128)(2,1)S(1)}, u32[]{:S(2)}, u32[]{:S(2)}) async-start(bf16[32,88,256]{2,1,0:T(8,128)(2,1)} %get-tuple-element.35), calls=%async_computation.2 | async-start | bytes 2883584 | tf_op jit(solution)/shard_map/all_to_all | solution.py:409
  75.2 34.8 %collective-permute-start = (bf16[32,88,256]{2,1,0:T(8,128)(2,1)}, bf16[32,88,256]{2,1,0:T(8,128)(2,1)}, u32[]{:S(2)}, u32[]{:S(2)}) collective-permute-start(bf16[32,88,256]{2,1,0:T(8,128)(2,1)} %copy-done.2), channel_id=1, source_target_pairs={{0,4},{4,0},{8,12},{12,8},{16,20},{20,16},{24,28},{28,24},{1,5},{5... | collective-permute-start | bytes 4325384 | tf_op jit(solution)/shard_map/ppermute | solution.py:414
  78.0 3.5 %collective-permute-start.1 = (bf16[4,88,256]{2,1,0:T(8,128)(2,1)}, bf16[4,88,256]{2,1,0:T(8,128)(2,1)S(1)}, u32[]{:S(2)}, u32[]{:S(2)}) collective-permute-start(bf16[4,88,256]{2,1,0:T(8,128)(2,1)} %get-tuple-element.40), channel_id=1, source_target_pairs={{0,4},{4,0},{8,12},{12,8},{16,20},{20,16},{24,28},{28,24},{1,5},{5... | collective-permute-start | bytes 540680 | tf_op jit(solution)/shard_map/ppermute | solution.py:414
  78.2 14.8 %collective-permute-start.2 = (bf16[4,88,256]{2,1,0:T(8,128)(2,1)}, bf16[4,88,256]{2,1,0:T(8,128)(2,1)S(1)}, u32[]{:S(2)}, u32[]{:S(2)}) collective-permute-start(bf16[4,88,256]{2,1,0:T(8,128)(2,1)} %get-tuple-element.41), channel_id=1, source_target_pairs={{0,8},{4,12},{8,0},{12,4},{16,24},{20,28},{24,16},{28,20},{1,9},{5... | collective-permute-start | bytes 540680 | tf_op jit(solution)/shard_map/ppermute | solution.py:414
  80.0 17.0 %collective-permute-start.3 = (bf16[4,88,256]{2,1,0:T(8,128)(2,1)}, bf16[4,88,256]{2,1,0:T(8,128)(2,1)S(1)}, u32[]{:S(2)}, u32[]{:S(2)}) collective-permute-start(bf16[4,88,256]{2,1,0:T(8,128)(2,1)} %get-tuple-element.42), channel_id=1, source_target_pairs={{0,12},{4,8},{8,4},{12,0},{16,28},{20,24},{24,20},{28,16},{1,13},{... | collective-permute-start | bytes 540680 | tf_op jit(solution)/shard_map/ppermute | solution.py:414
  80.0 20.0 %collective-permute-start.4 = (bf16[4,88,256]{2,1,0:T(8,128)(2,1)}, bf16[4,88,256]{2,1,0:T(8,128)(2,1)S(1)}, u32[]{:S(2)}, u32[]{:S(2)}) collective-permute-start(bf16[4,88,256]{2,1,0:T(8,128)(2,1)} %get-tuple-element.43), channel_id=1, source_target_pairs={{0,16},{4,20},{8,24},{12,28},{16,0},{20,4},{24,8},{28,12},{1,17},{... | collective-permute-start | bytes 540680 | tf_op jit(solution)/shard_map/ppermute | solution.py:414
  81.5 28.5 %copy-start.3 = (bf16[4,88,256]{2,1,0:T(8,128)(2,1)}, bf16[4,88,256]{2,1,0:T(8,128)(2,1)S(1)}, u32[]{:S(2)}) copy-start(bf16[4,88,256]{2,1,0:T(8,128)(2,1)S(1)} %collective-permute-done.1.refs_1_) | copy-start | bytes 540676
  81.5 18.5 %collective-permute-start.5 = (bf16[4,88,256]{2,1,0:T(8,128)(2,1)}, bf16[4,88,256]{2,1,0:T(8,128)(2,1)S(1)}, u32[]{:S(2)}, u32[]{:S(2)}) collective-permute-start(bf16[4,88,256]{2,1,0:T(8,128)(2,1)} %get-tuple-element.44), channel_id=1, source_target_pairs={{0,20},{4,16},{8,28},{12,24},{16,4},{20,0},{24,12},{28,8},{1,21},{... | collective-permute-start | bytes 540680 | tf_op jit(solution)/shard_map/ppermute | solution.py:414
  93.0 17.0 %copy-start.4 = (bf16[4,88,256]{2,1,0:T(8,128)(2,1)}, bf16[4,88,256]{2,1,0:T(8,128)(2,1)S(1)}, u32[]{:S(2)}) copy-start(bf16[4,88,256]{2,1,0:T(8,128)(2,1)S(1)} %collective-permute-done.2.refs_2_) | copy-start | bytes 540676
  93.0 13.1 %collective-permute-start.6 = (bf16[4,88,256]{2,1,0:T(8,128)(2,1)}, bf16[4,88,256]{2,1,0:T(8,128)(2,1)S(1)}, u32[]{:S(2)}, u32[]{:S(2)}) collective-permute-start(bf16[4,88,256]{2,1,0:T(8,128)(2,1)} %get-tuple-element.45), channel_id=1, source_target_pairs={{0,24},{4,28},{8,16},{12,20},{16,8},{20,12},{24,0},{28,4},{1,25},{... | collective-permute-start | bytes 540680 | tf_op jit(solution)/shard_map/ppermute | solution.py:414
  97.0 13.0 %copy-start.5 = (bf16[4,88,256]{2,1,0:T(8,128)(2,1)}, bf16[4,88,256]{2,1,0:T(8,128)(2,1)S(1)}, u32[]{:S(2)}) copy-start(bf16[4,88,256]{2,1,0:T(8,128)(2,1)S(1)} %collective-permute-done.3.refs_3_) | copy-start | bytes 540676
  97.0 13.0 %collective-permute-start.7 = (bf16[4,88,256]{2,1,0:T(8,128)(2,1)}, bf16[4,88,256]{2,1,0:T(8,128)(2,1)S(1)}, u32[]{:S(2)}, u32[]{:S(2)}) collective-permute-start(bf16[4,88,256]{2,1,0:T(8,128)(2,1)} %get-tuple-element.46), channel_id=1, source_target_pairs={{0,28},{4,24},{8,20},{12,16},{16,12},{20,8},{24,4},{28,0},{1,29},{... | collective-permute-start | bytes 540680 | tf_op jit(solution)/shard_map/ppermute | solution.py:414
  100.0 10.0 %copy-start.6 = (bf16[4,88,256]{2,1,0:T(8,128)(2,1)}, bf16[4,88,256]{2,1,0:T(8,128)(2,1)S(1)}, u32[]{:S(2)}) copy-start(bf16[4,88,256]{2,1,0:T(8,128)(2,1)S(1)} %collective-permute-done.4.refs_4_) | copy-start | bytes 540676
  100.0 10.0 %copy-start.7 = (bf16[4,88,256]{2,1,0:T(8,128)(2,1)}, bf16[4,88,256]{2,1,0:T(8,128)(2,1)S(1)}, u32[]{:S(2)}) copy-start(bf16[4,88,256]{2,1,0:T(8,128)(2,1)S(1)} %collective-permute-done.5.refs_5_) | copy-start | bytes 540676
  106.1 3.9 %copy-start.8 = (bf16[4,88,256]{2,1,0:T(8,128)(2,1)}, bf16[4,88,256]{2,1,0:T(8,128)(2,1)S(1)}, u32[]{:S(2)}) copy-start(bf16[4,88,256]{2,1,0:T(8,128)(2,1)S(1)} %collective-permute-done.6.refs_6_) | copy-start | bytes 540676
  110.0 0.7 copy-start.9
  120.9 1.1 copy-start

commit v5 on v4

--- a/solution.py
+++ b/solution.py
@@ -18,8 +18,9 @@
 epsilon = 1e-07
 
 AXES = ("dp", "owner")
-VMEM_BYTES = 60 * 1024 * 1024
-PARAMS = pltpu.CompilerParams(vmem_limit_bytes=VMEM_BYTES)
+MIB = 1024 * 1024
+PARAMS = pltpu.CompilerParams(vmem_limit_bytes=24 * MIB)
+PACK_PARAMS = pltpu.CompilerParams(vmem_limit_bytes=60 * MIB)
 SMEM = pl.BlockSpec(memory_space=pltpu.SMEM)
 
 NOTHING, SINGLE, PAIRED = 0, 1, 2
@@ -124,7 +125,7 @@
             jax.ShapeDtypeStruct((devices,), jnp.int32),
             jax.ShapeDtypeStruct((1,), jnp.int32),
         ],
-        compiler_params=PARAMS,
+        compiler_params=PACK_PARAMS,
         cost_estimate=pl.CostEstimate(
             flops=4 * mats * rows * cols, bytes_accessed=8 * mats * rows * cols, transcendentals=0
         ),
@@ -133,9 +134,11 @@
 
 
 def momentum_kernel(
-    chunk, col_size, room, owner_ref, host_ref, kind_ref, g_ref, m_ref, nm_ref, near_ref, far_ref
+    chunk, col_size, room, owner_ref, host_ref, kind_ref, g_ref, m_ref, nm_ref, *refs
 ):
+    near_refs, far_ref, held = refs[:col_size], refs[col_size], refs[col_size + 1]
     step = pl.program_id(0)
+    here = lax.axis_index("owner")
     for j in range(chunk):
         new, nesterov = nesterov_of(g_ref, m_ref, j)
         nm_ref[j] = new
@@ -146,36 +149,45 @@
 
         @pl.when(second & (place < room))
         def _():
-            near_ref[layer * room + place] = nesterov
+            held[(layer ^ here) * room + place] = nesterov
 
         @pl.when(second & (place >= room))
         def _():
             far_ref[layer * room + place - room] = nesterov
+
+    @pl.when(step == pl.num_programs(0) - 1)
+    def _():
+        for offset in range(col_size):
+            near_refs[offset][...] = held[offset * room : (offset + 1) * room]
 
 
 def update_momentum(gradients, momentum, owner_table, host, kind, col_size, room):
     mats, rows, cols = gradients.shape
     chunk = 8
     block = pl.BlockSpec((chunk, rows, cols), lambda i, *_: (i, 0, 0))
-    part = jax.ShapeDtypeStruct((col_size * room, rows, cols), jnp.bfloat16)
-    return pl.pallas_call(
+    near = jax.ShapeDtypeStruct((room, rows, cols), jnp.bfloat16)
+    far = jax.ShapeDtypeStruct((col_size * room, rows, cols), jnp.bfloat16)
+    new_momentum, *near, far = pl.pallas_call(
         functools.partial(momentum_kernel, chunk, col_size, room),
         grid_spec=pltpu.PrefetchScalarGridSpec(
             num_scalar_prefetch=3,
             grid=(mats // chunk,),
             in_specs=[block, block],
-            out_specs=[block, whole(part.shape), whole(part.shape)],
-        ),
-        out_shape=[jax.ShapeDtypeStruct(momentum.shape, jnp.float32), part, part],
+            out_specs=[block] + [whole(near.shape)] * col_size + [whole(far.shape)],
+            scratch_shapes=[pltpu.VMEM(far.shape, jnp.bfloat16)],
+        ),
+        out_shape=[jax.ShapeDtypeStruct(momentum.shape, jnp.float32)] + [near] * col_size + [far],
         compiler_params=PARAMS,
         cost_estimate=pl.CostEstimate(
             flops=4 * mats * rows * cols, bytes_accessed=12 * mats * rows * cols, transcendentals=0
         ),
         name="update_momentum",
     )(owner_table, host, kind, gradients, momentum)
-
-
-def forward_kernel(col_size, row_size, room, kind_ref, near_ref, far_ref, *out_refs):
+    return new_momentum, near, far
+
+
+def forward_kernel(col_size, row_size, room, kind_ref, *refs):
+    near_refs, far_ref, out_refs = refs[:col_size], refs[col_size], refs[col_size + 1 :]
     row, col = lax.axis_index("dp"), lax.axis_index("owner")
     for offset in range(row_size):
         place = jnp.maximum(kind_ref[(row ^ offset) * col_size + col] - PAIRED, 0)
@@ -183,7 +195,7 @@
         @pl.when(place < room)
         def _():
             for z in range(col_size):
-                out_refs[offset][z] = near_ref[z * room + place]
+                out_refs[offset][col ^ z] = near_refs[z][place]
 
         @pl.when(place >= room)
         def _():
@@ -197,7 +209,7 @@
     return pl.pallas_call(
         functools.partial(forward_kernel, col_size, row_size, room),
         grid=(1,),
-        in_specs=[SMEM, whole(near.shape), whole(far.shape)],
+        in_specs=[SMEM] + [whole(near[0].shape)] * col_size + [whole(far.shape)],
         out_specs=[whole(out.shape)] * row_size,
         out_shape=[out] * row_size,
         compiler_params=PARAMS,
@@ -205,7 +217,7 @@
             flops=0, bytes_accessed=8 * col_size * room * rows * cols, transcendentals=0
         ),
         name="forward",
-    )(kind, near, far)
+    )(kind, *near, far)
 
 
 def matmul(lhs, rhs, rhs_dim):
@@ -426,10 +438,11 @@
         gradients, momentum, owner_table, host, kind, col_size, room
     )
     arrived, near, far = lax.optimization_barrier((arrived, near, far))
-    near = exchange(near, "owner")
+    near = [near[0]] + [swap(near[z], "owner", z) for z in range(1, col_size)]
     shared = swap(arrived, "dp", 1)
     owned, back = orthogonalize_hosted(kind, arrived, row_size, col_size)
     far = lax.cond(most[0] > room, lambda part: exchange(part, "owner"), lambda part: part, far)
+    back, near, shared = lax.optimization_barrier((back, near, shared))
     returned = exchange(back, AXES)
     by_row = forward(kind, near, far, row_size, col_size, room)
     by_row = [by_row[0]] + [swap(by_row[r], "dp", r) for r in range(1, row_size)]

time: 126 us -> 118 us (0.937)
  Pallas kernels: 36.9 us -> 30.8 us
  waiting for transfers between devices: 60.5 us -> 58.3 us
    all_to_all x3 -> x2, waiting for transfers between devices: 36.7 us -> 27.9 us  [exchange(): return lax.all_to_all(blocks, axes, split_axis=0, concat_axis=0, tiled=True)]
    ppermute x8 -> x11, waiting for transfers between devices: 23.8 us -> 30.3 us  [swap(): return lax.ppermute(block, axis, [(i, i ^ offset) for i in range(size)])]
    ppermute x8 -> x11, starting transfers between devices: 8.52 us -> 12.5 us  [swap(): return lax.ppermute(block, axis, [(i, i ^ offset) for i in range(size)])]
    all_to_all x3 -> x2, starting transfers between devices: 14.7 us -> 11.5 us  [exchange(): return lax.all_to_all(blocks, axes, split_axis=0, concat_axis=0, tiled=True)]
    pallas_call x1, Pallas kernels: 5.55 us -> 3.22 us  [update_momentum(): pl.pallas_call(functools.partial(momentum_kernel, chunk, col_size, room),...]
    pallas_call x1, Pallas kernels: 3.68 us -> 2.2 us  [unpack(): pl.pallas_call(functools.partial(unpack_kernel, chunk), grid_spec=pltpu.P...]
    pallas_call x1, Pallas kernels: 10.3 us -> 8.99 us  [orthogonalize_second(): pl.pallas_call(functools.partial(second_kernel, row_size, col_size), grid...]
    unnamed x20 -> x16, local copies, waits for them, and re-layouts: 3.73 us -> 3.19 us
  transfers between devices with their start and end apart: 11 -> 13, of which waited for: 6 -> 7; matrix products, arithmetic and copies ran while one was open for 0% -> 0% of each run, Pallas kernels for 22% -> 20%
where the time goes in v5:
time: 118 us
  waiting for transfers between devices  58.3 us (49%)
  Pallas kernels  30.8 us (26%)
  starting transfers between devices  24 us (20%)
  local copies, waits for them, and re-layouts  3.19 us (3%)
  between operations  1.34 us (1%)
    ppermute x11, waiting for transfers between devices, swap(): return lax.ppermute(block, axis, [(i, i ^ offset) for i in range(size)])  30.3 us
    all_to_all x2, waiting for transfers between devices, exchange(): return lax.all_to_all(blocks, axes, split_axis=0, concat_axis=0, tiled=True)  27.9 us
    ppermute x11, starting transfers between devices, swap(): return lax.ppermute(block, axis, [(i, i ^ offset) for i in range(size)])  12.5 us
    all_to_all x2, starting transfers between devices, exchange(): return lax.all_to_all(blocks, axes, split_axis=0, concat_axis=0, tiled=True)  11.5 us
    pallas_call x1, Pallas kernels, orthogonalize_hosted(): pl.pallas_call(functools.partial(hosted_kernel, row_size, col_size), grid...  9.93 us
    pallas_call x1, Pallas kernels, orthogonalize_second(): pl.pallas_call(functools.partial(second_kernel, row_size, col_size), grid...  8.99 us
    pallas_call x1, Pallas kernels, pack(): pl.pallas_call(functools.partial(pack_kernel, chunk, col_size), grid_spec...  4.99 us
    pallas_call x1, Pallas kernels, update_momentum(): pl.pallas_call(functools.partial(momentum_kernel, chunk, col_size, room),...  3.22 us
  transfers between devices with their start and end apart: 13, of which 7 were waited for; matrix products, arithmetic and copies ran while one was open for 0% of the time, Pallas kernels for 20%

profile of v5, /device:TPU:0, one launch (start us, length us, event | category | flops | bytes accessed | tf_op | source)
XLA Modules:
  0.0 117.6 jit_solution(5356706468716247141)
XLA Ops:
  0.6 5.0 %pack.1 = (bf16[32,88,256]{2,1,0:T(8,128)(2,1)}, s32[32]{0:T(128)}, s32[32]{0:T(128)}, s32[1]{0:T(128)}) custom-call(s32[32]{0:T(128)} %owner_ref.3, bf16[32,88,256]{2,1,0:T(8,128)(2,1)} %g_ref.3, f32[32,88,256]{2,1,0:T(8,128)} %m_ref.3), custom_call_target="tpu_custom_call" | custom-call | flops 2883584 | bytes 5767168 | tf_op jit(solution)/shard_map/pack/pallas_call | solution.py:109
  5.6 0.0 copy-start
  5.6 0.0 copy-start.2
  5.7 0.0 copy-start.3
  5.7 0.0 copy-start.4
  5.7 7.4 %all-to-all-start.1 = ((bf16[32,88,256]{2,1,0:T(8,128)(2,1)}), bf16[32,88,256]{2,1,0:T(8,128)(2,1)}, u32[]{:S(2)}, u32[]{:S(2)}) async-start(bf16[32,88,256]{2,1,0:T(8,128)(2,1)} %get-tuple-element.43), calls=%async_computation.1 | async-start | bytes 2883584 | tf_op jit(solution)/shard_map/all_to_all | solution.py:421
  13.1 0.0 copy-done
  13.1 0.0 copy-done.2
  13.1 0.0 copy-done.3
  13.1 0.0 copy-done.4
  13.1 0.0 copy-start.1
  13.2 1.4 %copy-done.1 = bf16[32,88,256]{2,1,0:T(8,128)(2,1)S(1)} copy-done((bf16[32,88,256]{2,1,0:T(8,128)(2,1)S(1)}, bf16[32,88,256]{2,1,0:T(8,128)(2,1)}, u32[]{:S(2)}) %copy-start.1) | copy-done | bytes 1441816
  14.5 3.2 %update_momentum.1 = (f32[32,88,256]{2,1,0:T(8,128)}, bf16[4,88,256]{2,1,0:T(8,128)(2,1)S(1)}, bf16[4,88,256]{2,1,0:T(8,128)(2,1)S(1)}, bf16[4,88,256]{2,1,0:T(8...) custom-call(s32[32]{0:T(128)S(1)} %copy-done.2, s32[32]{0:T(128)S(1)} %copy-done.3, ...), custom_call_target="tpu_custom_call" | custom-call | flops 2883584 | bytes 8650752 | tf_op jit(solution)/shard_map/update_momentum/pallas_call | solution.py:170
  17.7 0.0 copy-start.7
  17.7 0.7 copy-done.7
  18.4 27.9 %all-to-all-done.1.x_ref = bf16[32,88,256]{2,1,0:T(8,128)(2,1)} async-done(((bf16[32,88,256]{2,1,0:T(8,128)(2,1)}), bf16[32,88,256]{2,1,0:T(8,128)(2,1)}, u32[]{:S(2)}, u32[]{:S(2)}) %all-to-all-start.1) | async-done | bytes 1441824 | tf_op jit(solution)/shard_map/all_to_all | solution.py:421
  46.3 1.7 %collective-permute-start.3 = (bf16[32,88,256]{2,1,0:T(8,128)(2,1)}, bf16[32,88,256]{2,1,0:T(8,128)(2,1)S(1)}, u32[]{:S(2)}, u32[]{:S(2)}) collective-permute-start(bf16[32,88,256]{2,1,0:T(8,128)(2,1)} %all-to-all-done.1.x_ref), channel_id=1, source_target_pairs={{0,4},{4,0},{8,12},{12,8},{16,20},{20,16},{24,28},{28,24},{1,5},{5... | collective-permute-start | bytes 4325384 | tf_op jit(solution)/shard_map/ppermute | solution.py:426
  48.6 1.8 %collective-permute-start = (bf16[4,88,256]{2,1,0:T(8,128)(2,1)}, bf16[4,88,256]{2,1,0:T(8,128)(2,1)S(1)}, u32[]{:S(2)}, u32[]{:S(2)}) collective-permute-start(bf16[4,88,256]{2,1,0:T(8,128)(2,1)} %copy-done.7), channel_id=1, source_target_pairs={{0,1},{1,0},{2,3},{3,2},{4,5},{5,4},{6,7},{7,6},{8,9},{9,8},{10,11... | collective-permute-start | bytes 540680 | tf_op jit(solution)/shard_map/ppermute | solution.py:426
  50.3 0.5 collective-permute-start.1
  50.8 2.2 %collective-permute-start.2 = (bf16[4,88,256]{2,1,0:T(8,128)(2,1)S(1)}, bf16[4,88,256]{2,1,0:T(8,128)(2,1)S(1)}, u32[]{:S(2)}, u32[]{:S(2)}) collective-permute-start(bf16[4,88,256]{2,1,0:T(8,128)(2,1)S(1)} %get-tuple-element.54), channel_id=1, source_target_pairs={{0,3},{1,2},{2,1},{3,0},{4,7},{5,6},{6,5},{7,4},{8,11},{9,10},{10,... | collective-permute-start | bytes 540680 | tf_op jit(solution)/shard_map/ppermute | solution.py:426
  53.0 9.9 %orthogonalize_hosted.1 = (bf16[2,704,1024]{2,1,0:T(8,128)(2,1)}, bf16[32,88,256]{2,1,0:T(8,128)(2,1)}) custom-call(s32[32]{0:T(128)S(1)} %copy-done.4, bf16[32,88,256]{2,1,0:T(8,128)(2,1)} %all-to-all-done.1.x_ref), custom_call_target="tpu_custom_call" | custom-call | flops 6643777536 | bytes 4718592 | tf_op jit(solution)/shard_map/orthogonalize_hosted/pallas_call | solution.py:358
  63.0 0.0 collective-permute-done.refs_1_
  63.0 3.4 %collective-permute-done.1.refs_2_ = bf16[4,88,256]{2,1,0:T(8,128)(2,1)S(1)} collective-permute-done((bf16[4,88,256]{2,1,0:T(8,128)(2,1)S(1)}, bf16[4,88,256]{2,1,0:T(8,128)(2,1)S(1)}, u32[]{:S(2)}, u32[]{:S(2)}) %collective-permute-start.1) | collective-permute-done | bytes 180256 | tf_op jit(solution)/shard_map/ppermute | solution.py:426
  66.4 0.0 collective-permute-done.2.refs_3_
  66.4 0.0 collective-permute-done.3.shared_ref
  66.4 0.0 copy-start.5
  66.4 1.1 copy-done.5
  67.5 4.1 %all-to-all-start.2 = ((bf16[32,88,256]{2,1,0:T(8,128)(2,1)}), bf16[32,88,256]{2,1,0:T(8,128)(2,1)S(1)}, u32[]{:S(2)}, u32[]{:S(2)}) async-start(bf16[32,88,256]{2,1,0:T(8,128)(2,1)} %get-tuple-element.55), calls=%async_computation.2 | async-start | bytes 2883584 | tf_op jit(solution)/shard_map/all_to_all | solution.py:421
  71.6 0.0 copy-start.6
  71.6 1.5 %forward.1 = (bf16[4,88,256]{2,1,0:T(8,128)(2,1)S(1)}, bf16[4,88,256]{2,1,0:T(8,128)(2,1)S(1)}, bf16[4,88,256]{2,1,0:T(8,128)(2,1)S(1)}, bf16[4,88,256]{2,1,0:T(...) custom-call(s32[32]{0:T(128)S(1)} %copy-done.4, ...), custom_call_target="tpu_custom_call" | custom-call | bytes 2883584 | tf_op jit(solution)/shard_map/forward/pallas_call | solution.py:209
  73.1 0.3 collective-permute-start.4
  73.5 1.7 %collective-permute-start.5 = (bf16[4,88,256]{2,1,0:T(8,128)(2,1)S(1)}, bf16[4,88,256]{2,1,0:T(8,128)(2,1)S(1)}, u32[]{:S(2)}, u32[]{:S(2)}) collective-permute-start(bf16[4,88,256]{2,1,0:T(8,128)(2,1)S(1)} %get-tuple-element.65), channel_id=1, source_target_pairs={{0,8},{4,12},{8,0},{12,4},{16,24},{20,28},{24,16},{28,20},{1,9},{5... | collective-permute-start | bytes 540680 | tf_op jit(solution)/shard_map/ppermute | solution.py:426
  75.1 0.0 collective-permute-start.6
  75.1 1.7 %collective-permute-start.7 = (bf16[4,88,256]{2,1,0:T(8,128)(2,1)S(1)}, bf16[4,88,256]{2,1,0:T(8,128)(2,1)S(1)}, u32[]{:S(2)}, u32[]{:S(2)}) collective-permute-start(bf16[4,88,256]{2,1,0:T(8,128)(2,1)S(1)} %get-tuple-element.67), channel_id=1, source_target_pairs={{0,16},{4,20},{8,24},{12,28},{16,0},{20,4},{24,8},{28,12},{1,17},{... | collective-permute-start | bytes 540680 | tf_op jit(solution)/shard_map/ppermute | solution.py:426
  76.8 0.1 collective-permute-start.8
  77.0 0.0 collective-permute-done.4.refs_1_
  77.0 2.6 %collective-permute-start.9 = (bf16[4,88,256]{2,1,0:T(8,128)(2,1)S(1)}, bf16[4,88,256]{2,1,0:T(8,128)(2,1)S(1)}, u32[]{:S(2)}, u32[]{:S(2)}) collective-permute-start(bf16[4,88,256]{2,1,0:T(8,128)(2,1)S(1)} %get-tuple-element.69), channel_id=1, source_target_pairs={{0,24},{4,28},{8,16},{12,20},{16,8},{20,12},{24,0},{28,4},{1,25},{... | collective-permute-start | bytes 540680 | tf_op jit(solution)/shard_map/ppermute | solution.py:426
  79.5 9.9 %collective-permute-done.5.refs_2_ = bf16[4,88,256]{2,1,0:T(8,128)(2,1)S(1)} collective-permute-done((bf16[4,88,256]{2,1,0:T(8,128)(2,1)S(1)}, bf16[4,88,256]{2,1,0:T(8,128)(2,1)S(1)}, u32[]{:S(2)}, u32[]{:S(2)}) %collective-permute-start.5) | collective-permute-done | bytes 180256 | tf_op jit(solution)/shard_map/ppermute | solution.py:426
  89.5 0.0 collective-permute-start.10
  89.5 4.0 %collective-permute-done.6.refs_3_ = bf16[4,88,256]{2,1,0:T(8,128)(2,1)S(1)} collective-permute-done((bf16[4,88,256]{2,1,0:T(8,128)(2,1)S(1)}, bf16[4,88,256]{2,1,0:T(8,128)(2,1)S(1)}, u32[]{:S(2)}, u32[]{:S(2)}) %collective-permute-start.6) | collective-permute-done | bytes 180256 | tf_op jit(solution)/shard_map/ppermute | solution.py:426
  93.4 0.0 collective-permute-done.7.refs_4_
  93.4 0.3 collective-permute-done.8.refs_5_
  93.7 8.8 %collective-permute-done.9.refs_6_ = bf16[4,88,256]{2,1,0:T(8,128)(2,1)S(1)} collective-permute-done((bf16[4,88,256]{2,1,0:T(8,128)(2,1)S(1)}, bf16[4,88,256]{2,1,0:T(8,128)(2,1)S(1)}, u32[]{:S(2)}, u32[]{:S(2)}) %collective-permute-start.9) | collective-permute-done | bytes 180256 | tf_op jit(solution)/shard_map/ppermute | solution.py:426
  102.6 3.9 %collective-permute-done.10.refs_7_ = bf16[4,88,256]{2,1,0:T(8,128)(2,1)S(1)} collective-permute-done((bf16[4,88,256]{2,1,0:T(8,128)(2,1)S(1)}, bf16[4,88,256]{2,1,0:T(8,128)(2,1)S(1)}, u32[]{:S(2)}, u32[]{:S(2)}) %collective-permute-start.10) | collective-permute-done | bytes 180256 | tf_op jit(solution)/shard_map/ppermute | solution.py:426
  106.4 0.0 copy-done.6
  106.4 9.0 %orthogonalize_second.1 = bf16[2,704,1024]{2,1,0:T(8,128)(2,1)} custom-call(s32[32]{0:T(128)S(1)} %copy-done.4, bf16[32,88,256]{2,1,0:T(8,128)(2,1)S(1)} %copy-done.6, bf16[4,88,256]{2,1,0:T(8,128)(2,1)S(1)} %get-tuple-element.63.refs_0_, bf16[4,88,256]{2,1,0:T(8,128)(2,1)S(1)} %collective-permute-done.4.refs_1_, ...), custom_call_target="tpu_custom_call", output_to_operand_aliasing={{}: (10, {})} | custom-call | flops 6643777536 | bytes 4718592 | tf_op jit(solution)/shard_map/orthogonalize_second/pallas_call | solution.py:377
  115.4 0.0 all-to-all-done.2.back_ref
  115.4 2.2 %unpack.1 = bf16[32,88,256]{2,1,0:T(8,128)(2,1)} custom-call(s32[32]{0:T(128)S(1)} %copy-done.3, bf16[32,88,256]{2,1,0:T(8,128)(2,1)S(1)} %all-to-all-done.2.back_ref), custom_call_target="tpu_custom_call" | custom-call | bytes 2883584 | tf_op jit(solution)/shard_map/unpack/pallas_call | solution.py:403
  (1 shorter events, 0.0 us)
Async XLA Ops:
  5.6 7.5 %copy-start = (f32[32,88,256]{2,1,0:T(8,128)S(1)}, f32[32,88,256]{2,1,0:T(8,128)}, u32[]{:S(2)}) copy-start(f32[32,88,256]{2,1,0:T(8,128)} %m_ref.3) | copy-start | bytes 8650756
  5.6 7.5 %copy-start.2 = (s32[32]{0:T(128)S(1)}, s32[32]{0:T(128)}, u32[]{:S(2)}) copy-start(s32[32]{0:T(128)} %owner_ref.3) | copy-start | bytes 388
  5.7 7.5 %copy-start.3 = (s32[32]{0:T(128)S(1)}, s32[32]{0:T(128)}, u32[]{:S(2)}) copy-start(s32[32]{0:T(128)} %get-tuple-element.40.host_ref) | copy-start | bytes 388
  5.7 7.5 %copy-start.4 = (s32[32]{0:T(128)S(1)}, s32[32]{0:T(128)}, u32[]{:S(2)}) copy-start(s32[32]{0:T(128)} %get-tuple-element.41.kind_ref) | copy-start | bytes 388
  5.7 40.6 %all-to-all-start.1 = ((bf16[32,88,256]{2,1,0:T(8,128)(2,1)}), bf16[32,88,256]{2,1,0:T(8,128)(2,1)}, u32[]{:S(2)}, u32[]{:S(2)}) async-start(bf16[32,88,256]{2,1,0:T(8,128)(2,1)} %get-tuple-element.43), calls=%async_computation.1 | async-start | bytes 2883584 | tf_op jit(solution)/shard_map/all_to_all | solution.py:421
  13.1 1.4 %copy-start.1 = (bf16[32,88,256]{2,1,0:T(8,128)(2,1)S(1)}, bf16[32,88,256]{2,1,0:T(8,128)(2,1)}, u32[]{:S(2)}) copy-start(bf16[32,88,256]{2,1,0:T(8,128)(2,1)} %g_ref.3) | copy-start | bytes 4325380
  17.7 0.7 copy-start.7
  46.3 20.1 %collective-permute-start.3 = (bf16[32,88,256]{2,1,0:T(8,128)(2,1)}, bf16[32,88,256]{2,1,0:T(8,128)(2,1)S(1)}, u32[]{:S(2)}, u32[]{:S(2)}) collective-permute-start(bf16[32,88,256]{2,1,0:T(8,128)(2,1)} %all-to-all-done.1.x_ref), channel_id=1, source_target_pairs={{0,4},{4,0},{8,12},{12,8},{16,20},{20,16},{24,28},{28,24},{1,5},{5... | collective-permute-start | bytes 4325384 | tf_op jit(solution)/shard_map/ppermute | solution.py:426
  48.6 14.4 %collective-permute-start = (bf16[4,88,256]{2,1,0:T(8,128)(2,1)}, bf16[4,88,256]{2,1,0:T(8,128)(2,1)S(1)}, u32[]{:S(2)}, u32[]{:S(2)}) collective-permute-start(bf16[4,88,256]{2,1,0:T(8,128)(2,1)} %copy-done.7), channel_id=1, source_target_pairs={{0,1},{1,0},{2,3},{3,2},{4,5},{5,4},{6,7},{7,6},{8,9},{9,8},{10,11... | collective-permute-start | bytes 540680 | tf_op jit(solution)/shard_map/ppermute | solution.py:426
  50.3 16.1 %collective-permute-start.1 = (bf16[4,88,256]{2,1,0:T(8,128)(2,1)S(1)}, bf16[4,88,256]{2,1,0:T(8,128)(2,1)S(1)}, u32[]{:S(2)}, u32[]{:S(2)}) collective-permute-start(bf16[4,88,256]{2,1,0:T(8,128)(2,1)S(1)} %get-tuple-element.53), channel_id=1, source_target_pairs={{0,2},{1,3},{2,0},{3,1},{4,6},{5,7},{6,4},{7,5},{8,10},{9,11},{10,... | collective-permute-start | bytes 540680 | tf_op jit(solution)/shard_map/ppermute | solution.py:426
  50.8 15.6 %collective-permute-start.2 = (bf16[4,88,256]{2,1,0:T(8,128)(2,1)S(1)}, bf16[4,88,256]{2,1,0:T(8,128)(2,1)S(1)}, u32[]{:S(2)}, u32[]{:S(2)}) collective-permute-start(bf16[4,88,256]{2,1,0:T(8,128)(2,1)S(1)} %get-tuple-element.54), channel_id=1, source_target_pairs={{0,3},{1,2},{2,1},{3,0},{4,7},{5,6},{6,5},{7,4},{8,11},{9,10},{10,... | collective-permute-start | bytes 540680 | tf_op jit(solution)/shard_map/ppermute | solution.py:426
  66.4 1.1 copy-start.5
  67.5 47.9 %all-to-all-start.2 = ((bf16[32,88,256]{2,1,0:T(8,128)(2,1)}), bf16[32,88,256]{2,1,0:T(8,128)(2,1)S(1)}, u32[]{:S(2)}, u32[]{:S(2)}) async-start(bf16[32,88,256]{2,1,0:T(8,128)(2,1)} %get-tuple-element.55), calls=%async_computation.2 | async-start | bytes 2883584 | tf_op jit(solution)/shard_map/all_to_all | solution.py:421
  71.6 34.8 %copy-start.6 = (bf16[32,88,256]{2,1,0:T(8,128)(2,1)S(1)}, bf16[32,88,256]{2,1,0:T(8,128)(2,1)}, u32[]{:S(2)}) copy-start(bf16[32,88,256]{2,1,0:T(8,128)(2,1)} %copy-done.5) | copy-start | bytes 4325380
  73.1 3.8 %collective-permute-start.4 = (bf16[4,88,256]{2,1,0:T(8,128)(2,1)S(1)}, bf16[4,88,256]{2,1,0:T(8,128)(2,1)S(1)}, u32[]{:S(2)}, u32[]{:S(2)}) collective-permute-start(bf16[4,88,256]{2,1,0:T(8,128)(2,1)S(1)} %get-tuple-element.64), channel_id=1, source_target_pairs={{0,4},{4,0},{8,12},{12,8},{16,20},{20,16},{24,28},{28,24},{1,5},{5... | collective-permute-start | bytes 540680 | tf_op jit(solution)/shard_map/ppermute | solution.py:426
  73.5 16.0 %collective-permute-start.5 = (bf16[4,88,256]{2,1,0:T(8,128)(2,1)S(1)}, bf16[4,88,256]{2,1,0:T(8,128)(2,1)S(1)}, u32[]{:S(2)}, u32[]{:S(2)}) collective-permute-start(bf16[4,88,256]{2,1,0:T(8,128)(2,1)S(1)} %get-tuple-element.65), channel_id=1, source_target_pairs={{0,8},{4,12},{8,0},{12,4},{16,24},{20,28},{24,16},{28,20},{1,9},{5... | collective-permute-start | bytes 540680 | tf_op jit(solution)/shard_map/ppermute | solution.py:426
  75.1 18.3 %collective-permute-start.6 = (bf16[4,88,256]{2,1,0:T(8,128)(2,1)S(1)}, bf16[4,88,256]{2,1,0:T(8,128)(2,1)S(1)}, u32[]{:S(2)}, u32[]{:S(2)}) collective-permute-start(bf16[4,88,256]{2,1,0:T(8,128)(2,1)S(1)} %get-tuple-element.66), channel_id=1, source_target_pairs={{0,12},{4,8},{8,4},{12,0},{16,28},{20,24},{24,20},{28,16},{1,13},{... | collective-permute-start | bytes 540680 | tf_op jit(solution)/shard_map/ppermute | solution.py:426
  75.1 18.3 %collective-permute-start.7 = (bf16[4,88,256]{2,1,0:T(8,128)(2,1)S(1)}, bf16[4,88,256]{2,1,0:T(8,128)(2,1)S(1)}, u32[]{:S(2)}, u32[]{:S(2)}) collective-permute-start(bf16[4,88,256]{2,1,0:T(8,128)(2,1)S(1)} %get-tuple-element.67), channel_id=1, source_target_pairs={{0,16},{4,20},{8,24},{12,28},{16,0},{20,4},{24,8},{28,12},{1,17},{... | collective-permute-start | bytes 540680 | tf_op jit(solution)/shard_map/ppermute | solution.py:426
  76.8 16.9 %collective-permute-start.8 = (bf16[4,88,256]{2,1,0:T(8,128)(2,1)S(1)}, bf16[4,88,256]{2,1,0:T(8,128)(2,1)S(1)}, u32[]{:S(2)}, u32[]{:S(2)}) collective-permute-start(bf16[4,88,256]{2,1,0:T(8,128)(2,1)S(1)} %get-tuple-element.68), channel_id=1, source_target_pairs={{0,20},{4,16},{8,28},{12,24},{16,4},{20,0},{24,12},{28,8},{1,21},{... | collective-permute-start | bytes 540680 | tf_op jit(solution)/shard_map/ppermute | solution.py:426
  77.0 25.6 %collective-permute-start.9 = (bf16[4,88,256]{2,1,0:T(8,128)(2,1)S(1)}, bf16[4,88,256]{2,1,0:T(8,128)(2,1)S(1)}, u32[]{:S(2)}, u32[]{:S(2)}) collective-permute-start(bf16[4,88,256]{2,1,0:T(8,128)(2,1)S(1)} %get-tuple-element.69), channel_id=1, source_target_pairs={{0,24},{4,28},{8,16},{12,20},{16,8},{20,12},{24,0},{28,4},{1,25},{... | collective-permute-start | bytes 540680 | tf_op jit(solution)/shard_map/ppermute | solution.py:426
  89.5 17.0 %collective-permute-start.10 = (bf16[4,88,256]{2,1,0:T(8,128)(2,1)S(1)}, bf16[4,88,256]{2,1,0:T(8,128)(2,1)S(1)}, u32[]{:S(2)}, u32[]{:S(2)}) collective-permute-start(bf16[4,88,256]{2,1,0:T(8,128)(2,1)S(1)} %get-tuple-element.70), channel_id=1, source_target_pairs={{0,28},{4,24},{8,20},{12,16},{16,12},{20,8},{24,4},{28,0},{1,29},{... | collective-permute-start | bytes 540680 | tf_op jit(solution)/shard_map/ppermute | solution.py:426

commit v6 on v1

v6 whole, which is shorter than its diff:
```python
import functools
import math

import jax
import jax.numpy as jnp
from jax import lax
from jax.experimental import pallas as pl
from jax.experimental.pallas import tpu as pltpu
from jax.sharding import PartitionSpec as P

ITERS = 2
CAP = 2
HALVES = 2

coef_a = 3.4445
coef_b = -4.775
coef_c = 2.0315
momentum_beta = 0.95
epsilon = 1e-07

AXES = ("dp", "owner")
MIB = 1024 * 1024
PARAMS = pltpu.CompilerParams(vmem_limit_bytes=24 * MIB)
PACK_PARAMS = pltpu.CompilerParams(vmem_limit_bytes=60 * MIB)
SMEM = pl.BlockSpec(memory_space=pltpu.SMEM)


def round_up(value, multiple):
    return -(-value // multiple) * multiple


def whole(shape):
    return pl.BlockSpec(shape, lambda *_: (0,) * len(shape))


def nesterov_of(grad_ref, momentum_ref, j):
    grad = grad_ref[j].astype(jnp.float32)
    new = momentum_beta * momentum_ref[j] + grad
    return new, (grad + momentum_beta * new).astype(jnp.bfloat16)


def store_slot(slot, plan, i, owner, nesterov, slot_ref):
    other_ref, rank_ref = plan

    @pl.when(rank_ref[i] == slot)
    def _():
        slot_ref[owner] = nesterov
        slot_ref[other_ref[owner]] = nesterov


def pack_kernel(
    chunk, col_size, owner_ref, g_ref, m_ref, first_ref, other_ref, rank_ref, count_ref, list_ref
):
    step = pl.program_id(0)
    devices = first_ref.shape[0]
    mats = rank_ref.shape[0]

    def half_of(d):
        return (d % col_size) // (col_size // HALVES)

    @pl.when(step == 0)
    def _():
        @pl.loop(0, devices)
        def _(d):
            count_ref[d] = 0

        def rank_matrix(i, _):
            owner = owner_ref[i]
            rank_ref[i] = count_ref[owner]
            count_ref[owner] = count_ref[owner] + 1
            return 0

        lax.fori_loop(0, mats, rank_matrix, 0)

        def list_device(d, found):
            owns = jnp.minimum(count_ref[d], 1)
            half = half_of(d)
            row = 2 * jnp.where(owns == 1, half, 1 - half) + owns
            place = found[0]
            for k in range(1, 2 * HALVES):
                place = jnp.where(row == k, found[k], place)
            list_ref[row * devices + place] = d
            return tuple(n + jnp.where(row == k, 1, 0) for k, n in enumerate(found))

        found = lax.fori_loop(0, devices, list_device, (0,) * (2 * HALVES))
        for half in range(HALVES):

            def pair(k, _):
                idle = list_ref[2 * half * devices + k]
                other_ref[list_ref[(2 * half + 1) * devices + k]] = idle
                other_ref[idle] = idle
                return 0

            lax.fori_loop(0, found[2 * half + 1], pair, 0)

    for j in range(chunk):
        i = step * chunk + j
        _, nesterov = nesterov_of(g_ref, m_ref, j)
        store_slot(0, (other_ref, rank_ref), i, owner_ref[i], nesterov, first_ref)


def pack(gradients, momentum, owner_table, devices, col_size):
    mats, rows, cols = gradients.shape
    chunk = 8
    block = pl.BlockSpec((chunk, rows, cols), lambda i, *_: (i, 0, 0))
    return pl.pallas_call(
        functools.partial(pack_kernel, chunk, col_size),
        grid_spec=pltpu.PrefetchScalarGridSpec(
            num_scalar_prefetch=1,
            grid=(mats // chunk,),
            in_specs=[block, block],
            out_specs=[whole((devices, rows, cols)), SMEM, SMEM],
            scratch_shapes=[
                pltpu.SMEM((devices,), jnp.int32),
                pltpu.SMEM((2 * HALVES * devices,), jnp.int32),
            ],
        ),
        out_shape=[
            jax.ShapeDtypeStruct((devices, rows, cols), jnp.bfloat16),
            jax.ShapeDtypeStruct((devices,), jnp.int32),
            jax.ShapeDtypeStruct((mats,), jnp.int32),
        ],
        compiler_params=PACK_PARAMS,
        cost_estimate=pl.CostEstimate(
            flops=4 * mats * rows * cols, bytes_accessed=8 * mats * rows * cols, transcendentals=0
        ),
        name="pack",
    )(owner_table, gradients, momentum)


def momentum_kernel(chunk, owner_ref, other_ref, rank_ref, g_ref, m_ref, nm_ref, second_ref):
    step = pl.program_id(0)
    for j in range(chunk):
        i = step * chunk + j
        new, nesterov = nesterov_of(g_ref, m_ref, j)
        nm_ref[j] = new
        store_slot(1, (other_ref, rank_ref), i, owner_ref[i], nesterov, second_ref)


def update_momentum(gradients, momentum, owner_table, other, rank):
    mats, rows, cols = gradients.shape
    devices = other.shape[0]
    chunk = 8
    block = pl.BlockSpec((chunk, rows, cols), lambda i, *_: (i, 0, 0))
    return pl.pallas_call(
        functools.partial(momentum_kernel, chunk),
        grid_spec=pltpu.PrefetchScalarGridSpec(
            num_scalar_prefetch=3,
            grid=(mats // chunk,),
            in_specs=[block, block],
            out_specs=[block, whole((devices, rows, cols))],
        ),
        out_shape=[
            jax.ShapeDtypeStruct(momentum.shape, jnp.float32),
            jax.ShapeDtypeStruct((devices, rows, cols), jnp.bfloat16),
        ],
        compiler_params=PARAMS,
        cost_estimate=pl.CostEstimate(
            flops=4 * mats * rows * cols, bytes_accessed=12 * mats * rows * cols, transcendentals=0
        ),
        name="update_momentum",
    )(owner_table, other, rank, gradients, momentum)


def matmul(lhs, rhs, rhs_dim):
    return lax.dot_general(
        lhs, rhs, (((1,), (rhs_dim,)), ((), ())), preferred_element_type=jnp.float32
    )


def newton_schulz(rows, cols, row_size, col_size, x_s, y_s, gram_s, mix_s, write):
    padded = round_up(rows, 16)
    tile_blocks = max(row_size // 2, 1)
    tile = padded * tile_blocks
    tiles = row_size // tile_blocks

    total = jnp.zeros((1, cols), jnp.float32)
    for r in range(row_size):
        for c in range(col_size):
            wide = x_s[r * padded : (r + 1) * padded, c * cols : (c + 1) * cols]
            wide = wide.astype(jnp.float32)
            total += jnp.sum(wide * wide, axis=0, keepdims=True)
    magnitude = jnp.sqrt(jnp.sum(total, axis=1, keepdims=True))
    inverse = 1.0 / (magnitude + epsilon)
    update_scale = 0.2 * math.sqrt(max(rows * row_size, cols * col_size))

    for iteration in range(ITERS):
        src = x_s if iteration == 0 else y_s
        for t in range(tiles):
            span = slice(t * tile, (t + 1) * tile)
            gram = matmul(src[span, :], src[...], 1)
            if iteration == 0:
                gram = gram * (inverse * inverse)
            gram_s[span, :] = gram.astype(jnp.bfloat16)
        for t in range(tiles):
            span = slice(t * tile, (t + 1) * tile)
            square = matmul(gram_s[span, :], gram_s[...], 0)
            mix_s[span, :] = (
                coef_b * gram_s[span, :].astype(jnp.float32) + coef_c * square
            ).astype(jnp.bfloat16)
        for t in range(tiles):
            span = slice(t * tile, (t + 1) * tile)
            combined = coef_a * src[span, :].astype(jnp.float32) + matmul(
                mix_s[span, :], src[...], 0
            )
            if iteration == 0:
                combined = combined * inverse
            if iteration + 1 < ITERS:
                y_s[span, :] = combined.astype(jnp.bfloat16)
            else:
                result = (update_scale * combined).astype(jnp.bfloat16)
                for j in range(tile_blocks):
                    write(t * tile_blocks + j, result[j * padded : j * padded + rows, :])


def clear_padding(x_s, rows, row_size):
    padded = round_up(rows, 16)
    if padded > rows:
        for r in range(row_size):
            x_s[r * padded + rows : (r + 1) * padded, :] = jnp.zeros(
                (padded - rows, x_s.shape[1]), x_s.dtype
            )


def gather_blocks(x_ref, x_s, row_size, col_size):
    _, rows, cols = x_ref.shape
    padded = round_up(rows, 16)
    for r in range(row_size):
        for c in range(col_size):
            x_s[r * padded : r * padded + rows, c * cols : (c + 1) * cols] = x_ref[
                r * col_size + c
            ]


def ortho_kernel(row_size, col_size, slot, other_ref, x_ref, *refs):
    owned_ref, back_ref = refs[slot : slot + 2]
    scratch = refs[slot + 2 :]
    _, rows, cols = x_ref.shape
    width = col_size // HALVES
    col = lax.axis_index("owner")
    me = lax.axis_index("dp") * col_size + col
    owns = other_ref[me] != me
    low = col < width
    clear_padding(scratch[0], rows, row_size)
    gather_blocks(x_ref, scratch[0], row_size, col_size)

    def write(r, block):
        owned_ref[0, r * rows : (r + 1) * rows, :] = jnp.where(owns, block, jnp.zeros_like(block))
        for c in range(width):
            back_ref[r * width + c] = jnp.where(
                low,
                block[:, c * cols : (c + 1) * cols],
                block[:, (c + width) * cols : (c + width + 1) * cols],
            )

    newton_schulz(rows, cols, row_size, col_size, *scratch, write)


def orthogonalize(slot, other, arrived, row_size, col_size, owned=None):
    devices, rows, cols = arrived.shape
    height, width = rows * row_size, cols * col_size
    padded = round_up(rows, 16) * row_size
    in_specs, operands = [SMEM, whole(arrived.shape)], [other, arrived]
    if slot:
        in_specs.append(pl.BlockSpec(memory_space=pl.ANY))
        operands.append(owned)
    back = (devices // HALVES, rows, cols)
    return pl.pallas_call(
        functools.partial(ortho_kernel, row_size, col_size, slot),
        grid=(1,),
        in_specs=in_specs,
        out_specs=[pl.BlockSpec((1, height, width), lambda i: (slot, 0, 0)), whole(back)],
        out_shape=[
            jax.ShapeDtypeStruct((CAP, height, width), jnp.bfloat16),
            jax.ShapeDtypeStruct(back, jnp.bfloat16),
        ],
        scratch_shapes=[
            pltpu.VMEM((padded, width), jnp.bfloat16),
            pltpu.VMEM((padded, width), jnp.bfloat16),
            pltpu.VMEM((padded, padded), jnp.bfloat16),
            pltpu.VMEM((padded, padded), jnp.bfloat16),
        ],
        input_output_aliases={2: 0} if slot else {},
        compiler_params=PARAMS,
        cost_estimate=pl.CostEstimate(
            flops=2 * ITERS * padded * padded * (2 * width + padded),
            bytes_accessed=6 * padded * width,
            transcendentals=0,
        ),
        name="orthogonalize",
    )(*operands)


def unpack_kernel(
    chunk, col_size, owner_ref, other_ref, rank_ref, first_ref, second_ref, update_ref
):
    step = pl.program_id(0)
    width = col_size // HALVES
    half = lax.axis_index("owner") // width
    for j in range(chunk):
        i = step * chunk + j
        owner = owner_ref[i]
        host = jnp.where((owner % col_size) // width == half, owner, other_ref[owner])
        place = (host // col_size) * width + host % width

        @pl.when(rank_ref[i] == 0)
        def _():
            update_ref[j] = first_ref[place]

        @pl.when(rank_ref[i] == 1)
        def _():
            update_ref[j] = second_ref[place]


def unpack(owner_table, other, rank, first, second, col_size):
    places, rows, cols = first.shape
    mats = owner_table.shape[0]
    chunk = 8
    return pl.pallas_call(
        functools.partial(unpack_kernel, chunk, col_size),
        grid_spec=pltpu.PrefetchScalarGridSpec(
            num_scalar_prefetch=3,
            grid=(mats // chunk,),
            in_specs=[whole(first.shape)] * 2,
            out_specs=pl.BlockSpec((chunk, rows, cols), lambda i, *_: (i, 0, 0)),
        ),
        out_shape=jax.ShapeDtypeStruct((mats, rows, cols), jnp.bfloat16),
        compiler_params=PARAMS,
        cost_estimate=pl.CostEstimate(
            flops=0, bytes_accessed=4 * mats * rows * cols, transcendentals=0
        ),
        name="unpack",
    )(owner_table, other, rank, first, second)


def exchange(blocks, groups=None):
    return lax.all_to_all(
        blocks, AXES, split_axis=0, concat_axis=0, tiled=True, axis_index_groups=groups
    )


def on_device(gradients, momentum, owner_table):
    row_size = lax.axis_size("dp")
    col_size = lax.axis_size("owner")
    devices = row_size * col_size
    width = col_size // HALVES
    halves = [
        [r * col_size + half * width + c for r in range(row_size) for c in range(width)]
        for half in range(HALVES)
    ]
    first, other, rank = pack(gradients, momentum, owner_table, devices, col_size)
    arrived_first = exchange(first)
    new_momentum, second = update_momentum(gradients, momentum, owner_table, other, rank)
    arrived_first, second = lax.optimization_barrier((arrived_first, second))
    arrived_second = exchange(second)
    owned, back_first = orthogonalize(0, other, arrived_first, row_size, col_size)
    back_first, arrived_second = lax.optimization_barrier((back_first, arrived_second))
    returned_first = exchange(back_first, halves)
    owned, back_second = orthogonalize(1, other, arrived_second, row_size, col_size, owned)
    returned_second = exchange(back_second, halves)
    update = unpack(owner_table, other, rank, returned_first, returned_second, col_size)
    return (new_momentum, update, owned)


def solution(mesh):
    return jax.shard_map(
        on_device,
        mesh=mesh,
        in_specs=(P(None, "dp", "owner"), P(None, "dp", "owner"), P()),
        out_specs=(P(None, "dp", "owner"), P(None, "dp", "owner"), P(("dp", "owner"), None, None)),
        check_vma=False,
    )
```

time: 169 us -> 118 us (0.70)
  blocking collectives: 80.7 us -> 15.1 us
  starting transfers between devices: 8.6 us -> 16.7 us
  waiting for transfers between devices: 46.4 us -> 53.6 us
    all_to_all x2 -> x1, blocking collectives: 80.7 us -> 15.1 us  [exchange(): lax.all_to_all(blocks, AXES, split_axis=0, concat_axis=0, tiled=True, axi...]
    all_to_all x2 -> x3, starting transfers between devices: 8.6 us -> 16.7 us  [exchange(): lax.all_to_all(blocks, AXES, split_axis=0, concat_axis=0, tiled=True, axi...]
    all_to_all x2 -> x3, waiting for transfers between devices: 46.4 us -> 53.6 us  [exchange(): lax.all_to_all(blocks, AXES, split_axis=0, concat_axis=0, tiled=True, axi...]
    pallas_call x4 -> x5, Pallas kernels: 30.5 us -> 29.2 us  [the longest x2 18.4 us: orthogonalize(): pl.pallas_call(functools.partial(ortho_kernel, row_size, col_size, slot),...]
  transfers between devices with their start and end apart: 2 -> 3, of which waited for: 2 -> 3; matrix products, arithmetic and copies ran while one was open for 0% -> 0% of each run, Pallas kernels for 12% -> 18%
where the time goes in v6:
time: 118 us
  waiting for transfers between devices  53.6 us (45%)
  Pallas kernels  29.2 us (25%)
  starting transfers between devices  16.7 us (14%)
  blocking collectives  15.1 us (13%)
  local copies, waits for them, and re-layouts  2.49 us (2%)
    all_to_all x3, waiting for transfers between devices, exchange(): lax.all_to_all(blocks, AXES, split_axis=0, concat_axis=0, tiled=True, axi...  53.6 us
    pallas_call x2, Pallas kernels, orthogonalize(): pl.pallas_call(functools.partial(ortho_kernel, row_size, col_size, slot),...  18.4 us
    all_to_all x3, starting transfers between devices, exchange(): lax.all_to_all(blocks, AXES, split_axis=0, concat_axis=0, tiled=True, axi...  16.7 us
    all_to_all x1, blocking collectives, exchange(): lax.all_to_all(blocks, AXES, split_axis=0, concat_axis=0, tiled=True, axi...  15.1 us
    pallas_call x1, Pallas kernels, pack(): pl.pallas_call(functools.partial(pack_kernel, chunk, col_size), grid_spec...  5.14 us
    pallas_call x1, Pallas kernels, update_momentum(): pl.pallas_call(functools.partial(momentum_kernel, chunk), grid_spec=pltpu...  2.84 us
    pallas_call x1, Pallas kernels, unpack(): pl.pallas_call(functools.partial(unpack_kernel, chunk, col_size), grid_sp...  2.82 us
    unnamed x12, local copies, waits for them, and re-layouts  2.49 us
  transfers between devices with their start and end apart: 3, of which 3 were waited for; matrix products, arithmetic and copies ran while one was open for 0% of the time, Pallas kernels for 18%

profile of v6, /device:TPU:0, one launch (start us, length us, event | category | flops | bytes accessed | tf_op | source)
XLA Modules:
  0.0 117.8 jit_solution(16925666050738239636)
XLA Ops:
  0.6 5.1 %pack.1 = (bf16[32,88,256]{2,1,0:T(8,128)(2,1)}, s32[32]{0:T(128)}, s32[32]{0:T(128)}) custom-call(s32[32]{0:T(128)} %owner_ref.5, bf16[32,88,256]{2,1,0:T(8,128)(2,1)} %g_ref.3, f32[32,88,256]{2,1,0:T(8,128)} %m_ref.3), custom_call_target="tpu_custom_call" | custom-call | flops 2883584 | bytes 5767168 | tf_op jit(solution)/shard_map/pack/pallas_call | solution.py:106
  5.8 0.0 copy-start
  5.8 0.0 copy-start.3
  5.8 0.0 copy-start.4
  5.8 0.0 copy-start.5
  5.8 7.4 %all-to-all-start = ((bf16[32,88,256]{2,1,0:T(8,128)(2,1)}), bf16[32,88,256]{2,1,0:T(8,128)(2,1)}, u32[]{:S(2)}, u32[]{:S(2)}) async-start(bf16[32,88,256]{2,1,0:T(8,128)(2,1)} %get-tuple-element.19), calls=%async_computation | async-start | bytes 2883584 | tf_op jit(solution)/shard_map/all_to_all | solution.py:337
  13.3 0.0 copy-done
  13.3 0.0 copy-done.3
  13.3 0.0 copy-done.4
  13.3 0.0 copy-done.5
  13.3 0.0 copy-start.1
  13.3 1.4 %copy-done.1 = bf16[32,88,256]{2,1,0:T(8,128)(2,1)S(1)} copy-done((bf16[32,88,256]{2,1,0:T(8,128)(2,1)S(1)}, bf16[32,88,256]{2,1,0:T(8,128)(2,1)}, u32[]{:S(2)}) %copy-start.1) | copy-done | bytes 1441816
  14.7 2.8 %update_momentum.1 = (f32[32,88,256]{2,1,0:T(8,128)}, bf16[32,88,256]{2,1,0:T(8,128)(2,1)S(1)}) custom-call(s32[32]{0:T(128)S(1)} %copy-done.3, s32[32]{0:T(128)S(1)} %copy-done.4, s32[32]{0:T(128)S(1)} %copy-done.5, bf16[32,88,256]{2,1,0:T(8,128)(2,1)S(1)} %copy-done.1, f32[32,88,256]{2,1,0:T(8,128)S(1)} %copy-done), custom_call_target="tpu_custom_call" | custom-call | flops 2883584 | bytes 8650752 | tf_op jit(solution)/shard_map/update_momentum/pallas_call | solution.py:145
  17.5 0.0 copy-start.2
  17.5 1.1 copy-done.2
  18.6 27.9 %all-to-all-done.x_ref = bf16[32,88,256]{2,1,0:T(8,128)(2,1)} async-done(((bf16[32,88,256]{2,1,0:T(8,128)(2,1)}), bf16[32,88,256]{2,1,0:T(8,128)(2,1)}, u32[]{:S(2)}, u32[]{:S(2)}) %all-to-all-start) | async-done | bytes 1441824 | tf_op jit(solution)/shard_map/all_to_all | solution.py:337
  46.5 4.6 %all-to-all-start.1 = ((bf16[32,88,256]{2,1,0:T(8,128)(2,1)}), bf16[32,88,256]{2,1,0:T(8,128)(2,1)S(1)}, u32[]{:S(2)}, u32[]{:S(2)}) async-start(bf16[32,88,256]{2,1,0:T(8,128)(2,1)} %copy-done.2), calls=%async_computation.1 | async-start | bytes 2883584 | tf_op jit(solution)/shard_map/all_to_all | solution.py:337
  51.0 9.7 %orthogonalize.2 = (bf16[2,704,1024]{2,1,0:T(8,128)(2,1)}, bf16[16,88,256]{2,1,0:T(8,128)(2,1)}) custom-call(s32[32]{0:T(128)S(1)} %copy-done.4, bf16[32,88,256]{2,1,0:T(8,128)(2,1)} %all-to-all-done.x_ref), custom_call_target="tpu_custom_call" | custom-call | flops 6643777536 | bytes 4718592 | tf_op jit(solution)/shard_map/orthogonalize/pallas_call | solution.py:268
  60.7 23.5 %all-to-all-done.1.x_ref = bf16[32,88,256]{2,1,0:T(8,128)(2,1)S(1)} async-done(((bf16[32,88,256]{2,1,0:T(8,128)(2,1)}), bf16[32,88,256]{2,1,0:T(8,128)(2,1)S(1)}, u32[]{:S(2)}, u32[]{:S(2)}) %all-to-all-start.1) | async-done | bytes 1441824 | tf_op jit(solution)/shard_map/all_to_all | solution.py:337
  84.3 4.7 %all-to-all-start.2 = ((bf16[16,88,256]{2,1,0:T(8,128)(2,1)}), bf16[16,88,256]{2,1,0:T(8,128)(2,1)S(1)}, u32[]{:S(2)}, u32[]{:S(2)}) async-start(bf16[16,88,256]{2,1,0:T(8,128)(2,1)} %get-tuple-element.24), calls=%async_computation.2 | async-start | bytes 1441792 | tf_op jit(solution)/shard_map/all_to_all | solution.py:337
  89.0 8.7 %orthogonalize.3 = (bf16[2,704,1024]{2,1,0:T(8,128)(2,1)}, bf16[16,88,256]{2,1,0:T(8,128)(2,1)S(1)}) custom-call(s32[32]{0:T(128)S(1)} %copy-done.4, bf16[32,88,256]{2,1,0:T(8,128)(2,1)S(1)} %all-to-all-done.1.x_ref, bf16[2,704,1024]{2,1,0:T(8,128)(2,1)} %get-tuple-element.26.refs_0_), custom_call_target="tpu_custom_call", output_to_operand_aliasing={{0}: (2, {})} | custom-call | flops 6643777536 | bytes 4718592 | tf_op jit(solution)/shard_map/orthogonalize/pallas_call | solution.py:268
  97.7 2.2 %all-to-all-done.2.first_ref = bf16[16,88,256]{2,1,0:T(8,128)(2,1)S(1)} async-done(((bf16[16,88,256]{2,1,0:T(8,128)(2,1)}), bf16[16,88,256]{2,1,0:T(8,128)(2,1)S(1)}, u32[]{:S(2)}, u32[]{:S(2)}) %all-to-all-start.2) | async-done | bytes 720928 | tf_op jit(solution)/shard_map/all_to_all | solution.py:337
  99.9 15.1 %all_to_all.20.second_ref = bf16[16,88,256]{2,1,0:T(8,128)(2,1)S(1)} all-to-all(bf16[16,88,256]{2,1,0:T(8,128)(2,1)S(1)} %get-tuple-element.27), channel_id=1, replica_groups={{0,1,4,5,8,9,12,13,16,17,20,21,24,25,28,29},{2,3,6,7,10,11,14,15,18,19,..., dimensions={0} | all-to-all | bytes 1441792 | tf_op jit(solution)/shard_map/all_to_all | solution.py:337
  115.0 2.8 %unpack.1 = bf16[32,88,256]{2,1,0:T(8,128)(2,1)} custom-call(s32[32]{0:T(128)S(1)} %copy-done.3, s32[32]{0:T(128)S(1)} %copy-done.4, s32[32]{0:T(128)S(1)} %copy-done.5, bf16[16,88,256]{2,1,0:T(8,128)(2,1)S(1)} %all-to-all-done.2.first_ref, bf16[16,88,256]{2,1,0:T(8,128)(2,1)S(1)} %all_to_all.20.second_ref), custom_call_target="tpu_custom_call" | custom-call | bytes 2883584 | tf_op jit(solution)/shard_map/unpack/pallas_call | solution.py:319
Async XLA Ops:
  5.8 7.5 %copy-start = (f32[32,88,256]{2,1,0:T(8,128)S(1)}, f32[32,88,256]{2,1,0:T(8,128)}, u32[]{:S(2)}) copy-start(f32[32,88,256]{2,1,0:T(8,128)} %m_ref.3) | copy-start | bytes 8650756
  5.8 7.5 %copy-start.3 = (s32[32]{0:T(128)S(1)}, s32[32]{0:T(128)}, u32[]{:S(2)}) copy-start(s32[32]{0:T(128)} %owner_ref.5) | copy-start | bytes 388
  5.8 7.5 %copy-start.4 = (s32[32]{0:T(128)S(1)}, s32[32]{0:T(128)}, u32[]{:S(2)}) copy-start(s32[32]{0:T(128)} %get-tuple-element.16.other_ref) | copy-start | bytes 388
  5.8 7.5 %copy-start.5 = (s32[32]{0:T(128)S(1)}, s32[32]{0:T(128)}, u32[]{:S(2)}) copy-start(s32[32]{0:T(128)} %get-tuple-element.17.rank_ref) | copy-start | bytes 388
  5.8 40.6 %all-to-all-start = ((bf16[32,88,256]{2,1,0:T(8,128)(2,1)}), bf16[32,88,256]{2,1,0:T(8,128)(2,1)}, u32[]{:S(2)}, u32[]{:S(2)}) async-start(bf16[32,88,256]{2,1,0:T(8,128)(2,1)} %get-tuple-element.19), calls=%async_computation | async-start | bytes 2883584 | tf_op jit(solution)/shard_map/all_to_all | solution.py:337
  13.3 1.4 %copy-start.1 = (bf16[32,88,256]{2,1,0:T(8,128)(2,1)S(1)}, bf16[32,88,256]{2,1,0:T(8,128)(2,1)}, u32[]{:S(2)}) copy-start(bf16[32,88,256]{2,1,0:T(8,128)(2,1)} %g_ref.3) | copy-start | bytes 4325380
  17.5 1.1 copy-start.2
  46.5 37.8 %all-to-all-start.1 = ((bf16[32,88,256]{2,1,0:T(8,128)(2,1)}), bf16[32,88,256]{2,1,0:T(8,128)(2,1)S(1)}, u32[]{:S(2)}, u32[]{:S(2)}) async-start(bf16[32,88,256]{2,1,0:T(8,128)(2,1)} %copy-done.2), calls=%async_computation.1 | async-start | bytes 2883584 | tf_op jit(solution)/shard_map/all_to_all | solution.py:337
  84.3 15.6 %all-to-all-start.2 = ((bf16[16,88,256]{2,1,0:T(8,128)(2,1)}), bf16[16,88,256]{2,1,0:T(8,128)(2,1)S(1)}, u32[]{:S(2)}, u32[]{:S(2)}) async-start(bf16[16,88,256]{2,1,0:T(8,128)(2,1)} %get-tuple-element.24), calls=%async_computation.2 | async-start | bytes 1441792 | tf_op jit(solution)/shard_map/all_to_all | solution.py:337

commit v7 on v6

--- a/solution.py
+++ b/solution.py
@@ -233,12 +233,17 @@
 
 
 def ortho_kernel(row_size, col_size, slot, other_ref, x_ref, *refs):
-    owned_ref, back_ref = refs[slot : slot + 2]
-    scratch = refs[slot + 2 :]
     _, rows, cols = x_ref.shape
     width = col_size // HALVES
-    col = lax.axis_index("owner")
-    me = lax.axis_index("dp") * col_size + col
+    places = row_size * width
+    if slot:
+        owned_ref, back_ref = refs[1:3]
+        scratch = refs[3:]
+    else:
+        owned_ref, offset_refs, back_ref = refs[0], refs[1 : 1 + places], refs[-1]
+        scratch = refs[1 + places : -1]
+    row, col = lax.axis_index("dp"), lax.axis_index("owner")
+    me = row * col_size + col
     owns = other_ref[me] != me
     low = col < width
     clear_padding(scratch[0], rows, row_size)
@@ -247,39 +252,47 @@
     def write(r, block):
         owned_ref[0, r * rows : (r + 1) * rows, :] = jnp.where(owns, block, jnp.zeros_like(block))
         for c in range(width):
-            back_ref[r * width + c] = jnp.where(
+            place = r * width + c if slot else (r ^ row) * width + (c ^ (col % width))
+            back_ref[place] = jnp.where(
                 low,
                 block[:, c * cols : (c + 1) * cols],
                 block[:, (c + width) * cols : (c + width + 1) * cols],
             )
 
     newton_schulz(rows, cols, row_size, col_size, *scratch, write)
+    if not slot:
+        for offset in range(places):
+            offset_refs[offset][...] = back_ref[offset]
 
 
 def orthogonalize(slot, other, arrived, row_size, col_size, owned=None):
     devices, rows, cols = arrived.shape
     height, width = rows * row_size, cols * col_size
     padded = round_up(rows, 16) * row_size
+    places = devices // HALVES
     in_specs, operands = [SMEM, whole(arrived.shape)], [other, arrived]
+    scratch_shapes = [
+        pltpu.VMEM((padded, width), jnp.bfloat16),
+        pltpu.VMEM((padded, width), jnp.bfloat16),
+        pltpu.VMEM((padded, padded), jnp.bfloat16),
+        pltpu.VMEM((padded, padded), jnp.bfloat16),
+    ]
     if slot:
         in_specs.append(pl.BlockSpec(memory_space=pl.ANY))
         operands.append(owned)
-    back = (devices // HALVES, rows, cols)
-    return pl.pallas_call(
+        back = [(places, rows, cols)]
+    else:
+        back = [(rows, cols)] * places
+        scratch_shapes.append(pltpu.VMEM((places, rows, cols), jnp.bfloat16))
+    owned, *back = pl.pallas_call(
         functools.partial(ortho_kernel, row_size, col_size, slot),
         grid=(1,),
         in_specs=in_specs,
-        out_specs=[pl.BlockSpec((1, height, width), lambda i: (slot, 0, 0)), whole(back)],
-        out_shape=[
-            jax.ShapeDtypeStruct((CAP, height, width), jnp.bfloat16),
-            jax.ShapeDtypeStruct(back, jnp.bfloat16),
-        ],
-        scratch_shapes=[
-            pltpu.VMEM((padded, width), jnp.bfloat16),
-            pltpu.VMEM((padded, width), jnp.bfloat16),
-            pltpu.VMEM((padded, padded), jnp.bfloat16),
-            pltpu.VMEM((padded, padded), jnp.bfloat16),
-        ],
+        out_specs=[pl.BlockSpec((1, height, width), lambda i: (slot, 0, 0))]
+        + [whole(shape) for shape in back],
+        out_shape=[jax.ShapeDtypeStruct((CAP, height, width), jnp.bfloat16)]
+        + [jax.ShapeDtypeStruct(shape, jnp.bfloat16) for shape in back],
+        scratch_shapes=scratch_shapes,
         input_output_aliases={2: 0} if slot else {},
         compiler_params=PARAMS,
         cost_estimate=pl.CostEstimate(
@@ -289,40 +302,49 @@
         ),
         name="orthogonalize",
     )(*operands)
-
-
-def unpack_kernel(
-    chunk, col_size, owner_ref, other_ref, rank_ref, first_ref, second_ref, update_ref
-):
+    return owned, back
+
+
+def unpack_kernel(chunk, col_size, row_size, owner_ref, other_ref, rank_ref, *refs):
+    width = col_size // HALVES
+    places = row_size * width
+    offset_refs, second_ref, update_ref, first_ref = refs[:places], *refs[places:]
     step = pl.program_id(0)
-    width = col_size // HALVES
-    half = lax.axis_index("owner") // width
+    row, col = lax.axis_index("dp"), lax.axis_index("owner")
+    half = col // width
+
+    @pl.when(step == 0)
+    def _():
+        for offset in range(places):
+            first_ref[offset] = offset_refs[offset][...]
+
     for j in range(chunk):
         i = step * chunk + j
         owner = owner_ref[i]
         host = jnp.where((owner % col_size) // width == half, owner, other_ref[owner])
-        place = (host // col_size) * width + host % width
+        host_row, host_col = host // col_size, host % width
 
         @pl.when(rank_ref[i] == 0)
         def _():
-            update_ref[j] = first_ref[place]
+            update_ref[j] = first_ref[(host_row ^ row) * width + (host_col ^ (col % width))]
 
         @pl.when(rank_ref[i] == 1)
         def _():
-            update_ref[j] = second_ref[place]
-
-
-def unpack(owner_table, other, rank, first, second, col_size):
-    places, rows, cols = first.shape
+            update_ref[j] = second_ref[host_row * width + host_col]
+
+
+def unpack(owner_table, other, rank, first, second, row_size, col_size):
+    places, rows, cols = second.shape
     mats = owner_table.shape[0]
     chunk = 8
     return pl.pallas_call(
-        functools.partial(unpack_kernel, chunk, col_size),
+        functools.partial(unpack_kernel, chunk, col_size, row_size),
         grid_spec=pltpu.PrefetchScalarGridSpec(
             num_scalar_prefetch=3,
             grid=(mats // chunk,),
-            in_specs=[whole(first.shape)] * 2,
+            in_specs=[whole((rows, cols))] * places + [whole(second.shape)],
             out_specs=pl.BlockSpec((chunk, rows, cols), lambda i, *_: (i, 0, 0)),
+            scratch_shapes=[pltpu.VMEM(second.shape, jnp.bfloat16)],
         ),
         out_shape=jax.ShapeDtypeStruct((mats, rows, cols), jnp.bfloat16),
         compiler_params=PARAMS,
@@ -330,13 +352,17 @@
             flops=0, bytes_accessed=4 * mats * rows * cols, transcendentals=0
         ),
         name="unpack",
-    )(owner_table, other, rank, first, second)
+    )(owner_table, other, rank, *first, second)
 
 
 def exchange(blocks, groups=None):
     return lax.all_to_all(
         blocks, AXES, split_axis=0, concat_axis=0, tiled=True, axis_index_groups=groups
     )
+
+
+def swap(block, offset, devices):
+    return lax.ppermute(block, AXES, [(d, d ^ offset) for d in range(devices)])
 
 
 def on_device(gradients, momentum, owner_table):
@@ -354,11 +380,18 @@
     arrived_first, second = lax.optimization_barrier((arrived_first, second))
     arrived_second = exchange(second)
     owned, back_first = orthogonalize(0, other, arrived_first, row_size, col_size)
-    back_first, arrived_second = lax.optimization_barrier((back_first, arrived_second))
-    returned_first = exchange(back_first, halves)
+    returned_first = [back_first[0]] + [
+        swap(back_first[r * width + c], r * col_size + c, devices)
+        for r in range(row_size)
+        for c in range(width)
+        if r or c
+    ]
+    returned_first, arrived_second = lax.optimization_barrier((returned_first, arrived_second))
     owned, back_second = orthogonalize(1, other, arrived_second, row_size, col_size, owned)
-    returned_second = exchange(back_second, halves)
-    update = unpack(owner_table, other, rank, returned_first, returned_second, col_size)
+    returned_second = exchange(back_second[0], halves)
+    update = unpack(
+        owner_table, other, rank, returned_first, returned_second, row_size, col_size
+    )
     return (new_momentum, update, owned)
 
 

time: 118 us -> 121 us (1.025)
  starting transfers between devices: 16.7 us -> 32.6 us
  waiting for transfers between devices: 53.6 us -> 40.4 us
    all_to_all x3 -> x2, waiting for transfers between devices: 53.6 us -> 27.8 us  [exchange(): lax.all_to_all(blocks, AXES, split_axis=0, concat_axis=0, tiled=True, axi...]
    ppermute x0 -> x15, starting transfers between devices: none -> 20.6 us  [swap(): return lax.ppermute(block, AXES, [(d, d ^ offset) for d in range(devices)])]
    ppermute x0 -> x15, waiting for transfers between devices: none -> 12.5 us  [swap(): return lax.ppermute(block, AXES, [(d, d ^ offset) for d in range(devices)])]
    all_to_all x3 -> x2, starting transfers between devices: 16.7 us -> 12 us  [exchange(): lax.all_to_all(blocks, AXES, split_axis=0, concat_axis=0, tiled=True, axi...]
  transfers between devices with their start and end apart: 3 -> 17, of which waited for: 3 -> 4; matrix products, arithmetic and copies ran while one was open for 0% -> 0% of each run, Pallas kernels for 18% -> 10%
where the time goes in v7:
time: 121 us
  waiting for transfers between devices  40.4 us (33%)
  starting transfers between devices  32.6 us (27%)
  Pallas kernels  29.1 us (24%)
  blocking collectives  15.9 us (13%)
  local copies, waits for them, and re-layouts  2.49 us (2%)
    all_to_all x2, waiting for transfers between devices, exchange(): lax.all_to_all(blocks, AXES, split_axis=0, concat_axis=0, tiled=True, axi...  27.8 us
    ppermute x15, starting transfers between devices, swap(): return lax.ppermute(block, AXES, [(d, d ^ offset) for d in range(devices)])  20.6 us
    pallas_call x2, Pallas kernels, orthogonalize(): pl.pallas_call(functools.partial(ortho_kernel, row_size, col_size, slot),...  18.1 us
    all_to_all x1, blocking collectives, exchange(): lax.all_to_all(blocks, AXES, split_axis=0, concat_axis=0, tiled=True, axi...  15.9 us
    ppermute x15, waiting for transfers between devices, swap(): return lax.ppermute(block, AXES, [(d, d ^ offset) for d in range(devices)])  12.5 us
    all_to_all x2, starting transfers between devices, exchange(): lax.all_to_all(blocks, AXES, split_axis=0, concat_axis=0, tiled=True, axi...  12 us
    pallas_call x1, Pallas kernels, pack(): pl.pallas_call(functools.partial(pack_kernel, chunk, col_size), grid_spec...  5.14 us
    pallas_call x1, Pallas kernels, unpack(): pl.pallas_call(functools.partial(unpack_kernel, chunk, col_size, row_size...  2.95 us
  transfers between devices with their start and end apart: 17, of which 4 were waited for; matrix products, arithmetic and copies ran while one was open for 0% of the time, Pallas kernels for 10%

profile of v7, /device:TPU:0, one launch (start us, length us, event | category | flops | bytes accessed | tf_op | source)
XLA Modules:
  0.0 121.1 jit_solution(3348756145202913327)
XLA Ops:
  0.6 5.1 %pack.1 = (bf16[32,88,256]{2,1,0:T(8,128)(2,1)}, s32[32]{0:T(128)}, s32[32]{0:T(128)}) custom-call(s32[32]{0:T(128)} %owner_ref.5, bf16[32,88,256]{2,1,0:T(8,128)(2,1)} %g_ref.3, f32[32,88,256]{2,1,0:T(8,128)} %m_ref.3), custom_call_target="tpu_custom_call" | custom-call | flops 2883584 | bytes 5767168 | tf_op jit(solution)/shard_map/pack/pallas_call | solution.py:106
  5.8 0.0 copy-start
  5.8 0.0 copy-start.3
  5.8 0.0 copy-start.4
  5.8 0.0 copy-start.5
  5.8 7.4 %all-to-all-start = ((bf16[32,88,256]{2,1,0:T(8,128)(2,1)}), bf16[32,88,256]{2,1,0:T(8,128)(2,1)}, u32[]{:S(2)}, u32[]{:S(2)}) async-start(bf16[32,88,256]{2,1,0:T(8,128)(2,1)} %get-tuple-element.49), calls=%async_computation | async-start | bytes 2883584 | tf_op jit(solution)/shard_map/all_to_all | solution.py:359
  13.3 0.0 copy-done
  13.3 0.0 copy-start.1
  13.3 1.4 %copy-done.1 = bf16[32,88,256]{2,1,0:T(8,128)(2,1)S(1)} copy-done((bf16[32,88,256]{2,1,0:T(8,128)(2,1)S(1)}, bf16[32,88,256]{2,1,0:T(8,128)(2,1)}, u32[]{:S(2)}) %copy-start.1) | copy-done | bytes 1441816
  14.7 2.9 %update_momentum.1 = (f32[32,88,256]{2,1,0:T(8,128)}, bf16[32,88,256]{2,1,0:T(8,128)(2,1)S(1)}) custom-call(s32[32]{0:T(128)S(1)} %copy-done.3, s32[32]{0:T(128)S(1)} %copy-done.4, s32[32]{0:T(128)S(1)} %copy-done.5, bf16[32,88,256]{2,1,0:T(8,128)(2,1)S(1)} %copy-done.1, f32[32,88,256]{2,1,0:T(8,128)S(1)} %copy-done), custom_call_target="tpu_custom_call" | custom-call | flops 2883584 | bytes 8650752 | tf_op jit(solution)/shard_map/update_momentum/pallas_call | solution.py:145
  17.5 1.1 copy-done.2
  18.6 27.8 %all-to-all-done.x_ref = bf16[32,88,256]{2,1,0:T(8,128)(2,1)} async-done(((bf16[32,88,256]{2,1,0:T(8,128)(2,1)}), bf16[32,88,256]{2,1,0:T(8,128)(2,1)}, u32[]{:S(2)}, u32[]{:S(2)}) %all-to-all-start) | async-done | bytes 1441824 | tf_op jit(solution)/shard_map/all_to_all | solution.py:359
  46.5 4.6 %all-to-all-start.1 = ((bf16[32,88,256]{2,1,0:T(8,128)(2,1)}), bf16[32,88,256]{2,1,0:T(8,128)(2,1)S(1)}, u32[]{:S(2)}, u32[]{:S(2)}) async-start(bf16[32,88,256]{2,1,0:T(8,128)(2,1)} %copy-done.2), calls=%async_computation.1 | async-start | bytes 2883584 | tf_op jit(solution)/shard_map/all_to_all | solution.py:359
  51.0 9.5 %orthogonalize.2 = (bf16[2,704,1024]{2,1,0:T(8,128)(2,1)}, bf16[88,256]{1,0:T(8,128)(2,1)S(1)}, bf16[88,256]{1,0:T(8,128)(2,1)S(1)}, bf16[88,256]{1,0:T(8,128)(2...) custom-call(s32[32]{0:T(128)S(1)} %copy-done.4, ...), custom_call_target="tpu_custom_call" | custom-call | flops 6643777536 | bytes 4718592 | tf_op jit(solution)/shard_map/orthogonalize/pallas_call | solution.py:287
  60.5 1.8 %collective-permute-start = (bf16[88,256]{1,0:T(8,128)(2,1)S(1)}, bf16[88,256]{1,0:T(8,128)(2,1)S(1)}, u32[]{:S(2)}, u32[]{:S(2)}) collective-permute-start(bf16[88,256]{1,0:T(8,128)(2,1)S(1)} %get-tuple-element.53), channel_id=1, source_target_pairs={{0,1},{1,0},{2,3},{3,2},{4,5},{5,4},{6,7},{7,6},{8,9},{9,8},{10,11... | collective-permute-start | bytes 135176 | tf_op jit(solution)/shard_map/ppermute | solution.py:365
  62.3 0.0 collective-permute-start.1
  62.3 0.4 collective-permute-start.2
  62.6 1.8 %collective-permute-start.3 = (bf16[88,256]{1,0:T(8,128)(2,1)S(1)}, bf16[88,256]{1,0:T(8,128)(2,1)S(1)}, u32[]{:S(2)}, u32[]{:S(2)}) collective-permute-start(bf16[88,256]{1,0:T(8,128)(2,1)S(1)} %get-tuple-element.56), channel_id=1, source_target_pairs={{0,8},{1,9},{2,10},{3,11},{4,12},{5,13},{6,14},{7,15},{8,0},{9,1},... | collective-permute-start | bytes 135176 | tf_op jit(solution)/shard_map/ppermute | solution.py:365
  64.4 1.5 %collective-permute-start.4 = (bf16[88,256]{1,0:T(8,128)(2,1)S(1)}, bf16[88,256]{1,0:T(8,128)(2,1)S(1)}, u32[]{:S(2)}, u32[]{:S(2)}) collective-permute-start(bf16[88,256]{1,0:T(8,128)(2,1)S(1)} %get-tuple-element.57), channel_id=1, source_target_pairs={{0,9},{1,8},{2,11},{3,10},{4,13},{5,12},{6,15},{7,14},{8,1},{9,0},... | collective-permute-start | bytes 135176 | tf_op jit(solution)/shard_map/ppermute | solution.py:365
  65.9 10.4 %collective-permute-done.refs_1_ = bf16[88,256]{1,0:T(8,128)(2,1)S(1)} collective-permute-done((bf16[88,256]{1,0:T(8,128)(2,1)S(1)}, bf16[88,256]{1,0:T(8,128)(2,1)S(1)}, u32[]{:S(2)}, u32[]{:S(2)}) %collective-permute-start) | collective-permute-done | bytes 45088 | tf_op jit(solution)/shard_map/ppermute | solution.py:365
  76.3 0.6 collective-permute-start.5
  76.8 0.0 collective-permute-done.1.refs_2_
  76.8 3.1 %collective-permute-start.6 = (bf16[88,256]{1,0:T(8,128)(2,1)S(1)}, bf16[88,256]{1,0:T(8,128)(2,1)S(1)}, u32[]{:S(2)}, u32[]{:S(2)}) collective-permute-start(bf16[88,256]{1,0:T(8,128)(2,1)S(1)} %get-tuple-element.59), channel_id=1, source_target_pairs={{0,13},{1,12},{2,15},{3,14},{4,9},{5,8},{6,11},{7,10},{8,5},{9,4},... | collective-permute-start | bytes 135176 | tf_op jit(solution)/shard_map/ppermute | solution.py:365
  79.9 0.0 collective-permute-done.2.refs_3_
  79.9 1.8 %collective-permute-start.7 = (bf16[88,256]{1,0:T(8,128)(2,1)S(1)}, bf16[88,256]{1,0:T(8,128)(2,1)S(1)}, u32[]{:S(2)}, u32[]{:S(2)}) collective-permute-start(bf16[88,256]{1,0:T(8,128)(2,1)S(1)} %get-tuple-element.60), channel_id=1, source_target_pairs={{0,16},{1,17},{2,18},{3,19},{4,20},{5,21},{6,22},{7,23},{8,24},{9,... | collective-permute-start | bytes 135176 | tf_op jit(solution)/shard_map/ppermute | solution.py:365
  81.7 0.0 collective-permute-done.3.refs_4_
  81.7 0.0 collective-permute-start.8
  81.7 0.0 collective-permute-done.4.refs_5_
  81.7 1.0 collective-permute-start.9
  82.7 0.0 collective-permute-done.5.refs_6_
  82.7 2.3 %collective-permute-start.10 = (bf16[88,256]{1,0:T(8,128)(2,1)S(1)}, bf16[88,256]{1,0:T(8,128)(2,1)S(1)}, u32[]{:S(2)}, u32[]{:S(2)}) collective-permute-start(bf16[88,256]{1,0:T(8,128)(2,1)S(1)} %get-tuple-element.63), channel_id=1, source_target_pairs={{0,21},{1,20},{2,23},{3,22},{4,17},{5,16},{6,19},{7,18},{8,29},{9,... | collective-permute-start | bytes 135176 | tf_op jit(solution)/shard_map/ppermute | solution.py:365
  85.0 0.0 collective-permute-done.6.refs_7_
  85.0 2.3 %collective-permute-start.11 = (bf16[88,256]{1,0:T(8,128)(2,1)S(1)}, bf16[88,256]{1,0:T(8,128)(2,1)S(1)}, u32[]{:S(2)}, u32[]{:S(2)}) collective-permute-start(bf16[88,256]{1,0:T(8,128)(2,1)S(1)} %get-tuple-element.64), channel_id=1, source_target_pairs={{0,24},{1,25},{2,26},{3,27},{4,28},{5,29},{6,30},{7,31},{8,16},{9,... | collective-permute-start | bytes 135176 | tf_op jit(solution)/shard_map/ppermute | solution.py:365
  87.3 0.0 collective-permute-done.7.refs_8_
  87.3 0.1 collective-permute-start.12
  87.4 0.0 collective-permute-done.8.refs_9_
  87.4 0.9 collective-permute-start.13
  88.3 0.0 collective-permute-done.9.refs_10_
  88.3 3.2 %collective-permute-start.14 = (bf16[88,256]{1,0:T(8,128)(2,1)S(1)}, bf16[88,256]{1,0:T(8,128)(2,1)S(1)}, u32[]{:S(2)}, u32[]{:S(2)}) collective-permute-start(bf16[88,256]{1,0:T(8,128)(2,1)S(1)} %get-tuple-element.67), channel_id=1, source_target_pairs={{0,29},{1,28},{2,31},{3,30},{4,25},{5,24},{6,27},{7,26},{8,21},{9,... | collective-permute-start | bytes 135176 | tf_op jit(solution)/shard_map/ppermute | solution.py:365
  91.5 0.0 collective-permute-done.10.refs_11_
  91.5 0.0 collective-permute-done.11.refs_12_
  91.5 1.8 %collective-permute-done.12.refs_13_ = bf16[88,256]{1,0:T(8,128)(2,1)S(1)} collective-permute-done((bf16[88,256]{1,0:T(8,128)(2,1)S(1)}, bf16[88,256]{1,0:T(8,128)(2,1)S(1)}, u32[]{:S(2)}, u32[]{:S(2)}) %collective-permute-start.12) | collective-permute-done | bytes 45088 | tf_op jit(solution)/shard_map/ppermute | solution.py:365
  93.3 0.0 collective-permute-done.13.refs_14_
  93.3 0.3 collective-permute-done.14.refs_15_
  93.6 0.0 all-to-all-done.1.x_ref
  93.6 8.6 %orthogonalize.3 = (bf16[2,704,1024]{2,1,0:T(8,128)(2,1)}, bf16[16,88,256]{2,1,0:T(8,128)(2,1)S(1)}) custom-call(s32[32]{0:T(128)S(1)} %copy-done.4, bf16[32,88,256]{2,1,0:T(8,128)(2,1)S(1)} %all-to-all-done.1.x_ref, bf16[2,704,1024]{2,1,0:T(8,128)(2,1)} %get-tuple-element.86.refs_0_), custom_call_target="tpu_custom_call", output_to_operand_aliasing={{0}: (2, {})} | custom-call | flops 6643777536 | bytes 4718592 | tf_op jit(solution)/shard_map/orthogonalize/pallas_call | solution.py:287
  102.3 15.9 %all_to_all.15.refs_16_ = bf16[16,88,256]{2,1,0:T(8,128)(2,1)S(1)} all-to-all(bf16[16,88,256]{2,1,0:T(8,128)(2,1)S(1)} %get-tuple-element.87), channel_id=1, replica_groups={{0,1,4,5,8,9,12,13,16,17,20,21,24,25,28,29},{2,3,6,7,10,11,14,15,18,19,..., dimensions={0} | all-to-all | bytes 1441792 | tf_op jit(solution)/shard_map/all_to_all | solution.py:359
  118.1 3.0 %unpack.1 = bf16[32,88,256]{2,1,0:T(8,128)(2,1)} custom-call(s32[32]{0:T(128)S(1)} %copy-done.3, s32[32]{0:T(128)S(1)} %copy-done.4, s32[32]{0:T(128)S(1)} %copy-done.5, bf16[88,256]{1,0:T(8,128)(2,1)S(1)} %get-tuple-element.69.refs_0_, bf16[88,256]{1,0:T(8,128)(2,1)S(1)} %collective-permute-done.refs_1_, ...), custom_call_target="tpu_custom_call" | custom-call | bytes 2883584 | tf_op jit(solution)/shard_map/unpack/pallas_call | solution.py:340
  (4 shorter events, 0.0 us)
Async XLA Ops:
  5.8 7.5 %copy-start = (f32[32,88,256]{2,1,0:T(8,128)S(1)}, f32[32,88,256]{2,1,0:T(8,128)}, u32[]{:S(2)}) copy-start(f32[32,88,256]{2,1,0:T(8,128)} %m_ref.3) | copy-start | bytes 8650756
  5.8 7.5 %copy-start.3 = (s32[32]{0:T(128)S(1)}, s32[32]{0:T(128)}, u32[]{:S(2)}) copy-start(s32[32]{0:T(128)} %owner_ref.5) | copy-start | bytes 388
  5.8 7.5 %copy-start.4 = (s32[32]{0:T(128)S(1)}, s32[32]{0:T(128)}, u32[]{:S(2)}) copy-start(s32[32]{0:T(128)} %get-tuple-element.46.other_ref) | copy-start | bytes 388
  5.8 7.5 %copy-start.5 = (s32[32]{0:T(128)S(1)}, s32[32]{0:T(128)}, u32[]{:S(2)}) copy-start(s32[32]{0:T(128)} %get-tuple-element.47.rank_ref) | copy-start | bytes 388
  5.8 40.6 %all-to-all-start = ((bf16[32,88,256]{2,1,0:T(8,128)(2,1)}), bf16[32,88,256]{2,1,0:T(8,128)(2,1)}, u32[]{:S(2)}, u32[]{:S(2)}) async-start(bf16[32,88,256]{2,1,0:T(8,128)(2,1)} %get-tuple-element.49), calls=%async_computation | async-start | bytes 2883584 | tf_op jit(solution)/shard_map/all_to_all | solution.py:359
  13.3 1.4 %copy-start.1 = (bf16[32,88,256]{2,1,0:T(8,128)(2,1)S(1)}, bf16[32,88,256]{2,1,0:T(8,128)(2,1)}, u32[]{:S(2)}) copy-start(bf16[32,88,256]{2,1,0:T(8,128)(2,1)} %g_ref.3) | copy-start | bytes 4325380
  17.5 1.1 copy-start.2
  46.5 47.2 %all-to-all-start.1 = ((bf16[32,88,256]{2,1,0:T(8,128)(2,1)}), bf16[32,88,256]{2,1,0:T(8,128)(2,1)S(1)}, u32[]{:S(2)}, u32[]{:S(2)}) async-start(bf16[32,88,256]{2,1,0:T(8,128)(2,1)} %copy-done.2), calls=%async_computation.1 | async-start | bytes 2883584 | tf_op jit(solution)/shard_map/all_to_all | solution.py:359
  60.5 15.8 %collective-permute-start = (bf16[88,256]{1,0:T(8,128)(2,1)S(1)}, bf16[88,256]{1,0:T(8,128)(2,1)S(1)}, u32[]{:S(2)}, u32[]{:S(2)}) collective-permute-start(bf16[88,256]{1,0:T(8,128)(2,1)S(1)} %get-tuple-element.53), channel_id=1, source_target_pairs={{0,1},{1,0},{2,3},{3,2},{4,5},{5,4},{6,7},{7,6},{8,9},{9,8},{10,11... | collective-permute-start | bytes 135176 | tf_op jit(solution)/shard_map/ppermute | solution.py:365
  62.3 14.5 %collective-permute-start.1 = (bf16[88,256]{1,0:T(8,128)(2,1)S(1)}, bf16[88,256]{1,0:T(8,128)(2,1)S(1)}, u32[]{:S(2)}, u32[]{:S(2)}) collective-permute-start(bf16[88,256]{1,0:T(8,128)(2,1)S(1)} %get-tuple-element.54), channel_id=1, source_target_pairs={{0,4},{1,5},{2,6},{3,7},{4,0},{5,1},{6,2},{7,3},{8,12},{9,13},{10,... | collective-permute-start | bytes 135176 | tf_op jit(solution)/shard_map/ppermute | solution.py:365
  62.3 17.7 %collective-permute-start.2 = (bf16[88,256]{1,0:T(8,128)(2,1)S(1)}, bf16[88,256]{1,0:T(8,128)(2,1)S(1)}, u32[]{:S(2)}, u32[]{:S(2)}) collective-permute-start(bf16[88,256]{1,0:T(8,128)(2,1)S(1)} %get-tuple-element.55), channel_id=1, source_target_pairs={{0,5},{1,4},{2,7},{3,6},{4,1},{5,0},{6,3},{7,2},{8,13},{9,12},{10,... | collective-permute-start | bytes 135176 | tf_op jit(solution)/shard_map/ppermute | solution.py:365
  62.6 19.1 %collective-permute-start.3 = (bf16[88,256]{1,0:T(8,128)(2,1)S(1)}, bf16[88,256]{1,0:T(8,128)(2,1)S(1)}, u32[]{:S(2)}, u32[]{:S(2)}) collective-permute-start(bf16[88,256]{1,0:T(8,128)(2,1)S(1)} %get-tuple-element.56), channel_id=1, source_target_pairs={{0,8},{1,9},{2,10},{3,11},{4,12},{5,13},{6,14},{7,15},{8,0},{9,1},... | collective-permute-start | bytes 135176 | tf_op jit(solution)/shard_map/ppermute | solution.py:365
  64.4 17.3 %collective-permute-start.4 = (bf16[88,256]{1,0:T(8,128)(2,1)S(1)}, bf16[88,256]{1,0:T(8,128)(2,1)S(1)}, u32[]{:S(2)}, u32[]{:S(2)}) collective-permute-start(bf16[88,256]{1,0:T(8,128)(2,1)S(1)} %get-tuple-element.57), channel_id=1, source_target_pairs={{0,9},{1,8},{2,11},{3,10},{4,13},{5,12},{6,15},{7,14},{8,1},{9,0},... | collective-permute-start | bytes 135176 | tf_op jit(solution)/shard_map/ppermute | solution.py:365
  76.3 6.4 %collective-permute-start.5 = (bf16[88,256]{1,0:T(8,128)(2,1)S(1)}, bf16[88,256]{1,0:T(8,128)(2,1)S(1)}, u32[]{:S(2)}, u32[]{:S(2)}) collective-permute-start(bf16[88,256]{1,0:T(8,128)(2,1)S(1)} %get-tuple-element.58), channel_id=1, source_target_pairs={{0,12},{1,13},{2,14},{3,15},{4,8},{5,9},{6,10},{7,11},{8,4},{9,5},... | collective-permute-start | bytes 135176 | tf_op jit(solution)/shard_map/ppermute | solution.py:365
  76.8 8.2 %collective-permute-start.6 = (bf16[88,256]{1,0:T(8,128)(2,1)S(1)}, bf16[88,256]{1,0:T(8,128)(2,1)S(1)}, u32[]{:S(2)}, u32[]{:S(2)}) collective-permute-start(bf16[88,256]{1,0:T(8,128)(2,1)S(1)} %get-tuple-element.59), channel_id=1, source_target_pairs={{0,13},{1,12},{2,15},{3,14},{4,9},{5,8},{6,11},{7,10},{8,5},{9,4},... | collective-permute-start | bytes 135176 | tf_op jit(solution)/shard_map/ppermute | solution.py:365
  79.9 7.4 %collective-permute-start.7 = (bf16[88,256]{1,0:T(8,128)(2,1)S(1)}, bf16[88,256]{1,0:T(8,128)(2,1)S(1)}, u32[]{:S(2)}, u32[]{:S(2)}) collective-permute-start(bf16[88,256]{1,0:T(8,128)(2,1)S(1)} %get-tuple-element.60), channel_id=1, source_target_pairs={{0,16},{1,17},{2,18},{3,19},{4,20},{5,21},{6,22},{7,23},{8,24},{9,... | collective-permute-start | bytes 135176 | tf_op jit(solution)/shard_map/ppermute | solution.py:365
  81.7 5.7 %collective-permute-start.8 = (bf16[88,256]{1,0:T(8,128)(2,1)S(1)}, bf16[88,256]{1,0:T(8,128)(2,1)S(1)}, u32[]{:S(2)}, u32[]{:S(2)}) collective-permute-start(bf16[88,256]{1,0:T(8,128)(2,1)S(1)} %get-tuple-element.61), channel_id=1, source_target_pairs={{0,17},{1,16},{2,19},{3,18},{4,21},{5,20},{6,23},{7,22},{8,25},{9,... | collective-permute-start | bytes 135176 | tf_op jit(solution)/shard_map/ppermute | solution.py:365
  81.7 6.6 %collective-permute-start.9 = (bf16[88,256]{1,0:T(8,128)(2,1)S(1)}, bf16[88,256]{1,0:T(8,128)(2,1)S(1)}, u32[]{:S(2)}, u32[]{:S(2)}) collective-permute-start(bf16[88,256]{1,0:T(8,128)(2,1)S(1)} %get-tuple-element.62), channel_id=1, source_target_pairs={{0,20},{1,21},{2,22},{3,23},{4,16},{5,17},{6,18},{7,19},{8,28},{9,... | collective-permute-start | bytes 135176 | tf_op jit(solution)/shard_map/ppermute | solution.py:365
  82.7 8.8 %collective-permute-start.10 = (bf16[88,256]{1,0:T(8,128)(2,1)S(1)}, bf16[88,256]{1,0:T(8,128)(2,1)S(1)}, u32[]{:S(2)}, u32[]{:S(2)}) collective-permute-start(bf16[88,256]{1,0:T(8,128)(2,1)S(1)} %get-tuple-element.63), channel_id=1, source_target_pairs={{0,21},{1,20},{2,23},{3,22},{4,17},{5,16},{6,19},{7,18},{8,29},{9,... | collective-permute-start | bytes 135176 | tf_op jit(solution)/shard_map/ppermute | solution.py:365
  85.0 6.5 %collective-permute-start.11 = (bf16[88,256]{1,0:T(8,128)(2,1)S(1)}, bf16[88,256]{1,0:T(8,128)(2,1)S(1)}, u32[]{:S(2)}, u32[]{:S(2)}) collective-permute-start(bf16[88,256]{1,0:T(8,128)(2,1)S(1)} %get-tuple-element.64), channel_id=1, source_target_pairs={{0,24},{1,25},{2,26},{3,27},{4,28},{5,29},{6,30},{7,31},{8,16},{9,... | collective-permute-start | bytes 135176 | tf_op jit(solution)/shard_map/ppermute | solution.py:365
  87.3 6.0 %collective-permute-start.12 = (bf16[88,256]{1,0:T(8,128)(2,1)S(1)}, bf16[88,256]{1,0:T(8,128)(2,1)S(1)}, u32[]{:S(2)}, u32[]{:S(2)}) collective-permute-start(bf16[88,256]{1,0:T(8,128)(2,1)S(1)} %get-tuple-element.65), channel_id=1, source_target_pairs={{0,25},{1,24},{2,27},{3,26},{4,29},{5,28},{6,31},{7,30},{8,17},{9,... | collective-permute-start | bytes 135176 | tf_op jit(solution)/shard_map/ppermute | solution.py:365
  87.4 5.9 %collective-permute-start.13 = (bf16[88,256]{1,0:T(8,128)(2,1)S(1)}, bf16[88,256]{1,0:T(8,128)(2,1)S(1)}, u32[]{:S(2)}, u32[]{:S(2)}) collective-permute-start(bf16[88,256]{1,0:T(8,128)(2,1)S(1)} %get-tuple-element.66), channel_id=1, source_target_pairs={{0,28},{1,29},{2,30},{3,31},{4,24},{5,25},{6,26},{7,27},{8,20},{9,... | collective-permute-start | bytes 135176 | tf_op jit(solution)/shard_map/ppermute | solution.py:365
  88.3 5.3 %collective-permute-start.14 = (bf16[88,256]{1,0:T(8,128)(2,1)S(1)}, bf16[88,256]{1,0:T(8,128)(2,1)S(1)}, u32[]{:S(2)}, u32[]{:S(2)}) collective-permute-start(bf16[88,256]{1,0:T(8,128)(2,1)S(1)} %get-tuple-element.67), channel_id=1, source_target_pairs={{0,29},{1,28},{2,31},{3,30},{4,25},{5,24},{6,27},{7,26},{8,21},{9,... | collective-permute-start | bytes 135176 | tf_op jit(solution)/shard_map/ppermute | solution.py:365

commit v8 on v6

--- a/solution.py
+++ b/solution.py
@@ -11,6 +11,7 @@
 ITERS = 2
 CAP = 2
 HALVES = 2
+TILES = 2
 
 coef_a = 3.4445
 coef_b = -4.775
@@ -168,119 +169,112 @@
     )
 
 
-def newton_schulz(rows, cols, row_size, col_size, x_s, y_s, gram_s, mix_s, write):
-    padded = round_up(rows, 16)
-    tile_blocks = max(row_size // 2, 1)
-    tile = padded * tile_blocks
-    tiles = row_size // tile_blocks
-
-    total = jnp.zeros((1, cols), jnp.float32)
+def sum_rows(values):
+    rows, cols = values.shape
+    if rows % 8:
+        return jnp.sum(values, axis=0, keepdims=True)
+    return jnp.sum(values.reshape(rows // 8, 8, cols), axis=0)
+
+
+def gather_blocks(x_ref, x_s, row_size, col_size):
+    _, rows, cols = x_ref.shape
+    height = rows * row_size
+    total = 0.0
     for r in range(row_size):
         for c in range(col_size):
-            wide = x_s[r * padded : (r + 1) * padded, c * cols : (c + 1) * cols]
-            wide = wide.astype(jnp.float32)
-            total += jnp.sum(wide * wide, axis=0, keepdims=True)
-    magnitude = jnp.sqrt(jnp.sum(total, axis=1, keepdims=True))
-    inverse = 1.0 / (magnitude + epsilon)
-    update_scale = 0.2 * math.sqrt(max(rows * row_size, cols * col_size))
-
+            block = x_ref[r * col_size + c]
+            x_s[r * rows : (r + 1) * rows, c * cols : (c + 1) * cols] = block
+            wide = block.astype(jnp.float32)
+            total = total + sum_rows(wide * wide)
+    x_s[height:, :] = jnp.zeros((x_s.shape[0] - height, x_s.shape[1]), x_s.dtype)
+    return 1.0 / (jnp.sqrt(jnp.sum(total, keepdims=True)) + epsilon)
+
+
+def newton_schulz(height, inverse, x_s, y_s, gram_s, write):
+    padded, width = x_s.shape
+    tile = height // TILES
+    update_scale = 0.2 * math.sqrt(max(height, width))
+    for ref in (y_s, gram_s):
+        ref[height:, :] = jnp.zeros((padded - height, ref.shape[1]), ref.dtype)
     for iteration in range(ITERS):
         src = x_s if iteration == 0 else y_s
-        for t in range(tiles):
+        for t in range(TILES):
             span = slice(t * tile, (t + 1) * tile)
             gram = matmul(src[span, :], src[...], 1)
             if iteration == 0:
                 gram = gram * (inverse * inverse)
             gram_s[span, :] = gram.astype(jnp.bfloat16)
-        for t in range(tiles):
+        for t in range(TILES):
             span = slice(t * tile, (t + 1) * tile)
             square = matmul(gram_s[span, :], gram_s[...], 0)
-            mix_s[span, :] = (
-                coef_b * gram_s[span, :].astype(jnp.float32) + coef_c * square
-            ).astype(jnp.bfloat16)
-        for t in range(tiles):
-            span = slice(t * tile, (t + 1) * tile)
+            mixing = coef_b * gram_s[span, :].astype(jnp.float32) + coef_c * square
             combined = coef_a * src[span, :].astype(jnp.float32) + matmul(
-                mix_s[span, :], src[...], 0
+                mixing.astype(jnp.bfloat16), src[...], 0
             )
             if iteration == 0:
                 combined = combined * inverse
             if iteration + 1 < ITERS:
                 y_s[span, :] = combined.astype(jnp.bfloat16)
             else:
-                result = (update_scale * combined).astype(jnp.bfloat16)
-                for j in range(tile_blocks):
-                    write(t * tile_blocks + j, result[j * padded : j * padded + rows, :])
-
-
-def clear_padding(x_s, rows, row_size):
-    padded = round_up(rows, 16)
-    if padded > rows:
-        for r in range(row_size):
-            x_s[r * padded + rows : (r + 1) * padded, :] = jnp.zeros(
-                (padded - rows, x_s.shape[1]), x_s.dtype
-            )
-
-
-def gather_blocks(x_ref, x_s, row_size, col_size):
-    _, rows, cols = x_ref.shape
-    padded = round_up(rows, 16)
-    for r in range(row_size):
-        for c in range(col_size):
-            x_s[r * padded : r * padded + rows, c * cols : (c + 1) * cols] = x_ref[
-                r * col_size + c
-            ]
+                write(t, (update_scale * combined).astype(jnp.bfloat16))
 
 
 def ortho_kernel(row_size, col_size, slot, other_ref, x_ref, *refs):
-    owned_ref, back_ref = refs[slot : slot + 2]
-    scratch = refs[slot + 2 :]
+    owned_ref, back_ref, x_s, y_s, gram_s, out_s, sems = refs[-7:]
     _, rows, cols = x_ref.shape
     width = col_size // HALVES
+    height = rows * row_size
+    tile = height // TILES
     col = lax.axis_index("owner")
     me = lax.axis_index("dp") * col_size + col
     owns = other_ref[me] != me
     low = col < width
-    clear_padding(scratch[0], rows, row_size)
-    gather_blocks(x_ref, scratch[0], row_size, col_size)
-
-    def write(r, block):
-        owned_ref[0, r * rows : (r + 1) * rows, :] = jnp.where(owns, block, jnp.zeros_like(block))
-        for c in range(width):
-            back_ref[r * width + c] = jnp.where(
-                low,
-                block[:, c * cols : (c + 1) * cols],
-                block[:, (c + width) * cols : (c + width + 1) * cols],
-            )
-
-    newton_schulz(rows, cols, row_size, col_size, *scratch, write)
-
-
-def orthogonalize(slot, other, arrived, row_size, col_size, owned=None):
+    inverse = gather_blocks(x_ref, x_s, row_size, col_size)
+
+    def copy_out(t):
+        span = pl.ds(t * tile, tile)
+        return pltpu.make_async_copy(out_s.at[span], owned_ref.at[slot, span], sems.at[t])
+
+    def write(t, result):
+        out_s[t * tile : (t + 1) * tile, :] = jnp.where(owns, result, jnp.zeros_like(result))
+        copy_out(t).start()
+        for j in range(row_size // TILES):
+            block = result[j * rows : (j + 1) * rows, :]
+            for c in range(width):
+                back_ref[(t * (row_size // TILES) + j) * width + c, 0] = jnp.where(
+                    low,
+                    block[:, c * cols : (c + 1) * cols],
+                    block[:, (c + width) * cols : (c + width + 1) * cols],
+                )
+
+    newton_schulz(height, inverse, x_s, y_s, gram_s, write)
+    for t in range(TILES):
+        copy_out(t).wait()
+
+
+def orthogonalize(slot, other, arrived, row_size, col_size, made=()):
     devices, rows, cols = arrived.shape
     height, width = rows * row_size, cols * col_size
-    padded = round_up(rows, 16) * row_size
-    in_specs, operands = [SMEM, whole(arrived.shape)], [other, arrived]
-    if slot:
-        in_specs.append(pl.BlockSpec(memory_space=pl.ANY))
-        operands.append(owned)
-    back = (devices // HALVES, rows, cols)
+    padded = round_up(height, 256)
+    places = devices // HALVES
+    anywhere = pl.BlockSpec(memory_space=pl.ANY)
     return pl.pallas_call(
         functools.partial(ortho_kernel, row_size, col_size, slot),
         grid=(1,),
-        in_specs=in_specs,
-        out_specs=[pl.BlockSpec((1, height, width), lambda i: (slot, 0, 0)), whole(back)],
+        in_specs=[SMEM, whole(arrived.shape)] + [anywhere] * len(made),
+        out_specs=[anywhere, pl.BlockSpec((places, 1, rows, cols), lambda i: (0, slot, 0, 0))],
         out_shape=[
             jax.ShapeDtypeStruct((CAP, height, width), jnp.bfloat16),
-            jax.ShapeDtypeStruct(back, jnp.bfloat16),
+            jax.ShapeDtypeStruct((places, CAP, rows, cols), jnp.bfloat16),
         ],
         scratch_shapes=[
             pltpu.VMEM((padded, width), jnp.bfloat16),
             pltpu.VMEM((padded, width), jnp.bfloat16),
             pltpu.VMEM((padded, padded), jnp.bfloat16),
-            pltpu.VMEM((padded, padded), jnp.bfloat16),
+            pltpu.VMEM((height, width), jnp.bfloat16),
+            pltpu.SemaphoreType.DMA((TILES,)),
         ],
-        input_output_aliases={2: 0} if slot else {},
+        input_output_aliases={2 + k: k for k in range(len(made))},
         compiler_params=PARAMS,
         cost_estimate=pl.CostEstimate(
             flops=2 * ITERS * padded * padded * (2 * width + padded),
@@ -288,12 +282,10 @@
             transcendentals=0,
         ),
         name="orthogonalize",
-    )(*operands)
-
-
-def unpack_kernel(
-    chunk, col_size, owner_ref, other_ref, rank_ref, first_ref, second_ref, update_ref
-):
+    )(other, arrived, *made)
+
+
+def unpack_kernel(chunk, col_size, owner_ref, other_ref, rank_ref, back_ref, update_ref):
     step = pl.program_id(0)
     width = col_size // HALVES
     half = lax.axis_index("owner") // width
@@ -301,19 +293,11 @@
         i = step * chunk + j
         owner = owner_ref[i]
         host = jnp.where((owner % col_size) // width == half, owner, other_ref[owner])
-        place = (host // col_size) * width + host % width
-
-        @pl.when(rank_ref[i] == 0)
-        def _():
-            update_ref[j] = first_ref[place]
-
-        @pl.when(rank_ref[i] == 1)
-        def _():
-            update_ref[j] = second_ref[place]
-
-
-def unpack(owner_table, other, rank, first, second, col_size):
-    places, rows, cols = first.shape
+        update_ref[j] = back_ref[(host // col_size) * width + host % width, rank_ref[i]]
+
+
+def unpack(owner_table, other, rank, back, col_size):
+    _, _, rows, cols = back.shape
     mats = owner_table.shape[0]
     chunk = 8
     return pl.pallas_call(
@@ -321,7 +305,7 @@
         grid_spec=pltpu.PrefetchScalarGridSpec(
             num_scalar_prefetch=3,
             grid=(mats // chunk,),
-            in_specs=[whole(first.shape)] * 2,
+            in_specs=[whole(back.shape)],
             out_specs=pl.BlockSpec((chunk, rows, cols), lambda i, *_: (i, 0, 0)),
         ),
         out_shape=jax.ShapeDtypeStruct((mats, rows, cols), jnp.bfloat16),
@@ -330,7 +314,7 @@
             flops=0, bytes_accessed=4 * mats * rows * cols, transcendentals=0
         ),
         name="unpack",
-    )(owner_table, other, rank, first, second)
+    )(owner_table, other, rank, back)
 
 
 def exchange(blocks, groups=None):
@@ -353,12 +337,9 @@
     new_momentum, second = update_momentum(gradients, momentum, owner_table, other, rank)
     arrived_first, second = lax.optimization_barrier((arrived_first, second))
     arrived_second = exchange(second)
-    owned, back_first = orthogonalize(0, other, arrived_first, row_size, col_size)
-    back_first, arrived_second = lax.optimization_barrier((back_first, arrived_second))
-    returned_first = exchange(back_first, halves)
-    owned, back_second = orthogonalize(1, other, arrived_second, row_size, col_size, owned)
-    returned_second = exchange(back_second, halves)
-    update = unpack(owner_table, other, rank, returned_first, returned_second, col_size)
+    made = orthogonalize(0, other, arrived_first, row_size, col_size)
+    owned, back = orthogonalize(1, other, arrived_second, row_size, col_size, made)
+    update = unpack(owner_table, other, rank, exchange(back, halves), col_size)
     return (new_momentum, update, owned)
 
 

time: 118 us -> 119 us (level)
  blocking collectives: 15.1 us -> 23.4 us
  starting transfers between devices: 16.7 us -> 12 us
  Pallas kernels: 29.2 us -> 27.3 us
  waiting for transfers between devices: 53.6 us -> 52.2 us
    all_to_all x1, blocking collectives: 15.1 us -> 23.4 us  [exchange(): lax.all_to_all(blocks, AXES, split_axis=0, concat_axis=0, tiled=True, axi...]
    all_to_all x3 -> x2, starting transfers between devices: 16.7 us -> 12 us  [exchange(): lax.all_to_all(blocks, AXES, split_axis=0, concat_axis=0, tiled=True, axi...]
    pallas_call x2, Pallas kernels: 18.4 us -> 16.8 us  [orthogonalize(): pl.pallas_call(functools.partial(ortho_kernel, row_size, col_size, slot),...]
    all_to_all x3 -> x2, waiting for transfers between devices: 53.6 us -> 52.2 us  [exchange(): lax.all_to_all(blocks, AXES, split_axis=0, concat_axis=0, tiled=True, axi...]
  transfers between devices with their start and end apart: 3 -> 2, of which waited for: 3 -> 2; matrix products, arithmetic and copies ran while one was open for 0% -> 0% of each run, Pallas kernels for 18% -> 10%
where the time goes in v8:
time: 119 us; the launch traced here: 118 us
  waiting for transfers between devices  52.2 us (44%)
  Pallas kernels  27.3 us (23%)
  blocking collectives  23.4 us (20%)
  starting transfers between devices  12 us (10%)
  local copies, waits for them, and re-layouts  2.5 us (2%)
    all_to_all x2, waiting for transfers between devices, exchange(): lax.all_to_all(blocks, AXES, split_axis=0, concat_axis=0, tiled=True, axi...  52.2 us
    all_to_all x1, blocking collectives, exchange(): lax.all_to_all(blocks, AXES, split_axis=0, concat_axis=0, tiled=True, axi...  23.4 us
    pallas_call x2, Pallas kernels, orthogonalize(): pl.pallas_call(functools.partial(ortho_kernel, row_size, col_size, slot),...  16.8 us
    all_to_all x2, starting transfers between devices, exchange(): lax.all_to_all(blocks, AXES, split_axis=0, concat_axis=0, tiled=True, axi...  12 us
    pallas_call x1, Pallas kernels, pack(): pl.pallas_call(functools.partial(pack_kernel, chunk, col_size), grid_spec...  5.14 us
    pallas_call x1, Pallas kernels, update_momentum(): pl.pallas_call(functools.partial(momentum_kernel, chunk), grid_spec=pltpu...  2.84 us
    unnamed x12, local copies, waits for them, and re-layouts  2.5 us
    pallas_call x1, Pallas kernels, unpack(): pl.pallas_call(functools.partial(unpack_kernel, chunk, col_size), grid_sp...  2.44 us
  transfers between devices with their start and end apart: 2, of which 2 were waited for; matrix products, arithmetic and copies ran while one was open for 0% of the time, Pallas kernels for 10%

profile of v8, /device:TPU:0, one launch (start us, length us, event | category | flops | bytes accessed | tf_op | source)
XLA Modules:
  0.0 118.2 jit_solution(4950012636862751460)
XLA Ops:
  0.6 5.1 %pack.1 = (bf16[32,88,256]{2,1,0:T(8,128)(2,1)}, s32[32]{0:T(128)}, s32[32]{0:T(128)}) custom-call(s32[32]{0:T(128)} %owner_ref.5, bf16[32,88,256]{2,1,0:T(8,128)(2,1)} %g_ref.3, f32[32,88,256]{2,1,0:T(8,128)} %m_ref.3), custom_call_target="tpu_custom_call" | custom-call | flops 2883584 | bytes 5767168 | tf_op jit(solution)/shard_map/pack/pallas_call | solution.py:107
  5.8 0.0 copy-start
  5.8 0.0 copy-start.3
  5.8 0.0 copy-start.4
  5.8 0.0 copy-start.5
  5.8 7.4 %all-to-all-start = ((bf16[32,88,256]{2,1,0:T(8,128)(2,1)}), bf16[32,88,256]{2,1,0:T(8,128)(2,1)}, u32[]{:S(2)}, u32[]{:S(2)}) async-start(bf16[32,88,256]{2,1,0:T(8,128)(2,1)} %get-tuple-element.17), calls=%async_computation | async-start | bytes 2883584 | tf_op jit(solution)/shard_map/all_to_all | solution.py:321
  13.3 0.0 copy-done
  13.3 0.0 copy-done.3
  13.3 0.0 copy-done.4
  13.3 0.0 copy-done.5
  13.3 0.0 copy-start.1
  13.3 1.4 %copy-done.1 = bf16[32,88,256]{2,1,0:T(8,128)(2,1)S(1)} copy-done((bf16[32,88,256]{2,1,0:T(8,128)(2,1)S(1)}, bf16[32,88,256]{2,1,0:T(8,128)(2,1)}, u32[]{:S(2)}) %copy-start.1) | copy-done | bytes 1441816
  14.7 2.8 %update_momentum.1 = (f32[32,88,256]{2,1,0:T(8,128)}, bf16[32,88,256]{2,1,0:T(8,128)(2,1)S(1)}) custom-call(s32[32]{0:T(128)S(1)} %copy-done.3, s32[32]{0:T(128)S(1)} %copy-done.4, s32[32]{0:T(128)S(1)} %copy-done.5, bf16[32,88,256]{2,1,0:T(8,128)(2,1)S(1)} %copy-done.1, f32[32,88,256]{2,1,0:T(8,128)S(1)} %copy-done), custom_call_target="tpu_custom_call" | custom-call | flops 2883584 | bytes 8650752 | tf_op jit(solution)/shard_map/update_momentum/pallas_call | solution.py:146
  17.5 0.0 copy-start.2
  17.5 1.1 copy-done.2
  18.6 27.8 %all-to-all-done.x_ref = bf16[32,88,256]{2,1,0:T(8,128)(2,1)} async-done(((bf16[32,88,256]{2,1,0:T(8,128)(2,1)}), bf16[32,88,256]{2,1,0:T(8,128)(2,1)}, u32[]{:S(2)}, u32[]{:S(2)}) %all-to-all-start) | async-done | bytes 1441824 | tf_op jit(solution)/shard_map/all_to_all | solution.py:321
  46.5 4.6 %all-to-all-start.1 = ((bf16[32,88,256]{2,1,0:T(8,128)(2,1)}), bf16[32,88,256]{2,1,0:T(8,128)(2,1)S(1)}, u32[]{:S(2)}, u32[]{:S(2)}) async-start(bf16[32,88,256]{2,1,0:T(8,128)(2,1)} %copy-done.2), calls=%async_computation.1 | async-start | bytes 2883584 | tf_op jit(solution)/shard_map/all_to_all | solution.py:321
  51.0 8.8 %orthogonalize.2 = (bf16[2,704,1024]{2,1,0:T(8,128)(2,1)}, bf16[16,2,88,256]{3,2,1,0:T(8,128)(2,1)S(1)}) custom-call(s32[32]{0:T(128)S(1)} %copy-done.4, bf16[32,88,256]{2,1,0:T(8,128)(2,1)} %all-to-all-done.x_ref), custom_call_target="tpu_custom_call" | custom-call | flops 6643777536 | bytes 4718592 | tf_op jit(solution)/shard_map/orthogonalize/pallas_call | solution.py:261
  59.9 24.4 %all-to-all-done.1.x_ref = bf16[32,88,256]{2,1,0:T(8,128)(2,1)S(1)} async-done(((bf16[32,88,256]{2,1,0:T(8,128)(2,1)}), bf16[32,88,256]{2,1,0:T(8,128)(2,1)S(1)}, u32[]{:S(2)}, u32[]{:S(2)}) %all-to-all-start.1) | async-done | bytes 1441824 | tf_op jit(solution)/shard_map/all_to_all | solution.py:321
  84.3 8.0 %orthogonalize.3 = (bf16[2,704,1024]{2,1,0:T(8,128)(2,1)}, bf16[16,2,88,256]{3,2,1,0:T(8,128)(2,1)S(1)}) custom-call(s32[32]{0:T(128)S(1)} %copy-done.4, bf16[32,88,256]{2,1,0:T(8,128)(2,1)S(1)} %all-to-all-done.1.x_ref, bf16[2,704,1024]{2,1,0:T(8,128)(2,1)} %get-tuple-element.21.refs_0_, ...), custom_call_target="tpu_custom_call", output_to_operand_aliasing={{0}: (2, {}), {1}: (3, {})} | custom-call | flops 6643777536 | bytes 4718592 | tf_op jit(solution)/shard_map/orthogonalize/pallas_call | solution.py:261
  92.3 23.4 %all_to_all.15.back_ref = bf16[16,2,88,256]{3,2,1,0:T(8,128)(2,1)S(1)} all-to-all(bf16[16,2,88,256]{3,2,1,0:T(8,128)(2,1)S(1)} %get-tuple-element.23), channel_id=1, replica_groups={{0,1,4,5,8,9,12,13,16,17,20,21,24,25,28,29},{2,3,6,7,10,11,14,15,18,19,..., dimensions={0} | all-to-all | bytes 2883584 | tf_op jit(solution)/shard_map/all_to_all | solution.py:321
  115.7 2.4 %unpack.1 = bf16[32,88,256]{2,1,0:T(8,128)(2,1)} custom-call(s32[32]{0:T(128)S(1)} %copy-done.3, s32[32]{0:T(128)S(1)} %copy-done.4, s32[32]{0:T(128)S(1)} %copy-done.5, bf16[16,2,88,256]{3,2,1,0:T(8,128)(2,1)S(1)} %all_to_all.15.back_ref), custom_call_target="tpu_custom_call" | custom-call | bytes 2883584 | tf_op jit(solution)/shard_map/unpack/pallas_call | solution.py:303
Async XLA Ops:
  5.8 7.5 %copy-start = (f32[32,88,256]{2,1,0:T(8,128)S(1)}, f32[32,88,256]{2,1,0:T(8,128)}, u32[]{:S(2)}) copy-start(f32[32,88,256]{2,1,0:T(8,128)} %m_ref.3) | copy-start | bytes 8650756
  5.8 7.5 %copy-start.3 = (s32[32]{0:T(128)S(1)}, s32[32]{0:T(128)}, u32[]{:S(2)}) copy-start(s32[32]{0:T(128)} %owner_ref.5) | copy-start | bytes 388
  5.8 7.5 %copy-start.4 = (s32[32]{0:T(128)S(1)}, s32[32]{0:T(128)}, u32[]{:S(2)}) copy-start(s32[32]{0:T(128)} %get-tuple-element.14.other_ref) | copy-start | bytes 388
  5.8 7.5 %copy-start.5 = (s32[32]{0:T(128)S(1)}, s32[32]{0:T(128)}, u32[]{:S(2)}) copy-start(s32[32]{0:T(128)} %get-tuple-element.15.rank_ref) | copy-start | bytes 388
  5.8 40.6 %all-to-all-start = ((bf16[32,88,256]{2,1,0:T(8,128)(2,1)}), bf16[32,88,256]{2,1,0:T(8,128)(2,1)}, u32[]{:S(2)}, u32[]{:S(2)}) async-start(bf16[32,88,256]{2,1,0:T(8,128)(2,1)} %get-tuple-element.17), calls=%async_computation | async-start | bytes 2883584 | tf_op jit(solution)/shard_map/all_to_all | solution.py:321
  13.3 1.4 %copy-start.1 = (bf16[32,88,256]{2,1,0:T(8,128)(2,1)S(1)}, bf16[32,88,256]{2,1,0:T(8,128)(2,1)}, u32[]{:S(2)}) copy-start(bf16[32,88,256]{2,1,0:T(8,128)(2,1)} %g_ref.3) | copy-start | bytes 4325380
  17.5 1.1 copy-start.2
  46.5 37.8 %all-to-all-start.1 = ((bf16[32,88,256]{2,1,0:T(8,128)(2,1)}), bf16[32,88,256]{2,1,0:T(8,128)(2,1)S(1)}, u32[]{:S(2)}, u32[]{:S(2)}) async-start(bf16[32,88,256]{2,1,0:T(8,128)(2,1)} %copy-done.2), calls=%async_computation.1 | async-start | bytes 2883584 | tf_op jit(solution)/shard_map/all_to_all | solution.py:321

commit v9 on v8

--- a/solution.py
+++ b/solution.py
@@ -220,13 +220,18 @@
 
 
 def ortho_kernel(row_size, col_size, slot, other_ref, x_ref, *refs):
-    owned_ref, back_ref, x_s, y_s, gram_s, out_s, sems = refs[-7:]
     _, rows, cols = x_ref.shape
     width = col_size // HALVES
+    places = row_size * width
     height = rows * row_size
     tile = height // TILES
-    col = lax.axis_index("owner")
-    me = lax.axis_index("dp") * col_size + col
+    if slot:
+        owned_ref, back_ref, x_s, y_s, gram_s, out_s, sems = refs[1:]
+    else:
+        owned_ref, offset_refs = refs[0], refs[1 : 1 + places]
+        x_s, y_s, gram_s, out_s, sems, back_ref = refs[1 + places :]
+    row, col = lax.axis_index("dp"), lax.axis_index("owner")
+    me = row * col_size + col
     owns = other_ref[me] != me
     low = col < width
     inverse = gather_blocks(x_ref, x_s, row_size, col_size)
@@ -240,41 +245,53 @@
         copy_out(t).start()
         for j in range(row_size // TILES):
             block = result[j * rows : (j + 1) * rows, :]
+            r = t * (row_size // TILES) + j
             for c in range(width):
-                back_ref[(t * (row_size // TILES) + j) * width + c, 0] = jnp.where(
+                place = r * width + c if slot else (r ^ row) * width + (c ^ (col % width))
+                back_ref[place] = jnp.where(
                     low,
                     block[:, c * cols : (c + 1) * cols],
                     block[:, (c + width) * cols : (c + width + 1) * cols],
                 )
 
     newton_schulz(height, inverse, x_s, y_s, gram_s, write)
+    if not slot:
+        for offset in range(places):
+            offset_refs[offset][...] = back_ref[offset]
     for t in range(TILES):
         copy_out(t).wait()
 
 
-def orthogonalize(slot, other, arrived, row_size, col_size, made=()):
+def orthogonalize(slot, other, arrived, row_size, col_size, owned=None):
     devices, rows, cols = arrived.shape
     height, width = rows * row_size, cols * col_size
     padded = round_up(height, 256)
     places = devices // HALVES
     anywhere = pl.BlockSpec(memory_space=pl.ANY)
-    return pl.pallas_call(
+    in_specs, operands = [SMEM, whole(arrived.shape)], [other, arrived]
+    scratch_shapes = [
+        pltpu.VMEM((padded, width), jnp.bfloat16),
+        pltpu.VMEM((padded, width), jnp.bfloat16),
+        pltpu.VMEM((padded, padded), jnp.bfloat16),
+        pltpu.VMEM((height, width), jnp.bfloat16),
+        pltpu.SemaphoreType.DMA((TILES,)),
+    ]
+    if slot:
+        in_specs.append(anywhere)
+        operands.append(owned)
+        back = [(places, rows, cols)]
+    else:
+        back = [(rows, cols)] * places
+        scratch_shapes.append(pltpu.VMEM((places, rows, cols), jnp.bfloat16))
+    owned, *back = pl.pallas_call(
         functools.partial(ortho_kernel, row_size, col_size, slot),
         grid=(1,),
-        in_specs=[SMEM, whole(arrived.shape)] + [anywhere] * len(made),
-        out_specs=[anywhere, pl.BlockSpec((places, 1, rows, cols), lambda i: (0, slot, 0, 0))],
-        out_shape=[
-            jax.ShapeDtypeStruct((CAP, height, width), jnp.bfloat16),
-            jax.ShapeDtypeStruct((places, CAP, rows, cols), jnp.bfloat16),
-        ],
-        scratch_shapes=[
-            pltpu.VMEM((padded, width), jnp.bfloat16),
-            pltpu.VMEM((padded, width), jnp.bfloat16),
-            pltpu.VMEM((padded, padded), jnp.bfloat16),
-            pltpu.VMEM((height, width), jnp.bfloat16),
-            pltpu.SemaphoreType.DMA((TILES,)),
-        ],
-        input_output_aliases={2 + k: k for k in range(len(made))},
+        in_specs=in_specs,
+        out_specs=[anywhere] + [whole(shape) for shape in back],
+        out_shape=[jax.ShapeDtypeStruct((CAP, height, width), jnp.bfloat16)]
+        + [jax.ShapeDtypeStruct(shape, jnp.bfloat16) for shape in back],
+        scratch_shapes=scratch_shapes,
+        input_output_aliases={2: 0} if slot else {},
         compiler_params=PARAMS,
         cost_estimate=pl.CostEstimate(
             flops=2 * ITERS * padded * padded * (2 * width + padded),
@@ -282,31 +299,50 @@
             transcendentals=0,
         ),
         name="orthogonalize",
-    )(other, arrived, *made)
-
-
-def unpack_kernel(chunk, col_size, owner_ref, other_ref, rank_ref, back_ref, update_ref):
+    )(*operands)
+    return owned, back
+
+
+def unpack_kernel(chunk, col_size, row_size, owner_ref, other_ref, rank_ref, *refs):
+    width = col_size // HALVES
+    places = row_size * width
+    offset_refs, second_ref, update_ref, first_ref = refs[:places], *refs[places:]
     step = pl.program_id(0)
-    width = col_size // HALVES
-    half = lax.axis_index("owner") // width
+    row, col = lax.axis_index("dp"), lax.axis_index("owner")
+    half = col // width
+
+    @pl.when(step == 0)
+    def _():
+        for offset in range(places):
+            first_ref[offset] = offset_refs[offset][...]
+
     for j in range(chunk):
         i = step * chunk + j
         owner = owner_ref[i]
         host = jnp.where((owner % col_size) // width == half, owner, other_ref[owner])
-        update_ref[j] = back_ref[(host // col_size) * width + host % width, rank_ref[i]]
-
-
-def unpack(owner_table, other, rank, back, col_size):
-    _, _, rows, cols = back.shape
+        host_row, host_col = host // col_size, host % width
+
+        @pl.when(rank_ref[i] == 0)
+        def _():
+            update_ref[j] = first_ref[(host_row ^ row) * width + (host_col ^ (col % width))]
+
+        @pl.when(rank_ref[i] == 1)
+        def _():
+            update_ref[j] = second_ref[host_row * width + host_col]
+
+
+def unpack(owner_table, other, rank, first, second, row_size, col_size):
+    places, rows, cols = second.shape
     mats = owner_table.shape[0]
     chunk = 8
     return pl.pallas_call(
-        functools.partial(unpack_kernel, chunk, col_size),
+        functools.partial(unpack_kernel, chunk, col_size, row_size),
         grid_spec=pltpu.PrefetchScalarGridSpec(
             num_scalar_prefetch=3,
             grid=(mats // chunk,),
-            in_specs=[whole(back.shape)],
+            in_specs=[whole((rows, cols))] * places + [whole(second.shape)],
             out_specs=pl.BlockSpec((chunk, rows, cols), lambda i, *_: (i, 0, 0)),
+            scratch_shapes=[pltpu.VMEM(second.shape, jnp.bfloat16)],
         ),
         out_shape=jax.ShapeDtypeStruct((mats, rows, cols), jnp.bfloat16),
         compiler_params=PARAMS,
@@ -314,13 +350,17 @@
             flops=0, bytes_accessed=4 * mats * rows * cols, transcendentals=0
         ),
         name="unpack",
-    )(owner_table, other, rank, back)
+    )(owner_table, other, rank, *first, second)
 
 
 def exchange(blocks, groups=None):
     return lax.all_to_all(
         blocks, AXES, split_axis=0, concat_axis=0, tiled=True, axis_index_groups=groups
     )
+
+
+def swap(block, offset, devices):
+    return lax.ppermute(block, AXES, [(d, d ^ offset) for d in range(devices)])
 
 
 def on_device(gradients, momentum, owner_table):
@@ -337,9 +377,19 @@
     new_momentum, second = update_momentum(gradients, momentum, owner_table, other, rank)
     arrived_first, second = lax.optimization_barrier((arrived_first, second))
     arrived_second = exchange(second)
-    made = orthogonalize(0, other, arrived_first, row_size, col_size)
-    owned, back = orthogonalize(1, other, arrived_second, row_size, col_size, made)
-    update = unpack(owner_table, other, rank, exchange(back, halves), col_size)
+    owned, back_first = orthogonalize(0, other, arrived_first, row_size, col_size)
+    returned_first = [back_first[0]] + [
+        swap(back_first[r * width + c], r * col_size + c, devices)
+        for r in range(row_size)
+        for c in range(width)
+        if r or c
+    ]
+    owned, back_second = orthogonalize(1, other, arrived_second, row_size, col_size, owned)
+    returned_first, back_second = lax.optimization_barrier((returned_first, back_second))
+    returned_second = exchange(back_second[0], halves)
+    update = unpack(
+        owner_table, other, rank, returned_first, returned_second, row_size, col_size
+    )
     return (new_momentum, update, owned)
 
 

time: 119 us -> 118 us (level)
  starting transfers between devices: 12 us -> 32.6 us
  waiting for transfers between devices: 52.2 us -> 38.9 us
  blocking collectives: 23.4 us -> 15 us
    all_to_all x2, waiting for transfers between devices: 52.2 us -> 27.9 us  [exchange(): lax.all_to_all(blocks, AXES, split_axis=0, concat_axis=0, tiled=True, axi...]
    ppermute x0 -> x15, starting transfers between devices: none -> 20.6 us  [swap(): return lax.ppermute(block, AXES, [(d, d ^ offset) for d in range(devices)])]
    ppermute x0 -> x15, waiting for transfers between devices: none -> 11 us  [swap(): return lax.ppermute(block, AXES, [(d, d ^ offset) for d in range(devices)])]
    all_to_all x1, blocking collectives: 23.4 us -> 15 us  [exchange(): lax.all_to_all(blocks, AXES, split_axis=0, concat_axis=0, tiled=True, axi...]
  transfers between devices with their start and end apart: 2 -> 17, of which waited for: 2 -> 2; matrix products, arithmetic and copies ran while one was open for 0% -> 0% of each run, Pallas kernels for 10% -> 17%
where the time goes in v9:
time: 118 us; the launch traced here: 117 us
  waiting for transfers between devices  38.9 us (33%)
  starting transfers between devices  32.6 us (28%)
  Pallas kernels  27.7 us (23%)
  blocking collectives  15 us (13%)
  local copies, waits for them, and re-layouts  2.49 us (2%)
    all_to_all x2, waiting for transfers between devices, exchange(): lax.all_to_all(blocks, AXES, split_axis=0, concat_axis=0, tiled=True, axi...  27.9 us
    ppermute x15, starting transfers between devices, swap(): return lax.ppermute(block, AXES, [(d, d ^ offset) for d in range(devices)])  20.6 us
    pallas_call x2, Pallas kernels, orthogonalize(): pl.pallas_call(functools.partial(ortho_kernel, row_size, col_size, slot),...  16.7 us
    all_to_all x1, blocking collectives, exchange(): lax.all_to_all(blocks, AXES, split_axis=0, concat_axis=0, tiled=True, axi...  15 us
    all_to_all x2, starting transfers between devices, exchange(): lax.all_to_all(blocks, AXES, split_axis=0, concat_axis=0, tiled=True, axi...  12 us
    ppermute x15, waiting for transfers between devices, swap(): return lax.ppermute(block, AXES, [(d, d ^ offset) for d in range(devices)])  11 us
    pallas_call x1, Pallas kernels, pack(): pl.pallas_call(functools.partial(pack_kernel, chunk, col_size), grid_spec...  5.14 us
    pallas_call x1, Pallas kernels, unpack(): pl.pallas_call(functools.partial(unpack_kernel, chunk, col_size, row_size...  2.95 us
  transfers between devices with their start and end apart: 17, of which 2 were waited for; matrix products, arithmetic and copies ran while one was open for 0% of the time, Pallas kernels for 17%

profile of v9, /device:TPU:0, one launch (start us, length us, event | category | flops | bytes accessed | tf_op | source)
XLA Modules:
  0.0 117.5 jit_solution(6546520207973012205)
XLA Ops:
  0.6 5.1 %pack.1 = (bf16[32,88,256]{2,1,0:T(8,128)(2,1)}, s32[32]{0:T(128)}, s32[32]{0:T(128)}) custom-call(s32[32]{0:T(128)} %owner_ref.5, bf16[32,88,256]{2,1,0:T(8,128)(2,1)} %g_ref.3, f32[32,88,256]{2,1,0:T(8,128)} %m_ref.3), custom_call_target="tpu_custom_call" | custom-call | flops 2883584 | bytes 5767168 | tf_op jit(solution)/shard_map/pack/pallas_call | solution.py:107
  5.8 0.0 copy-start
  5.8 0.0 copy-start.3
  5.8 0.0 copy-start.4
  5.8 0.0 copy-start.5
  5.8 7.4 %all-to-all-start = ((bf16[32,88,256]{2,1,0:T(8,128)(2,1)}), bf16[32,88,256]{2,1,0:T(8,128)(2,1)}, u32[]{:S(2)}, u32[]{:S(2)}) async-start(bf16[32,88,256]{2,1,0:T(8,128)(2,1)} %get-tuple-element.49), calls=%async_computation | async-start | bytes 2883584 | tf_op jit(solution)/shard_map/all_to_all | solution.py:357
  13.3 0.0 copy-done
  13.3 0.0 copy-start.1
  13.3 1.4 %copy-done.1 = bf16[32,88,256]{2,1,0:T(8,128)(2,1)S(1)} copy-done((bf16[32,88,256]{2,1,0:T(8,128)(2,1)S(1)}, bf16[32,88,256]{2,1,0:T(8,128)(2,1)}, u32[]{:S(2)}) %copy-start.1) | copy-done | bytes 1441816
  14.7 2.8 %update_momentum.1 = (f32[32,88,256]{2,1,0:T(8,128)}, bf16[32,88,256]{2,1,0:T(8,128)(2,1)S(1)}) custom-call(s32[32]{0:T(128)S(1)} %copy-done.3, s32[32]{0:T(128)S(1)} %copy-done.4, s32[32]{0:T(128)S(1)} %copy-done.5, bf16[32,88,256]{2,1,0:T(8,128)(2,1)S(1)} %copy-done.1, f32[32,88,256]{2,1,0:T(8,128)S(1)} %copy-done), custom_call_target="tpu_custom_call" | custom-call | flops 2883584 | bytes 8650752 | tf_op jit(solution)/shard_map/update_momentum/pallas_call | solution.py:146
  17.5 1.1 copy-done.2
  18.6 27.9 %all-to-all-done.x_ref = bf16[32,88,256]{2,1,0:T(8,128)(2,1)} async-done(((bf16[32,88,256]{2,1,0:T(8,128)(2,1)}), bf16[32,88,256]{2,1,0:T(8,128)(2,1)}, u32[]{:S(2)}, u32[]{:S(2)}) %all-to-all-start) | async-done | bytes 1441824 | tf_op jit(solution)/shard_map/all_to_all | solution.py:357
  46.5 4.6 %all-to-all-start.1 = ((bf16[32,88,256]{2,1,0:T(8,128)(2,1)}), bf16[32,88,256]{2,1,0:T(8,128)(2,1)S(1)}, u32[]{:S(2)}, u32[]{:S(2)}) async-start(bf16[32,88,256]{2,1,0:T(8,128)(2,1)} %copy-done.2), calls=%async_computation.1 | async-start | bytes 2883584 | tf_op jit(solution)/shard_map/all_to_all | solution.py:357
  51.0 8.8 %orthogonalize.2 = (bf16[2,704,1024]{2,1,0:T(8,128)(2,1)}, bf16[88,256]{1,0:T(8,128)(2,1)S(1)}, bf16[88,256]{1,0:T(8,128)(2,1)S(1)}, bf16[88,256]{1,0:T(8,128)(2...) custom-call(s32[32]{0:T(128)S(1)} %copy-done.4, ...), custom_call_target="tpu_custom_call" | custom-call | flops 6643777536 | bytes 4718592 | tf_op jit(solution)/shard_map/orthogonalize/pallas_call | solution.py:286
  59.8 1.8 %collective-permute-start = (bf16[88,256]{1,0:T(8,128)(2,1)S(1)}, bf16[88,256]{1,0:T(8,128)(2,1)S(1)}, u32[]{:S(2)}, u32[]{:S(2)}) collective-permute-start(bf16[88,256]{1,0:T(8,128)(2,1)S(1)} %get-tuple-element.53), channel_id=1, source_target_pairs={{0,1},{1,0},{2,3},{3,2},{4,5},{5,4},{6,7},{7,6},{8,9},{9,8},{10,11... | collective-permute-start | bytes 135176 | tf_op jit(solution)/shard_map/ppermute | solution.py:363
  61.7 0.0 collective-permute-start.1
  61.7 0.4 collective-permute-start.2
  62.0 1.8 %collective-permute-start.3 = (bf16[88,256]{1,0:T(8,128)(2,1)S(1)}, bf16[88,256]{1,0:T(8,128)(2,1)S(1)}, u32[]{:S(2)}, u32[]{:S(2)}) collective-permute-start(bf16[88,256]{1,0:T(8,128)(2,1)S(1)} %get-tuple-element.56), channel_id=1, source_target_pairs={{0,8},{1,9},{2,10},{3,11},{4,12},{5,13},{6,14},{7,15},{8,0},{9,1},... | collective-permute-start | bytes 135176 | tf_op jit(solution)/shard_map/ppermute | solution.py:363
  63.8 1.5 %collective-permute-start.4 = (bf16[88,256]{1,0:T(8,128)(2,1)S(1)}, bf16[88,256]{1,0:T(8,128)(2,1)S(1)}, u32[]{:S(2)}, u32[]{:S(2)}) collective-permute-start(bf16[88,256]{1,0:T(8,128)(2,1)S(1)} %get-tuple-element.57), channel_id=1, source_target_pairs={{0,9},{1,8},{2,11},{3,10},{4,13},{5,12},{6,15},{7,14},{8,1},{9,0},... | collective-permute-start | bytes 135176 | tf_op jit(solution)/shard_map/ppermute | solution.py:363
  65.3 11.0 %collective-permute-done.refs_1_ = bf16[88,256]{1,0:T(8,128)(2,1)S(1)} collective-permute-done((bf16[88,256]{1,0:T(8,128)(2,1)S(1)}, bf16[88,256]{1,0:T(8,128)(2,1)S(1)}, u32[]{:S(2)}, u32[]{:S(2)}) %collective-permute-start) | collective-permute-done | bytes 45088 | tf_op jit(solution)/shard_map/ppermute | solution.py:363
  76.3 0.6 collective-permute-start.5
  76.8 0.0 collective-permute-done.1.refs_2_
  76.8 3.1 %collective-permute-start.6 = (bf16[88,256]{1,0:T(8,128)(2,1)S(1)}, bf16[88,256]{1,0:T(8,128)(2,1)S(1)}, u32[]{:S(2)}, u32[]{:S(2)}) collective-permute-start(bf16[88,256]{1,0:T(8,128)(2,1)S(1)} %get-tuple-element.59), channel_id=1, source_target_pairs={{0,13},{1,12},{2,15},{3,14},{4,9},{5,8},{6,11},{7,10},{8,5},{9,4},... | collective-permute-start | bytes 135176 | tf_op jit(solution)/shard_map/ppermute | solution.py:363
  79.9 0.0 collective-permute-done.2.refs_3_
  79.9 1.8 %collective-permute-start.7 = (bf16[88,256]{1,0:T(8,128)(2,1)S(1)}, bf16[88,256]{1,0:T(8,128)(2,1)S(1)}, u32[]{:S(2)}, u32[]{:S(2)}) collective-permute-start(bf16[88,256]{1,0:T(8,128)(2,1)S(1)} %get-tuple-element.60), channel_id=1, source_target_pairs={{0,16},{1,17},{2,18},{3,19},{4,20},{5,21},{6,22},{7,23},{8,24},{9,... | collective-permute-start | bytes 135176 | tf_op jit(solution)/shard_map/ppermute | solution.py:363
  81.7 0.0 collective-permute-done.3.refs_4_
  81.7 0.0 collective-permute-start.8
  81.7 0.0 collective-permute-done.4.refs_5_
  81.7 1.0 collective-permute-start.9
  82.7 0.0 collective-permute-done.5.refs_6_
  82.7 2.3 %collective-permute-start.10 = (bf16[88,256]{1,0:T(8,128)(2,1)S(1)}, bf16[88,256]{1,0:T(8,128)(2,1)S(1)}, u32[]{:S(2)}, u32[]{:S(2)}) collective-permute-start(bf16[88,256]{1,0:T(8,128)(2,1)S(1)} %get-tuple-element.63), channel_id=1, source_target_pairs={{0,21},{1,20},{2,23},{3,22},{4,17},{5,16},{6,19},{7,18},{8,29},{9,... | collective-permute-start | bytes 135176 | tf_op jit(solution)/shard_map/ppermute | solution.py:363
  85.0 0.0 collective-permute-done.6.refs_7_
  85.0 2.3 %collective-permute-start.11 = (bf16[88,256]{1,0:T(8,128)(2,1)S(1)}, bf16[88,256]{1,0:T(8,128)(2,1)S(1)}, u32[]{:S(2)}, u32[]{:S(2)}) collective-permute-start(bf16[88,256]{1,0:T(8,128)(2,1)S(1)} %get-tuple-element.64), channel_id=1, source_target_pairs={{0,24},{1,25},{2,26},{3,27},{4,28},{5,29},{6,30},{7,31},{8,16},{9,... | collective-permute-start | bytes 135176 | tf_op jit(solution)/shard_map/ppermute | solution.py:363
  87.3 0.0 collective-permute-done.7.refs_8_
  87.3 0.1 collective-permute-start.12
  87.4 0.0 collective-permute-done.8.refs_9_
  87.4 0.9 collective-permute-start.13
  88.3 0.0 collective-permute-done.9.refs_10_
  88.3 3.2 %collective-permute-start.14 = (bf16[88,256]{1,0:T(8,128)(2,1)S(1)}, bf16[88,256]{1,0:T(8,128)(2,1)S(1)}, u32[]{:S(2)}, u32[]{:S(2)}) collective-permute-start(bf16[88,256]{1,0:T(8,128)(2,1)S(1)} %get-tuple-element.67), channel_id=1, source_target_pairs={{0,29},{1,28},{2,31},{3,30},{4,25},{5,24},{6,27},{7,26},{8,21},{9,... | collective-permute-start | bytes 135176 | tf_op jit(solution)/shard_map/ppermute | solution.py:363
  91.5 0.0 all-to-all-done.1.x_ref
  91.5 7.9 %orthogonalize.3 = (bf16[2,704,1024]{2,1,0:T(8,128)(2,1)}, bf16[16,88,256]{2,1,0:T(8,128)(2,1)S(1)}) custom-call(s32[32]{0:T(128)S(1)} %copy-done.4, bf16[32,88,256]{2,1,0:T(8,128)(2,1)S(1)} %all-to-all-done.1.x_ref, bf16[2,704,1024]{2,1,0:T(8,128)(2,1)} %get-tuple-element.69.refs_0_), custom_call_target="tpu_custom_call", output_to_operand_aliasing={{0}: (2, {})} | custom-call | flops 6643777536 | bytes 4718592 | tf_op jit(solution)/shard_map/orthogonalize/pallas_call | solution.py:286
  99.5 0.0 collective-permute-done.10.refs_11_
  99.5 0.0 collective-permute-done.11.refs_12_
  99.5 0.0 collective-permute-done.12.refs_13_
  99.5 0.0 collective-permute-done.13.refs_14_
  99.5 0.0 collective-permute-done.14.refs_15_
  99.5 15.0 %all_to_all.15.refs_16_ = bf16[16,88,256]{2,1,0:T(8,128)(2,1)S(1)} all-to-all(bf16[16,88,256]{2,1,0:T(8,128)(2,1)S(1)} %get-tuple-element.87), channel_id=1, replica_groups={{0,1,4,5,8,9,12,13,16,17,20,21,24,25,28,29},{2,3,6,7,10,11,14,15,18,19,..., dimensions={0} | all-to-all | bytes 1441792 | tf_op jit(solution)/shard_map/all_to_all | solution.py:357
  114.5 3.0 %unpack.1 = bf16[32,88,256]{2,1,0:T(8,128)(2,1)} custom-call(s32[32]{0:T(128)S(1)} %copy-done.3, s32[32]{0:T(128)S(1)} %copy-done.4, s32[32]{0:T(128)S(1)} %copy-done.5, bf16[88,256]{1,0:T(8,128)(2,1)S(1)} %get-tuple-element.71.refs_0_, bf16[88,256]{1,0:T(8,128)(2,1)S(1)} %collective-permute-done.refs_1_, ...), custom_call_target="tpu_custom_call" | custom-call | bytes 2883584 | tf_op jit(solution)/shard_map/unpack/pallas_call | solution.py:338
  (4 shorter events, 0.0 us)
Async XLA Ops:
  5.8 7.5 %copy-start = (f32[32,88,256]{2,1,0:T(8,128)S(1)}, f32[32,88,256]{2,1,0:T(8,128)}, u32[]{:S(2)}) copy-start(f32[32,88,256]{2,1,0:T(8,128)} %m_ref.3) | copy-start | bytes 8650756
  5.8 7.5 %copy-start.3 = (s32[32]{0:T(128)S(1)}, s32[32]{0:T(128)}, u32[]{:S(2)}) copy-start(s32[32]{0:T(128)} %owner_ref.5) | copy-start | bytes 388
  5.8 7.5 %copy-start.4 = (s32[32]{0:T(128)S(1)}, s32[32]{0:T(128)}, u32[]{:S(2)}) copy-start(s32[32]{0:T(128)} %get-tuple-element.46.other_ref) | copy-start | bytes 388
  5.8 7.5 %copy-start.5 = (s32[32]{0:T(128)S(1)}, s32[32]{0:T(128)}, u32[]{:S(2)}) copy-start(s32[32]{0:T(128)} %get-tuple-element.47.rank_ref) | copy-start | bytes 388
  5.8 40.6 %all-to-all-start = ((bf16[32,88,256]{2,1,0:T(8,128)(2,1)}), bf16[32,88,256]{2,1,0:T(8,128)(2,1)}, u32[]{:S(2)}, u32[]{:S(2)}) async-start(bf16[32,88,256]{2,1,0:T(8,128)(2,1)} %get-tuple-element.49), calls=%async_computation | async-start | bytes 2883584 | tf_op jit(solution)/shard_map/all_to_all | solution.py:357
  13.3 1.4 %copy-start.1 = (bf16[32,88,256]{2,1,0:T(8,128)(2,1)S(1)}, bf16[32,88,256]{2,1,0:T(8,128)(2,1)}, u32[]{:S(2)}) copy-start(bf16[32,88,256]{2,1,0:T(8,128)(2,1)} %g_ref.3) | copy-start | bytes 4325380
  17.5 1.1 copy-start.2
  46.5 45.1 %all-to-all-start.1 = ((bf16[32,88,256]{2,1,0:T(8,128)(2,1)}), bf16[32,88,256]{2,1,0:T(8,128)(2,1)S(1)}, u32[]{:S(2)}, u32[]{:S(2)}) async-start(bf16[32,88,256]{2,1,0:T(8,128)(2,1)} %copy-done.2), calls=%async_computation.1 | async-start | bytes 2883584 | tf_op jit(solution)/shard_map/all_to_all | solution.py:357
  59.8 16.4 %collective-permute-start = (bf16[88,256]{1,0:T(8,128)(2,1)S(1)}, bf16[88,256]{1,0:T(8,128)(2,1)S(1)}, u32[]{:S(2)}, u32[]{:S(2)}) collective-permute-start(bf16[88,256]{1,0:T(8,128)(2,1)S(1)} %get-tuple-element.53), channel_id=1, source_target_pairs={{0,1},{1,0},{2,3},{3,2},{4,5},{5,4},{6,7},{7,6},{8,9},{9,8},{10,11... | collective-permute-start | bytes 135176 | tf_op jit(solution)/shard_map/ppermute | solution.py:363
  61.7 15.2 %collective-permute-start.1 = (bf16[88,256]{1,0:T(8,128)(2,1)S(1)}, bf16[88,256]{1,0:T(8,128)(2,1)S(1)}, u32[]{:S(2)}, u32[]{:S(2)}) collective-permute-start(bf16[88,256]{1,0:T(8,128)(2,1)S(1)} %get-tuple-element.54), channel_id=1, source_target_pairs={{0,4},{1,5},{2,6},{3,7},{4,0},{5,1},{6,2},{7,3},{8,12},{9,13},{10,... | collective-permute-start | bytes 135176 | tf_op jit(solution)/shard_map/ppermute | solution.py:363
  61.7 18.3 %collective-permute-start.2 = (bf16[88,256]{1,0:T(8,128)(2,1)S(1)}, bf16[88,256]{1,0:T(8,128)(2,1)S(1)}, u32[]{:S(2)}, u32[]{:S(2)}) collective-permute-start(bf16[88,256]{1,0:T(8,128)(2,1)S(1)} %get-tuple-element.55), channel_id=1, source_target_pairs={{0,5},{1,4},{2,7},{3,6},{4,1},{5,0},{6,3},{7,2},{8,13},{9,12},{10,... | collective-permute-start | bytes 135176 | tf_op jit(solution)/shard_map/ppermute | solution.py:363
  62.0 19.7 %collective-permute-start.3 = (bf16[88,256]{1,0:T(8,128)(2,1)S(1)}, bf16[88,256]{1,0:T(8,128)(2,1)S(1)}, u32[]{:S(2)}, u32[]{:S(2)}) collective-permute-start(bf16[88,256]{1,0:T(8,128)(2,1)S(1)} %get-tuple-element.56), channel_id=1, source_target_pairs={{0,8},{1,9},{2,10},{3,11},{4,12},{5,13},{6,14},{7,15},{8,0},{9,1},... | collective-permute-start | bytes 135176 | tf_op jit(solution)/shard_map/ppermute | solution.py:363
  63.8 17.9 %collective-permute-start.4 = (bf16[88,256]{1,0:T(8,128)(2,1)S(1)}, bf16[88,256]{1,0:T(8,128)(2,1)S(1)}, u32[]{:S(2)}, u32[]{:S(2)}) collective-permute-start(bf16[88,256]{1,0:T(8,128)(2,1)S(1)} %get-tuple-element.57), channel_id=1, source_target_pairs={{0,9},{1,8},{2,11},{3,10},{4,13},{5,12},{6,15},{7,14},{8,1},{9,0},... | collective-permute-start | bytes 135176 | tf_op jit(solution)/shard_map/ppermute | solution.py:363
  76.3 6.4 %collective-permute-start.5 = (bf16[88,256]{1,0:T(8,128)(2,1)S(1)}, bf16[88,256]{1,0:T(8,128)(2,1)S(1)}, u32[]{:S(2)}, u32[]{:S(2)}) collective-permute-start(bf16[88,256]{1,0:T(8,128)(2,1)S(1)} %get-tuple-element.58), channel_id=1, source_target_pairs={{0,12},{1,13},{2,14},{3,15},{4,8},{5,9},{6,10},{7,11},{8,4},{9,5},... | collective-permute-start | bytes 135176 | tf_op jit(solution)/shard_map/ppermute | solution.py:363
  76.8 8.2 %collective-permute-start.6 = (bf16[88,256]{1,0:T(8,128)(2,1)S(1)}, bf16[88,256]{1,0:T(8,128)(2,1)S(1)}, u32[]{:S(2)}, u32[]{:S(2)}) collective-permute-start(bf16[88,256]{1,0:T(8,128)(2,1)S(1)} %get-tuple-element.59), channel_id=1, source_target_pairs={{0,13},{1,12},{2,15},{3,14},{4,9},{5,8},{6,11},{7,10},{8,5},{9,4},... | collective-permute-start | bytes 135176 | tf_op jit(solution)/shard_map/ppermute | solution.py:363
  79.9 7.4 %collective-permute-start.7 = (bf16[88,256]{1,0:T(8,128)(2,1)S(1)}, bf16[88,256]{1,0:T(8,128)(2,1)S(1)}, u32[]{:S(2)}, u32[]{:S(2)}) collective-permute-start(bf16[88,256]{1,0:T(8,128)(2,1)S(1)} %get-tuple-element.60), channel_id=1, source_target_pairs={{0,16},{1,17},{2,18},{3,19},{4,20},{5,21},{6,22},{7,23},{8,24},{9,... | collective-permute-start | bytes 135176 | tf_op jit(solution)/shard_map/ppermute | solution.py:363
  81.7 5.7 %collective-permute-start.8 = (bf16[88,256]{1,0:T(8,128)(2,1)S(1)}, bf16[88,256]{1,0:T(8,128)(2,1)S(1)}, u32[]{:S(2)}, u32[]{:S(2)}) collective-permute-start(bf16[88,256]{1,0:T(8,128)(2,1)S(1)} %get-tuple-element.61), channel_id=1, source_target_pairs={{0,17},{1,16},{2,19},{3,18},{4,21},{5,20},{6,23},{7,22},{8,25},{9,... | collective-permute-start | bytes 135176 | tf_op jit(solution)/shard_map/ppermute | solution.py:363
  81.7 6.6 %collective-permute-start.9 = (bf16[88,256]{1,0:T(8,128)(2,1)S(1)}, bf16[88,256]{1,0:T(8,128)(2,1)S(1)}, u32[]{:S(2)}, u32[]{:S(2)}) collective-permute-start(bf16[88,256]{1,0:T(8,128)(2,1)S(1)} %get-tuple-element.62), channel_id=1, source_target_pairs={{0,20},{1,21},{2,22},{3,23},{4,16},{5,17},{6,18},{7,19},{8,28},{9,... | collective-permute-start | bytes 135176 | tf_op jit(solution)/shard_map/ppermute | solution.py:363
  82.7 16.8 %collective-permute-start.10 = (bf16[88,256]{1,0:T(8,128)(2,1)S(1)}, bf16[88,256]{1,0:T(8,128)(2,1)S(1)}, u32[]{:S(2)}, u32[]{:S(2)}) collective-permute-start(bf16[88,256]{1,0:T(8,128)(2,1)S(1)} %get-tuple-element.63), channel_id=1, source_target_pairs={{0,21},{1,20},{2,23},{3,22},{4,17},{5,16},{6,19},{7,18},{8,29},{9,... | collective-permute-start | bytes 135176 | tf_op jit(solution)/shard_map/ppermute | solution.py:363
  85.0 14.5 %collective-permute-start.11 = (bf16[88,256]{1,0:T(8,128)(2,1)S(1)}, bf16[88,256]{1,0:T(8,128)(2,1)S(1)}, u32[]{:S(2)}, u32[]{:S(2)}) collective-permute-start(bf16[88,256]{1,0:T(8,128)(2,1)S(1)} %get-tuple-element.64), channel_id=1, source_target_pairs={{0,24},{1,25},{2,26},{3,27},{4,28},{5,29},{6,30},{7,31},{8,16},{9,... | collective-permute-start | bytes 135176 | tf_op jit(solution)/shard_map/ppermute | solution.py:363
  87.3 12.2 %collective-permute-start.12 = (bf16[88,256]{1,0:T(8,128)(2,1)S(1)}, bf16[88,256]{1,0:T(8,128)(2,1)S(1)}, u32[]{:S(2)}, u32[]{:S(2)}) collective-permute-start(bf16[88,256]{1,0:T(8,128)(2,1)S(1)} %get-tuple-element.65), channel_id=1, source_target_pairs={{0,25},{1,24},{2,27},{3,26},{4,29},{5,28},{6,31},{7,30},{8,17},{9,... | collective-permute-start | bytes 135176 | tf_op jit(solution)/shard_map/ppermute | solution.py:363
  87.4 12.1 %collective-permute-start.13 = (bf16[88,256]{1,0:T(8,128)(2,1)S(1)}, bf16[88,256]{1,0:T(8,128)(2,1)S(1)}, u32[]{:S(2)}, u32[]{:S(2)}) collective-permute-start(bf16[88,256]{1,0:T(8,128)(2,1)S(1)} %get-tuple-element.66), channel_id=1, source_target_pairs={{0,28},{1,29},{2,30},{3,31},{4,24},{5,25},{6,26},{7,27},{8,20},{9,... | collective-permute-start | bytes 135176 | tf_op jit(solution)/shard_map/ppermute | solution.py:363
  88.3 11.2 %collective-permute-start.14 = (bf16[88,256]{1,0:T(8,128)(2,1)S(1)}, bf16[88,256]{1,0:T(8,128)(2,1)S(1)}, u32[]{:S(2)}, u32[]{:S(2)}) collective-permute-start(bf16[88,256]{1,0:T(8,128)(2,1)S(1)} %get-tuple-element.67), channel_id=1, source_target_pairs={{0,29},{1,28},{2,31},{3,30},{4,25},{5,24},{6,27},{7,26},{8,21},{9,... | collective-permute-start | bytes 135176 | tf_op jit(solution)/shard_map/ppermute | solution.py:363

commit v10 on v9

--- a/solution.py
+++ b/solution.py
@@ -12,6 +12,7 @@
 CAP = 2
 HALVES = 2
 TILES = 2
+LOW = 4
 
 coef_a = 3.4445
 coef_b = -4.775
@@ -219,6 +220,11 @@
                 write(t, (update_scale * combined).astype(jnp.bfloat16))
 
 
+def stage_place(row_offset, col_offset, row_size, width):
+    high = row_offset // LOW * width + col_offset
+    return row_offset % LOW * (row_size // LOW * width) + high
+
+
 def ortho_kernel(row_size, col_size, slot, other_ref, x_ref, *refs):
     _, rows, cols = x_ref.shape
     width = col_size // HALVES
@@ -228,8 +234,8 @@
     if slot:
         owned_ref, back_ref, x_s, y_s, gram_s, out_s, sems = refs[1:]
     else:
-        owned_ref, offset_refs = refs[0], refs[1 : 1 + places]
-        x_s, y_s, gram_s, out_s, sems, back_ref = refs[1 + places :]
+        owned_ref, low_refs = refs[0], refs[1 : 1 + LOW]
+        x_s, y_s, gram_s, out_s, sems, back_ref = refs[1 + LOW :]
     row, col = lax.axis_index("dp"), lax.axis_index("owner")
     me = row * col_size + col
     owns = other_ref[me] != me
@@ -247,7 +253,10 @@
             block = result[j * rows : (j + 1) * rows, :]
             r = t * (row_size // TILES) + j
             for c in range(width):
-                place = r * width + c if slot else (r ^ row) * width + (c ^ (col % width))
+                if slot:
+                    place = r * width + c
+                else:
+                    place = stage_place(r ^ row, c ^ (col % width), row_size, width)
                 back_ref[place] = jnp.where(
                     low,
                     block[:, c * cols : (c + 1) * cols],
@@ -256,8 +265,8 @@
 
     newton_schulz(height, inverse, x_s, y_s, gram_s, write)
     if not slot:
-        for offset in range(places):
-            offset_refs[offset][...] = back_ref[offset]
+        for k in range(LOW):
+            low_refs[k][...] = back_ref[k * places // LOW : (k + 1) * places // LOW]
     for t in range(TILES):
         copy_out(t).wait()
 
@@ -281,7 +290,7 @@
         operands.append(owned)
         back = [(places, rows, cols)]
     else:
-        back = [(rows, cols)] * places
+        back = [(places // LOW, rows, cols)] * LOW
         scratch_shapes.append(pltpu.VMEM((places, rows, cols), jnp.bfloat16))
     owned, *back = pl.pallas_call(
         functools.partial(ortho_kernel, row_size, col_size, slot),
@@ -303,44 +312,69 @@
     return owned, back
 
 
-def unpack_kernel(chunk, col_size, row_size, owner_ref, other_ref, rank_ref, *refs):
+def restage_kernel(*refs):
+    low_refs, high_refs = refs[:LOW], refs[LOW:]
+    for h, high_ref in enumerate(high_refs):
+        for k, low_ref in enumerate(low_refs):
+            high_ref[k] = low_ref[h]
+
+
+def restage(blocks):
+    highs, rows, cols = blocks[0].shape
+    out = jax.ShapeDtypeStruct((LOW, rows, cols), blocks[0].dtype)
+    return pl.pallas_call(
+        restage_kernel,
+        grid=(1,),
+        in_specs=[whole(blocks[0].shape)] * LOW,
+        out_specs=[whole(out.shape)] * highs,
+        out_shape=[out] * highs,
+        compiler_params=PARAMS,
+        cost_estimate=pl.CostEstimate(
+            flops=0, bytes_accessed=4 * LOW * highs * rows * cols, transcendentals=0
+        ),
+        name="restage",
+    )(*blocks)
+
+
+def unpack_kernel(chunk, col_size, owner_ref, other_ref, rank_ref, *refs):
     width = col_size // HALVES
-    places = row_size * width
-    offset_refs, second_ref, update_ref, first_ref = refs[:places], *refs[places:]
+    high_refs, second_ref, update_ref, first_ref = refs[:-3], *refs[-3:]
     step = pl.program_id(0)
     row, col = lax.axis_index("dp"), lax.axis_index("owner")
     half = col // width
 
     @pl.when(step == 0)
     def _():
-        for offset in range(places):
-            first_ref[offset] = offset_refs[offset][...]
+        for h, high_ref in enumerate(high_refs):
+            first_ref[h * LOW : (h + 1) * LOW] = high_ref[...]
 
     for j in range(chunk):
         i = step * chunk + j
         owner = owner_ref[i]
         host = jnp.where((owner % col_size) // width == half, owner, other_ref[owner])
         host_row, host_col = host // col_size, host % width
+        offset = host_row ^ row
+        high = offset // LOW * width + (host_col ^ (col % width))
 
         @pl.when(rank_ref[i] == 0)
         def _():
-            update_ref[j] = first_ref[(host_row ^ row) * width + (host_col ^ (col % width))]
+            update_ref[j] = first_ref[high * LOW + offset % LOW]
 
         @pl.when(rank_ref[i] == 1)
         def _():
             update_ref[j] = second_ref[host_row * width + host_col]
 
 
-def unpack(owner_table, other, rank, first, second, row_size, col_size):
-    places, rows, cols = second.shape
+def unpack(owner_table, other, rank, first, second, col_size):
+    _, rows, cols = second.shape
     mats = owner_table.shape[0]
     chunk = 8
     return pl.pallas_call(
-        functools.partial(unpack_kernel, chunk, col_size, row_size),
+        functools.partial(unpack_kernel, chunk, col_size),
         grid_spec=pltpu.PrefetchScalarGridSpec(
             num_scalar_prefetch=3,
             grid=(mats // chunk,),
-            in_specs=[whole((rows, cols))] * places + [whole(second.shape)],
+            in_specs=[whole(first[0].shape)] * len(first) + [whole(second.shape)],
             out_specs=pl.BlockSpec((chunk, rows, cols), lambda i, *_: (i, 0, 0)),
             scratch_shapes=[pltpu.VMEM(second.shape, jnp.bfloat16)],
         ),
@@ -378,18 +412,21 @@
     arrived_first, second = lax.optimization_barrier((arrived_first, second))
     arrived_second = exchange(second)
     owned, back_first = orthogonalize(0, other, arrived_first, row_size, col_size)
-    returned_first = [back_first[0]] + [
-        swap(back_first[r * width + c], r * col_size + c, devices)
-        for r in range(row_size)
+    low = [back_first[0]] + [
+        swap(back_first[k], k * col_size, devices) for k in range(1, LOW)
+    ]
+    high = restage(low)
+    high, arrived_second = lax.optimization_barrier((high, arrived_second))
+    returned_first = [high[0]] + [
+        swap(high[r * width + c], r * LOW * col_size + c, devices)
+        for r in range(row_size // LOW)
         for c in range(width)
         if r or c
     ]
     owned, back_second = orthogonalize(1, other, arrived_second, row_size, col_size, owned)
     returned_first, back_second = lax.optimization_barrier((returned_first, back_second))
     returned_second = exchange(back_second[0], halves)
-    update = unpack(
-        owner_table, other, rank, returned_first, returned_second, row_size, col_size
-    )
+    update = unpack(owner_table, other, rank, returned_first, returned_second, col_size)
     return (new_momentum, update, owned)
 
 

time: 118 us -> 115 us (0.975)
  starting transfers between devices: 32.6 us -> 18.8 us
  waiting for transfers between devices: 38.9 us -> 50.2 us
    ppermute x15 -> x6, starting transfers between devices: 20.6 us -> 6.82 us  [swap(): return lax.ppermute(block, AXES, [(d, d ^ offset) for d in range(devices)])]
    all_to_all x2, waiting for transfers between devices: 27.9 us -> 37.2 us  [exchange(): lax.all_to_all(blocks, AXES, split_axis=0, concat_axis=0, tiled=True, axi...]
    ppermute x15 -> x6, waiting for transfers between devices: 11 us -> 13 us  [swap(): return lax.ppermute(block, AXES, [(d, d ^ offset) for d in range(devices)])]
    pallas_call x1 -> x2, Pallas kernels: 2.95 us -> 3.09 us  [the longest x1 3.04 us: unpack(): pl.pallas_call(functools.partial(unpack_kernel, chunk, col_size), grid_sp...]
  transfers between devices with their start and end apart: 17 -> 8, of which waited for: 2 -> 4; matrix products, arithmetic and copies ran while one was open for 0% -> 0% of each run, Pallas kernels for 17% -> 17%
where the time goes in v10:
time: 115 us
  waiting for transfers between devices  50.2 us (44%)
  Pallas kernels  27.8 us (24%)
  starting transfers between devices  18.8 us (16%)
  blocking collectives  14.7 us (13%)
  local copies, waits for them, and re-layouts  2.5 us (2%)
    all_to_all x2, waiting for transfers between devices, exchange(): lax.all_to_all(blocks, AXES, split_axis=0, concat_axis=0, tiled=True, axi...  37.2 us
    pallas_call x2, Pallas kernels, orthogonalize(): pl.pallas_call(functools.partial(ortho_kernel, row_size, col_size, slot),...  16.7 us
    all_to_all x1, blocking collectives, exchange(): lax.all_to_all(blocks, AXES, split_axis=0, concat_axis=0, tiled=True, axi...  14.7 us
    ppermute x6, waiting for transfers between devices, swap(): return lax.ppermute(block, AXES, [(d, d ^ offset) for d in range(devices)])  13 us
    all_to_all x2, starting transfers between devices, exchange(): lax.all_to_all(blocks, AXES, split_axis=0, concat_axis=0, tiled=True, axi...  12 us
    ppermute x6, starting transfers between devices, swap(): return lax.ppermute(block, AXES, [(d, d ^ offset) for d in range(devices)])  6.82 us
    pallas_call x1, Pallas kernels, pack(): pl.pallas_call(functools.partial(pack_kernel, chunk, col_size), grid_spec...  5.14 us
    pallas_call x1, Pallas kernels, unpack(): pl.pallas_call(functools.partial(unpack_kernel, chunk, col_size), grid_sp...  3.04 us
  transfers between devices with their start and end apart: 8, of which 4 were waited for; matrix products, arithmetic and copies ran while one was open for 0% of the time, Pallas kernels for 17%

profile of v10, /device:TPU:0, one launch (start us, length us, event | category | flops | bytes accessed | tf_op | source)
XLA Modules:
  0.0 114.9 jit_solution(2128173545467311245)
XLA Ops:
  0.6 5.1 %pack.1 = (bf16[32,88,256]{2,1,0:T(8,128)(2,1)}, s32[32]{0:T(128)}, s32[32]{0:T(128)}) custom-call(s32[32]{0:T(128)} %owner_ref.5, bf16[32,88,256]{2,1,0:T(8,128)(2,1)} %g_ref.3, f32[32,88,256]{2,1,0:T(8,128)} %m_ref.3), custom_call_target="tpu_custom_call" | custom-call | flops 2883584 | bytes 5767168 | tf_op jit(solution)/shard_map/pack/pallas_call | solution.py:108
  5.8 0.0 copy-start
  5.8 0.0 copy-start.3
  5.8 0.0 copy-start.4
  5.8 0.0 copy-start.5
  5.8 7.4 %all-to-all-start = ((bf16[32,88,256]{2,1,0:T(8,128)(2,1)}), bf16[32,88,256]{2,1,0:T(8,128)(2,1)}, u32[]{:S(2)}, u32[]{:S(2)}) async-start(bf16[32,88,256]{2,1,0:T(8,128)(2,1)} %get-tuple-element.34), calls=%async_computation | async-start | bytes 2883584 | tf_op jit(solution)/shard_map/all_to_all | solution.py:391
  13.3 0.0 copy-done
  13.3 0.0 copy-done.3
  13.3 0.0 copy-done.4
  13.3 0.0 copy-done.5
  13.3 0.0 copy-start.1
  13.3 1.4 %copy-done.1 = bf16[32,88,256]{2,1,0:T(8,128)(2,1)S(1)} copy-done((bf16[32,88,256]{2,1,0:T(8,128)(2,1)S(1)}, bf16[32,88,256]{2,1,0:T(8,128)(2,1)}, u32[]{:S(2)}) %copy-start.1) | copy-done | bytes 1441816
  14.7 2.9 %update_momentum.1 = (f32[32,88,256]{2,1,0:T(8,128)}, bf16[32,88,256]{2,1,0:T(8,128)(2,1)S(1)}) custom-call(s32[32]{0:T(128)S(1)} %copy-done.3, s32[32]{0:T(128)S(1)} %copy-done.4, s32[32]{0:T(128)S(1)} %copy-done.5, bf16[32,88,256]{2,1,0:T(8,128)(2,1)S(1)} %copy-done.1, f32[32,88,256]{2,1,0:T(8,128)S(1)} %copy-done), custom_call_target="tpu_custom_call" | custom-call | flops 2883584 | bytes 8650752 | tf_op jit(solution)/shard_map/update_momentum/pallas_call | solution.py:147
  17.5 0.0 copy-start.2
  17.5 1.1 copy-done.2
  18.6 27.8 %all-to-all-done.x_ref = bf16[32,88,256]{2,1,0:T(8,128)(2,1)} async-done(((bf16[32,88,256]{2,1,0:T(8,128)(2,1)}), bf16[32,88,256]{2,1,0:T(8,128)(2,1)}, u32[]{:S(2)}, u32[]{:S(2)}) %all-to-all-start) | async-done | bytes 1441824 | tf_op jit(solution)/shard_map/all_to_all | solution.py:391
  46.5 4.6 %all-to-all-start.1 = ((bf16[32,88,256]{2,1,0:T(8,128)(2,1)}), bf16[32,88,256]{2,1,0:T(8,128)(2,1)S(1)}, u32[]{:S(2)}, u32[]{:S(2)}) async-start(bf16[32,88,256]{2,1,0:T(8,128)(2,1)} %copy-done.2), calls=%async_computation.1 | async-start | bytes 2883584 | tf_op jit(solution)/shard_map/all_to_all | solution.py:391
  51.0 8.8 %orthogonalize.2 = (bf16[2,704,1024]{2,1,0:T(8,128)(2,1)}, bf16[4,88,256]{2,1,0:T(8,128)(2,1)S(1)}, bf16[4,88,256]{2,1,0:T(8,128)(2,1)S(1)}, bf16[4,88,256]{2,1,0:T(8,128)(2,1)S(1)}, bf16[4,88,256]{2,1,0:T(8,128)(2,1)S(1)}) custom-call(s32[32]{0:T(128)S(1)} %copy-done.4, bf16[32,88,256]{2,1,0:T(8,128)(2,1)} %all-to-all-done.x_ref), custom_call_target="tpu_custom_call" | custom-call | flops 6643777536 | bytes 4718592 | tf_op jit(solution)/shard_map/orthogonalize/pallas_call | solution.py:295
  59.8 0.3 collective-permute-start
  60.1 1.7 %collective-permute-start.1 = (bf16[4,88,256]{2,1,0:T(8,128)(2,1)S(1)}, bf16[4,88,256]{2,1,0:T(8,128)(2,1)S(1)}, u32[]{:S(2)}, u32[]{:S(2)}) collective-permute-start(bf16[4,88,256]{2,1,0:T(8,128)(2,1)S(1)} %get-tuple-element.39), channel_id=1, source_target_pairs={{0,8},{1,9},{2,10},{3,11},{4,12},{5,13},{6,14},{7,15},{8,0},{9,1},... | collective-permute-start | bytes 540680 | tf_op jit(solution)/shard_map/ppermute | solution.py:397
  61.8 0.0 collective-permute-start.2
  61.8 0.0 collective-permute-done.refs_1_
  61.8 8.8 %collective-permute-done.1.refs_2_ = bf16[4,88,256]{2,1,0:T(8,128)(2,1)S(1)} collective-permute-done((bf16[4,88,256]{2,1,0:T(8,128)(2,1)S(1)}, bf16[4,88,256]{2,1,0:T(8,128)(2,1)S(1)}, u32[]{:S(2)}, u32[]{:S(2)}) %collective-permute-start.1) | collective-permute-done | bytes 180256 | tf_op jit(solution)/shard_map/ppermute | solution.py:397
  70.6 4.2 %collective-permute-done.2.refs_3_ = bf16[4,88,256]{2,1,0:T(8,128)(2,1)S(1)} collective-permute-done((bf16[4,88,256]{2,1,0:T(8,128)(2,1)S(1)}, bf16[4,88,256]{2,1,0:T(8,128)(2,1)S(1)}, u32[]{:S(2)}, u32[]{:S(2)}) %collective-permute-start.2) | collective-permute-done | bytes 180256 | tf_op jit(solution)/shard_map/ppermute | solution.py:397
  74.9 9.4 %all-to-all-done.1.x_ref = bf16[32,88,256]{2,1,0:T(8,128)(2,1)S(1)} async-done(((bf16[32,88,256]{2,1,0:T(8,128)(2,1)}), bf16[32,88,256]{2,1,0:T(8,128)(2,1)S(1)}, u32[]{:S(2)}, u32[]{:S(2)}) %all-to-all-start.1) | async-done | bytes 1441824 | tf_op jit(solution)/shard_map/all_to_all | solution.py:391
  84.3 3.4 %collective-permute-start.3 = (bf16[4,88,256]{2,1,0:T(8,128)(2,1)S(1)}, bf16[4,88,256]{2,1,0:T(8,128)(2,1)S(1)}, u32[]{:S(2)}, u32[]{:S(2)}) collective-permute-start(bf16[4,88,256]{2,1,0:T(8,128)(2,1)S(1)} %get-tuple-element.47), channel_id=1, source_target_pairs={{0,1},{1,0},{2,3},{3,2},{4,5},{5,4},{6,7},{7,6},{8,9},{9,8},{10,11... | collective-permute-start | bytes 540680 | tf_op jit(solution)/shard_map/ppermute | solution.py:397
  87.6 0.5 collective-permute-start.4
  88.1 0.9 collective-permute-start.5
  89.1 7.9 %orthogonalize.3 = (bf16[2,704,1024]{2,1,0:T(8,128)(2,1)}, bf16[16,88,256]{2,1,0:T(8,128)(2,1)S(1)}) custom-call(s32[32]{0:T(128)S(1)} %copy-done.4, bf16[32,88,256]{2,1,0:T(8,128)(2,1)S(1)} %all-to-all-done.1.x_ref, bf16[2,704,1024]{2,1,0:T(8,128)(2,1)} %get-tuple-element.51.refs_0_), custom_call_target="tpu_custom_call", output_to_operand_aliasing={{0}: (2, {})} | custom-call | flops 6643777536 | bytes 4718592 | tf_op jit(solution)/shard_map/orthogonalize/pallas_call | solution.py:295
  97.0 0.0 collective-permute-done.3.refs_1_
  97.0 0.0 collective-permute-done.4.refs_2_
  97.1 0.0 collective-permute-done.5.refs_3_
  97.1 14.7 %all_to_all.15.refs_4_ = bf16[16,88,256]{2,1,0:T(8,128)(2,1)S(1)} all-to-all(bf16[16,88,256]{2,1,0:T(8,128)(2,1)S(1)} %get-tuple-element.57), channel_id=1, replica_groups={{0,1,4,5,8,9,12,13,16,17,20,21,24,25,28,29},{2,3,6,7,10,11,14,15,18,19,..., dimensions={0} | all-to-all | bytes 1441792 | tf_op jit(solution)/shard_map/all_to_all | solution.py:391
  111.8 3.0 %unpack.1 = bf16[32,88,256]{2,1,0:T(8,128)(2,1)} custom-call(s32[32]{0:T(128)S(1)} %copy-done.3, s32[32]{0:T(128)S(1)} %copy-done.4, s32[32]{0:T(128)S(1)} %copy-done.5, bf16[4,88,256]{2,1,0:T(8,128)(2,1)S(1)} %get-tuple-element.53.refs_0_, bf16[4,88,256]{2,1,0:T(8,128)(2,1)S(1)} %collective-permute-done.3.refs_1_, ...), custom_call_target="tpu_custom_call" | custom-call | bytes 2883584 | tf_op jit(solution)/shard_map/unpack/pallas_call | solution.py:372
  (1 shorter events, 0.0 us)
Async XLA Ops:
  5.8 7.5 %copy-start = (f32[32,88,256]{2,1,0:T(8,128)S(1)}, f32[32,88,256]{2,1,0:T(8,128)}, u32[]{:S(2)}) copy-start(f32[32,88,256]{2,1,0:T(8,128)} %m_ref.3) | copy-start | bytes 8650756
  5.8 7.5 %copy-start.3 = (s32[32]{0:T(128)S(1)}, s32[32]{0:T(128)}, u32[]{:S(2)}) copy-start(s32[32]{0:T(128)} %owner_ref.5) | copy-start | bytes 388
  5.8 7.5 %copy-start.4 = (s32[32]{0:T(128)S(1)}, s32[32]{0:T(128)}, u32[]{:S(2)}) copy-start(s32[32]{0:T(128)} %get-tuple-element.31.other_ref) | copy-start | bytes 388
  5.8 7.5 %copy-start.5 = (s32[32]{0:T(128)S(1)}, s32[32]{0:T(128)}, u32[]{:S(2)}) copy-start(s32[32]{0:T(128)} %get-tuple-element.32.rank_ref) | copy-start | bytes 388
  5.8 40.6 %all-to-all-start = ((bf16[32,88,256]{2,1,0:T(8,128)(2,1)}), bf16[32,88,256]{2,1,0:T(8,128)(2,1)}, u32[]{:S(2)}, u32[]{:S(2)}) async-start(bf16[32,88,256]{2,1,0:T(8,128)(2,1)} %get-tuple-element.34), calls=%async_computation | async-start | bytes 2883584 | tf_op jit(solution)/shard_map/all_to_all | solution.py:391
  13.3 1.4 %copy-start.1 = (bf16[32,88,256]{2,1,0:T(8,128)(2,1)S(1)}, bf16[32,88,256]{2,1,0:T(8,128)(2,1)}, u32[]{:S(2)}) copy-start(bf16[32,88,256]{2,1,0:T(8,128)(2,1)} %g_ref.3) | copy-start | bytes 4325380
  17.5 1.1 copy-start.2
  46.5 37.8 %all-to-all-start.1 = ((bf16[32,88,256]{2,1,0:T(8,128)(2,1)}), bf16[32,88,256]{2,1,0:T(8,128)(2,1)S(1)}, u32[]{:S(2)}, u32[]{:S(2)}) async-start(bf16[32,88,256]{2,1,0:T(8,128)(2,1)} %copy-done.2), calls=%async_computation.1 | async-start | bytes 2883584 | tf_op jit(solution)/shard_map/all_to_all | solution.py:391
  59.8 2.0 %collective-permute-start = (bf16[4,88,256]{2,1,0:T(8,128)(2,1)S(1)}, bf16[4,88,256]{2,1,0:T(8,128)(2,1)S(1)}, u32[]{:S(2)}, u32[]{:S(2)}) collective-permute-start(bf16[4,88,256]{2,1,0:T(8,128)(2,1)S(1)} %get-tuple-element.38), channel_id=1, source_target_pairs={{0,4},{1,5},{2,6},{3,7},{4,0},{5,1},{6,2},{7,3},{8,12},{9,13},{10,... | collective-permute-start | bytes 540680 | tf_op jit(solution)/shard_map/ppermute | solution.py:397
  60.1 10.4 %collective-permute-start.1 = (bf16[4,88,256]{2,1,0:T(8,128)(2,1)S(1)}, bf16[4,88,256]{2,1,0:T(8,128)(2,1)S(1)}, u32[]{:S(2)}, u32[]{:S(2)}) collective-permute-start(bf16[4,88,256]{2,1,0:T(8,128)(2,1)S(1)} %get-tuple-element.39), channel_id=1, source_target_pairs={{0,8},{1,9},{2,10},{3,11},{4,12},{5,13},{6,14},{7,15},{8,0},{9,1},... | collective-permute-start | bytes 540680 | tf_op jit(solution)/shard_map/ppermute | solution.py:397
  61.8 13.0 %collective-permute-start.2 = (bf16[4,88,256]{2,1,0:T(8,128)(2,1)S(1)}, bf16[4,88,256]{2,1,0:T(8,128)(2,1)S(1)}, u32[]{:S(2)}, u32[]{:S(2)}) collective-permute-start(bf16[4,88,256]{2,1,0:T(8,128)(2,1)S(1)} %get-tuple-element.40), channel_id=1, source_target_pairs={{0,12},{1,13},{2,14},{3,15},{4,8},{5,9},{6,10},{7,11},{8,4},{9,5},... | collective-permute-start | bytes 540680 | tf_op jit(solution)/shard_map/ppermute | solution.py:397
  84.3 12.8 %collective-permute-start.3 = (bf16[4,88,256]{2,1,0:T(8,128)(2,1)S(1)}, bf16[4,88,256]{2,1,0:T(8,128)(2,1)S(1)}, u32[]{:S(2)}, u32[]{:S(2)}) collective-permute-start(bf16[4,88,256]{2,1,0:T(8,128)(2,1)S(1)} %get-tuple-element.47), channel_id=1, source_target_pairs={{0,1},{1,0},{2,3},{3,2},{4,5},{5,4},{6,7},{7,6},{8,9},{9,8},{10,11... | collective-permute-start | bytes 540680 | tf_op jit(solution)/shard_map/ppermute | solution.py:397
  87.6 9.4 %collective-permute-start.4 = (bf16[4,88,256]{2,1,0:T(8,128)(2,1)S(1)}, bf16[4,88,256]{2,1,0:T(8,128)(2,1)S(1)}, u32[]{:S(2)}, u32[]{:S(2)}) collective-permute-start(bf16[4,88,256]{2,1,0:T(8,128)(2,1)S(1)} %get-tuple-element.48), channel_id=1, source_target_pairs={{0,16},{1,17},{2,18},{3,19},{4,20},{5,21},{6,22},{7,23},{8,24},{9,... | collective-permute-start | bytes 540680 | tf_op jit(solution)/shard_map/ppermute | solution.py:397
  88.1 8.9 %collective-permute-start.5 = (bf16[4,88,256]{2,1,0:T(8,128)(2,1)S(1)}, bf16[4,88,256]{2,1,0:T(8,128)(2,1)S(1)}, u32[]{:S(2)}, u32[]{:S(2)}) collective-permute-start(bf16[4,88,256]{2,1,0:T(8,128)(2,1)S(1)} %get-tuple-element.49), channel_id=1, source_target_pairs={{0,17},{1,16},{2,19},{3,18},{4,21},{5,20},{6,23},{7,22},{8,25},{9,... | collective-permute-start | bytes 540680 | tf_op jit(solution)/shard_map/ppermute | solution.py:397

commit v11 on v10

--- a/solution.py
+++ b/solution.py
@@ -46,75 +46,95 @@
 
     @pl.when(rank_ref[i] == slot)
     def _():
-        slot_ref[owner] = nesterov
-        slot_ref[other_ref[owner]] = nesterov
+        block = nesterov()
+        slot_ref[owner] = block
+        slot_ref[other_ref[owner]] = block
+
+
+def make_plan(col_size, owner_ref, other_ref, rank_ref, count_ref, list_ref):
+    devices, mats = other_ref.shape[0], rank_ref.shape[0]
+
+    def clear(d, _):
+        count_ref[d] = 0
+        return 0
+
+    lax.fori_loop(0, devices, clear, 0, unroll=8)
+
+    def rank_matrix(i, _):
+        owner = owner_ref[i]
+        rank = count_ref[owner]
+        rank_ref[i] = rank
+        count_ref[owner] = rank + 1
+        return 0
+
+    lax.fori_loop(0, mats, rank_matrix, 0, unroll=8)
+
+    def list_device(d, found):
+        owns = jnp.minimum(count_ref[d], 1)
+        half = (d % col_size) // (col_size // HALVES)
+        row = 2 * jnp.where(owns == 1, half, 1 - half) + owns
+        place = found[0]
+        for k in range(1, 2 * HALVES):
+            place = jnp.where(row == k, found[k], place)
+        list_ref[row * devices + place] = d
+        return tuple(n + jnp.where(row == k, 1, 0) for k, n in enumerate(found))
+
+    found = lax.fori_loop(0, devices, list_device, (0,) * (2 * HALVES), unroll=8)
+    for half in range(HALVES):
+
+        def pair(k, _):
+            idle = list_ref[2 * half * devices + k]
+            other_ref[list_ref[(2 * half + 1) * devices + k]] = idle
+            other_ref[idle] = idle
+            return 0
+
+        lax.fori_loop(0, found[2 * half + 1], pair, 0)
 
 
 def pack_kernel(
-    chunk, col_size, owner_ref, g_ref, m_ref, first_ref, other_ref, rank_ref, count_ref, list_ref
+    chunk, col_size, owner_ref, g_ref, m_ref, first_ref, other_ref, rank_ref,
+    count_ref, list_ref, g_s, m_s, sems,
 ):
-    step = pl.program_id(0)
-    devices = first_ref.shape[0]
     mats = rank_ref.shape[0]
 
-    def half_of(d):
-        return (d % col_size) // (col_size // HALVES)
-
-    @pl.when(step == 0)
-    def _():
-        @pl.loop(0, devices)
-        def _(d):
-            count_ref[d] = 0
-
-        def rank_matrix(i, _):
-            owner = owner_ref[i]
-            rank_ref[i] = count_ref[owner]
-            count_ref[owner] = count_ref[owner] + 1
-            return 0
-
-        lax.fori_loop(0, mats, rank_matrix, 0)
-
-        def list_device(d, found):
-            owns = jnp.minimum(count_ref[d], 1)
-            half = half_of(d)
-            row = 2 * jnp.where(owns == 1, half, 1 - half) + owns
-            place = found[0]
-            for k in range(1, 2 * HALVES):
-                place = jnp.where(row == k, found[k], place)
-            list_ref[row * devices + place] = d
-            return tuple(n + jnp.where(row == k, 1, 0) for k, n in enumerate(found))
-
-        found = lax.fori_loop(0, devices, list_device, (0,) * (2 * HALVES))
-        for half in range(HALVES):
-
-            def pair(k, _):
-                idle = list_ref[2 * half * devices + k]
-                other_ref[list_ref[(2 * half + 1) * devices + k]] = idle
-                other_ref[idle] = idle
-                return 0
-
-            lax.fori_loop(0, found[2 * half + 1], pair, 0)
-
-    for j in range(chunk):
-        i = step * chunk + j
-        _, nesterov = nesterov_of(g_ref, m_ref, j)
-        store_slot(0, (other_ref, rank_ref), i, owner_ref[i], nesterov, first_ref)
+    def loads(k):
+        span = pl.ds(k * chunk, chunk)
+        return (
+            pltpu.make_async_copy(g_ref.at[span], g_s.at[span], sems.at[0, k]),
+            pltpu.make_async_copy(m_ref.at[span], m_s.at[span], sems.at[1, k]),
+        )
+
+    for k in range(mats // chunk):
+        for load in loads(k):
+            load.start()
+    make_plan(col_size, owner_ref, other_ref, rank_ref, count_ref, list_ref)
+    for k in range(mats // chunk):
+        for load in loads(k):
+            load.wait()
+        for i in range(k * chunk, (k + 1) * chunk):
+            store_slot(
+                0, (other_ref, rank_ref), i, owner_ref[i],
+                lambda: nesterov_of(g_s, m_s, i)[1], first_ref,
+            )
 
 
 def pack(gradients, momentum, owner_table, devices, col_size):
     mats, rows, cols = gradients.shape
     chunk = 8
-    block = pl.BlockSpec((chunk, rows, cols), lambda i, *_: (i, 0, 0))
+    anywhere = pl.BlockSpec(memory_space=pl.ANY)
     return pl.pallas_call(
         functools.partial(pack_kernel, chunk, col_size),
         grid_spec=pltpu.PrefetchScalarGridSpec(
             num_scalar_prefetch=1,
-            grid=(mats // chunk,),
-            in_specs=[block, block],
+            grid=(1,),
+            in_specs=[anywhere, anywhere],
             out_specs=[whole((devices, rows, cols)), SMEM, SMEM],
             scratch_shapes=[
                 pltpu.SMEM((devices,), jnp.int32),
                 pltpu.SMEM((2 * HALVES * devices,), jnp.int32),
+                pltpu.VMEM(gradients.shape, gradients.dtype),
+                pltpu.VMEM(momentum.shape, momentum.dtype),
+                pltpu.SemaphoreType.DMA((2, mats // chunk)),
             ],
         ),
         out_shape=[
@@ -136,7 +156,7 @@
         i = step * chunk + j
         new, nesterov = nesterov_of(g_ref, m_ref, j)
         nm_ref[j] = new
-        store_slot(1, (other_ref, rank_ref), i, owner_ref[i], nesterov, second_ref)
+        store_slot(1, (other_ref, rank_ref), i, owner_ref[i], lambda: nesterov, second_ref)
 
 
 def update_momentum(gradients, momentum, owner_table, other, rank):
@@ -338,18 +358,18 @@
 
 def unpack_kernel(chunk, col_size, owner_ref, other_ref, rank_ref, *refs):
     width = col_size // HALVES
-    high_refs, second_ref, update_ref, first_ref = refs[:-3], *refs[-3:]
-    step = pl.program_id(0)
+    high_refs, second_ref, update_ref, first_s, update_s, sems = refs[:-5], *refs[-5:]
     row, col = lax.axis_index("dp"), lax.axis_index("owner")
     half = col // width
-
-    @pl.when(step == 0)
-    def _():
-        for h, high_ref in enumerate(high_refs):
-            first_ref[h * LOW : (h + 1) * LOW] = high_ref[...]
-
-    for j in range(chunk):
-        i = step * chunk + j
+    for h, high_ref in enumerate(high_refs):
+        first_s[h * LOW : (h + 1) * LOW] = high_ref[...]
+
+    def copy_out(k):
+        span = pl.ds(k * chunk, chunk)
+        return pltpu.make_async_copy(update_s.at[span], update_ref.at[span], sems.at[k])
+
+    chunks = update_s.shape[0] // chunk
+    for i in range(chunks * chunk):
         owner = owner_ref[i]
         host = jnp.where((owner % col_size) // width == half, owner, other_ref[owner])
         host_row, host_col = host // col_size, host % width
@@ -358,11 +378,16 @@
 
         @pl.when(rank_ref[i] == 0)
         def _():
-            update_ref[j] = first_ref[high * LOW + offset % LOW]
+            update_s[i] = first_s[high * LOW + offset % LOW]
 
         @pl.when(rank_ref[i] == 1)
         def _():
-            update_ref[j] = second_ref[host_row * width + host_col]
+            update_s[i] = second_ref[host_row * width + host_col]
+
+        if i % chunk == chunk - 1:
+            copy_out(i // chunk).start()
+    for k in range(chunks):
+        copy_out(k).wait()
 
 
 def unpack(owner_table, other, rank, first, second, col_size):
@@ -373,10 +398,14 @@
         functools.partial(unpack_kernel, chunk, col_size),
         grid_spec=pltpu.PrefetchScalarGridSpec(
             num_scalar_prefetch=3,
-            grid=(mats // chunk,),
+            grid=(1,),
             in_specs=[whole(first[0].shape)] * len(first) + [whole(second.shape)],
-            out_specs=pl.BlockSpec((chunk, rows, cols), lambda i, *_: (i, 0, 0)),
-            scratch_shapes=[pltpu.VMEM(second.shape, jnp.bfloat16)],
+            out_specs=pl.BlockSpec(memory_space=pl.ANY),
+            scratch_shapes=[
+                pltpu.VMEM(second.shape, jnp.bfloat16),
+                pltpu.VMEM((mats, rows, cols), jnp.bfloat16),
+                pltpu.SemaphoreType.DMA((mats // chunk,)),
+            ],
         ),
         out_shape=jax.ShapeDtypeStruct((mats, rows, cols), jnp.bfloat16),
         compiler_params=PARAMS,
@@ -416,7 +445,7 @@
         swap(back_first[k], k * col_size, devices) for k in range(1, LOW)
     ]
     high = restage(low)
-    high, arrived_second = lax.optimization_barrier((high, arrived_second))
+    _, arrived_second = lax.optimization_barrier((high, arrived_second))
     returned_first = [high[0]] + [
         swap(high[r * width + c], r * LOW * col_size + c, devices)
         for r in range(row_size // LOW)

time: 115 us -> 111 us (0.965)
  waiting for transfers between devices: 50.2 us -> 45.3 us
  blocking collectives: 14.7 us -> 16.6 us
  Pallas kernels: 27.8 us -> 26.4 us
    all_to_all x2, waiting for transfers between devices: 37.2 us -> 32.3 us  [exchange(): lax.all_to_all(blocks, AXES, split_axis=0, concat_axis=0, tiled=True, axi...]
    all_to_all x1, blocking collectives: 14.7 us -> 16.6 us  [exchange(): lax.all_to_all(blocks, AXES, split_axis=0, concat_axis=0, tiled=True, axi...]
  transfers between devices with their start and end apart: 8 -> 8, of which waited for: 4 -> 4; matrix products, arithmetic and copies ran while one was open for 0% -> 0% of each run, Pallas kernels for 17% -> 18%
where the time goes in v11:
time: 111 us; the launch traced here: 110 us
  waiting for transfers between devices  45.3 us (41%)
  Pallas kernels  26.4 us (24%)
  starting transfers between devices  18.9 us (17%)
  blocking collectives  16.6 us (15%)
  local copies, waits for them, and re-layouts  2.5 us (2%)
    all_to_all x2, waiting for transfers between devices, exchange(): lax.all_to_all(blocks, AXES, split_axis=0, concat_axis=0, tiled=True, axi...  32.3 us
    pallas_call x2, Pallas kernels, orthogonalize(): pl.pallas_call(functools.partial(ortho_kernel, row_size, col_size, slot),...  16.7 us
    all_to_all x1, blocking collectives, exchange(): lax.all_to_all(blocks, AXES, split_axis=0, concat_axis=0, tiled=True, axi...  16.6 us
    ppermute x6, waiting for transfers between devices, swap(): return lax.ppermute(block, AXES, [(d, d ^ offset) for d in range(devices)])  13 us
    all_to_all x2, starting transfers between devices, exchange(): lax.all_to_all(blocks, AXES, split_axis=0, concat_axis=0, tiled=True, axi...  12 us
    ppermute x6, starting transfers between devices, swap(): return lax.ppermute(block, AXES, [(d, d ^ offset) for d in range(devices)])  6.95 us
    pallas_call x1, Pallas kernels, pack(): pl.pallas_call(functools.partial(pack_kernel, chunk, col_size), grid_spec...  4.04 us
    pallas_call x1, Pallas kernels, update_momentum(): pl.pallas_call(functools.partial(momentum_kernel, chunk), grid_spec=pltpu...  2.87 us
  transfers between devices with their start and end apart: 8, of which 4 were waited for; matrix products, arithmetic and copies ran while one was open for 0% of the time, Pallas kernels for 18%

profile of v11, /device:TPU:0, one launch (start us, length us, event | category | flops | bytes accessed | tf_op | source)
XLA Modules:
  0.0 110.4 jit_solution(17859743208771546207)
XLA Ops:
  0.6 4.0 %pack.1 = (bf16[32,88,256]{2,1,0:T(8,128)(2,1)}, s32[32]{0:T(128)}, s32[32]{0:T(128)}) custom-call(s32[32]{0:T(128)} %owner_ref.5, bf16[32,88,256]{2,1,0:T(8,128)(2,1)} %g_ref.3, f32[32,88,256]{2,1,0:T(8,128)} %m_ref.3), custom_call_target="tpu_custom_call" | custom-call | flops 2883584 | bytes 5767168 | tf_op jit(solution)/shard_map/pack/pallas_call | solution.py:125
  4.7 0.0 copy-start
  4.7 0.0 copy-start.3
  4.7 0.0 copy-start.4
  4.7 0.0 copy-start.5
  4.7 7.4 %all-to-all-start = ((bf16[32,88,256]{2,1,0:T(8,128)(2,1)}), bf16[32,88,256]{2,1,0:T(8,128)(2,1)}, u32[]{:S(2)}, u32[]{:S(2)}) async-start(bf16[32,88,256]{2,1,0:T(8,128)(2,1)} %get-tuple-element.30), calls=%async_computation | async-start | bytes 2883584 | tf_op jit(solution)/shard_map/all_to_all | solution.py:420
  12.2 0.0 copy-done
  12.2 0.0 copy-done.3
  12.2 0.0 copy-done.4
  12.2 0.0 copy-done.5
  12.2 0.0 copy-start.1
  12.2 1.4 %copy-done.1 = bf16[32,88,256]{2,1,0:T(8,128)(2,1)S(1)} copy-done((bf16[32,88,256]{2,1,0:T(8,128)(2,1)S(1)}, bf16[32,88,256]{2,1,0:T(8,128)(2,1)}, u32[]{:S(2)}) %copy-start.1) | copy-done | bytes 1441816
  13.6 2.9 %update_momentum.1 = (f32[32,88,256]{2,1,0:T(8,128)}, bf16[32,88,256]{2,1,0:T(8,128)(2,1)S(1)}) custom-call(s32[32]{0:T(128)S(1)} %copy-done.3, s32[32]{0:T(128)S(1)} %copy-done.4, s32[32]{0:T(128)S(1)} %copy-done.5, bf16[32,88,256]{2,1,0:T(8,128)(2,1)S(1)} %copy-done.1, f32[32,88,256]{2,1,0:T(8,128)S(1)} %copy-done), custom_call_target="tpu_custom_call" | custom-call | flops 2883584 | bytes 8650752 | tf_op jit(solution)/shard_map/update_momentum/pallas_call | solution.py:167
  16.4 0.0 copy-start.2
  16.4 1.1 %copy-done.2 = bf16[32,88,256]{2,1,0:T(8,128)(2,1)} copy-done((bf16[32,88,256]{2,1,0:T(8,128)(2,1)}, bf16[32,88,256]{2,1,0:T(8,128)(2,1)S(1)}, u32[]{:S(2)}) %copy-start.2) | copy-done | bytes 1441816
  17.5 27.8 %all-to-all-done.x_ref = bf16[32,88,256]{2,1,0:T(8,128)(2,1)} async-done(((bf16[32,88,256]{2,1,0:T(8,128)(2,1)}), bf16[32,88,256]{2,1,0:T(8,128)(2,1)}, u32[]{:S(2)}, u32[]{:S(2)}) %all-to-all-start) | async-done | bytes 1441824 | tf_op jit(solution)/shard_map/all_to_all | solution.py:420
  45.4 4.6 %all-to-all-start.1 = ((bf16[32,88,256]{2,1,0:T(8,128)(2,1)}), bf16[32,88,256]{2,1,0:T(8,128)(2,1)S(1)}, u32[]{:S(2)}, u32[]{:S(2)}) async-start(bf16[32,88,256]{2,1,0:T(8,128)(2,1)} %copy-done.2), calls=%async_computation.1 | async-start | bytes 2883584 | tf_op jit(solution)/shard_map/all_to_all | solution.py:420
  49.9 8.8 %orthogonalize.2 = (bf16[2,704,1024]{2,1,0:T(8,128)(2,1)}, bf16[4,88,256]{2,1,0:T(8,128)(2,1)S(1)}, bf16[4,88,256]{2,1,0:T(8,128)(2,1)S(1)}, bf16[4,88,256]{2,1,0:T(8,128)(2,1)S(1)}, bf16[4,88,256]{2,1,0:T(8,128)(2,1)S(1)}) custom-call(s32[32]{0:T(128)S(1)} %copy-done.4, bf16[32,88,256]{2,1,0:T(8,128)(2,1)} %all-to-all-done.x_ref), custom_call_target="tpu_custom_call" | custom-call | flops 6643777536 | bytes 4718592 | tf_op jit(solution)/shard_map/orthogonalize/pallas_call | solution.py:315
  58.7 0.3 collective-permute-start
  59.0 1.7 %collective-permute-start.1 = (bf16[4,88,256]{2,1,0:T(8,128)(2,1)S(1)}, bf16[4,88,256]{2,1,0:T(8,128)(2,1)S(1)}, u32[]{:S(2)}, u32[]{:S(2)}) collective-permute-start(bf16[4,88,256]{2,1,0:T(8,128)(2,1)S(1)} %get-tuple-element.35), channel_id=1, source_target_pairs={{0,8},{1,9},{2,10},{3,11},{4,12},{5,13},{6,14},{7,15},{8,0},{9,1},... | collective-permute-start | bytes 540680 | tf_op jit(solution)/shard_map/ppermute | solution.py:426
  60.7 0.0 collective-permute-start.2
  60.7 0.0 collective-permute-done.refs_1_
  60.7 8.8 %collective-permute-done.1.refs_2_ = bf16[4,88,256]{2,1,0:T(8,128)(2,1)S(1)} collective-permute-done((bf16[4,88,256]{2,1,0:T(8,128)(2,1)S(1)}, bf16[4,88,256]{2,1,0:T(8,128)(2,1)S(1)}, u32[]{:S(2)}, u32[]{:S(2)}) %collective-permute-start.1) | collective-permute-done | bytes 180256 | tf_op jit(solution)/shard_map/ppermute | solution.py:426
  69.5 4.2 %collective-permute-done.2.refs_3_ = bf16[4,88,256]{2,1,0:T(8,128)(2,1)S(1)} collective-permute-done((bf16[4,88,256]{2,1,0:T(8,128)(2,1)S(1)}, bf16[4,88,256]{2,1,0:T(8,128)(2,1)S(1)}, u32[]{:S(2)}, u32[]{:S(2)}) %collective-permute-start.2) | collective-permute-done | bytes 180256 | tf_op jit(solution)/shard_map/ppermute | solution.py:426
  73.8 3.4 %collective-permute-start.3 = (bf16[4,88,256]{2,1,0:T(8,128)(2,1)S(1)}, bf16[4,88,256]{2,1,0:T(8,128)(2,1)S(1)}, u32[]{:S(2)}, u32[]{:S(2)}) collective-permute-start(bf16[4,88,256]{2,1,0:T(8,128)(2,1)S(1)} %get-tuple-element.38), channel_id=1, source_target_pairs={{0,1},{1,0},{2,3},{3,2},{4,5},{5,4},{6,7},{7,6},{8,9},{9,8},{10,11... | collective-permute-start | bytes 540680 | tf_op jit(solution)/shard_map/ppermute | solution.py:426
  77.2 1.5 %collective-permute-start.4 = (bf16[4,88,256]{2,1,0:T(8,128)(2,1)S(1)}, bf16[4,88,256]{2,1,0:T(8,128)(2,1)S(1)}, u32[]{:S(2)}, u32[]{:S(2)}) collective-permute-start(bf16[4,88,256]{2,1,0:T(8,128)(2,1)S(1)} %get-tuple-element.39), channel_id=1, source_target_pairs={{0,16},{1,17},{2,18},{3,19},{4,20},{5,21},{6,22},{7,23},{8,24},{9,... | collective-permute-start | bytes 540680 | tf_op jit(solution)/shard_map/ppermute | solution.py:426
  78.6 0.1 collective-permute-start.5
  78.7 4.4 %all-to-all-done.1.x_ref = bf16[32,88,256]{2,1,0:T(8,128)(2,1)S(1)} async-done(((bf16[32,88,256]{2,1,0:T(8,128)(2,1)}), bf16[32,88,256]{2,1,0:T(8,128)(2,1)S(1)}, u32[]{:S(2)}, u32[]{:S(2)}) %all-to-all-start.1) | async-done | bytes 1441824 | tf_op jit(solution)/shard_map/all_to_all | solution.py:420
  83.2 7.9 %orthogonalize.3 = (bf16[2,704,1024]{2,1,0:T(8,128)(2,1)}, bf16[16,88,256]{2,1,0:T(8,128)(2,1)S(1)}) custom-call(s32[32]{0:T(128)S(1)} %copy-done.4, bf16[32,88,256]{2,1,0:T(8,128)(2,1)S(1)} %all-to-all-done.1.x_ref, bf16[2,704,1024]{2,1,0:T(8,128)(2,1)} %get-tuple-element.43.refs_0_), custom_call_target="tpu_custom_call", output_to_operand_aliasing={{0}: (2, {})} | custom-call | flops 6643777536 | bytes 4718592 | tf_op jit(solution)/shard_map/orthogonalize/pallas_call | solution.py:315
  91.1 0.0 collective-permute-done.3.refs_1_
  91.1 0.0 collective-permute-done.4.refs_2_
  91.1 0.0 collective-permute-done.5.refs_3_
  91.1 16.6 %all_to_all.15.refs_4_ = bf16[16,88,256]{2,1,0:T(8,128)(2,1)S(1)} all-to-all(bf16[16,88,256]{2,1,0:T(8,128)(2,1)S(1)} %get-tuple-element.49), channel_id=1, replica_groups={{0,1,4,5,8,9,12,13,16,17,20,21,24,25,28,29},{2,3,6,7,10,11,14,15,18,19,..., dimensions={0} | all-to-all | bytes 1441792 | tf_op jit(solution)/shard_map/all_to_all | solution.py:420
  107.7 2.7 %unpack.1 = bf16[32,88,256]{2,1,0:T(8,128)(2,1)} custom-call(s32[32]{0:T(128)S(1)} %copy-done.3, s32[32]{0:T(128)S(1)} %copy-done.4, s32[32]{0:T(128)S(1)} %copy-done.5, bf16[4,88,256]{2,1,0:T(8,128)(2,1)S(1)} %get-tuple-element.45.refs_0_, bf16[4,88,256]{2,1,0:T(8,128)(2,1)S(1)} %collective-permute-done.3.refs_1_, ...), custom_call_target="tpu_custom_call" | custom-call | bytes 2883584 | tf_op jit(solution)/shard_map/unpack/pallas_call | solution.py:397
  (1 shorter events, 0.0 us)
Async XLA Ops:
  4.7 7.5 %copy-start = (f32[32,88,256]{2,1,0:T(8,128)S(1)}, f32[32,88,256]{2,1,0:T(8,128)}, u32[]{:S(2)}) copy-start(f32[32,88,256]{2,1,0:T(8,128)} %m_ref.3) | copy-start | bytes 8650756
  4.7 7.5 %copy-start.3 = (s32[32]{0:T(128)S(1)}, s32[32]{0:T(128)}, u32[]{:S(2)}) copy-start(s32[32]{0:T(128)} %owner_ref.5) | copy-start | bytes 388
  4.7 7.5 %copy-start.4 = (s32[32]{0:T(128)S(1)}, s32[32]{0:T(128)}, u32[]{:S(2)}) copy-start(s32[32]{0:T(128)} %get-tuple-element.27.other_ref) | copy-start | bytes 388
  4.7 7.5 %copy-start.5 = (s32[32]{0:T(128)S(1)}, s32[32]{0:T(128)}, u32[]{:S(2)}) copy-start(s32[32]{0:T(128)} %get-tuple-element.28.rank_ref) | copy-start | bytes 388
  4.7 40.6 %all-to-all-start = ((bf16[32,88,256]{2,1,0:T(8,128)(2,1)}), bf16[32,88,256]{2,1,0:T(8,128)(2,1)}, u32[]{:S(2)}, u32[]{:S(2)}) async-start(bf16[32,88,256]{2,1,0:T(8,128)(2,1)} %get-tuple-element.30), calls=%async_computation | async-start | bytes 2883584 | tf_op jit(solution)/shard_map/all_to_all | solution.py:420
  12.2 1.4 %copy-start.1 = (bf16[32,88,256]{2,1,0:T(8,128)(2,1)S(1)}, bf16[32,88,256]{2,1,0:T(8,128)(2,1)}, u32[]{:S(2)}) copy-start(bf16[32,88,256]{2,1,0:T(8,128)(2,1)} %g_ref.3) | copy-start | bytes 4325380
  16.4 1.1 %copy-start.2 = (bf16[32,88,256]{2,1,0:T(8,128)(2,1)}, bf16[32,88,256]{2,1,0:T(8,128)(2,1)S(1)}, u32[]{:S(2)}) copy-start(bf16[32,88,256]{2,1,0:T(8,128)(2,1)S(1)} %get-tuple-element.41) | copy-start | bytes 4325380
  45.4 37.8 %all-to-all-start.1 = ((bf16[32,88,256]{2,1,0:T(8,128)(2,1)}), bf16[32,88,256]{2,1,0:T(8,128)(2,1)S(1)}, u32[]{:S(2)}, u32[]{:S(2)}) async-start(bf16[32,88,256]{2,1,0:T(8,128)(2,1)} %copy-done.2), calls=%async_computation.1 | async-start | bytes 2883584 | tf_op jit(solution)/shard_map/all_to_all | solution.py:420
  58.7 2.0 %collective-permute-start = (bf16[4,88,256]{2,1,0:T(8,128)(2,1)S(1)}, bf16[4,88,256]{2,1,0:T(8,128)(2,1)S(1)}, u32[]{:S(2)}, u32[]{:S(2)}) collective-permute-start(bf16[4,88,256]{2,1,0:T(8,128)(2,1)S(1)} %get-tuple-element.34), channel_id=1, source_target_pairs={{0,4},{1,5},{2,6},{3,7},{4,0},{5,1},{6,2},{7,3},{8,12},{9,13},{10,... | collective-permute-start | bytes 540680 | tf_op jit(solution)/shard_map/ppermute | solution.py:426
  59.0 10.5 %collective-permute-start.1 = (bf16[4,88,256]{2,1,0:T(8,128)(2,1)S(1)}, bf16[4,88,256]{2,1,0:T(8,128)(2,1)S(1)}, u32[]{:S(2)}, u32[]{:S(2)}) collective-permute-start(bf16[4,88,256]{2,1,0:T(8,128)(2,1)S(1)} %get-tuple-element.35), channel_id=1, source_target_pairs={{0,8},{1,9},{2,10},{3,11},{4,12},{5,13},{6,14},{7,15},{8,0},{9,1},... | collective-permute-start | bytes 540680 | tf_op jit(solution)/shard_map/ppermute | solution.py:426
  60.7 13.0 %collective-permute-start.2 = (bf16[4,88,256]{2,1,0:T(8,128)(2,1)S(1)}, bf16[4,88,256]{2,1,0:T(8,128)(2,1)S(1)}, u32[]{:S(2)}, u32[]{:S(2)}) collective-permute-start(bf16[4,88,256]{2,1,0:T(8,128)(2,1)S(1)} %get-tuple-element.36), channel_id=1, source_target_pairs={{0,12},{1,13},{2,14},{3,15},{4,8},{5,9},{6,10},{7,11},{8,4},{9,5},... | collective-permute-start | bytes 540680 | tf_op jit(solution)/shard_map/ppermute | solution.py:426
  73.8 17.3 %collective-permute-start.3 = (bf16[4,88,256]{2,1,0:T(8,128)(2,1)S(1)}, bf16[4,88,256]{2,1,0:T(8,128)(2,1)S(1)}, u32[]{:S(2)}, u32[]{:S(2)}) collective-permute-start(bf16[4,88,256]{2,1,0:T(8,128)(2,1)S(1)} %get-tuple-element.38), channel_id=1, source_target_pairs={{0,1},{1,0},{2,3},{3,2},{4,5},{5,4},{6,7},{7,6},{8,9},{9,8},{10,11... | collective-permute-start | bytes 540680 | tf_op jit(solution)/shard_map/ppermute | solution.py:426
  77.2 13.9 %collective-permute-start.4 = (bf16[4,88,256]{2,1,0:T(8,128)(2,1)S(1)}, bf16[4,88,256]{2,1,0:T(8,128)(2,1)S(1)}, u32[]{:S(2)}, u32[]{:S(2)}) collective-permute-start(bf16[4,88,256]{2,1,0:T(8,128)(2,1)S(1)} %get-tuple-element.39), channel_id=1, source_target_pairs={{0,16},{1,17},{2,18},{3,19},{4,20},{5,21},{6,22},{7,23},{8,24},{9,... | collective-permute-start | bytes 540680 | tf_op jit(solution)/shard_map/ppermute | solution.py:426
  78.6 12.5 %collective-permute-start.5 = (bf16[4,88,256]{2,1,0:T(8,128)(2,1)S(1)}, bf16[4,88,256]{2,1,0:T(8,128)(2,1)S(1)}, u32[]{:S(2)}, u32[]{:S(2)}) collective-permute-start(bf16[4,88,256]{2,1,0:T(8,128)(2,1)S(1)} %get-tuple-element.40), channel_id=1, source_target_pairs={{0,17},{1,16},{2,19},{3,18},{4,21},{5,20},{6,23},{7,22},{8,25},{9,... | collective-permute-start | bytes 540680 | tf_op jit(solution)/shard_map/ppermute | solution.py:426

commit v12 on v11

--- a/solution.py
+++ b/solution.py
@@ -21,6 +21,7 @@
 epsilon = 1e-07
 
 AXES = ("dp", "owner")
+FORWARD_AXES = ("owner", "dp")
 MIB = 1024 * 1024
 PARAMS = pltpu.CompilerParams(vmem_limit_bytes=24 * MIB)
 PACK_PARAMS = pltpu.CompilerParams(vmem_limit_bytes=60 * MIB)
@@ -41,14 +42,18 @@
     return new, (grad + momentum_beta * new).astype(jnp.bfloat16)
 
 
-def store_slot(slot, plan, i, owner, nesterov, slot_ref):
+def store_slot(slot, plan, i, owner, nesterov, slot_ref, col_size):
     other_ref, rank_ref = plan
+    row_size = slot_ref.shape[0] // col_size
+
+    def place(d):
+        return d % col_size * row_size + d // col_size
 
     @pl.when(rank_ref[i] == slot)
     def _():
         block = nesterov()
-        slot_ref[owner] = block
-        slot_ref[other_ref[owner]] = block
+        slot_ref[place(owner)] = block
+        slot_ref[place(other_ref[owner])] = block
 
 
 def make_plan(col_size, owner_ref, other_ref, rank_ref, count_ref, list_ref):
@@ -114,7 +119,7 @@
         for i in range(k * chunk, (k + 1) * chunk):
             store_slot(
                 0, (other_ref, rank_ref), i, owner_ref[i],
-                lambda: nesterov_of(g_s, m_s, i)[1], first_ref,
+                lambda: nesterov_of(g_s, m_s, i)[1], first_ref, col_size,
             )
 
 
@@ -150,31 +155,49 @@
     )(owner_table, gradients, momentum)
 
 
-def momentum_kernel(chunk, owner_ref, other_ref, rank_ref, g_ref, m_ref, nm_ref, second_ref):
+def momentum_kernel(
+    chunk, col_size, owner_ref, other_ref, rank_ref, g_ref, m_ref, nm_ref, second_ref, place_ref
+):
     step = pl.program_id(0)
+    width = col_size // HALVES
+    row, col = lax.axis_index("dp"), lax.axis_index("owner")
     for j in range(chunk):
         i = step * chunk + j
         new, nesterov = nesterov_of(g_ref, m_ref, j)
         nm_ref[j] = new
-        store_slot(1, (other_ref, rank_ref), i, owner_ref[i], lambda: nesterov, second_ref)
-
-
-def update_momentum(gradients, momentum, owner_table, other, rank):
+        owner = owner_ref[i]
+        plan = other_ref, rank_ref
+        store_slot(1, plan, i, owner, lambda: nesterov, second_ref, col_size)
+
+        near = (owner % col_size) // width == col // width
+        host = jnp.where(near, owner, other_ref[owner])
+        host_row, host_col = host // col_size, host % width
+        offset = host_row ^ row
+        high = offset // LOW * width + (host_col ^ (col % width))
+        place_ref[i] = jnp.where(
+            rank_ref[i] == 0,
+            high * LOW + offset % LOW,
+            second_ref.shape[0] // HALVES + host_row * width + host_col,
+        )
+
+
+def update_momentum(gradients, momentum, owner_table, other, rank, col_size):
     mats, rows, cols = gradients.shape
     devices = other.shape[0]
     chunk = 8
     block = pl.BlockSpec((chunk, rows, cols), lambda i, *_: (i, 0, 0))
     return pl.pallas_call(
-        functools.partial(momentum_kernel, chunk),
+        functools.partial(momentum_kernel, chunk, col_size),
         grid_spec=pltpu.PrefetchScalarGridSpec(
             num_scalar_prefetch=3,
             grid=(mats // chunk,),
             in_specs=[block, block],
-            out_specs=[block, whole((devices, rows, cols))],
+            out_specs=[block, whole((devices, rows, cols)), SMEM],
         ),
         out_shape=[
             jax.ShapeDtypeStruct(momentum.shape, jnp.float32),
             jax.ShapeDtypeStruct((devices, rows, cols), jnp.bfloat16),
+            jax.ShapeDtypeStruct((mats,), jnp.int32),
         ],
         compiler_params=PARAMS,
         cost_estimate=pl.CostEstimate(
@@ -203,7 +226,7 @@
     total = 0.0
     for r in range(row_size):
         for c in range(col_size):
-            block = x_ref[r * col_size + c]
+            block = x_ref[c * row_size + r]
             x_s[r * rows : (r + 1) * rows, c * cols : (c + 1) * cols] = block
             wide = block.astype(jnp.float32)
             total = total + sum_rows(wide * wide)
@@ -356,53 +379,38 @@
     )(*blocks)
 
 
-def unpack_kernel(chunk, col_size, owner_ref, other_ref, rank_ref, *refs):
-    width = col_size // HALVES
-    high_refs, second_ref, update_ref, first_s, update_s, sems = refs[:-5], *refs[-5:]
-    row, col = lax.axis_index("dp"), lax.axis_index("owner")
-    half = col // width
+def unpack_kernel(chunk, place_ref, *refs):
+    high_refs, second_ref, update_ref, back_s, update_s, sems = refs[:-5], *refs[-5:]
     for h, high_ref in enumerate(high_refs):
-        first_s[h * LOW : (h + 1) * LOW] = high_ref[...]
+        back_s[h * LOW : (h + 1) * LOW] = high_ref[...]
+    back_s[second_ref.shape[0] :] = second_ref[...]
 
     def copy_out(k):
         span = pl.ds(k * chunk, chunk)
         return pltpu.make_async_copy(update_s.at[span], update_ref.at[span], sems.at[k])
 
     chunks = update_s.shape[0] // chunk
-    for i in range(chunks * chunk):
-        owner = owner_ref[i]
-        host = jnp.where((owner % col_size) // width == half, owner, other_ref[owner])
-        host_row, host_col = host // col_size, host % width
-        offset = host_row ^ row
-        high = offset // LOW * width + (host_col ^ (col % width))
-
-        @pl.when(rank_ref[i] == 0)
-        def _():
-            update_s[i] = first_s[high * LOW + offset % LOW]
-
-        @pl.when(rank_ref[i] == 1)
-        def _():
-            update_s[i] = second_ref[host_row * width + host_col]
-
-        if i % chunk == chunk - 1:
-            copy_out(i // chunk).start()
+    for k in range(chunks):
+        for i in range(k * chunk, (k + 1) * chunk):
+            update_s[i] = back_s[place_ref[i]]
+        copy_out(k).start()
     for k in range(chunks):
         copy_out(k).wait()
 
 
-def unpack(owner_table, other, rank, first, second, col_size):
-    _, rows, cols = second.shape
-    mats = owner_table.shape[0]
+def unpack(place, first, second):
+    places, rows, cols = second.shape
+    mats = place.shape[0]
     chunk = 8
     return pl.pallas_call(
-        functools.partial(unpack_kernel, chunk, col_size),
+        functools.partial(unpack_kernel, chunk),
         grid_spec=pltpu.PrefetchScalarGridSpec(
-            num_scalar_prefetch=3,
+            num_scalar_prefetch=1,
             grid=(1,),
             in_specs=[whole(first[0].shape)] * len(first) + [whole(second.shape)],
             out_specs=pl.BlockSpec(memory_space=pl.ANY),
             scratch_shapes=[
-                pltpu.VMEM(second.shape, jnp.bfloat16),
+                pltpu.VMEM((CAP * places, rows, cols), jnp.bfloat16),
                 pltpu.VMEM((mats, rows, cols), jnp.bfloat16),
                 pltpu.SemaphoreType.DMA((mats // chunk,)),
             ],
@@ -413,12 +421,12 @@
             flops=0, bytes_accessed=4 * mats * rows * cols, transcendentals=0
         ),
         name="unpack",
-    )(owner_table, other, rank, *first, second)
-
-
-def exchange(blocks, groups=None):
+    )(place, *first, second)
+
+
+def exchange(blocks, axes, groups=None):
     return lax.all_to_all(
-        blocks, AXES, split_axis=0, concat_axis=0, tiled=True, axis_index_groups=groups
+        blocks, axes, split_axis=0, concat_axis=0, tiled=True, axis_index_groups=groups
     )
 
 
@@ -436,10 +444,12 @@
         for half in range(HALVES)
     ]
     first, other, rank = pack(gradients, momentum, owner_table, devices, col_size)
-    arrived_first = exchange(first)
-    new_momentum, second = update_momentum(gradients, momentum, owner_table, other, rank)
+    arrived_first = exchange(first, FORWARD_AXES)
+    new_momentum, second, place = update_momentum(
+        gradients, momentum, owner_table, other, rank, col_size
+    )
     arrived_first, second = lax.optimization_barrier((arrived_first, second))
-    arrived_second = exchange(second)
+    arrived_second = exchange(second, FORWARD_AXES)
     owned, back_first = orthogonalize(0, other, arrived_first, row_size, col_size)
     low = [back_first[0]] + [
         swap(back_first[k], k * col_size, devices) for k in range(1, LOW)
@@ -454,8 +464,8 @@
     ]
     owned, back_second = orthogonalize(1, other, arrived_second, row_size, col_size, owned)
     returned_first, back_second = lax.optimization_barrier((returned_first, back_second))
-    returned_second = exchange(back_second[0], halves)
-    update = unpack(owner_table, other, rank, returned_first, returned_second, col_size)
+    returned_second = exchange(back_second[0], AXES, halves)
+    update = unpack(place, returned_first, returned_second)
     return (new_momentum, update, owned)
 
 

time: 111 us -> 111 us (level)
  waiting for transfers between devices: 45.3 us -> 49.2 us
  blocking collectives: 16.6 us -> 14.9 us
  starting transfers between devices: 18.9 us -> 17.3 us
    all_to_all x2, waiting for transfers between devices: 32.3 us -> 35.6 us  [exchange(): lax.all_to_all(blocks, axes, split_axis=0, concat_axis=0, tiled=True, axi...]
    all_to_all x1, blocking collectives: 16.6 us -> 14.9 us  [exchange(): lax.all_to_all(blocks, axes, split_axis=0, concat_axis=0, tiled=True, axi...]
where the time goes in v12:
time: 111 us
  waiting for transfers between devices  49.2 us (44%)
  Pallas kernels  26 us (23%)
  starting transfers between devices  17.3 us (16%)
  blocking collectives  14.9 us (13%)
  local copies, waits for them, and re-layouts  2.5 us (2%)
    all_to_all x2, waiting for transfers between devices, exchange(): lax.all_to_all(blocks, axes, split_axis=0, concat_axis=0, tiled=True, axi...  35.6 us
    pallas_call x2, Pallas kernels, orthogonalize(): pl.pallas_call(functools.partial(ortho_kernel, row_size, col_size, slot),...  16.7 us
    all_to_all x1, blocking collectives, exchange(): lax.all_to_all(blocks, axes, split_axis=0, concat_axis=0, tiled=True, axi...  14.9 us
    ppermute x6, waiting for transfers between devices, swap(): return lax.ppermute(block, AXES, [(d, d ^ offset) for d in range(devices)])  13.6 us
    all_to_all x2, starting transfers between devices, exchange(): lax.all_to_all(blocks, axes, split_axis=0, concat_axis=0, tiled=True, axi...  11 us
    ppermute x6, starting transfers between devices, swap(): return lax.ppermute(block, AXES, [(d, d ^ offset) for d in range(devices)])  6.25 us
    pallas_call x1, Pallas kernels, pack(): pl.pallas_call(functools.partial(pack_kernel, chunk, col_size), grid_spec...  4.04 us
    pallas_call x1, Pallas kernels, update_momentum(): pl.pallas_call(functools.partial(momentum_kernel, chunk, col_size), grid_...  3.4 us
  transfers between devices with their start and end apart: 8, of which 4 were waited for; matrix products, arithmetic and copies ran while one was open for 0% of the time, Pallas kernels for 18%

profile of v12, /device:TPU:0, one launch (start us, length us, event | category | flops | bytes accessed | tf_op | source)
XLA Modules:
  0.0 110.7 jit_solution(16482186319616469288)
XLA Ops:
  0.6 4.0 %pack.1 = (bf16[32,88,256]{2,1,0:T(8,128)(2,1)}, s32[32]{0:T(128)}, s32[32]{0:T(128)}) custom-call(s32[32]{0:T(128)} %owner_ref.3, bf16[32,88,256]{2,1,0:T(8,128)(2,1)} %g_ref.3, f32[32,88,256]{2,1,0:T(8,128)} %m_ref.3), custom_call_target="tpu_custom_call" | custom-call | flops 2883584 | bytes 5767168 | tf_op jit(solution)/shard_map/pack/pallas_call | solution.py:130
  4.7 0.0 copy-start
  4.7 0.0 copy-start.3
  4.7 0.0 copy-start.4
  4.7 0.0 copy-start.5
  4.7 7.4 %all-to-all-start = ((bf16[32,88,256]{2,1,0:T(8,128)(2,1)}), bf16[32,88,256]{2,1,0:T(8,128)(2,1)}, u32[]{:S(2)}, u32[]{:S(2)}) async-start(bf16[32,88,256]{2,1,0:T(8,128)(2,1)} %get-tuple-element.32), calls=%async_computation | async-start | bytes 2883584 | tf_op jit(solution)/shard_map/all_to_all | solution.py:428
  12.2 0.0 copy-done
  12.2 0.0 copy-done.3
  12.2 0.0 copy-done.4
  12.2 0.0 copy-done.5
  12.2 0.0 copy-start.1
  12.2 1.4 %copy-done.1 = bf16[32,88,256]{2,1,0:T(8,128)(2,1)S(1)} copy-done((bf16[32,88,256]{2,1,0:T(8,128)(2,1)S(1)}, bf16[32,88,256]{2,1,0:T(8,128)(2,1)}, u32[]{:S(2)}) %copy-start.1) | copy-done | bytes 1441816
  13.6 3.4 %update_momentum.1 = (f32[32,88,256]{2,1,0:T(8,128)}, bf16[32,88,256]{2,1,0:T(8,128)(2,1)S(1)}, s32[32]{0:T(128)S(1)}) custom-call(s32[32]{0:T(128)S(1)} %copy-done.3, s32[32]{0:T(128)S(1)} %copy-done.4, s32[32]{0:T(128)S(1)} %copy-done.5, bf16[32,88,256]{2,1,0:T(8,128)(2,1)S(1)} %copy-done.1, f32[32,88,256]{2,1,0:T(8,128)S(1)} %copy-done), custom_call_target="tpu_custom_call" | custom-call | flops 2883584 | bytes 8650752 | tf_op jit(solution)/shard_map/update_momentum/pallas_call | solution.py:189
  17.0 0.0 copy-start.2
  17.0 1.1 %copy-done.2 = bf16[32,88,256]{2,1,0:T(8,128)(2,1)} copy-done((bf16[32,88,256]{2,1,0:T(8,128)(2,1)}, bf16[32,88,256]{2,1,0:T(8,128)(2,1)S(1)}, u32[]{:S(2)}) %copy-start.2) | copy-done | bytes 1441816
  18.1 29.1 %all-to-all-done.x_ref = bf16[32,88,256]{2,1,0:T(8,128)(2,1)} async-done(((bf16[32,88,256]{2,1,0:T(8,128)(2,1)}), bf16[32,88,256]{2,1,0:T(8,128)(2,1)}, u32[]{:S(2)}, u32[]{:S(2)}) %all-to-all-start) | async-done | bytes 1441824 | tf_op jit(solution)/shard_map/all_to_all | solution.py:428
  47.2 3.6 %all-to-all-start.1 = ((bf16[32,88,256]{2,1,0:T(8,128)(2,1)}), bf16[32,88,256]{2,1,0:T(8,128)(2,1)S(1)}, u32[]{:S(2)}, u32[]{:S(2)}) async-start(bf16[32,88,256]{2,1,0:T(8,128)(2,1)} %copy-done.2), calls=%async_computation.1 | async-start | bytes 2883584 | tf_op jit(solution)/shard_map/all_to_all | solution.py:428
  50.8 8.8 %orthogonalize.2 = (bf16[2,704,1024]{2,1,0:T(8,128)(2,1)}, bf16[4,88,256]{2,1,0:T(8,128)(2,1)S(1)}, bf16[4,88,256]{2,1,0:T(8,128)(2,1)S(1)}, bf16[4,88,256]{2,1,0:T(8,128)(2,1)S(1)}, bf16[4,88,256]{2,1,0:T(8,128)(2,1)S(1)}) custom-call(s32[32]{0:T(128)S(1)} %copy-done.4, bf16[32,88,256]{2,1,0:T(8,128)(2,1)} %all-to-all-done.x_ref), custom_call_target="tpu_custom_call" | custom-call | flops 6643777536 | bytes 4718592 | tf_op jit(solution)/shard_map/orthogonalize/pallas_call | solution.py:338
  59.6 0.3 collective-permute-start
  59.9 1.7 %collective-permute-start.1 = (bf16[4,88,256]{2,1,0:T(8,128)(2,1)S(1)}, bf16[4,88,256]{2,1,0:T(8,128)(2,1)S(1)}, u32[]{:S(2)}, u32[]{:S(2)}) collective-permute-start(bf16[4,88,256]{2,1,0:T(8,128)(2,1)S(1)} %get-tuple-element.37), channel_id=1, source_target_pairs={{0,8},{1,9},{2,10},{3,11},{4,12},{5,13},{6,14},{7,15},{8,0},{9,1},... | collective-permute-start | bytes 540680 | tf_op jit(solution)/shard_map/ppermute | solution.py:434
  61.6 0.0 collective-permute-start.2
  61.6 0.0 collective-permute-done.refs_1_
  61.6 9.0 %collective-permute-done.1.refs_2_ = bf16[4,88,256]{2,1,0:T(8,128)(2,1)S(1)} collective-permute-done((bf16[4,88,256]{2,1,0:T(8,128)(2,1)S(1)}, bf16[4,88,256]{2,1,0:T(8,128)(2,1)S(1)}, u32[]{:S(2)}, u32[]{:S(2)}) %collective-permute-start.1) | collective-permute-done | bytes 180256 | tf_op jit(solution)/shard_map/ppermute | solution.py:434
  70.6 4.6 %collective-permute-done.2.refs_3_ = bf16[4,88,256]{2,1,0:T(8,128)(2,1)S(1)} collective-permute-done((bf16[4,88,256]{2,1,0:T(8,128)(2,1)S(1)}, bf16[4,88,256]{2,1,0:T(8,128)(2,1)S(1)}, u32[]{:S(2)}, u32[]{:S(2)}) %collective-permute-start.2) | collective-permute-done | bytes 180256 | tf_op jit(solution)/shard_map/ppermute | solution.py:434
  75.2 2.7 %collective-permute-start.3 = (bf16[4,88,256]{2,1,0:T(8,128)(2,1)S(1)}, bf16[4,88,256]{2,1,0:T(8,128)(2,1)S(1)}, u32[]{:S(2)}, u32[]{:S(2)}) collective-permute-start(bf16[4,88,256]{2,1,0:T(8,128)(2,1)S(1)} %get-tuple-element.40), channel_id=1, source_target_pairs={{0,1},{1,0},{2,3},{3,2},{4,5},{5,4},{6,7},{7,6},{8,9},{9,8},{10,11... | collective-permute-start | bytes 540680 | tf_op jit(solution)/shard_map/ppermute | solution.py:434
  77.9 0.7 collective-permute-start.4
  78.7 0.8 collective-permute-start.5
  79.5 6.5 %all-to-all-done.1.x_ref = bf16[32,88,256]{2,1,0:T(8,128)(2,1)S(1)} async-done(((bf16[32,88,256]{2,1,0:T(8,128)(2,1)}), bf16[32,88,256]{2,1,0:T(8,128)(2,1)S(1)}, u32[]{:S(2)}, u32[]{:S(2)}) %all-to-all-start.1) | async-done | bytes 1441824 | tf_op jit(solution)/shard_map/all_to_all | solution.py:428
  86.0 7.9 %orthogonalize.3 = (bf16[2,704,1024]{2,1,0:T(8,128)(2,1)}, bf16[16,88,256]{2,1,0:T(8,128)(2,1)S(1)}) custom-call(s32[32]{0:T(128)S(1)} %copy-done.4, bf16[32,88,256]{2,1,0:T(8,128)(2,1)S(1)} %all-to-all-done.1.x_ref, bf16[2,704,1024]{2,1,0:T(8,128)(2,1)} %get-tuple-element.45.refs_0_), custom_call_target="tpu_custom_call", output_to_operand_aliasing={{0}: (2, {})} | custom-call | flops 6643777536 | bytes 4718592 | tf_op jit(solution)/shard_map/orthogonalize/pallas_call | solution.py:338
  94.0 0.0 collective-permute-done.3.refs_1_
  94.0 0.0 collective-permute-done.4.refs_2_
  94.0 0.0 collective-permute-done.5.refs_3_
  94.0 14.9 %all_to_all.15.refs_4_ = bf16[16,88,256]{2,1,0:T(8,128)(2,1)S(1)} all-to-all(bf16[16,88,256]{2,1,0:T(8,128)(2,1)S(1)} %get-tuple-element.51), channel_id=1, replica_groups={{0,1,4,5,8,9,12,13,16,17,20,21,24,25,28,29},{2,3,6,7,10,11,14,15,18,19,..., dimensions={0} | all-to-all | bytes 1441792 | tf_op jit(solution)/shard_map/all_to_all | solution.py:428
  108.9 1.8 %unpack.1 = bf16[32,88,256]{2,1,0:T(8,128)(2,1)} custom-call(s32[32]{0:T(128)S(1)} %get-tuple-element.31.place_ref, bf16[4,88,256]{2,1,0:T(8,128)(2,1)S(1)} %get-tuple-element.47.refs_0_, bf16[4,88,256]{2,1,0:T(8,128)(2,1)S(1)} %collective-permute-done.3.refs_1_, bf16[4,88,256]{2,1,0:T(8,128)(2,1)S(1)} %collective-permute-done.4.refs_2_, ...), custom_call_target="tpu_custom_call" | custom-call | bytes 2883584 | tf_op jit(solution)/shard_map/unpack/pallas_call | solution.py:405
  (1 shorter events, 0.0 us)
Async XLA Ops:
  4.7 7.5 %copy-start = (f32[32,88,256]{2,1,0:T(8,128)S(1)}, f32[32,88,256]{2,1,0:T(8,128)}, u32[]{:S(2)}) copy-start(f32[32,88,256]{2,1,0:T(8,128)} %m_ref.3) | copy-start | bytes 8650756
  4.7 7.5 %copy-start.3 = (s32[32]{0:T(128)S(1)}, s32[32]{0:T(128)}, u32[]{:S(2)}) copy-start(s32[32]{0:T(128)} %owner_ref.3) | copy-start | bytes 388
  4.7 7.5 %copy-start.4 = (s32[32]{0:T(128)S(1)}, s32[32]{0:T(128)}, u32[]{:S(2)}) copy-start(s32[32]{0:T(128)} %get-tuple-element.28.other_ref) | copy-start | bytes 388
  4.7 7.5 %copy-start.5 = (s32[32]{0:T(128)S(1)}, s32[32]{0:T(128)}, u32[]{:S(2)}) copy-start(s32[32]{0:T(128)} %get-tuple-element.29.rank_ref) | copy-start | bytes 388
  4.7 42.4 %all-to-all-start = ((bf16[32,88,256]{2,1,0:T(8,128)(2,1)}), bf16[32,88,256]{2,1,0:T(8,128)(2,1)}, u32[]{:S(2)}, u32[]{:S(2)}) async-start(bf16[32,88,256]{2,1,0:T(8,128)(2,1)} %get-tuple-element.32), calls=%async_computation | async-start | bytes 2883584 | tf_op jit(solution)/shard_map/all_to_all | solution.py:428
  12.2 1.4 %copy-start.1 = (bf16[32,88,256]{2,1,0:T(8,128)(2,1)S(1)}, bf16[32,88,256]{2,1,0:T(8,128)(2,1)}, u32[]{:S(2)}) copy-start(bf16[32,88,256]{2,1,0:T(8,128)(2,1)} %g_ref.3) | copy-start | bytes 4325380
  17.0 1.1 %copy-start.2 = (bf16[32,88,256]{2,1,0:T(8,128)(2,1)}, bf16[32,88,256]{2,1,0:T(8,128)(2,1)S(1)}, u32[]{:S(2)}) copy-start(bf16[32,88,256]{2,1,0:T(8,128)(2,1)S(1)} %get-tuple-element.43) | copy-start | bytes 4325380
  47.2 38.8 %all-to-all-start.1 = ((bf16[32,88,256]{2,1,0:T(8,128)(2,1)}), bf16[32,88,256]{2,1,0:T(8,128)(2,1)S(1)}, u32[]{:S(2)}, u32[]{:S(2)}) async-start(bf16[32,88,256]{2,1,0:T(8,128)(2,1)} %copy-done.2), calls=%async_computation.1 | async-start | bytes 2883584 | tf_op jit(solution)/shard_map/all_to_all | solution.py:428
  59.6 2.0 %collective-permute-start = (bf16[4,88,256]{2,1,0:T(8,128)(2,1)S(1)}, bf16[4,88,256]{2,1,0:T(8,128)(2,1)S(1)}, u32[]{:S(2)}, u32[]{:S(2)}) collective-permute-start(bf16[4,88,256]{2,1,0:T(8,128)(2,1)S(1)} %get-tuple-element.36), channel_id=1, source_target_pairs={{0,4},{1,5},{2,6},{3,7},{4,0},{5,1},{6,2},{7,3},{8,12},{9,13},{10,... | collective-permute-start | bytes 540680 | tf_op jit(solution)/shard_map/ppermute | solution.py:434
  59.9 10.7 %collective-permute-start.1 = (bf16[4,88,256]{2,1,0:T(8,128)(2,1)S(1)}, bf16[4,88,256]{2,1,0:T(8,128)(2,1)S(1)}, u32[]{:S(2)}, u32[]{:S(2)}) collective-permute-start(bf16[4,88,256]{2,1,0:T(8,128)(2,1)S(1)} %get-tuple-element.37), channel_id=1, source_target_pairs={{0,8},{1,9},{2,10},{3,11},{4,12},{5,13},{6,14},{7,15},{8,0},{9,1},... | collective-permute-start | bytes 540680 | tf_op jit(solution)/shard_map/ppermute | solution.py:434
  61.6 13.6 %collective-permute-start.2 = (bf16[4,88,256]{2,1,0:T(8,128)(2,1)S(1)}, bf16[4,88,256]{2,1,0:T(8,128)(2,1)S(1)}, u32[]{:S(2)}, u32[]{:S(2)}) collective-permute-start(bf16[4,88,256]{2,1,0:T(8,128)(2,1)S(1)} %get-tuple-element.38), channel_id=1, source_target_pairs={{0,12},{1,13},{2,14},{3,15},{4,8},{5,9},{6,10},{7,11},{8,4},{9,5},... | collective-permute-start | bytes 540680 | tf_op jit(solution)/shard_map/ppermute | solution.py:434
  75.2 18.7 %collective-permute-start.3 = (bf16[4,88,256]{2,1,0:T(8,128)(2,1)S(1)}, bf16[4,88,256]{2,1,0:T(8,128)(2,1)S(1)}, u32[]{:S(2)}, u32[]{:S(2)}) collective-permute-start(bf16[4,88,256]{2,1,0:T(8,128)(2,1)S(1)} %get-tuple-element.40), channel_id=1, source_target_pairs={{0,1},{1,0},{2,3},{3,2},{4,5},{5,4},{6,7},{7,6},{8,9},{9,8},{10,11... | collective-permute-start | bytes 540680 | tf_op jit(solution)/shard_map/ppermute | solution.py:434
  77.9 16.0 %collective-permute-start.4 = (bf16[4,88,256]{2,1,0:T(8,128)(2,1)S(1)}, bf16[4,88,256]{2,1,0:T(8,128)(2,1)S(1)}, u32[]{:S(2)}, u32[]{:S(2)}) collective-permute-start(bf16[4,88,256]{2,1,0:T(8,128)(2,1)S(1)} %get-tuple-element.41), channel_id=1, source_target_pairs={{0,16},{1,17},{2,18},{3,19},{4,20},{5,21},{6,22},{7,23},{8,24},{9,... | collective-permute-start | bytes 540680 | tf_op jit(solution)/shard_map/ppermute | solution.py:434
  78.7 15.3 %collective-permute-start.5 = (bf16[4,88,256]{2,1,0:T(8,128)(2,1)S(1)}, bf16[4,88,256]{2,1,0:T(8,128)(2,1)S(1)}, u32[]{:S(2)}, u32[]{:S(2)}) collective-permute-start(bf16[4,88,256]{2,1,0:T(8,128)(2,1)S(1)} %get-tuple-element.42), channel_id=1, source_target_pairs={{0,17},{1,16},{2,19},{3,18},{4,21},{5,20},{6,23},{7,22},{8,25},{9,... | collective-permute-start | bytes 540680 | tf_op jit(solution)/shard_map/ppermute | solution.py:434

commit v13 on v12

--- a/solution.py
+++ b/solution.py
@@ -21,11 +21,11 @@
 epsilon = 1e-07
 
 AXES = ("dp", "owner")
-FORWARD_AXES = ("owner", "dp")
 MIB = 1024 * 1024
 PARAMS = pltpu.CompilerParams(vmem_limit_bytes=24 * MIB)
 PACK_PARAMS = pltpu.CompilerParams(vmem_limit_bytes=60 * MIB)
 SMEM = pl.BlockSpec(memory_space=pltpu.SMEM)
+VMEM = pl.BlockSpec(memory_space=pltpu.VMEM)
 
 
 def round_up(value, multiple):
@@ -42,18 +42,14 @@
     return new, (grad + momentum_beta * new).astype(jnp.bfloat16)
 
 
-def store_slot(slot, plan, i, owner, nesterov, slot_ref, col_size):
+def store_slot(slot, plan, i, owner, nesterov, slot_ref):
     other_ref, rank_ref = plan
-    row_size = slot_ref.shape[0] // col_size
-
-    def place(d):
-        return d % col_size * row_size + d // col_size
 
     @pl.when(rank_ref[i] == slot)
     def _():
         block = nesterov()
-        slot_ref[place(owner)] = block
-        slot_ref[place(other_ref[owner])] = block
+        slot_ref[owner] = block
+        slot_ref[other_ref[owner]] = block
 
 
 def make_plan(col_size, owner_ref, other_ref, rank_ref, count_ref, list_ref):
@@ -119,7 +115,7 @@
         for i in range(k * chunk, (k + 1) * chunk):
             store_slot(
                 0, (other_ref, rank_ref), i, owner_ref[i],
-                lambda: nesterov_of(g_s, m_s, i)[1], first_ref, col_size,
+                lambda: nesterov_of(g_s, m_s, i)[1], first_ref,
             )
 
 
@@ -167,7 +163,7 @@
         nm_ref[j] = new
         owner = owner_ref[i]
         plan = other_ref, rank_ref
-        store_slot(1, plan, i, owner, lambda: nesterov, second_ref, col_size)
+        store_slot(1, plan, i, owner, lambda: nesterov, second_ref)
 
         near = (owner % col_size) // width == col // width
         host = jnp.where(near, owner, other_ref[owner])
@@ -226,7 +222,7 @@
     total = 0.0
     for r in range(row_size):
         for c in range(col_size):
-            block = x_ref[c * row_size + r]
+            block = x_ref[r * col_size + c]
             x_s[r * rows : (r + 1) * rows, c * cols : (c + 1) * cols] = block
             wide = block.astype(jnp.float32)
             total = total + sum_rows(wide * wide)
@@ -320,7 +316,7 @@
     padded = round_up(height, 256)
     places = devices // HALVES
     anywhere = pl.BlockSpec(memory_space=pl.ANY)
-    in_specs, operands = [SMEM, whole(arrived.shape)], [other, arrived]
+    in_specs, operands = [SMEM, VMEM], [other, arrived]
     scratch_shapes = [
         pltpu.VMEM((padded, width), jnp.bfloat16),
         pltpu.VMEM((padded, width), jnp.bfloat16),
@@ -337,9 +333,8 @@
         scratch_shapes.append(pltpu.VMEM((places, rows, cols), jnp.bfloat16))
     owned, *back = pl.pallas_call(
         functools.partial(ortho_kernel, row_size, col_size, slot),
-        grid=(1,),
         in_specs=in_specs,
-        out_specs=[anywhere] + [whole(shape) for shape in back],
+        out_specs=[anywhere] + [VMEM] * len(back),
         out_shape=[jax.ShapeDtypeStruct((CAP, height, width), jnp.bfloat16)]
         + [jax.ShapeDtypeStruct(shape, jnp.bfloat16) for shape in back],
         scratch_shapes=scratch_shapes,
@@ -444,12 +439,12 @@
         for half in range(HALVES)
     ]
     first, other, rank = pack(gradients, momentum, owner_table, devices, col_size)
-    arrived_first = exchange(first, FORWARD_AXES)
+    arrived_first = exchange(first, AXES)
     new_momentum, second, place = update_momentum(
         gradients, momentum, owner_table, other, rank, col_size
     )
     arrived_first, second = lax.optimization_barrier((arrived_first, second))
-    arrived_second = exchange(second, FORWARD_AXES)
+    arrived_second = exchange(second, AXES)
     owned, back_first = orthogonalize(0, other, arrived_first, row_size, col_size)
     low = [back_first[0]] + [
         swap(back_first[k], k * col_size, devices) for k in range(1, LOW)

time: 111 us -> 110 us (level)
  waiting for transfers between devices: 49.2 us -> 44.9 us
  blocking collectives: 14.9 us -> 16.6 us
  starting transfers between devices: 17.3 us -> 18.9 us
    all_to_all x2, waiting for transfers between devices: 35.6 us -> 31.9 us  [exchange(): lax.all_to_all(blocks, axes, split_axis=0, concat_axis=0, tiled=True, axi...]
    all_to_all x1, blocking collectives: 14.9 us -> 16.6 us  [exchange(): lax.all_to_all(blocks, axes, split_axis=0, concat_axis=0, tiled=True, axi...]
where the time goes in v13:
time: 110 us
  waiting for transfers between devices  44.9 us (41%)
  Pallas kernels  25.8 us (23%)
  starting transfers between devices  18.9 us (17%)
  blocking collectives  16.6 us (15%)
  local copies, waits for them, and re-layouts  2.5 us (2%)
    all_to_all x2, waiting for transfers between devices, exchange(): lax.all_to_all(blocks, axes, split_axis=0, concat_axis=0, tiled=True, axi...  31.9 us
    pallas_call x2, Pallas kernels, orthogonalize(): pl.pallas_call(functools.partial(ortho_kernel, row_size, col_size, slot),...  16.7 us
    all_to_all x1, blocking collectives, exchange(): lax.all_to_all(blocks, axes, split_axis=0, concat_axis=0, tiled=True, axi...  16.6 us
    ppermute x6, waiting for transfers between devices, swap(): return lax.ppermute(block, AXES, [(d, d ^ offset) for d in range(devices)])  13 us
    all_to_all x2, starting transfers between devices, exchange(): lax.all_to_all(blocks, axes, split_axis=0, concat_axis=0, tiled=True, axi...  12 us
    ppermute x6, starting transfers between devices, swap(): return lax.ppermute(block, AXES, [(d, d ^ offset) for d in range(devices)])  6.95 us
    pallas_call x1, Pallas kernels, pack(): pl.pallas_call(functools.partial(pack_kernel, chunk, col_size), grid_spec...  4.04 us
    pallas_call x1, Pallas kernels, update_momentum(): pl.pallas_call(functools.partial(momentum_kernel, chunk, col_size), grid_...  3.22 us
  transfers between devices with their start and end apart: 8, of which 4 were waited for; matrix products, arithmetic and copies ran while one was open for 0% of the time, Pallas kernels for 18%

profile of v13, /device:TPU:0, one launch (start us, length us, event | category | flops | bytes accessed | tf_op | source)
XLA Modules:
  0.0 109.5 jit_solution(7807666522506652949)
XLA Ops:
  0.6 4.0 %pack.1 = (bf16[32,88,256]{2,1,0:T(8,128)(2,1)}, s32[32]{0:T(128)}, s32[32]{0:T(128)}) custom-call(s32[32]{0:T(128)} %owner_ref.3, bf16[32,88,256]{2,1,0:T(8,128)(2,1)} %g_ref.3, f32[32,88,256]{2,1,0:T(8,128)} %m_ref.3), custom_call_target="tpu_custom_call" | custom-call | flops 2883584 | bytes 5767168 | tf_op jit(solution)/shard_map/pack/pallas_call | solution.py:126
  4.7 0.0 copy-start
  4.7 0.0 copy-start.3
  4.7 0.0 copy-start.4
  4.7 0.0 copy-start.5
  4.7 7.4 %all-to-all-start = ((bf16[32,88,256]{2,1,0:T(8,128)(2,1)}), bf16[32,88,256]{2,1,0:T(8,128)(2,1)}, u32[]{:S(2)}, u32[]{:S(2)}) async-start(bf16[32,88,256]{2,1,0:T(8,128)(2,1)} %get-tuple-element.32), calls=%async_computation | async-start | bytes 2883584 | tf_op jit(solution)/shard_map/all_to_all | solution.py:423
  12.2 0.0 copy-done
  12.2 0.0 copy-done.3
  12.2 0.0 copy-done.4
  12.2 0.0 copy-done.5
  12.2 0.0 copy-start.1
  12.2 1.4 %copy-done.1 = bf16[32,88,256]{2,1,0:T(8,128)(2,1)S(1)} copy-done((bf16[32,88,256]{2,1,0:T(8,128)(2,1)S(1)}, bf16[32,88,256]{2,1,0:T(8,128)(2,1)}, u32[]{:S(2)}) %copy-start.1) | copy-done | bytes 1441816
  13.6 3.2 %update_momentum.1 = (f32[32,88,256]{2,1,0:T(8,128)}, bf16[32,88,256]{2,1,0:T(8,128)(2,1)S(1)}, s32[32]{0:T(128)S(1)}) custom-call(s32[32]{0:T(128)S(1)} %copy-done.3, s32[32]{0:T(128)S(1)} %copy-done.4, s32[32]{0:T(128)S(1)} %copy-done.5, bf16[32,88,256]{2,1,0:T(8,128)(2,1)S(1)} %copy-done.1, f32[32,88,256]{2,1,0:T(8,128)S(1)} %copy-done), custom_call_target="tpu_custom_call" | custom-call | flops 2883584 | bytes 8650752 | tf_op jit(solution)/shard_map/update_momentum/pallas_call | solution.py:185
  16.8 0.0 copy-start.2
  16.8 1.1 %copy-done.2 = bf16[32,88,256]{2,1,0:T(8,128)(2,1)} copy-done((bf16[32,88,256]{2,1,0:T(8,128)(2,1)}, bf16[32,88,256]{2,1,0:T(8,128)(2,1)S(1)}, u32[]{:S(2)}) %copy-start.2) | copy-done | bytes 1441816
  17.9 27.5 %all-to-all-done.x_ref = bf16[32,88,256]{2,1,0:T(8,128)(2,1)} async-done(((bf16[32,88,256]{2,1,0:T(8,128)(2,1)}), bf16[32,88,256]{2,1,0:T(8,128)(2,1)}, u32[]{:S(2)}, u32[]{:S(2)}) %all-to-all-start) | async-done | bytes 1441824 | tf_op jit(solution)/shard_map/all_to_all | solution.py:423
  45.4 4.6 %all-to-all-start.1 = ((bf16[32,88,256]{2,1,0:T(8,128)(2,1)}), bf16[32,88,256]{2,1,0:T(8,128)(2,1)S(1)}, u32[]{:S(2)}, u32[]{:S(2)}) async-start(bf16[32,88,256]{2,1,0:T(8,128)(2,1)} %copy-done.2), calls=%async_computation.1 | async-start | bytes 2883584 | tf_op jit(solution)/shard_map/all_to_all | solution.py:423
  49.9 8.8 %orthogonalize.2 = (bf16[2,704,1024]{2,1,0:T(8,128)(2,1)}, bf16[4,88,256]{2,1,0:T(8,128)(2,1)S(1)}, bf16[4,88,256]{2,1,0:T(8,128)(2,1)S(1)}, bf16[4,88,256]{2,1,0:T(8,128)(2,1)S(1)}, bf16[4,88,256]{2,1,0:T(8,128)(2,1)S(1)}) custom-call(s32[32]{0:T(128)S(1)} %copy-done.4, bf16[32,88,256]{2,1,0:T(8,128)(2,1)} %all-to-all-done.x_ref), custom_call_target="tpu_custom_call" | custom-call | flops 6643777536 | bytes 4718592 | tf_op jit(solution)/shard_map/orthogonalize/pallas_call | solution.py:334
  58.7 0.3 collective-permute-start
  59.0 1.7 %collective-permute-start.1 = (bf16[4,88,256]{2,1,0:T(8,128)(2,1)S(1)}, bf16[4,88,256]{2,1,0:T(8,128)(2,1)S(1)}, u32[]{:S(2)}, u32[]{:S(2)}) collective-permute-start(bf16[4,88,256]{2,1,0:T(8,128)(2,1)S(1)} %get-tuple-element.37), channel_id=1, source_target_pairs={{0,8},{1,9},{2,10},{3,11},{4,12},{5,13},{6,14},{7,15},{8,0},{9,1},... | collective-permute-start | bytes 540680 | tf_op jit(solution)/shard_map/ppermute | solution.py:429
  60.7 0.0 collective-permute-start.2
  60.7 0.0 collective-permute-done.refs_1_
  60.7 8.8 %collective-permute-done.1.refs_2_ = bf16[4,88,256]{2,1,0:T(8,128)(2,1)S(1)} collective-permute-done((bf16[4,88,256]{2,1,0:T(8,128)(2,1)S(1)}, bf16[4,88,256]{2,1,0:T(8,128)(2,1)S(1)}, u32[]{:S(2)}, u32[]{:S(2)}) %collective-permute-start.1) | collective-permute-done | bytes 180256 | tf_op jit(solution)/shard_map/ppermute | solution.py:429
  69.5 4.2 %collective-permute-done.2.refs_3_ = bf16[4,88,256]{2,1,0:T(8,128)(2,1)S(1)} collective-permute-done((bf16[4,88,256]{2,1,0:T(8,128)(2,1)S(1)}, bf16[4,88,256]{2,1,0:T(8,128)(2,1)S(1)}, u32[]{:S(2)}, u32[]{:S(2)}) %collective-permute-start.2) | collective-permute-done | bytes 180256 | tf_op jit(solution)/shard_map/ppermute | solution.py:429
  73.8 3.4 %collective-permute-start.3 = (bf16[4,88,256]{2,1,0:T(8,128)(2,1)S(1)}, bf16[4,88,256]{2,1,0:T(8,128)(2,1)S(1)}, u32[]{:S(2)}, u32[]{:S(2)}) collective-permute-start(bf16[4,88,256]{2,1,0:T(8,128)(2,1)S(1)} %get-tuple-element.40), channel_id=1, source_target_pairs={{0,1},{1,0},{2,3},{3,2},{4,5},{5,4},{6,7},{7,6},{8,9},{9,8},{10,11... | collective-permute-start | bytes 540680 | tf_op jit(solution)/shard_map/ppermute | solution.py:429
  77.2 1.5 %collective-permute-start.4 = (bf16[4,88,256]{2,1,0:T(8,128)(2,1)S(1)}, bf16[4,88,256]{2,1,0:T(8,128)(2,1)S(1)}, u32[]{:S(2)}, u32[]{:S(2)}) collective-permute-start(bf16[4,88,256]{2,1,0:T(8,128)(2,1)S(1)} %get-tuple-element.41), channel_id=1, source_target_pairs={{0,16},{1,17},{2,18},{3,19},{4,20},{5,21},{6,22},{7,23},{8,24},{9,... | collective-permute-start | bytes 540680 | tf_op jit(solution)/shard_map/ppermute | solution.py:429
  78.6 0.1 collective-permute-start.5
  78.7 4.4 %all-to-all-done.1.x_ref = bf16[32,88,256]{2,1,0:T(8,128)(2,1)S(1)} async-done(((bf16[32,88,256]{2,1,0:T(8,128)(2,1)}), bf16[32,88,256]{2,1,0:T(8,128)(2,1)S(1)}, u32[]{:S(2)}, u32[]{:S(2)}) %all-to-all-start.1) | async-done | bytes 1441824 | tf_op jit(solution)/shard_map/all_to_all | solution.py:423
  83.2 7.9 %orthogonalize.3 = (bf16[2,704,1024]{2,1,0:T(8,128)(2,1)}, bf16[16,88,256]{2,1,0:T(8,128)(2,1)S(1)}) custom-call(s32[32]{0:T(128)S(1)} %copy-done.4, bf16[32,88,256]{2,1,0:T(8,128)(2,1)S(1)} %all-to-all-done.1.x_ref, bf16[2,704,1024]{2,1,0:T(8,128)(2,1)} %get-tuple-element.45.refs_0_), custom_call_target="tpu_custom_call", output_to_operand_aliasing={{0}: (2, {})} | custom-call | flops 6643777536 | bytes 4718592 | tf_op jit(solution)/shard_map/orthogonalize/pallas_call | solution.py:334
  91.1 0.0 collective-permute-done.3.refs_1_
  91.1 0.0 collective-permute-done.4.refs_2_
  91.1 0.0 collective-permute-done.5.refs_3_
  91.1 16.6 %all_to_all.15.refs_4_ = bf16[16,88,256]{2,1,0:T(8,128)(2,1)S(1)} all-to-all(bf16[16,88,256]{2,1,0:T(8,128)(2,1)S(1)} %get-tuple-element.51), channel_id=1, replica_groups={{0,1,4,5,8,9,12,13,16,17,20,21,24,25,28,29},{2,3,6,7,10,11,14,15,18,19,..., dimensions={0} | all-to-all | bytes 1441792 | tf_op jit(solution)/shard_map/all_to_all | solution.py:423
  107.7 1.8 %unpack.1 = bf16[32,88,256]{2,1,0:T(8,128)(2,1)} custom-call(s32[32]{0:T(128)S(1)} %get-tuple-element.31.place_ref, bf16[4,88,256]{2,1,0:T(8,128)(2,1)S(1)} %get-tuple-element.47.refs_0_, bf16[4,88,256]{2,1,0:T(8,128)(2,1)S(1)} %collective-permute-done.3.refs_1_, bf16[4,88,256]{2,1,0:T(8,128)(2,1)S(1)} %collective-permute-done.4.refs_2_, ...), custom_call_target="tpu_custom_call" | custom-call | bytes 2883584 | tf_op jit(solution)/shard_map/unpack/pallas_call | solution.py:400
  (1 shorter events, 0.0 us)
Async XLA Ops:
  4.7 7.5 %copy-start = (f32[32,88,256]{2,1,0:T(8,128)S(1)}, f32[32,88,256]{2,1,0:T(8,128)}, u32[]{:S(2)}) copy-start(f32[32,88,256]{2,1,0:T(8,128)} %m_ref.3) | copy-start | bytes 8650756
  4.7 7.5 %copy-start.3 = (s32[32]{0:T(128)S(1)}, s32[32]{0:T(128)}, u32[]{:S(2)}) copy-start(s32[32]{0:T(128)} %owner_ref.3) | copy-start | bytes 388
  4.7 7.5 %copy-start.4 = (s32[32]{0:T(128)S(1)}, s32[32]{0:T(128)}, u32[]{:S(2)}) copy-start(s32[32]{0:T(128)} %get-tuple-element.28.other_ref) | copy-start | bytes 388
  4.7 7.5 %copy-start.5 = (s32[32]{0:T(128)S(1)}, s32[32]{0:T(128)}, u32[]{:S(2)}) copy-start(s32[32]{0:T(128)} %get-tuple-element.29.rank_ref) | copy-start | bytes 388
  4.7 40.6 %all-to-all-start = ((bf16[32,88,256]{2,1,0:T(8,128)(2,1)}), bf16[32,88,256]{2,1,0:T(8,128)(2,1)}, u32[]{:S(2)}, u32[]{:S(2)}) async-start(bf16[32,88,256]{2,1,0:T(8,128)(2,1)} %get-tuple-element.32), calls=%async_computation | async-start | bytes 2883584 | tf_op jit(solution)/shard_map/all_to_all | solution.py:423
  12.2 1.4 %copy-start.1 = (bf16[32,88,256]{2,1,0:T(8,128)(2,1)S(1)}, bf16[32,88,256]{2,1,0:T(8,128)(2,1)}, u32[]{:S(2)}) copy-start(bf16[32,88,256]{2,1,0:T(8,128)(2,1)} %g_ref.3) | copy-start | bytes 4325380
  16.8 1.1 %copy-start.2 = (bf16[32,88,256]{2,1,0:T(8,128)(2,1)}, bf16[32,88,256]{2,1,0:T(8,128)(2,1)S(1)}, u32[]{:S(2)}) copy-start(bf16[32,88,256]{2,1,0:T(8,128)(2,1)S(1)} %get-tuple-element.43) | copy-start | bytes 4325380
  45.4 37.8 %all-to-all-start.1 = ((bf16[32,88,256]{2,1,0:T(8,128)(2,1)}), bf16[32,88,256]{2,1,0:T(8,128)(2,1)S(1)}, u32[]{:S(2)}, u32[]{:S(2)}) async-start(bf16[32,88,256]{2,1,0:T(8,128)(2,1)} %copy-done.2), calls=%async_computation.1 | async-start | bytes 2883584 | tf_op jit(solution)/shard_map/all_to_all | solution.py:423
  58.7 2.0 %collective-permute-start = (bf16[4,88,256]{2,1,0:T(8,128)(2,1)S(1)}, bf16[4,88,256]{2,1,0:T(8,128)(2,1)S(1)}, u32[]{:S(2)}, u32[]{:S(2)}) collective-permute-start(bf16[4,88,256]{2,1,0:T(8,128)(2,1)S(1)} %get-tuple-element.36), channel_id=1, source_target_pairs={{0,4},{1,5},{2,6},{3,7},{4,0},{5,1},{6,2},{7,3},{8,12},{9,13},{10,... | collective-permute-start | bytes 540680 | tf_op jit(solution)/shard_map/ppermute | solution.py:429
  59.0 10.5 %collective-permute-start.1 = (bf16[4,88,256]{2,1,0:T(8,128)(2,1)S(1)}, bf16[4,88,256]{2,1,0:T(8,128)(2,1)S(1)}, u32[]{:S(2)}, u32[]{:S(2)}) collective-permute-start(bf16[4,88,256]{2,1,0:T(8,128)(2,1)S(1)} %get-tuple-element.37), channel_id=1, source_target_pairs={{0,8},{1,9},{2,10},{3,11},{4,12},{5,13},{6,14},{7,15},{8,0},{9,1},... | collective-permute-start | bytes 540680 | tf_op jit(solution)/shard_map/ppermute | solution.py:429
  60.7 13.0 %collective-permute-start.2 = (bf16[4,88,256]{2,1,0:T(8,128)(2,1)S(1)}, bf16[4,88,256]{2,1,0:T(8,128)(2,1)S(1)}, u32[]{:S(2)}, u32[]{:S(2)}) collective-permute-start(bf16[4,88,256]{2,1,0:T(8,128)(2,1)S(1)} %get-tuple-element.38), channel_id=1, source_target_pairs={{0,12},{1,13},{2,14},{3,15},{4,8},{5,9},{6,10},{7,11},{8,4},{9,5},... | collective-permute-start | bytes 540680 | tf_op jit(solution)/shard_map/ppermute | solution.py:429
  73.8 17.3 %collective-permute-start.3 = (bf16[4,88,256]{2,1,0:T(8,128)(2,1)S(1)}, bf16[4,88,256]{2,1,0:T(8,128)(2,1)S(1)}, u32[]{:S(2)}, u32[]{:S(2)}) collective-permute-start(bf16[4,88,256]{2,1,0:T(8,128)(2,1)S(1)} %get-tuple-element.40), channel_id=1, source_target_pairs={{0,1},{1,0},{2,3},{3,2},{4,5},{5,4},{6,7},{7,6},{8,9},{9,8},{10,11... | collective-permute-start | bytes 540680 | tf_op jit(solution)/shard_map/ppermute | solution.py:429
  77.2 13.9 %collective-permute-start.4 = (bf16[4,88,256]{2,1,0:T(8,128)(2,1)S(1)}, bf16[4,88,256]{2,1,0:T(8,128)(2,1)S(1)}, u32[]{:S(2)}, u32[]{:S(2)}) collective-permute-start(bf16[4,88,256]{2,1,0:T(8,128)(2,1)S(1)} %get-tuple-element.41), channel_id=1, source_target_pairs={{0,16},{1,17},{2,18},{3,19},{4,20},{5,21},{6,22},{7,23},{8,24},{9,... | collective-permute-start | bytes 540680 | tf_op jit(solution)/shard_map/ppermute | solution.py:429
  78.6 12.5 %collective-permute-start.5 = (bf16[4,88,256]{2,1,0:T(8,128)(2,1)S(1)}, bf16[4,88,256]{2,1,0:T(8,128)(2,1)S(1)}, u32[]{:S(2)}, u32[]{:S(2)}) collective-permute-start(bf16[4,88,256]{2,1,0:T(8,128)(2,1)S(1)} %get-tuple-element.42), channel_id=1, source_target_pairs={{0,17},{1,16},{2,19},{3,18},{4,21},{5,20},{6,23},{7,22},{8,25},{9,... | collective-permute-start | bytes 540680 | tf_op jit(solution)/shard_map/ppermute | solution.py:429

commit v14 on v13

--- a/solution.py
+++ b/solution.py
@@ -11,7 +11,7 @@
 ITERS = 2
 CAP = 2
 HALVES = 2
-TILES = 2
+ROW_TILES = (1, 2)
 LOW = 4
 
 coef_a = 3.4445
@@ -26,6 +26,7 @@
 PACK_PARAMS = pltpu.CompilerParams(vmem_limit_bytes=60 * MIB)
 SMEM = pl.BlockSpec(memory_space=pltpu.SMEM)
 VMEM = pl.BlockSpec(memory_space=pltpu.VMEM)
+ANYWHERE = pl.BlockSpec(memory_space=pl.ANY)
 
 
 def round_up(value, multiple):
@@ -40,16 +41,6 @@
     grad = grad_ref[j].astype(jnp.float32)
     new = momentum_beta * momentum_ref[j] + grad
     return new, (grad + momentum_beta * new).astype(jnp.bfloat16)
-
-
-def store_slot(slot, plan, i, owner, nesterov, slot_ref):
-    other_ref, rank_ref = plan
-
-    @pl.when(rank_ref[i] == slot)
-    def _():
-        block = nesterov()
-        slot_ref[owner] = block
-        slot_ref[other_ref[owner]] = block
 
 
 def make_plan(col_size, owner_ref, other_ref, rank_ref, count_ref, list_ref):
@@ -94,16 +85,23 @@
 
 def pack_kernel(
     chunk, col_size, owner_ref, g_ref, m_ref, first_ref, other_ref, rank_ref,
-    count_ref, list_ref, g_s, m_s, sems,
+    count_ref, list_ref, g_s, m_s, block_s, load_sems, store_sems,
 ):
     mats = rank_ref.shape[0]
 
     def loads(k):
         span = pl.ds(k * chunk, chunk)
         return (
-            pltpu.make_async_copy(g_ref.at[span], g_s.at[span], sems.at[0, k]),
-            pltpu.make_async_copy(m_ref.at[span], m_s.at[span], sems.at[1, k]),
+            pltpu.make_async_copy(g_ref.at[span], g_s.at[span], load_sems.at[0, k]),
+            pltpu.make_async_copy(m_ref.at[span], m_s.at[span], load_sems.at[1, k]),
         )
+
+    def stores(i):
+        owner = owner_ref[i]
+        return [
+            pltpu.make_async_copy(block_s.at[i], first_ref.at[host], store_sems.at[n, i])
+            for n, host in enumerate((owner, other_ref[owner]))
+        ]
 
     for k in range(mats // chunk):
         for load in loads(k):
@@ -113,35 +111,41 @@
         for load in loads(k):
             load.wait()
         for i in range(k * chunk, (k + 1) * chunk):
-            store_slot(
-                0, (other_ref, rank_ref), i, owner_ref[i],
-                lambda: nesterov_of(g_s, m_s, i)[1], first_ref,
-            )
+
+            @pl.when(rank_ref[i] == 0)
+            def _():
+                block_s[i] = nesterov_of(g_s, m_s, i)[1]
+                for store in stores(i):
+                    store.start()
+
+    for i in range(mats):
+
+        @pl.when(rank_ref[i] == 0)
+        def _():
+            for store in stores(i):
+                store.wait()
 
 
 def pack(gradients, momentum, owner_table, devices, col_size):
     mats, rows, cols = gradients.shape
     chunk = 8
-    anywhere = pl.BlockSpec(memory_space=pl.ANY)
     return pl.pallas_call(
         functools.partial(pack_kernel, chunk, col_size),
-        grid_spec=pltpu.PrefetchScalarGridSpec(
-            num_scalar_prefetch=1,
-            grid=(1,),
-            in_specs=[anywhere, anywhere],
-            out_specs=[whole((devices, rows, cols)), SMEM, SMEM],
-            scratch_shapes=[
-                pltpu.SMEM((devices,), jnp.int32),
-                pltpu.SMEM((2 * HALVES * devices,), jnp.int32),
-                pltpu.VMEM(gradients.shape, gradients.dtype),
-                pltpu.VMEM(momentum.shape, momentum.dtype),
-                pltpu.SemaphoreType.DMA((2, mats // chunk)),
-            ],
-        ),
+        in_specs=[SMEM, ANYWHERE, ANYWHERE],
+        out_specs=[ANYWHERE, SMEM, SMEM],
         out_shape=[
             jax.ShapeDtypeStruct((devices, rows, cols), jnp.bfloat16),
             jax.ShapeDtypeStruct((devices,), jnp.int32),
             jax.ShapeDtypeStruct((mats,), jnp.int32),
+        ],
+        scratch_shapes=[
+            pltpu.SMEM((devices,), jnp.int32),
+            pltpu.SMEM((2 * HALVES * devices,), jnp.int32),
+            pltpu.VMEM(gradients.shape, gradients.dtype),
+            pltpu.VMEM(momentum.shape, momentum.dtype),
+            pltpu.VMEM(gradients.shape, jnp.bfloat16),
+            pltpu.SemaphoreType.DMA((2, mats // chunk)),
+            pltpu.SemaphoreType.DMA((2, mats)),
         ],
         compiler_params=PACK_PARAMS,
         cost_estimate=pl.CostEstimate(
@@ -162,8 +166,11 @@
         new, nesterov = nesterov_of(g_ref, m_ref, j)
         nm_ref[j] = new
         owner = owner_ref[i]
-        plan = other_ref, rank_ref
-        store_slot(1, plan, i, owner, lambda: nesterov, second_ref)
+
+        @pl.when(rank_ref[i] == 1)
+        def _():
+            second_ref[owner] = nesterov
+            second_ref[other_ref[owner]] = nesterov
 
         near = (owner % col_size) // width == col // width
         host = jnp.where(near, owner, other_ref[owner])
@@ -173,7 +180,7 @@
         place_ref[i] = jnp.where(
             rank_ref[i] == 0,
             high * LOW + offset % LOW,
-            second_ref.shape[0] // HALVES + host_row * width + host_col,
+            host_row * width + host_col,
         )
 
 
@@ -230,21 +237,21 @@
     return 1.0 / (jnp.sqrt(jnp.sum(total, keepdims=True)) + epsilon)
 
 
-def newton_schulz(height, inverse, x_s, y_s, gram_s, write):
+def newton_schulz(height, tiles, inverse, x_s, y_s, gram_s, write):
     padded, width = x_s.shape
-    tile = height // TILES
+    tile = height // tiles
     update_scale = 0.2 * math.sqrt(max(height, width))
     for ref in (y_s, gram_s):
         ref[height:, :] = jnp.zeros((padded - height, ref.shape[1]), ref.dtype)
     for iteration in range(ITERS):
         src = x_s if iteration == 0 else y_s
-        for t in range(TILES):
+        for t in range(tiles):
             span = slice(t * tile, (t + 1) * tile)
             gram = matmul(src[span, :], src[...], 1)
             if iteration == 0:
                 gram = gram * (inverse * inverse)
             gram_s[span, :] = gram.astype(jnp.bfloat16)
-        for t in range(TILES):
+        for t in range(tiles):
             span = slice(t * tile, (t + 1) * tile)
             square = matmul(gram_s[span, :], gram_s[...], 0)
             mixing = coef_b * gram_s[span, :].astype(jnp.float32) + coef_c * square
@@ -269,12 +276,13 @@
     width = col_size // HALVES
     places = row_size * width
     height = rows * row_size
-    tile = height // TILES
+    tiles = ROW_TILES[slot]
+    tile = height // tiles
     if slot:
-        owned_ref, back_ref, x_s, y_s, gram_s, out_s, sems = refs[1:]
+        whole_ref, back_ref, x_s, y_s, gram_s = refs
     else:
         owned_ref, low_refs = refs[0], refs[1 : 1 + LOW]
-        x_s, y_s, gram_s, out_s, sems, back_ref = refs[1 + LOW :]
+        x_s, y_s, gram_s, whole_ref, back_ref, sems = refs[1 + LOW :]
     row, col = lax.axis_index("dp"), lax.axis_index("owner")
     me = row * col_size + col
     owns = other_ref[me] != me
@@ -283,14 +291,15 @@
 
     def copy_out(t):
         span = pl.ds(t * tile, tile)
-        return pltpu.make_async_copy(out_s.at[span], owned_ref.at[slot, span], sems.at[t])
+        return pltpu.make_async_copy(whole_ref.at[span], owned_ref.at[slot, span], sems.at[t])
 
     def write(t, result):
-        out_s[t * tile : (t + 1) * tile, :] = jnp.where(owns, result, jnp.zeros_like(result))
-        copy_out(t).start()
-        for j in range(row_size // TILES):
+        whole_ref[t * tile : (t + 1) * tile, :] = jnp.where(owns, result, jnp.zeros_like(result))
+        if not slot:
+            copy_out(t).start()
+        for j in range(row_size // tiles):
             block = result[j * rows : (j + 1) * rows, :]
-            r = t * (row_size // TILES) + j
+            r = t * (row_size // tiles) + j
             for c in range(width):
                 if slot:
                     place = r * width + c
@@ -302,43 +311,41 @@
                     block[:, (c + width) * cols : (c + width + 1) * cols],
                 )
 
-    newton_schulz(height, inverse, x_s, y_s, gram_s, write)
+    newton_schulz(height, tiles, inverse, x_s, y_s, gram_s, write)
     if not slot:
         for k in range(LOW):
             low_refs[k][...] = back_ref[k * places // LOW : (k + 1) * places // LOW]
-    for t in range(TILES):
-        copy_out(t).wait()
-
-
-def orthogonalize(slot, other, arrived, row_size, col_size, owned=None):
+        for t in range(tiles):
+            copy_out(t).wait()
+
+
+def orthogonalize(slot, other, arrived, row_size, col_size):
     devices, rows, cols = arrived.shape
     height, width = rows * row_size, cols * col_size
     padded = round_up(height, 256)
     places = devices // HALVES
-    anywhere = pl.BlockSpec(memory_space=pl.ANY)
-    in_specs, operands = [SMEM, VMEM], [other, arrived]
     scratch_shapes = [
         pltpu.VMEM((padded, width), jnp.bfloat16),
         pltpu.VMEM((padded, width), jnp.bfloat16),
         pltpu.VMEM((padded, padded), jnp.bfloat16),
-        pltpu.VMEM((height, width), jnp.bfloat16),
-        pltpu.SemaphoreType.DMA((TILES,)),
     ]
     if slot:
-        in_specs.append(anywhere)
-        operands.append(owned)
-        back = [(places, rows, cols)]
+        out_specs = [VMEM, VMEM]
+        out = [(height, width), (places, rows, cols)]
     else:
-        back = [(places // LOW, rows, cols)] * LOW
-        scratch_shapes.append(pltpu.VMEM((places, rows, cols), jnp.bfloat16))
-    owned, *back = pl.pallas_call(
+        out_specs = [ANYWHERE] + [VMEM] * LOW
+        out = [(CAP, height, width)] + [(places // LOW, rows, cols)] * LOW
+        scratch_shapes += [
+            pltpu.VMEM((height, width), jnp.bfloat16),
+            pltpu.VMEM((places, rows, cols), jnp.bfloat16),
+            pltpu.SemaphoreType.DMA((ROW_TILES[slot],)),
+        ]
+    return pl.pallas_call(
         functools.partial(ortho_kernel, row_size, col_size, slot),
-        in_specs=in_specs,
-        out_specs=[anywhere] + [VMEM] * len(back),
-        out_shape=[jax.ShapeDtypeStruct((CAP, height, width), jnp.bfloat16)]
-        + [jax.ShapeDtypeStruct(shape, jnp.bfloat16) for shape in back],
+        in_specs=[SMEM, VMEM],
+        out_specs=out_specs,
+        out_shape=[jax.ShapeDtypeStruct(shape, jnp.bfloat16) for shape in out],
         scratch_shapes=scratch_shapes,
-        input_output_aliases={2: 0} if slot else {},
         compiler_params=PARAMS,
         cost_estimate=pl.CostEstimate(
             flops=2 * ITERS * padded * padded * (2 * width + padded),
@@ -346,8 +353,7 @@
             transcendentals=0,
         ),
         name="orthogonalize",
-    )(*operands)
-    return owned, back
+    )(other, arrived)
 
 
 def restage_kernel(*refs):
@@ -374,49 +380,78 @@
     )(*blocks)
 
 
-def unpack_kernel(chunk, place_ref, *refs):
-    high_refs, second_ref, update_ref, back_s, update_s, sems = refs[:-5], *refs[-5:]
+def copy_blocks(slot, rank_ref, place_ref, back_ref, update_ref, sems, act):
+    for i in range(update_ref.shape[0]):
+
+        @pl.when(rank_ref[i] == slot)
+        def _():
+            copy = pltpu.make_async_copy(
+                back_ref.at[place_ref[i]], update_ref.at[i], sems.at[i]
+            )
+            act(copy)
+
+
+def start(copy):
+    copy.start()
+
+
+def wait(copy):
+    copy.wait()
+
+
+def early_kernel(rank_ref, place_ref, whole_ref, owned_in, *refs):
+    high_refs, (owned_ref, update_ref, back_s, own_sem, sems) = refs[:-5], refs[-5:]
+    own = pltpu.make_async_copy(whole_ref, owned_ref.at[CAP - 1], own_sem)
+    own.start()
     for h, high_ref in enumerate(high_refs):
         back_s[h * LOW : (h + 1) * LOW] = high_ref[...]
-    back_s[second_ref.shape[0] :] = second_ref[...]
-
-    def copy_out(k):
-        span = pl.ds(k * chunk, chunk)
-        return pltpu.make_async_copy(update_s.at[span], update_ref.at[span], sems.at[k])
-
-    chunks = update_s.shape[0] // chunk
-    for k in range(chunks):
-        for i in range(k * chunk, (k + 1) * chunk):
-            update_s[i] = back_s[place_ref[i]]
-        copy_out(k).start()
-    for k in range(chunks):
-        copy_out(k).wait()
-
-
-def unpack(place, first, second):
-    places, rows, cols = second.shape
-    mats = place.shape[0]
-    chunk = 8
+    copy_blocks(0, rank_ref, place_ref, back_s, update_ref, sems, start)
+    copy_blocks(0, rank_ref, place_ref, back_s, update_ref, sems, wait)
+    own.wait()
+
+
+def store_early(rank, place, matrix, owned, first):
+    _, rows, cols = first[0].shape
+    mats = rank.shape[0]
     return pl.pallas_call(
-        functools.partial(unpack_kernel, chunk),
-        grid_spec=pltpu.PrefetchScalarGridSpec(
-            num_scalar_prefetch=1,
-            grid=(1,),
-            in_specs=[whole(first[0].shape)] * len(first) + [whole(second.shape)],
-            out_specs=pl.BlockSpec(memory_space=pl.ANY),
-            scratch_shapes=[
-                pltpu.VMEM((CAP * places, rows, cols), jnp.bfloat16),
-                pltpu.VMEM((mats, rows, cols), jnp.bfloat16),
-                pltpu.SemaphoreType.DMA((mats // chunk,)),
-            ],
-        ),
-        out_shape=jax.ShapeDtypeStruct((mats, rows, cols), jnp.bfloat16),
+        early_kernel,
+        in_specs=[SMEM, SMEM, VMEM, ANYWHERE] + [VMEM] * len(first),
+        out_specs=[ANYWHERE, ANYWHERE],
+        out_shape=[
+            jax.ShapeDtypeStruct(owned.shape, jnp.bfloat16),
+            jax.ShapeDtypeStruct((mats, rows, cols), jnp.bfloat16),
+        ],
+        scratch_shapes=[
+            pltpu.VMEM((LOW * len(first), rows, cols), jnp.bfloat16),
+            pltpu.SemaphoreType.DMA(()),
+            pltpu.SemaphoreType.DMA((mats,)),
+        ],
+        input_output_aliases={3: 0},
         compiler_params=PARAMS,
         cost_estimate=pl.CostEstimate(
-            flops=0, bytes_accessed=4 * mats * rows * cols, transcendentals=0
+            flops=0, bytes_accessed=8 * mats * rows * cols, transcendentals=0
         ),
-        name="unpack",
-    )(place, *first, second)
+        name="store_early",
+    )(rank, place, matrix, owned, *first)
+
+
+def late_kernel(rank_ref, place_ref, back_ref, update_in, update_ref, sems):
+    copy_blocks(1, rank_ref, place_ref, back_ref, update_ref, sems, start)
+    copy_blocks(1, rank_ref, place_ref, back_ref, update_ref, sems, wait)
+
+
+def store_late(rank, place, second, update):
+    return pl.pallas_call(
+        late_kernel,
+        in_specs=[SMEM, SMEM, VMEM, ANYWHERE],
+        out_specs=ANYWHERE,
+        out_shape=jax.ShapeDtypeStruct(update.shape, jnp.bfloat16),
+        scratch_shapes=[pltpu.SemaphoreType.DMA((rank.shape[0],))],
+        input_output_aliases={3: 0},
+        compiler_params=PARAMS,
+        cost_estimate=pl.CostEstimate(flops=0, bytes_accessed=4 * second.size, transcendentals=0),
+        name="store_late",
+    )(rank, place, second, update)
 
 
 def exchange(blocks, axes, groups=None):
@@ -445,7 +480,7 @@
     )
     arrived_first, second = lax.optimization_barrier((arrived_first, second))
     arrived_second = exchange(second, AXES)
-    owned, back_first = orthogonalize(0, other, arrived_first, row_size, col_size)
+    owned, *back_first = orthogonalize(0, other, arrived_first, row_size, col_size)
     low = [back_first[0]] + [
         swap(back_first[k], k * col_size, devices) for k in range(1, LOW)
     ]
@@ -457,10 +492,11 @@
         for c in range(width)
         if r or c
     ]
-    owned, back_second = orthogonalize(1, other, arrived_second, row_size, col_size, owned)
+    matrix, back_second = orthogonalize(1, other, arrived_second, row_size, col_size)
     returned_first, back_second = lax.optimization_barrier((returned_first, back_second))
-    returned_second = exchange(back_second[0], AXES, halves)
-    update = unpack(place, returned_first, returned_second)
+    returned_second = exchange(back_second, AXES, halves)
+    owned, update = store_early(rank, place, matrix, owned, returned_first)
+    update = store_late(rank, place, returned_second, update)
     return (new_momentum, update, owned)
 
 

time: 110 us -> 109 us (level)
  blocking collectives: 16.6 us -> 0 us
  waiting for transfers between devices: 44.9 us -> 51.8 us
  starting transfers between devices: 18.9 us -> 23.9 us
  Pallas kernels: 25.8 us -> 29 us
    all_to_all x1 -> x0, blocking collectives: 16.6 us -> none  [exchange(): lax.all_to_all(blocks, axes, split_axis=0, concat_axis=0, tiled=True, axi...]
    all_to_all x2 -> x3, waiting for transfers between devices: 31.9 us -> 38.7 us  [exchange(): lax.all_to_all(blocks, axes, split_axis=0, concat_axis=0, tiled=True, axi...]
    all_to_all x2 -> x3, starting transfers between devices: 12 us -> 16.9 us  [exchange(): lax.all_to_all(blocks, axes, split_axis=0, concat_axis=0, tiled=True, axi...]
    pallas_call x2 -> x3, Pallas kernels: 5.83 us -> 8.6 us  [the longest x1 4.27 us: pack(): pl.pallas_call(functools.partial(pack_kernel, chunk, col_size), in_specs=...]
    unnamed x12 -> x14, local copies, waits for them, and re-layouts: 2.5 us -> 3.37 us
  transfers between devices with their start and end apart: 8 -> 9, of which waited for: 4 -> 5; matrix products, arithmetic and copies ran while one was open for 0% -> 0% of each run, Pallas kernels for 18% -> 21%
where the time goes in v14:
time: 109 us
  waiting for transfers between devices  51.8 us (48%)
  Pallas kernels  29 us (27%)
  starting transfers between devices  23.9 us (22%)
  local copies, waits for them, and re-layouts  3.37 us (3%)
    all_to_all x3, waiting for transfers between devices, exchange(): lax.all_to_all(blocks, axes, split_axis=0, concat_axis=0, tiled=True, axi...  38.7 us
    all_to_all x3, starting transfers between devices, exchange(): lax.all_to_all(blocks, axes, split_axis=0, concat_axis=0, tiled=True, axi...  16.9 us
    pallas_call x2, Pallas kernels, orthogonalize(): pl.pallas_call(functools.partial(ortho_kernel, row_size, col_size, slot),...  16.4 us
    ppermute x6, waiting for transfers between devices, swap(): return lax.ppermute(block, AXES, [(d, d ^ offset) for d in range(devices)])  13.1 us
    ppermute x6, starting transfers between devices, swap(): return lax.ppermute(block, AXES, [(d, d ^ offset) for d in range(devices)])  6.96 us
    pallas_call x1, Pallas kernels, pack(): pl.pallas_call(functools.partial(pack_kernel, chunk, col_size), in_specs=...  4.27 us
    unnamed x14, local copies, waits for them, and re-layouts  3.37 us
    pallas_call x1, Pallas kernels, update_momentum(): pl.pallas_call(functools.partial(momentum_kernel, chunk, col_size), grid_...  3.21 us
  transfers between devices with their start and end apart: 9, of which 5 were waited for; matrix products, arithmetic and copies ran while one was open for 0% of the time, Pallas kernels for 21%

profile of v14, /device:TPU:0, one launch (start us, length us, event | category | flops | bytes accessed | tf_op | source)
XLA Modules:
  0.0 108.9 jit_solution(15398065973741043639)
XLA Ops:
  0.6 4.3 %pack.1 = (bf16[32,88,256]{2,1,0:T(8,128)(2,1)}, s32[32]{0:T(128)}, s32[32]{0:T(128)}) custom-call(s32[32]{0:T(128)} %owner_ref.3, bf16[32,88,256]{2,1,0:T(8,128)(2,1)} %g_ref.3, f32[32,88,256]{2,1,0:T(8,128)} %m_ref.3), custom_call_target="tpu_custom_call" | custom-call | flops 2883584 | bytes 5767168 | tf_op jit(solution)/shard_map/pack/pallas_call | solution.py:132
  4.9 0.0 copy-start
  4.9 0.0 copy-start.4
  4.9 0.0 copy-start.5
  4.9 0.0 copy-start.6
  5.0 7.4 %all-to-all-start = ((bf16[32,88,256]{2,1,0:T(8,128)(2,1)}), bf16[32,88,256]{2,1,0:T(8,128)(2,1)}, u32[]{:S(2)}, u32[]{:S(2)}) async-start(bf16[32,88,256]{2,1,0:T(8,128)(2,1)} %get-tuple-element.34), calls=%async_computation | async-start | bytes 2883584 | tf_op jit(solution)/shard_map/all_to_all | solution.py:458
  12.4 0.0 copy-done
  12.4 0.0 copy-done.4
  12.4 0.0 copy-done.5
  12.4 0.0 copy-done.6
  12.4 0.0 copy-start.1
  12.4 1.4 %copy-done.1 = bf16[32,88,256]{2,1,0:T(8,128)(2,1)S(1)} copy-done((bf16[32,88,256]{2,1,0:T(8,128)(2,1)S(1)}, bf16[32,88,256]{2,1,0:T(8,128)(2,1)}, u32[]{:S(2)}) %copy-start.1) | copy-done | bytes 1441816
  13.8 3.2 %update_momentum.1 = (f32[32,88,256]{2,1,0:T(8,128)}, bf16[32,88,256]{2,1,0:T(8,128)(2,1)S(1)}, s32[32]{0:T(128)S(1)}) custom-call(s32[32]{0:T(128)S(1)} %copy-done.5, s32[32]{0:T(128)S(1)} %copy-done.6, s32[32]{0:T(128)S(1)} %copy-done.4, bf16[32,88,256]{2,1,0:T(8,128)(2,1)S(1)} %copy-done.1, f32[32,88,256]{2,1,0:T(8,128)S(1)} %copy-done), custom_call_target="tpu_custom_call" | custom-call | flops 2883584 | bytes 8650752 | tf_op jit(solution)/shard_map/update_momentum/pallas_call | solution.py:192
  17.0 0.0 copy-start.2
  17.0 1.1 %copy-done.2 = bf16[32,88,256]{2,1,0:T(8,128)(2,1)} copy-done((bf16[32,88,256]{2,1,0:T(8,128)(2,1)}, bf16[32,88,256]{2,1,0:T(8,128)(2,1)S(1)}, u32[]{:S(2)}) %copy-start.2) | copy-done | bytes 1441816
  18.1 27.5 %all-to-all-done.x_ref = bf16[32,88,256]{2,1,0:T(8,128)(2,1)} async-done(((bf16[32,88,256]{2,1,0:T(8,128)(2,1)}), bf16[32,88,256]{2,1,0:T(8,128)(2,1)}, u32[]{:S(2)}, u32[]{:S(2)}) %all-to-all-start) | async-done | bytes 1441824 | tf_op jit(solution)/shard_map/all_to_all | solution.py:458
  45.6 4.6 %all-to-all-start.1 = ((bf16[32,88,256]{2,1,0:T(8,128)(2,1)}), bf16[32,88,256]{2,1,0:T(8,128)(2,1)S(1)}, u32[]{:S(2)}, u32[]{:S(2)}) async-start(bf16[32,88,256]{2,1,0:T(8,128)(2,1)} %copy-done.2), calls=%async_computation.1 | async-start | bytes 2883584 | tf_op jit(solution)/shard_map/all_to_all | solution.py:458
  50.2 9.3 %orthogonalize.2 = (bf16[2,704,1024]{2,1,0:T(8,128)(2,1)}, bf16[4,88,256]{2,1,0:T(8,128)(2,1)S(1)}, bf16[4,88,256]{2,1,0:T(8,128)(2,1)S(1)}, bf16[4,88,256]{2,1,0:T(8,128)(2,1)S(1)}, bf16[4,88,256]{2,1,0:T(8,128)(2,1)S(1)}) custom-call(s32[32]{0:T(128)S(1)} %copy-done.6, bf16[32,88,256]{2,1,0:T(8,128)(2,1)} %all-to-all-done.x_ref), custom_call_target="tpu_custom_call" | custom-call | flops 6643777536 | bytes 4718592 | tf_op jit(solution)/shard_map/orthogonalize/pallas_call | solution.py:343
  59.5 0.3 collective-permute-start
  59.8 1.7 %collective-permute-start.1 = (bf16[4,88,256]{2,1,0:T(8,128)(2,1)S(1)}, bf16[4,88,256]{2,1,0:T(8,128)(2,1)S(1)}, u32[]{:S(2)}, u32[]{:S(2)}) collective-permute-start(bf16[4,88,256]{2,1,0:T(8,128)(2,1)S(1)} %get-tuple-element.39), channel_id=1, source_target_pairs={{0,8},{1,9},{2,10},{3,11},{4,12},{5,13},{6,14},{7,15},{8,0},{9,1},... | collective-permute-start | bytes 540680 | tf_op jit(solution)/shard_map/ppermute | solution.py:464
  61.5 0.0 collective-permute-start.2
  61.5 0.0 collective-permute-done.refs_1_
  61.5 8.6 %collective-permute-done.1.refs_2_ = bf16[4,88,256]{2,1,0:T(8,128)(2,1)S(1)} collective-permute-done((bf16[4,88,256]{2,1,0:T(8,128)(2,1)S(1)}, bf16[4,88,256]{2,1,0:T(8,128)(2,1)S(1)}, u32[]{:S(2)}, u32[]{:S(2)}) %collective-permute-start.1) | collective-permute-done | bytes 180256 | tf_op jit(solution)/shard_map/ppermute | solution.py:464
  70.1 4.5 %collective-permute-done.2.refs_3_ = bf16[4,88,256]{2,1,0:T(8,128)(2,1)S(1)} collective-permute-done((bf16[4,88,256]{2,1,0:T(8,128)(2,1)S(1)}, bf16[4,88,256]{2,1,0:T(8,128)(2,1)S(1)}, u32[]{:S(2)}, u32[]{:S(2)}) %collective-permute-start.2) | collective-permute-done | bytes 180256 | tf_op jit(solution)/shard_map/ppermute | solution.py:464
  74.6 0.8 restage.1
  75.4 3.5 %collective-permute-start.3 = (bf16[4,88,256]{2,1,0:T(8,128)(2,1)}, bf16[4,88,256]{2,1,0:T(8,128)(2,1)S(1)}, u32[]{:S(2)}, u32[]{:S(2)}) collective-permute-start(bf16[4,88,256]{2,1,0:T(8,128)(2,1)} %get-tuple-element.42), channel_id=1, source_target_pairs={{0,1},{1,0},{2,3},{3,2},{4,5},{5,4},{6,7},{7,6},{8,9},{9,8},{10,11... | collective-permute-start | bytes 540680 | tf_op jit(solution)/shard_map/ppermute | solution.py:464
  78.9 1.5 %collective-permute-start.4 = (bf16[4,88,256]{2,1,0:T(8,128)(2,1)}, bf16[4,88,256]{2,1,0:T(8,128)(2,1)S(1)}, u32[]{:S(2)}, u32[]{:S(2)}) collective-permute-start(bf16[4,88,256]{2,1,0:T(8,128)(2,1)} %get-tuple-element.43), channel_id=1, source_target_pairs={{0,16},{1,17},{2,18},{3,19},{4,20},{5,21},{6,22},{7,23},{8,24},{9,... | collective-permute-start | bytes 540680 | tf_op jit(solution)/shard_map/ppermute | solution.py:464
  80.4 0.0 collective-permute-start.5
  80.4 3.0 %all-to-all-done.1.x_ref = bf16[32,88,256]{2,1,0:T(8,128)(2,1)S(1)} async-done(((bf16[32,88,256]{2,1,0:T(8,128)(2,1)}), bf16[32,88,256]{2,1,0:T(8,128)(2,1)S(1)}, u32[]{:S(2)}, u32[]{:S(2)}) %all-to-all-start.1) | async-done | bytes 1441824 | tf_op jit(solution)/shard_map/all_to_all | solution.py:458
  83.4 7.1 %orthogonalize.3 = (bf16[704,1024]{1,0:T(8,128)(2,1)S(1)}, bf16[16,88,256]{2,1,0:T(8,128)(2,1)S(1)}) custom-call(s32[32]{0:T(128)S(1)} %copy-done.6, bf16[32,88,256]{2,1,0:T(8,128)(2,1)S(1)} %all-to-all-done.1.x_ref), custom_call_target="tpu_custom_call" | custom-call | flops 6643777536 | bytes 4718592 | tf_op jit(solution)/shard_map/orthogonalize/pallas_call | solution.py:343
  90.5 0.0 copy-start.3
  90.5 0.9 copy-done.3
  91.3 0.0 collective-permute-done.3.refs_1_
  91.4 0.0 collective-permute-done.4.refs_2_
  91.4 0.0 collective-permute-done.5.refs_3_
  91.4 4.9 %all-to-all-start.2 = ((bf16[16,88,256]{2,1,0:T(8,128)(2,1)}), bf16[16,88,256]{2,1,0:T(8,128)(2,1)S(1)}, u32[]{:S(2)}, u32[]{:S(2)}) async-start(bf16[16,88,256]{2,1,0:T(8,128)(2,1)} %copy-done.3), calls=%async_computation.2 | async-start | bytes 1441792 | tf_op jit(solution)/shard_map/all_to_all | solution.py:458
  96.3 2.6 %store_early.1 = (bf16[2,704,1024]{2,1,0:T(8,128)(2,1)}, bf16[32,88,256]{2,1,0:T(8,128)(2,1)}) custom-call(s32[32]{0:T(128)S(1)} %copy-done.4, s32[32]{0:T(128)S(1)} %get-tuple-element.33.place_ref, bf16[704,1024]{1,0:T(8,128)(2,1)S(1)} %get-tuple-element.49.whole_ref, ...), custom_call_target="tpu_custom_call", output_to_operand_aliasing={{0}: (3, {})} | custom-call | bytes 5767168 | tf_op jit(solution)/shard_map/store_early/pallas_call | solution.py:416
  98.9 8.2 %all-to-all-done.2.back_ref = bf16[16,88,256]{2,1,0:T(8,128)(2,1)S(1)} async-done(((bf16[16,88,256]{2,1,0:T(8,128)(2,1)}), bf16[16,88,256]{2,1,0:T(8,128)(2,1)S(1)}, u32[]{:S(2)}, u32[]{:S(2)}) %all-to-all-start.2) | async-done | bytes 720928 | tf_op jit(solution)/shard_map/all_to_all | solution.py:458
  107.2 1.7 %store_late.1 = bf16[32,88,256]{2,1,0:T(8,128)(2,1)} custom-call(s32[32]{0:T(128)S(1)} %copy-done.4, s32[32]{0:T(128)S(1)} %get-tuple-element.33.place_ref, bf16[16,88,256]{2,1,0:T(8,128)(2,1)S(1)} %all-to-all-done.2.back_ref, bf16[32,88,256]{2,1,0:T(8,128)(2,1)} %get-tuple-element.55.update_in), custom_call_target="tpu_custom_call", output_to_operand_aliasing={{}: (3, {})} | custom-call | bytes 1441792 | tf_op jit(solution)/shard_map/store_late/pallas_call | solution.py:444
Async XLA Ops:
  4.9 7.5 %copy-start = (f32[32,88,256]{2,1,0:T(8,128)S(1)}, f32[32,88,256]{2,1,0:T(8,128)}, u32[]{:S(2)}) copy-start(f32[32,88,256]{2,1,0:T(8,128)} %m_ref.3) | copy-start | bytes 8650756
  4.9 7.5 %copy-start.4 = (s32[32]{0:T(128)S(1)}, s32[32]{0:T(128)}, u32[]{:S(2)}) copy-start(s32[32]{0:T(128)} %get-tuple-element.31.rank_ref) | copy-start | bytes 388
  4.9 7.5 %copy-start.5 = (s32[32]{0:T(128)S(1)}, s32[32]{0:T(128)}, u32[]{:S(2)}) copy-start(s32[32]{0:T(128)} %owner_ref.3) | copy-start | bytes 388
  4.9 7.5 %copy-start.6 = (s32[32]{0:T(128)S(1)}, s32[32]{0:T(128)}, u32[]{:S(2)}) copy-start(s32[32]{0:T(128)} %get-tuple-element.30.other_ref) | copy-start | bytes 388
  5.0 40.6 %all-to-all-start = ((bf16[32,88,256]{2,1,0:T(8,128)(2,1)}), bf16[32,88,256]{2,1,0:T(8,128)(2,1)}, u32[]{:S(2)}, u32[]{:S(2)}) async-start(bf16[32,88,256]{2,1,0:T(8,128)(2,1)} %get-tuple-element.34), calls=%async_computation | async-start | bytes 2883584 | tf_op jit(solution)/shard_map/all_to_all | solution.py:458
  12.4 1.4 %copy-start.1 = (bf16[32,88,256]{2,1,0:T(8,128)(2,1)S(1)}, bf16[32,88,256]{2,1,0:T(8,128)(2,1)}, u32[]{:S(2)}) copy-start(bf16[32,88,256]{2,1,0:T(8,128)(2,1)} %g_ref.3) | copy-start | bytes 4325380
  17.0 1.1 %copy-start.2 = (bf16[32,88,256]{2,1,0:T(8,128)(2,1)}, bf16[32,88,256]{2,1,0:T(8,128)(2,1)S(1)}, u32[]{:S(2)}) copy-start(bf16[32,88,256]{2,1,0:T(8,128)(2,1)S(1)} %get-tuple-element.45) | copy-start | bytes 4325380
  45.6 37.8 %all-to-all-start.1 = ((bf16[32,88,256]{2,1,0:T(8,128)(2,1)}), bf16[32,88,256]{2,1,0:T(8,128)(2,1)S(1)}, u32[]{:S(2)}, u32[]{:S(2)}) async-start(bf16[32,88,256]{2,1,0:T(8,128)(2,1)} %copy-done.2), calls=%async_computation.1 | async-start | bytes 2883584 | tf_op jit(solution)/shard_map/all_to_all | solution.py:458
  59.5 2.0 %collective-permute-start = (bf16[4,88,256]{2,1,0:T(8,128)(2,1)S(1)}, bf16[4,88,256]{2,1,0:T(8,128)(2,1)S(1)}, u32[]{:S(2)}, u32[]{:S(2)}) collective-permute-start(bf16[4,88,256]{2,1,0:T(8,128)(2,1)S(1)} %get-tuple-element.38), channel_id=1, source_target_pairs={{0,4},{1,5},{2,6},{3,7},{4,0},{5,1},{6,2},{7,3},{8,12},{9,13},{10,... | collective-permute-start | bytes 540680 | tf_op jit(solution)/shard_map/ppermute | solution.py:464
  59.8 10.3 %collective-permute-start.1 = (bf16[4,88,256]{2,1,0:T(8,128)(2,1)S(1)}, bf16[4,88,256]{2,1,0:T(8,128)(2,1)S(1)}, u32[]{:S(2)}, u32[]{:S(2)}) collective-permute-start(bf16[4,88,256]{2,1,0:T(8,128)(2,1)S(1)} %get-tuple-element.39), channel_id=1, source_target_pairs={{0,8},{1,9},{2,10},{3,11},{4,12},{5,13},{6,14},{7,15},{8,0},{9,1},... | collective-permute-start | bytes 540680 | tf_op jit(solution)/shard_map/ppermute | solution.py:464
  61.5 13.1 %collective-permute-start.2 = (bf16[4,88,256]{2,1,0:T(8,128)(2,1)S(1)}, bf16[4,88,256]{2,1,0:T(8,128)(2,1)S(1)}, u32[]{:S(2)}, u32[]{:S(2)}) collective-permute-start(bf16[4,88,256]{2,1,0:T(8,128)(2,1)S(1)} %get-tuple-element.40), channel_id=1, source_target_pairs={{0,12},{1,13},{2,14},{3,15},{4,8},{5,9},{6,10},{7,11},{8,4},{9,5},... | collective-permute-start | bytes 540680 | tf_op jit(solution)/shard_map/ppermute | solution.py:464
  75.4 15.9 %collective-permute-start.3 = (bf16[4,88,256]{2,1,0:T(8,128)(2,1)}, bf16[4,88,256]{2,1,0:T(8,128)(2,1)S(1)}, u32[]{:S(2)}, u32[]{:S(2)}) collective-permute-start(bf16[4,88,256]{2,1,0:T(8,128)(2,1)} %get-tuple-element.42), channel_id=1, source_target_pairs={{0,1},{1,0},{2,3},{3,2},{4,5},{5,4},{6,7},{7,6},{8,9},{9,8},{10,11... | collective-permute-start | bytes 540680 | tf_op jit(solution)/shard_map/ppermute | solution.py:464
  78.9 12.4 %collective-permute-start.4 = (bf16[4,88,256]{2,1,0:T(8,128)(2,1)}, bf16[4,88,256]{2,1,0:T(8,128)(2,1)S(1)}, u32[]{:S(2)}, u32[]{:S(2)}) collective-permute-start(bf16[4,88,256]{2,1,0:T(8,128)(2,1)} %get-tuple-element.43), channel_id=1, source_target_pairs={{0,16},{1,17},{2,18},{3,19},{4,20},{5,21},{6,22},{7,23},{8,24},{9,... | collective-permute-start | bytes 540680 | tf_op jit(solution)/shard_map/ppermute | solution.py:464
  80.4 11.0 %collective-permute-start.5 = (bf16[4,88,256]{2,1,0:T(8,128)(2,1)}, bf16[4,88,256]{2,1,0:T(8,128)(2,1)}, u32[]{:S(2)}, u32[]{:S(2)}) collective-permute-start(bf16[4,88,256]{2,1,0:T(8,128)(2,1)} %get-tuple-element.44), channel_id=1, source_target_pairs={{0,17},{1,16},{2,19},{3,18},{4,21},{5,20},{6,23},{7,22},{8,25},{9,... | collective-permute-start | bytes 540680 | tf_op jit(solution)/shard_map/ppermute | solution.py:464
  90.5 0.9 copy-start.3
  91.4 15.8 %all-to-all-start.2 = ((bf16[16,88,256]{2,1,0:T(8,128)(2,1)}), bf16[16,88,256]{2,1,0:T(8,128)(2,1)S(1)}, u32[]{:S(2)}, u32[]{:S(2)}) async-start(bf16[16,88,256]{2,1,0:T(8,128)(2,1)} %copy-done.3), calls=%async_computation.2 | async-start | bytes 1441792 | tf_op jit(solution)/shard_map/all_to_all | solution.py:458

commit v15 on v14

--- a/solution.py
+++ b/solution.py
@@ -11,7 +11,7 @@
 ITERS = 2
 CAP = 2
 HALVES = 2
-ROW_TILES = (1, 2)
+TILES = 2
 LOW = 4
 
 coef_a = 3.4445
@@ -85,23 +85,16 @@
 
 def pack_kernel(
     chunk, col_size, owner_ref, g_ref, m_ref, first_ref, other_ref, rank_ref,
-    count_ref, list_ref, g_s, m_s, block_s, load_sems, store_sems,
+    count_ref, list_ref, g_s, m_s, sems,
 ):
     mats = rank_ref.shape[0]
 
     def loads(k):
         span = pl.ds(k * chunk, chunk)
         return (
-            pltpu.make_async_copy(g_ref.at[span], g_s.at[span], load_sems.at[0, k]),
-            pltpu.make_async_copy(m_ref.at[span], m_s.at[span], load_sems.at[1, k]),
+            pltpu.make_async_copy(g_ref.at[span], g_s.at[span], sems.at[0, k]),
+            pltpu.make_async_copy(m_ref.at[span], m_s.at[span], sems.at[1, k]),
         )
-
-    def stores(i):
-        owner = owner_ref[i]
-        return [
-            pltpu.make_async_copy(block_s.at[i], first_ref.at[host], store_sems.at[n, i])
-            for n, host in enumerate((owner, other_ref[owner]))
-        ]
 
     for k in range(mats // chunk):
         for load in loads(k):
@@ -114,16 +107,9 @@
 
             @pl.when(rank_ref[i] == 0)
             def _():
-                block_s[i] = nesterov_of(g_s, m_s, i)[1]
-                for store in stores(i):
-                    store.start()
-
-    for i in range(mats):
-
-        @pl.when(rank_ref[i] == 0)
-        def _():
-            for store in stores(i):
-                store.wait()
+                nesterov = nesterov_of(g_s, m_s, i)[1]
+                first_ref[owner_ref[i]] = nesterov
+                first_ref[other_ref[owner_ref[i]]] = nesterov
 
 
 def pack(gradients, momentum, owner_table, devices, col_size):
@@ -131,22 +117,24 @@
     chunk = 8
     return pl.pallas_call(
         functools.partial(pack_kernel, chunk, col_size),
-        in_specs=[SMEM, ANYWHERE, ANYWHERE],
-        out_specs=[ANYWHERE, SMEM, SMEM],
+        grid_spec=pltpu.PrefetchScalarGridSpec(
+            num_scalar_prefetch=1,
+            grid=(1,),
+            in_specs=[ANYWHERE, ANYWHERE],
+            out_specs=[whole((devices, rows, cols)), SMEM, SMEM],
+            scratch_shapes=[
+                pltpu.SMEM((devices,), jnp.int32),
+                pltpu.SMEM((2 * HALVES * devices,), jnp.int32),
+                pltpu.VMEM(gradients.shape, gradients.dtype),
+                pltpu.VMEM(momentum.shape, momentum.dtype),
+                pltpu.SemaphoreType.DMA((2, mats // chunk)),
+            ],
+        ),
         out_shape=[
             jax.ShapeDtypeStruct((devices, rows, cols), jnp.bfloat16),
             jax.ShapeDtypeStruct((devices,), jnp.int32),
             jax.ShapeDtypeStruct((mats,), jnp.int32),
         ],
-        scratch_shapes=[
-            pltpu.SMEM((devices,), jnp.int32),
-            pltpu.SMEM((2 * HALVES * devices,), jnp.int32),
-            pltpu.VMEM(gradients.shape, gradients.dtype),
-            pltpu.VMEM(momentum.shape, momentum.dtype),
-            pltpu.VMEM(gradients.shape, jnp.bfloat16),
-            pltpu.SemaphoreType.DMA((2, mats // chunk)),
-            pltpu.SemaphoreType.DMA((2, mats)),
-        ],
         compiler_params=PACK_PARAMS,
         cost_estimate=pl.CostEstimate(
             flops=4 * mats * rows * cols, bytes_accessed=8 * mats * rows * cols, transcendentals=0
@@ -156,11 +144,19 @@
 
 
 def momentum_kernel(
-    chunk, col_size, owner_ref, other_ref, rank_ref, g_ref, m_ref, nm_ref, second_ref, place_ref
+    chunk, col_size, owner_ref, other_ref, rank_ref, g_ref, m_ref, nm_ref, second_ref, list_ref,
+    count_ref,
 ):
     step = pl.program_id(0)
     width = col_size // HALVES
     row, col = lax.axis_index("dp"), lax.axis_index("owner")
+    listed = list_ref.shape[0] // CAP
+
+    @pl.when(step == 0)
+    def _():
+        for slot in range(CAP):
+            count_ref[slot] = 0
+
     for j in range(chunk):
         i = step * chunk + j
         new, nesterov = nesterov_of(g_ref, m_ref, j)
@@ -177,11 +173,14 @@
         host_row, host_col = host // col_size, host % width
         offset = host_row ^ row
         high = offset // LOW * width + (host_col ^ (col % width))
-        place_ref[i] = jnp.where(
-            rank_ref[i] == 0,
-            high * LOW + offset % LOW,
-            host_row * width + host_col,
+        place = jnp.where(
+            rank_ref[i] == 0, high * LOW + offset % LOW, host_row * width + host_col
         )
+        rank = rank_ref[i]
+        entry = count_ref[rank]
+        count_ref[rank] = entry + 1
+        list_ref[rank * listed + 2 * entry] = i
+        list_ref[rank * listed + 2 * entry + 1] = place
 
 
 def update_momentum(gradients, momentum, owner_table, other, rank, col_size):
@@ -196,11 +195,12 @@
             grid=(mats // chunk,),
             in_specs=[block, block],
             out_specs=[block, whole((devices, rows, cols)), SMEM],
+            scratch_shapes=[pltpu.SMEM((CAP,), jnp.int32)],
         ),
         out_shape=[
             jax.ShapeDtypeStruct(momentum.shape, jnp.float32),
             jax.ShapeDtypeStruct((devices, rows, cols), jnp.bfloat16),
-            jax.ShapeDtypeStruct((mats,), jnp.int32),
+            jax.ShapeDtypeStruct((2 * mats,), jnp.int32),
         ],
         compiler_params=PARAMS,
         cost_estimate=pl.CostEstimate(
@@ -276,13 +276,13 @@
     width = col_size // HALVES
     places = row_size * width
     height = rows * row_size
-    tiles = ROW_TILES[slot]
+    tiles = TILES
     tile = height // tiles
     if slot:
-        whole_ref, back_ref, x_s, y_s, gram_s = refs
+        whole_ref, out_ref, x_s, y_s, gram_s, back_ref, sems = refs
     else:
         owned_ref, low_refs = refs[0], refs[1 : 1 + LOW]
-        x_s, y_s, gram_s, whole_ref, back_ref, sems = refs[1 + LOW :]
+        x_s, y_s, gram_s, back_ref, sems, whole_ref = refs[1 + LOW :]
     row, col = lax.axis_index("dp"), lax.axis_index("owner")
     me = row * col_size + col
     owns = other_ref[me] != me
@@ -290,13 +290,14 @@
     inverse = gather_blocks(x_ref, x_s, row_size, col_size)
 
     def copy_out(t):
+        if slot:
+            span = pl.ds(t * (places // tiles), places // tiles)
+            return pltpu.make_async_copy(back_ref.at[span], out_ref.at[span], sems.at[t])
         span = pl.ds(t * tile, tile)
         return pltpu.make_async_copy(whole_ref.at[span], owned_ref.at[slot, span], sems.at[t])
 
     def write(t, result):
         whole_ref[t * tile : (t + 1) * tile, :] = jnp.where(owns, result, jnp.zeros_like(result))
-        if not slot:
-            copy_out(t).start()
         for j in range(row_size // tiles):
             block = result[j * rows : (j + 1) * rows, :]
             r = t * (row_size // tiles) + j
@@ -310,13 +311,14 @@
                     block[:, c * cols : (c + 1) * cols],
                     block[:, (c + width) * cols : (c + width + 1) * cols],
                 )
+        copy_out(t).start()
 
     newton_schulz(height, tiles, inverse, x_s, y_s, gram_s, write)
     if not slot:
         for k in range(LOW):
             low_refs[k][...] = back_ref[k * places // LOW : (k + 1) * places // LOW]
-        for t in range(tiles):
-            copy_out(t).wait()
+    for t in range(tiles):
+        copy_out(t).wait()
 
 
 def orthogonalize(slot, other, arrived, row_size, col_size):
@@ -328,18 +330,16 @@
         pltpu.VMEM((padded, width), jnp.bfloat16),
         pltpu.VMEM((padded, width), jnp.bfloat16),
         pltpu.VMEM((padded, padded), jnp.bfloat16),
+        pltpu.VMEM((places, rows, cols), jnp.bfloat16),
+        pltpu.SemaphoreType.DMA((TILES,)),
     ]
     if slot:
-        out_specs = [VMEM, VMEM]
+        out_specs = [VMEM, ANYWHERE]
         out = [(height, width), (places, rows, cols)]
     else:
         out_specs = [ANYWHERE] + [VMEM] * LOW
         out = [(CAP, height, width)] + [(places // LOW, rows, cols)] * LOW
-        scratch_shapes += [
-            pltpu.VMEM((height, width), jnp.bfloat16),
-            pltpu.VMEM((places, rows, cols), jnp.bfloat16),
-            pltpu.SemaphoreType.DMA((ROW_TILES[slot],)),
-        ]
+        scratch_shapes.append(pltpu.VMEM((height, width), jnp.bfloat16))
     return pl.pallas_call(
         functools.partial(ortho_kernel, row_size, col_size, slot),
         in_specs=[SMEM, VMEM],
@@ -380,42 +380,35 @@
     )(*blocks)
 
 
-def copy_blocks(slot, rank_ref, place_ref, back_ref, update_ref, sems, act):
-    for i in range(update_ref.shape[0]):
-
-        @pl.when(rank_ref[i] == slot)
-        def _():
-            copy = pltpu.make_async_copy(
-                back_ref.at[place_ref[i]], update_ref.at[i], sems.at[i]
-            )
-            act(copy)
-
-
-def start(copy):
-    copy.start()
-
-
-def wait(copy):
-    copy.wait()
-
-
-def early_kernel(rank_ref, place_ref, whole_ref, owned_in, *refs):
-    high_refs, (owned_ref, update_ref, back_s, own_sem, sems) = refs[:-5], refs[-5:]
+def start_blocks(slot, list_ref, back_ref, update_ref, sem):
+    listed = list_ref.shape[0] // CAP
+    for k in range(update_ref.shape[0] // CAP):
+        matrix = list_ref[slot * listed + 2 * k]
+        place = list_ref[slot * listed + 2 * k + 1]
+        pltpu.make_async_copy(back_ref.at[place], update_ref.at[matrix], sem).start()
+
+
+def wait_blocks(back_ref, update_ref, sem):
+    span = pl.ds(0, update_ref.shape[0] // CAP)
+    pltpu.make_async_copy(back_ref.at[span], update_ref.at[span], sem).wait()
+
+
+def early_kernel(list_ref, whole_ref, owned_in, *refs):
+    high_refs, (owned_ref, update_ref, back_s, own_sem, sem) = refs[:-5], refs[-5:]
     own = pltpu.make_async_copy(whole_ref, owned_ref.at[CAP - 1], own_sem)
     own.start()
     for h, high_ref in enumerate(high_refs):
         back_s[h * LOW : (h + 1) * LOW] = high_ref[...]
-    copy_blocks(0, rank_ref, place_ref, back_s, update_ref, sems, start)
-    copy_blocks(0, rank_ref, place_ref, back_s, update_ref, sems, wait)
+    start_blocks(0, list_ref, back_s, update_ref, sem)
+    wait_blocks(back_s, update_ref, sem)
     own.wait()
 
 
-def store_early(rank, place, matrix, owned, first):
+def store_early(places, mats, matrix, owned, first):
     _, rows, cols = first[0].shape
-    mats = rank.shape[0]
     return pl.pallas_call(
         early_kernel,
-        in_specs=[SMEM, SMEM, VMEM, ANYWHERE] + [VMEM] * len(first),
+        in_specs=[SMEM, VMEM, ANYWHERE] + [VMEM] * len(first),
         out_specs=[ANYWHERE, ANYWHERE],
         out_shape=[
             jax.ShapeDtypeStruct(owned.shape, jnp.bfloat16),
@@ -424,34 +417,34 @@
         scratch_shapes=[
             pltpu.VMEM((LOW * len(first), rows, cols), jnp.bfloat16),
             pltpu.SemaphoreType.DMA(()),
-            pltpu.SemaphoreType.DMA((mats,)),
+            pltpu.SemaphoreType.DMA(()),
         ],
-        input_output_aliases={3: 0},
+        input_output_aliases={2: 0},
         compiler_params=PARAMS,
         cost_estimate=pl.CostEstimate(
             flops=0, bytes_accessed=8 * mats * rows * cols, transcendentals=0
         ),
         name="store_early",
-    )(rank, place, matrix, owned, *first)
-
-
-def late_kernel(rank_ref, place_ref, back_ref, update_in, update_ref, sems):
-    copy_blocks(1, rank_ref, place_ref, back_ref, update_ref, sems, start)
-    copy_blocks(1, rank_ref, place_ref, back_ref, update_ref, sems, wait)
-
-
-def store_late(rank, place, second, update):
+    )(places, matrix, owned, *first)
+
+
+def late_kernel(list_ref, back_ref, update_in, update_ref, sem):
+    start_blocks(1, list_ref, back_ref, update_ref, sem)
+    wait_blocks(back_ref, update_ref, sem)
+
+
+def store_late(places, second, update):
     return pl.pallas_call(
         late_kernel,
-        in_specs=[SMEM, SMEM, VMEM, ANYWHERE],
+        in_specs=[SMEM, VMEM, ANYWHERE],
         out_specs=ANYWHERE,
         out_shape=jax.ShapeDtypeStruct(update.shape, jnp.bfloat16),
-        scratch_shapes=[pltpu.SemaphoreType.DMA((rank.shape[0],))],
-        input_output_aliases={3: 0},
+        scratch_shapes=[pltpu.SemaphoreType.DMA(())],
+        input_output_aliases={2: 0},
         compiler_params=PARAMS,
         cost_estimate=pl.CostEstimate(flops=0, bytes_accessed=4 * second.size, transcendentals=0),
         name="store_late",
-    )(rank, place, second, update)
+    )(places, second, update)
 
 
 def exchange(blocks, axes, groups=None):
@@ -475,7 +468,7 @@
     ]
     first, other, rank = pack(gradients, momentum, owner_table, devices, col_size)
     arrived_first = exchange(first, AXES)
-    new_momentum, second, place = update_momentum(
+    new_momentum, second, places = update_momentum(
         gradients, momentum, owner_table, other, rank, col_size
     )
     arrived_first, second = lax.optimization_barrier((arrived_first, second))
@@ -495,8 +488,10 @@
     matrix, back_second = orthogonalize(1, other, arrived_second, row_size, col_size)
     returned_first, back_second = lax.optimization_barrier((returned_first, back_second))
     returned_second = exchange(back_second, AXES, halves)
-    owned, update = store_early(rank, place, matrix, owned, returned_first)
-    update = store_late(rank, place, returned_second, update)
+    owned, update = store_early(
+        places, owner_table.shape[0], matrix, owned, returned_first
+    )
+    update = store_late(places, returned_second, update)
     return (new_momentum, update, owned)
 
 

time: 109 us -> 109 us (level)
    all_to_all x3, waiting for transfers between devices: 38.7 us -> 39.8 us  [exchange(): lax.all_to_all(blocks, axes, split_axis=0, concat_axis=0, tiled=True, axi...]
where the time goes in v15:
time: 109 us
  waiting for transfers between devices  52.8 us (48%)
  Pallas kernels  28.3 us (26%)
  starting transfers between devices  23.7 us (22%)
  local copies, waits for them, and re-layouts  3.37 us (3%)
    all_to_all x3, waiting for transfers between devices, exchange(): lax.all_to_all(blocks, axes, split_axis=0, concat_axis=0, tiled=True, axi...  39.8 us
    all_to_all x3, starting transfers between devices, exchange(): lax.all_to_all(blocks, axes, split_axis=0, concat_axis=0, tiled=True, axi...  16.9 us
    pallas_call x2, Pallas kernels, orthogonalize(): pl.pallas_call(functools.partial(ortho_kernel, row_size, col_size, slot),...  16.5 us
    ppermute x6, waiting for transfers between devices, swap(): return lax.ppermute(block, AXES, [(d, d ^ offset) for d in range(devices)])  13 us
    ppermute x6, starting transfers between devices, swap(): return lax.ppermute(block, AXES, [(d, d ^ offset) for d in range(devices)])  6.81 us
    pallas_call x1, Pallas kernels, pack(): pl.pallas_call(functools.partial(pack_kernel, chunk, col_size), grid_spec...  4.04 us
    unnamed x14, local copies, waits for them, and re-layouts  3.37 us
    pallas_call x1, Pallas kernels, update_momentum(): pl.pallas_call(functools.partial(momentum_kernel, chunk, col_size), grid_...  3.21 us
  transfers between devices with their start and end apart: 9, of which 5 were waited for; matrix products, arithmetic and copies ran while one was open for 0% of the time, Pallas kernels for 21%

profile of v15, /device:TPU:0, one launch (start us, length us, event | category | flops | bytes accessed | tf_op | source)
XLA Modules:
  0.0 109.0 jit_solution(10447886996719678317)
XLA Ops:
  0.6 4.0 %pack.1 = (bf16[32,88,256]{2,1,0:T(8,128)(2,1)}, s32[32]{0:T(128)}, s32[32]{0:T(128)}) custom-call(s32[32]{0:T(128)} %owner_ref.3, bf16[32,88,256]{2,1,0:T(8,128)(2,1)} %g_ref.3, f32[32,88,256]{2,1,0:T(8,128)} %m_ref.3), custom_call_target="tpu_custom_call" | custom-call | flops 2883584 | bytes 5767168 | tf_op jit(solution)/shard_map/pack/pallas_call | solution.py:118
  4.7 0.0 copy-start
  4.7 0.0 copy-start.4
  4.7 0.0 copy-start.5
  4.7 0.0 copy-start.6
  4.7 7.4 %all-to-all-start = ((bf16[32,88,256]{2,1,0:T(8,128)(2,1)}), bf16[32,88,256]{2,1,0:T(8,128)(2,1)}, u32[]{:S(2)}, u32[]{:S(2)}) async-start(bf16[32,88,256]{2,1,0:T(8,128)(2,1)} %get-tuple-element.34), calls=%async_computation | async-start | bytes 2883584 | tf_op jit(solution)/shard_map/all_to_all | solution.py:451
  12.2 0.0 copy-done
  12.2 0.0 copy-done.4
  12.2 0.0 copy-done.5
  12.2 0.0 copy-done.6
  12.2 0.0 copy-start.1
  12.2 1.4 %copy-done.1 = bf16[32,88,256]{2,1,0:T(8,128)(2,1)S(1)} copy-done((bf16[32,88,256]{2,1,0:T(8,128)(2,1)S(1)}, bf16[32,88,256]{2,1,0:T(8,128)(2,1)}, u32[]{:S(2)}) %copy-start.1) | copy-done | bytes 1441816
  13.6 3.2 %update_momentum.1 = (f32[32,88,256]{2,1,0:T(8,128)}, bf16[32,88,256]{2,1,0:T(8,128)(2,1)S(1)}, s32[64]{0:T(128)S(1)}) custom-call(s32[32]{0:T(128)S(1)} %copy-done.4, s32[32]{0:T(128)S(1)} %copy-done.5, s32[32]{0:T(128)S(1)} %copy-done.6, bf16[32,88,256]{2,1,0:T(8,128)(2,1)S(1)} %copy-done.1, f32[32,88,256]{2,1,0:T(8,128)S(1)} %copy-done), custom_call_target="tpu_custom_call" | custom-call | flops 2883584 | bytes 8650752 | tf_op jit(solution)/shard_map/update_momentum/pallas_call | solution.py:191
  16.8 0.0 copy-start.2
  16.8 1.1 %copy-done.2 = bf16[32,88,256]{2,1,0:T(8,128)(2,1)} copy-done((bf16[32,88,256]{2,1,0:T(8,128)(2,1)}, bf16[32,88,256]{2,1,0:T(8,128)(2,1)S(1)}, u32[]{:S(2)}) %copy-start.2) | copy-done | bytes 1441816
  17.9 27.5 %all-to-all-done.x_ref = bf16[32,88,256]{2,1,0:T(8,128)(2,1)} async-done(((bf16[32,88,256]{2,1,0:T(8,128)(2,1)}), bf16[32,88,256]{2,1,0:T(8,128)(2,1)}, u32[]{:S(2)}, u32[]{:S(2)}) %all-to-all-start) | async-done | bytes 1441824 | tf_op jit(solution)/shard_map/all_to_all | solution.py:451
  45.4 4.6 %all-to-all-start.1 = ((bf16[32,88,256]{2,1,0:T(8,128)(2,1)}), bf16[32,88,256]{2,1,0:T(8,128)(2,1)S(1)}, u32[]{:S(2)}, u32[]{:S(2)}) async-start(bf16[32,88,256]{2,1,0:T(8,128)(2,1)} %copy-done.2), calls=%async_computation.1 | async-start | bytes 2883584 | tf_op jit(solution)/shard_map/all_to_all | solution.py:451
  49.9 8.8 %orthogonalize.2 = (bf16[2,704,1024]{2,1,0:T(8,128)(2,1)}, bf16[4,88,256]{2,1,0:T(8,128)(2,1)S(1)}, bf16[4,88,256]{2,1,0:T(8,128)(2,1)S(1)}, bf16[4,88,256]{2,1,0:T(8,128)(2,1)S(1)}, bf16[4,88,256]{2,1,0:T(8,128)(2,1)S(1)}) custom-call(s32[32]{0:T(128)S(1)} %copy-done.5, bf16[32,88,256]{2,1,0:T(8,128)(2,1)} %all-to-all-done.x_ref), custom_call_target="tpu_custom_call" | custom-call | flops 6643777536 | bytes 4718592 | tf_op jit(solution)/shard_map/orthogonalize/pallas_call | solution.py:343
  58.7 0.3 collective-permute-start
  59.0 1.7 %collective-permute-start.1 = (bf16[4,88,256]{2,1,0:T(8,128)(2,1)S(1)}, bf16[4,88,256]{2,1,0:T(8,128)(2,1)S(1)}, u32[]{:S(2)}, u32[]{:S(2)}) collective-permute-start(bf16[4,88,256]{2,1,0:T(8,128)(2,1)S(1)} %get-tuple-element.39), channel_id=1, source_target_pairs={{0,8},{1,9},{2,10},{3,11},{4,12},{5,13},{6,14},{7,15},{8,0},{9,1},... | collective-permute-start | bytes 540680 | tf_op jit(solution)/shard_map/ppermute | solution.py:457
  60.7 0.0 collective-permute-start.2
  60.7 0.0 collective-permute-done.refs_1_
  60.7 8.8 %collective-permute-done.1.refs_2_ = bf16[4,88,256]{2,1,0:T(8,128)(2,1)S(1)} collective-permute-done((bf16[4,88,256]{2,1,0:T(8,128)(2,1)S(1)}, bf16[4,88,256]{2,1,0:T(8,128)(2,1)S(1)}, u32[]{:S(2)}, u32[]{:S(2)}) %collective-permute-start.1) | collective-permute-done | bytes 180256 | tf_op jit(solution)/shard_map/ppermute | solution.py:457
  69.5 4.2 %collective-permute-done.2.refs_3_ = bf16[4,88,256]{2,1,0:T(8,128)(2,1)S(1)} collective-permute-done((bf16[4,88,256]{2,1,0:T(8,128)(2,1)S(1)}, bf16[4,88,256]{2,1,0:T(8,128)(2,1)S(1)}, u32[]{:S(2)}, u32[]{:S(2)}) %collective-permute-start.2) | collective-permute-done | bytes 180256 | tf_op jit(solution)/shard_map/ppermute | solution.py:457
  73.7 0.8 restage.1
  74.5 3.3 %collective-permute-start.3 = (bf16[4,88,256]{2,1,0:T(8,128)(2,1)}, bf16[4,88,256]{2,1,0:T(8,128)(2,1)S(1)}, u32[]{:S(2)}, u32[]{:S(2)}) collective-permute-start(bf16[4,88,256]{2,1,0:T(8,128)(2,1)} %get-tuple-element.42), channel_id=1, source_target_pairs={{0,1},{1,0},{2,3},{3,2},{4,5},{5,4},{6,7},{7,6},{8,9},{9,8},{10,11... | collective-permute-start | bytes 540680 | tf_op jit(solution)/shard_map/ppermute | solution.py:457
  77.9 1.5 %collective-permute-start.4 = (bf16[4,88,256]{2,1,0:T(8,128)(2,1)}, bf16[4,88,256]{2,1,0:T(8,128)(2,1)S(1)}, u32[]{:S(2)}, u32[]{:S(2)}) collective-permute-start(bf16[4,88,256]{2,1,0:T(8,128)(2,1)} %get-tuple-element.43), channel_id=1, source_target_pairs={{0,16},{1,17},{2,18},{3,19},{4,20},{5,21},{6,22},{7,23},{8,24},{9,... | collective-permute-start | bytes 540680 | tf_op jit(solution)/shard_map/ppermute | solution.py:457
  79.4 0.0 collective-permute-start.5
  79.4 3.8 %all-to-all-done.1.x_ref = bf16[32,88,256]{2,1,0:T(8,128)(2,1)S(1)} async-done(((bf16[32,88,256]{2,1,0:T(8,128)(2,1)}), bf16[32,88,256]{2,1,0:T(8,128)(2,1)S(1)}, u32[]{:S(2)}, u32[]{:S(2)}) %all-to-all-start.1) | async-done | bytes 1441824 | tf_op jit(solution)/shard_map/all_to_all | solution.py:451
  83.2 7.8 %orthogonalize.3 = (bf16[704,1024]{1,0:T(8,128)(2,1)S(1)}, bf16[16,88,256]{2,1,0:T(8,128)(2,1)S(1)}) custom-call(s32[32]{0:T(128)S(1)} %copy-done.5, bf16[32,88,256]{2,1,0:T(8,128)(2,1)S(1)} %all-to-all-done.1.x_ref), custom_call_target="tpu_custom_call" | custom-call | flops 6643777536 | bytes 4718592 | tf_op jit(solution)/shard_map/orthogonalize/pallas_call | solution.py:343
  90.9 0.0 copy-start.3
  90.9 0.9 copy-done.3
  91.8 0.0 collective-permute-done.3.refs_1_
  91.8 0.0 collective-permute-done.4.refs_2_
  91.8 0.0 collective-permute-done.5.refs_3_
  91.8 4.9 %all-to-all-start.2 = ((bf16[16,88,256]{2,1,0:T(8,128)(2,1)}), bf16[16,88,256]{2,1,0:T(8,128)(2,1)S(1)}, u32[]{:S(2)}, u32[]{:S(2)}) async-start(bf16[16,88,256]{2,1,0:T(8,128)(2,1)} %copy-done.3), calls=%async_computation.2 | async-start | bytes 1441792 | tf_op jit(solution)/shard_map/all_to_all | solution.py:451
  96.8 2.3 %store_early.1 = (bf16[2,704,1024]{2,1,0:T(8,128)(2,1)}, bf16[32,88,256]{2,1,0:T(8,128)(2,1)}) custom-call(s32[64]{0:T(128)S(1)} %get-tuple-element.33.list_ref, bf16[704,1024]{1,0:T(8,128)(2,1)S(1)} %get-tuple-element.49.whole_ref, bf16[2,704,1024]{2,1,0:T(8,128)(2,1)} %get-tuple-element.50.owned_in, ...), custom_call_target="tpu_custom_call", output_to_operand_aliasing={{0}: (2, {})} | custom-call | bytes 5767168 | tf_op jit(solution)/shard_map/store_early/pallas_call | solution.py:409
  99.1 8.5 %all-to-all-done.2.back_ref = bf16[16,88,256]{2,1,0:T(8,128)(2,1)S(1)} async-done(((bf16[16,88,256]{2,1,0:T(8,128)(2,1)}), bf16[16,88,256]{2,1,0:T(8,128)(2,1)S(1)}, u32[]{:S(2)}, u32[]{:S(2)}) %all-to-all-start.2) | async-done | bytes 720928 | tf_op jit(solution)/shard_map/all_to_all | solution.py:451
  107.6 1.4 %store_late.1 = bf16[32,88,256]{2,1,0:T(8,128)(2,1)} custom-call(s32[64]{0:T(128)S(1)} %get-tuple-element.33.list_ref, bf16[16,88,256]{2,1,0:T(8,128)(2,1)S(1)} %all-to-all-done.2.back_ref, bf16[32,88,256]{2,1,0:T(8,128)(2,1)} %get-tuple-element.55.update_in), custom_call_target="tpu_custom_call", output_to_operand_aliasing={{}: (2, {})} | custom-call | bytes 1441792 | tf_op jit(solution)/shard_map/store_late/pallas_call | solution.py:437
Async XLA Ops:
  4.7 7.5 %copy-start = (f32[32,88,256]{2,1,0:T(8,128)S(1)}, f32[32,88,256]{2,1,0:T(8,128)}, u32[]{:S(2)}) copy-start(f32[32,88,256]{2,1,0:T(8,128)} %m_ref.3) | copy-start | bytes 8650756
  4.7 7.5 %copy-start.4 = (s32[32]{0:T(128)S(1)}, s32[32]{0:T(128)}, u32[]{:S(2)}) copy-start(s32[32]{0:T(128)} %owner_ref.3) | copy-start | bytes 388
  4.7 7.5 %copy-start.5 = (s32[32]{0:T(128)S(1)}, s32[32]{0:T(128)}, u32[]{:S(2)}) copy-start(s32[32]{0:T(128)} %get-tuple-element.30.other_ref) | copy-start | bytes 388
  4.7 7.5 %copy-start.6 = (s32[32]{0:T(128)S(1)}, s32[32]{0:T(128)}, u32[]{:S(2)}) copy-start(s32[32]{0:T(128)} %get-tuple-element.31.rank_ref) | copy-start | bytes 388
  4.7 40.6 %all-to-all-start = ((bf16[32,88,256]{2,1,0:T(8,128)(2,1)}), bf16[32,88,256]{2,1,0:T(8,128)(2,1)}, u32[]{:S(2)}, u32[]{:S(2)}) async-start(bf16[32,88,256]{2,1,0:T(8,128)(2,1)} %get-tuple-element.34), calls=%async_computation | async-start | bytes 2883584 | tf_op jit(solution)/shard_map/all_to_all | solution.py:451
  12.2 1.4 %copy-start.1 = (bf16[32,88,256]{2,1,0:T(8,128)(2,1)S(1)}, bf16[32,88,256]{2,1,0:T(8,128)(2,1)}, u32[]{:S(2)}) copy-start(bf16[32,88,256]{2,1,0:T(8,128)(2,1)} %g_ref.3) | copy-start | bytes 4325380
  16.8 1.1 %copy-start.2 = (bf16[32,88,256]{2,1,0:T(8,128)(2,1)}, bf16[32,88,256]{2,1,0:T(8,128)(2,1)S(1)}, u32[]{:S(2)}) copy-start(bf16[32,88,256]{2,1,0:T(8,128)(2,1)S(1)} %get-tuple-element.45) | copy-start | bytes 4325380
  45.4 37.8 %all-to-all-start.1 = ((bf16[32,88,256]{2,1,0:T(8,128)(2,1)}), bf16[32,88,256]{2,1,0:T(8,128)(2,1)S(1)}, u32[]{:S(2)}, u32[]{:S(2)}) async-start(bf16[32,88,256]{2,1,0:T(8,128)(2,1)} %copy-done.2), calls=%async_computation.1 | async-start | bytes 2883584 | tf_op jit(solution)/shard_map/all_to_all | solution.py:451
  58.7 2.0 %collective-permute-start = (bf16[4,88,256]{2,1,0:T(8,128)(2,1)S(1)}, bf16[4,88,256]{2,1,0:T(8,128)(2,1)S(1)}, u32[]{:S(2)}, u32[]{:S(2)}) collective-permute-start(bf16[4,88,256]{2,1,0:T(8,128)(2,1)S(1)} %get-tuple-element.38), channel_id=1, source_target_pairs={{0,4},{1,5},{2,6},{3,7},{4,0},{5,1},{6,2},{7,3},{8,12},{9,13},{10,... | collective-permute-start | bytes 540680 | tf_op jit(solution)/shard_map/ppermute | solution.py:457
  59.0 10.5 %collective-permute-start.1 = (bf16[4,88,256]{2,1,0:T(8,128)(2,1)S(1)}, bf16[4,88,256]{2,1,0:T(8,128)(2,1)S(1)}, u32[]{:S(2)}, u32[]{:S(2)}) collective-permute-start(bf16[4,88,256]{2,1,0:T(8,128)(2,1)S(1)} %get-tuple-element.39), channel_id=1, source_target_pairs={{0,8},{1,9},{2,10},{3,11},{4,12},{5,13},{6,14},{7,15},{8,0},{9,1},... | collective-permute-start | bytes 540680 | tf_op jit(solution)/shard_map/ppermute | solution.py:457
  60.7 13.0 %collective-permute-start.2 = (bf16[4,88,256]{2,1,0:T(8,128)(2,1)S(1)}, bf16[4,88,256]{2,1,0:T(8,128)(2,1)S(1)}, u32[]{:S(2)}, u32[]{:S(2)}) collective-permute-start(bf16[4,88,256]{2,1,0:T(8,128)(2,1)S(1)} %get-tuple-element.40), channel_id=1, source_target_pairs={{0,12},{1,13},{2,14},{3,15},{4,8},{5,9},{6,10},{7,11},{8,4},{9,5},... | collective-permute-start | bytes 540680 | tf_op jit(solution)/shard_map/ppermute | solution.py:457
  74.5 17.2 %collective-permute-start.3 = (bf16[4,88,256]{2,1,0:T(8,128)(2,1)}, bf16[4,88,256]{2,1,0:T(8,128)(2,1)S(1)}, u32[]{:S(2)}, u32[]{:S(2)}) collective-permute-start(bf16[4,88,256]{2,1,0:T(8,128)(2,1)} %get-tuple-element.42), channel_id=1, source_target_pairs={{0,1},{1,0},{2,3},{3,2},{4,5},{5,4},{6,7},{7,6},{8,9},{9,8},{10,11... | collective-permute-start | bytes 540680 | tf_op jit(solution)/shard_map/ppermute | solution.py:457
  77.9 13.9 %collective-permute-start.4 = (bf16[4,88,256]{2,1,0:T(8,128)(2,1)}, bf16[4,88,256]{2,1,0:T(8,128)(2,1)S(1)}, u32[]{:S(2)}, u32[]{:S(2)}) collective-permute-start(bf16[4,88,256]{2,1,0:T(8,128)(2,1)} %get-tuple-element.43), channel_id=1, source_target_pairs={{0,16},{1,17},{2,18},{3,19},{4,20},{5,21},{6,22},{7,23},{8,24},{9,... | collective-permute-start | bytes 540680 | tf_op jit(solution)/shard_map/ppermute | solution.py:457
  79.4 12.4 %collective-permute-start.5 = (bf16[4,88,256]{2,1,0:T(8,128)(2,1)}, bf16[4,88,256]{2,1,0:T(8,128)(2,1)}, u32[]{:S(2)}, u32[]{:S(2)}) collective-permute-start(bf16[4,88,256]{2,1,0:T(8,128)(2,1)} %get-tuple-element.44), channel_id=1, source_target_pairs={{0,17},{1,16},{2,19},{3,18},{4,21},{5,20},{6,23},{7,22},{8,25},{9,... | collective-permute-start | bytes 540680 | tf_op jit(solution)/shard_map/ppermute | solution.py:457
  90.9 0.9 copy-start.3
  91.8 15.8 %all-to-all-start.2 = ((bf16[16,88,256]{2,1,0:T(8,128)(2,1)}), bf16[16,88,256]{2,1,0:T(8,128)(2,1)S(1)}, u32[]{:S(2)}, u32[]{:S(2)}) async-start(bf16[16,88,256]{2,1,0:T(8,128)(2,1)} %copy-done.3), calls=%async_computation.2 | async-start | bytes 1441792 | tf_op jit(solution)/shard_map/all_to_all | solution.py:451

commit v16 on v15

--- a/solution.py
+++ b/solution.py
@@ -344,7 +344,12 @@
         functools.partial(ortho_kernel, row_size, col_size, slot),
         in_specs=[SMEM, VMEM],
         out_specs=out_specs,
-        out_shape=[jax.ShapeDtypeStruct(shape, jnp.bfloat16) for shape in out],
+        out_shape=[
+            pltpu.HBM(shape, jnp.bfloat16)
+            if spec is ANYWHERE
+            else jax.ShapeDtypeStruct(shape, jnp.bfloat16)
+            for spec, shape in zip(out_specs, out)
+        ],
         scratch_shapes=scratch_shapes,
         compiler_params=PARAMS,
         cost_estimate=pl.CostEstimate(

time: 109 us -> 109 us (level)
    unnamed x14 -> x12, local copies, waits for them, and re-layouts: 3.37 us -> 2.51 us
where the time goes in v16:
time: 109 us; the launch traced here: 108 us
  waiting for transfers between devices  52.8 us (48%)
  Pallas kernels  28.4 us (26%)
  starting transfers between devices  23.7 us (22%)
  local copies, waits for them, and re-layouts  2.51 us (2%)
    all_to_all x3, waiting for transfers between devices, exchange(): lax.all_to_all(blocks, axes, split_axis=0, concat_axis=0, tiled=True, axi...  39.8 us
    all_to_all x3, starting transfers between devices, exchange(): lax.all_to_all(blocks, axes, split_axis=0, concat_axis=0, tiled=True, axi...  16.9 us
    pallas_call x2, Pallas kernels, orthogonalize(): pl.pallas_call(functools.partial(ortho_kernel, row_size, col_size, slot),...  16.6 us
    ppermute x6, waiting for transfers between devices, swap(): return lax.ppermute(block, AXES, [(d, d ^ offset) for d in range(devices)])  13 us
    ppermute x6, starting transfers between devices, swap(): return lax.ppermute(block, AXES, [(d, d ^ offset) for d in range(devices)])  6.81 us
    pallas_call x1, Pallas kernels, pack(): pl.pallas_call(functools.partial(pack_kernel, chunk, col_size), grid_spec...  4.04 us
    pallas_call x1, Pallas kernels, update_momentum(): pl.pallas_call(functools.partial(momentum_kernel, chunk, col_size), grid_...  3.21 us
    unnamed x12, local copies, waits for them, and re-layouts  2.51 us
  transfers between devices with their start and end apart: 9, of which 5 were waited for; matrix products, arithmetic and copies ran while one was open for 0% of the time, Pallas kernels for 21%

profile of v16, /device:TPU:0, one launch (start us, length us, event | category | flops | bytes accessed | tf_op | source)
XLA Modules:
  0.0 108.2 jit_solution(16675447046881391301)
XLA Ops:
  0.6 4.0 %pack.1 = (bf16[32,88,256]{2,1,0:T(8,128)(2,1)}, s32[32]{0:T(128)}, s32[32]{0:T(128)}) custom-call(s32[32]{0:T(128)} %owner_ref.3, bf16[32,88,256]{2,1,0:T(8,128)(2,1)} %g_ref.3, f32[32,88,256]{2,1,0:T(8,128)} %m_ref.3), custom_call_target="tpu_custom_call" | custom-call | flops 2883584 | bytes 5767168 | tf_op jit(solution)/shard_map/pack/pallas_call | solution.py:118
  4.7 0.0 copy-start
  4.7 0.0 copy-start.3
  4.7 0.0 copy-start.4
  4.7 0.0 copy-start.5
  4.7 7.4 %all-to-all-start = ((bf16[32,88,256]{2,1,0:T(8,128)(2,1)}), bf16[32,88,256]{2,1,0:T(8,128)(2,1)}, u32[]{:S(2)}, u32[]{:S(2)}) async-start(bf16[32,88,256]{2,1,0:T(8,128)(2,1)} %get-tuple-element.34), calls=%async_computation | async-start | bytes 2883584 | tf_op jit(solution)/shard_map/all_to_all | solution.py:456
  12.2 0.0 copy-done
  12.2 0.0 copy-done.3
  12.2 0.0 copy-done.4
  12.2 0.0 copy-done.5
  12.2 0.0 copy-start.1
  12.2 1.4 %copy-done.1 = bf16[32,88,256]{2,1,0:T(8,128)(2,1)S(1)} copy-done((bf16[32,88,256]{2,1,0:T(8,128)(2,1)S(1)}, bf16[32,88,256]{2,1,0:T(8,128)(2,1)}, u32[]{:S(2)}) %copy-start.1) | copy-done | bytes 1441816
  13.6 3.2 %update_momentum.1 = (f32[32,88,256]{2,1,0:T(8,128)}, bf16[32,88,256]{2,1,0:T(8,128)(2,1)S(1)}, s32[64]{0:T(128)S(1)}) custom-call(s32[32]{0:T(128)S(1)} %copy-done.3, s32[32]{0:T(128)S(1)} %copy-done.4, s32[32]{0:T(128)S(1)} %copy-done.5, bf16[32,88,256]{2,1,0:T(8,128)(2,1)S(1)} %copy-done.1, f32[32,88,256]{2,1,0:T(8,128)S(1)} %copy-done), custom_call_target="tpu_custom_call" | custom-call | flops 2883584 | bytes 8650752 | tf_op jit(solution)/shard_map/update_momentum/pallas_call | solution.py:191
  16.8 0.0 copy-start.2
  16.8 1.1 %copy-done.2 = bf16[32,88,256]{2,1,0:T(8,128)(2,1)} copy-done((bf16[32,88,256]{2,1,0:T(8,128)(2,1)}, bf16[32,88,256]{2,1,0:T(8,128)(2,1)S(1)}, u32[]{:S(2)}) %copy-start.2) | copy-done | bytes 1441816
  17.9 27.5 %all-to-all-done.x_ref = bf16[32,88,256]{2,1,0:T(8,128)(2,1)} async-done(((bf16[32,88,256]{2,1,0:T(8,128)(2,1)}), bf16[32,88,256]{2,1,0:T(8,128)(2,1)}, u32[]{:S(2)}, u32[]{:S(2)}) %all-to-all-start) | async-done | bytes 1441824 | tf_op jit(solution)/shard_map/all_to_all | solution.py:456
  45.4 4.6 %all-to-all-start.1 = ((bf16[32,88,256]{2,1,0:T(8,128)(2,1)}), bf16[32,88,256]{2,1,0:T(8,128)(2,1)S(1)}, u32[]{:S(2)}, u32[]{:S(2)}) async-start(bf16[32,88,256]{2,1,0:T(8,128)(2,1)} %copy-done.2), calls=%async_computation.1 | async-start | bytes 2883584 | tf_op jit(solution)/shard_map/all_to_all | solution.py:456
  49.9 8.8 %orthogonalize.2 = (bf16[2,704,1024]{2,1,0:T(8,128)(2,1)}, bf16[4,88,256]{2,1,0:T(8,128)(2,1)S(1)}, bf16[4,88,256]{2,1,0:T(8,128)(2,1)S(1)}, bf16[4,88,256]{2,1,0:T(8,128)(2,1)S(1)}, bf16[4,88,256]{2,1,0:T(8,128)(2,1)S(1)}) custom-call(s32[32]{0:T(128)S(1)} %copy-done.4, bf16[32,88,256]{2,1,0:T(8,128)(2,1)} %all-to-all-done.x_ref), custom_call_target="tpu_custom_call" | custom-call | flops 6643777536 | bytes 4718592 | tf_op jit(solution)/shard_map/orthogonalize/pallas_call | solution.py:343
  58.7 0.3 collective-permute-start
  59.0 1.7 %collective-permute-start.1 = (bf16[4,88,256]{2,1,0:T(8,128)(2,1)S(1)}, bf16[4,88,256]{2,1,0:T(8,128)(2,1)S(1)}, u32[]{:S(2)}, u32[]{:S(2)}) collective-permute-start(bf16[4,88,256]{2,1,0:T(8,128)(2,1)S(1)} %get-tuple-element.39), channel_id=1, source_target_pairs={{0,8},{1,9},{2,10},{3,11},{4,12},{5,13},{6,14},{7,15},{8,0},{9,1},... | collective-permute-start | bytes 540680 | tf_op jit(solution)/shard_map/ppermute | solution.py:462
  60.7 0.0 collective-permute-start.2
  60.7 0.0 collective-permute-done.refs_1_
  60.7 8.8 %collective-permute-done.1.refs_2_ = bf16[4,88,256]{2,1,0:T(8,128)(2,1)S(1)} collective-permute-done((bf16[4,88,256]{2,1,0:T(8,128)(2,1)S(1)}, bf16[4,88,256]{2,1,0:T(8,128)(2,1)S(1)}, u32[]{:S(2)}, u32[]{:S(2)}) %collective-permute-start.1) | collective-permute-done | bytes 180256 | tf_op jit(solution)/shard_map/ppermute | solution.py:462
  69.5 4.2 %collective-permute-done.2.refs_3_ = bf16[4,88,256]{2,1,0:T(8,128)(2,1)S(1)} collective-permute-done((bf16[4,88,256]{2,1,0:T(8,128)(2,1)S(1)}, bf16[4,88,256]{2,1,0:T(8,128)(2,1)S(1)}, u32[]{:S(2)}, u32[]{:S(2)}) %collective-permute-start.2) | collective-permute-done | bytes 180256 | tf_op jit(solution)/shard_map/ppermute | solution.py:462
  73.7 0.8 restage.1
  74.5 3.3 %collective-permute-start.3 = (bf16[4,88,256]{2,1,0:T(8,128)(2,1)}, bf16[4,88,256]{2,1,0:T(8,128)(2,1)S(1)}, u32[]{:S(2)}, u32[]{:S(2)}) collective-permute-start(bf16[4,88,256]{2,1,0:T(8,128)(2,1)} %get-tuple-element.42), channel_id=1, source_target_pairs={{0,1},{1,0},{2,3},{3,2},{4,5},{5,4},{6,7},{7,6},{8,9},{9,8},{10,11... | collective-permute-start | bytes 540680 | tf_op jit(solution)/shard_map/ppermute | solution.py:462
  77.9 1.5 %collective-permute-start.4 = (bf16[4,88,256]{2,1,0:T(8,128)(2,1)}, bf16[4,88,256]{2,1,0:T(8,128)(2,1)S(1)}, u32[]{:S(2)}, u32[]{:S(2)}) collective-permute-start(bf16[4,88,256]{2,1,0:T(8,128)(2,1)} %get-tuple-element.43), channel_id=1, source_target_pairs={{0,16},{1,17},{2,18},{3,19},{4,20},{5,21},{6,22},{7,23},{8,24},{9,... | collective-permute-start | bytes 540680 | tf_op jit(solution)/shard_map/ppermute | solution.py:462
  79.3 0.0 collective-permute-start.5
  79.4 3.8 %all-to-all-done.1.x_ref = bf16[32,88,256]{2,1,0:T(8,128)(2,1)S(1)} async-done(((bf16[32,88,256]{2,1,0:T(8,128)(2,1)}), bf16[32,88,256]{2,1,0:T(8,128)(2,1)S(1)}, u32[]{:S(2)}, u32[]{:S(2)}) %all-to-all-start.1) | async-done | bytes 1441824 | tf_op jit(solution)/shard_map/all_to_all | solution.py:456
  83.2 7.8 %orthogonalize.3 = (bf16[704,1024]{1,0:T(8,128)(2,1)S(1)}, bf16[16,88,256]{2,1,0:T(8,128)(2,1)}) custom-call(s32[32]{0:T(128)S(1)} %copy-done.4, bf16[32,88,256]{2,1,0:T(8,128)(2,1)S(1)} %all-to-all-done.1.x_ref), custom_call_target="tpu_custom_call" | custom-call | flops 6643777536 | bytes 4718592 | tf_op jit(solution)/shard_map/orthogonalize/pallas_call | solution.py:343
  91.0 0.0 collective-permute-done.3.refs_1_
  91.0 0.0 collective-permute-done.4.refs_2_
  91.0 0.0 collective-permute-done.5.refs_3_
  91.0 4.9 %all-to-all-start.2 = ((bf16[16,88,256]{2,1,0:T(8,128)(2,1)}), bf16[16,88,256]{2,1,0:T(8,128)(2,1)S(1)}, u32[]{:S(2)}, u32[]{:S(2)}) async-start(bf16[16,88,256]{2,1,0:T(8,128)(2,1)} %get-tuple-element.48), calls=%async_computation.2 | async-start | bytes 1441792 | tf_op jit(solution)/shard_map/all_to_all | solution.py:456
  96.0 2.3 %store_early.1 = (bf16[2,704,1024]{2,1,0:T(8,128)(2,1)}, bf16[32,88,256]{2,1,0:T(8,128)(2,1)}) custom-call(s32[64]{0:T(128)S(1)} %get-tuple-element.33.list_ref, bf16[704,1024]{1,0:T(8,128)(2,1)S(1)} %get-tuple-element.49.whole_ref, bf16[2,704,1024]{2,1,0:T(8,128)(2,1)} %get-tuple-element.50.owned_in, ...), custom_call_target="tpu_custom_call", output_to_operand_aliasing={{0}: (2, {})} | custom-call | bytes 5767168 | tf_op jit(solution)/shard_map/store_early/pallas_call | solution.py:414
  98.3 8.5 %all-to-all-done.2.back_ref = bf16[16,88,256]{2,1,0:T(8,128)(2,1)S(1)} async-done(((bf16[16,88,256]{2,1,0:T(8,128)(2,1)}), bf16[16,88,256]{2,1,0:T(8,128)(2,1)S(1)}, u32[]{:S(2)}, u32[]{:S(2)}) %all-to-all-start.2) | async-done | bytes 720928 | tf_op jit(solution)/shard_map/all_to_all | solution.py:456
  106.8 1.4 %store_late.1 = bf16[32,88,256]{2,1,0:T(8,128)(2,1)} custom-call(s32[64]{0:T(128)S(1)} %get-tuple-element.33.list_ref, bf16[16,88,256]{2,1,0:T(8,128)(2,1)S(1)} %all-to-all-done.2.back_ref, bf16[32,88,256]{2,1,0:T(8,128)(2,1)} %get-tuple-element.55.update_in), custom_call_target="tpu_custom_call", output_to_operand_aliasing={{}: (2, {})} | custom-call | bytes 1441792 | tf_op jit(solution)/shard_map/store_late/pallas_call | solution.py:442
Async XLA Ops:
  4.7 7.5 %copy-start = (f32[32,88,256]{2,1,0:T(8,128)S(1)}, f32[32,88,256]{2,1,0:T(8,128)}, u32[]{:S(2)}) copy-start(f32[32,88,256]{2,1,0:T(8,128)} %m_ref.3) | copy-start | bytes 8650756
  4.7 7.5 %copy-start.3 = (s32[32]{0:T(128)S(1)}, s32[32]{0:T(128)}, u32[]{:S(2)}) copy-start(s32[32]{0:T(128)} %owner_ref.3) | copy-start | bytes 388
  4.7 7.5 %copy-start.4 = (s32[32]{0:T(128)S(1)}, s32[32]{0:T(128)}, u32[]{:S(2)}) copy-start(s32[32]{0:T(128)} %get-tuple-element.30.other_ref) | copy-start | bytes 388
  4.7 7.5 %copy-start.5 = (s32[32]{0:T(128)S(1)}, s32[32]{0:T(128)}, u32[]{:S(2)}) copy-start(s32[32]{0:T(128)} %get-tuple-element.31.rank_ref) | copy-start | bytes 388
  4.7 40.6 %all-to-all-start = ((bf16[32,88,256]{2,1,0:T(8,128)(2,1)}), bf16[32,88,256]{2,1,0:T(8,128)(2,1)}, u32[]{:S(2)}, u32[]{:S(2)}) async-start(bf16[32,88,256]{2,1,0:T(8,128)(2,1)} %get-tuple-element.34), calls=%async_computation | async-start | bytes 2883584 | tf_op jit(solution)/shard_map/all_to_all | solution.py:456
  12.2 1.4 %copy-start.1 = (bf16[32,88,256]{2,1,0:T(8,128)(2,1)S(1)}, bf16[32,88,256]{2,1,0:T(8,128)(2,1)}, u32[]{:S(2)}) copy-start(bf16[32,88,256]{2,1,0:T(8,128)(2,1)} %g_ref.3) | copy-start | bytes 4325380
  16.8 1.1 %copy-start.2 = (bf16[32,88,256]{2,1,0:T(8,128)(2,1)}, bf16[32,88,256]{2,1,0:T(8,128)(2,1)S(1)}, u32[]{:S(2)}) copy-start(bf16[32,88,256]{2,1,0:T(8,128)(2,1)S(1)} %get-tuple-element.45) | copy-start | bytes 4325380
  45.4 37.8 %all-to-all-start.1 = ((bf16[32,88,256]{2,1,0:T(8,128)(2,1)}), bf16[32,88,256]{2,1,0:T(8,128)(2,1)S(1)}, u32[]{:S(2)}, u32[]{:S(2)}) async-start(bf16[32,88,256]{2,1,0:T(8,128)(2,1)} %copy-done.2), calls=%async_computation.1 | async-start | bytes 2883584 | tf_op jit(solution)/shard_map/all_to_all | solution.py:456
  58.7 2.0 %collective-permute-start = (bf16[4,88,256]{2,1,0:T(8,128)(2,1)S(1)}, bf16[4,88,256]{2,1,0:T(8,128)(2,1)S(1)}, u32[]{:S(2)}, u32[]{:S(2)}) collective-permute-start(bf16[4,88,256]{2,1,0:T(8,128)(2,1)S(1)} %get-tuple-element.38), channel_id=1, source_target_pairs={{0,4},{1,5},{2,6},{3,7},{4,0},{5,1},{6,2},{7,3},{8,12},{9,13},{10,... | collective-permute-start | bytes 540680 | tf_op jit(solution)/shard_map/ppermute | solution.py:462
  59.0 10.5 %collective-permute-start.1 = (bf16[4,88,256]{2,1,0:T(8,128)(2,1)S(1)}, bf16[4,88,256]{2,1,0:T(8,128)(2,1)S(1)}, u32[]{:S(2)}, u32[]{:S(2)}) collective-permute-start(bf16[4,88,256]{2,1,0:T(8,128)(2,1)S(1)} %get-tuple-element.39), channel_id=1, source_target_pairs={{0,8},{1,9},{2,10},{3,11},{4,12},{5,13},{6,14},{7,15},{8,0},{9,1},... | collective-permute-start | bytes 540680 | tf_op jit(solution)/shard_map/ppermute | solution.py:462
  60.7 13.0 %collective-permute-start.2 = (bf16[4,88,256]{2,1,0:T(8,128)(2,1)S(1)}, bf16[4,88,256]{2,1,0:T(8,128)(2,1)S(1)}, u32[]{:S(2)}, u32[]{:S(2)}) collective-permute-start(bf16[4,88,256]{2,1,0:T(8,128)(2,1)S(1)} %get-tuple-element.40), channel_id=1, source_target_pairs={{0,12},{1,13},{2,14},{3,15},{4,8},{5,9},{6,10},{7,11},{8,4},{9,5},... | collective-permute-start | bytes 540680 | tf_op jit(solution)/shard_map/ppermute | solution.py:462
  74.5 16.5 %collective-permute-start.3 = (bf16[4,88,256]{2,1,0:T(8,128)(2,1)}, bf16[4,88,256]{2,1,0:T(8,128)(2,1)S(1)}, u32[]{:S(2)}, u32[]{:S(2)}) collective-permute-start(bf16[4,88,256]{2,1,0:T(8,128)(2,1)} %get-tuple-element.42), channel_id=1, source_target_pairs={{0,1},{1,0},{2,3},{3,2},{4,5},{5,4},{6,7},{7,6},{8,9},{9,8},{10,11... | collective-permute-start | bytes 540680 | tf_op jit(solution)/shard_map/ppermute | solution.py:462
  77.9 13.1 %collective-permute-start.4 = (bf16[4,88,256]{2,1,0:T(8,128)(2,1)}, bf16[4,88,256]{2,1,0:T(8,128)(2,1)S(1)}, u32[]{:S(2)}, u32[]{:S(2)}) collective-permute-start(bf16[4,88,256]{2,1,0:T(8,128)(2,1)} %get-tuple-element.43), channel_id=1, source_target_pairs={{0,16},{1,17},{2,18},{3,19},{4,20},{5,21},{6,22},{7,23},{8,24},{9,... | collective-permute-start | bytes 540680 | tf_op jit(solution)/shard_map/ppermute | solution.py:462
  79.3 11.7 %collective-permute-start.5 = (bf16[4,88,256]{2,1,0:T(8,128)(2,1)}, bf16[4,88,256]{2,1,0:T(8,128)(2,1)}, u32[]{:S(2)}, u32[]{:S(2)}) collective-permute-start(bf16[4,88,256]{2,1,0:T(8,128)(2,1)} %get-tuple-element.44), channel_id=1, source_target_pairs={{0,17},{1,16},{2,19},{3,18},{4,21},{5,20},{6,23},{7,22},{8,25},{9,... | collective-permute-start | bytes 540680 | tf_op jit(solution)/shard_map/ppermute | solution.py:462
  91.0 15.8 %all-to-all-start.2 = ((bf16[16,88,256]{2,1,0:T(8,128)(2,1)}), bf16[16,88,256]{2,1,0:T(8,128)(2,1)S(1)}, u32[]{:S(2)}, u32[]{:S(2)}) async-start(bf16[16,88,256]{2,1,0:T(8,128)(2,1)} %get-tuple-element.48), calls=%async_computation.2 | async-start | bytes 1441792 | tf_op jit(solution)/shard_map/all_to_all | solution.py:456

commit v17 on v16

--- a/solution.py
+++ b/solution.py
@@ -43,7 +43,13 @@
     return new, (grad + momentum_beta * new).astype(jnp.bfloat16)
 
 
-def make_plan(col_size, owner_ref, other_ref, rank_ref, count_ref, list_ref):
+def order_place(d, col_size):
+    width = col_size // HALVES
+    col = d % col_size
+    return d - col + col % width * HALVES + col // width
+
+
+def make_plan(col_size, owner_ref, other_ref, rank_ref, count_ref, list_ref, first_list):
     devices, mats = other_ref.shape[0], rank_ref.shape[0]
 
     def clear(d, _):
@@ -52,12 +58,13 @@
 
     lax.fori_loop(0, devices, clear, 0, unroll=8)
 
-    def rank_matrix(i, _):
+    def rank_matrix(i, found):
         owner = owner_ref[i]
         rank = count_ref[owner]
         rank_ref[i] = rank
         count_ref[owner] = rank + 1
-        return 0
+        first_list[found] = i
+        return found + 1 - rank
 
     lax.fori_loop(0, mats, rank_matrix, 0, unroll=8)
 
@@ -85,31 +92,29 @@
 
 def pack_kernel(
     chunk, col_size, owner_ref, g_ref, m_ref, first_ref, other_ref, rank_ref,
-    count_ref, list_ref, g_s, m_s, sems,
+    count_ref, list_ref, first_list, g_s, m_s, block_s, load_sems, store_sem,
 ):
     mats = rank_ref.shape[0]
-
-    def loads(k):
+    loads = []
+    for k in range(mats // chunk):
         span = pl.ds(k * chunk, chunk)
-        return (
-            pltpu.make_async_copy(g_ref.at[span], g_s.at[span], sems.at[0, k]),
-            pltpu.make_async_copy(m_ref.at[span], m_s.at[span], sems.at[1, k]),
-        )
-
-    for k in range(mats // chunk):
-        for load in loads(k):
-            load.start()
-    make_plan(col_size, owner_ref, other_ref, rank_ref, count_ref, list_ref)
-    for k in range(mats // chunk):
-        for load in loads(k):
-            load.wait()
-        for i in range(k * chunk, (k + 1) * chunk):
-
-            @pl.when(rank_ref[i] == 0)
-            def _():
-                nesterov = nesterov_of(g_s, m_s, i)[1]
-                first_ref[owner_ref[i]] = nesterov
-                first_ref[other_ref[owner_ref[i]]] = nesterov
+        loads += [
+            pltpu.make_async_copy(g_ref.at[span], g_s.at[span], load_sems.at[0, k]),
+            pltpu.make_async_copy(m_ref.at[span], m_s.at[span], load_sems.at[1, k]),
+        ]
+    for load in loads:
+        load.start()
+    make_plan(col_size, owner_ref, other_ref, rank_ref, count_ref, list_ref, first_list)
+    for load in loads:
+        load.wait()
+    for k in range(mats // CAP):
+        i = first_list[k]
+        block_s[k] = nesterov_of(g_s, m_s, i)[1]
+        owner = owner_ref[i]
+        for host in (owner, other_ref[owner]):
+            place = order_place(host, col_size)
+            pltpu.make_async_copy(block_s.at[k], first_ref.at[place], store_sem).start()
+    pltpu.make_async_copy(first_ref, first_ref, store_sem).wait()
 
 
 def pack(gradients, momentum, owner_table, devices, col_size):
@@ -117,23 +122,22 @@
     chunk = 8
     return pl.pallas_call(
         functools.partial(pack_kernel, chunk, col_size),
-        grid_spec=pltpu.PrefetchScalarGridSpec(
-            num_scalar_prefetch=1,
-            grid=(1,),
-            in_specs=[ANYWHERE, ANYWHERE],
-            out_specs=[whole((devices, rows, cols)), SMEM, SMEM],
-            scratch_shapes=[
-                pltpu.SMEM((devices,), jnp.int32),
-                pltpu.SMEM((2 * HALVES * devices,), jnp.int32),
-                pltpu.VMEM(gradients.shape, gradients.dtype),
-                pltpu.VMEM(momentum.shape, momentum.dtype),
-                pltpu.SemaphoreType.DMA((2, mats // chunk)),
-            ],
-        ),
+        in_specs=[SMEM, ANYWHERE, ANYWHERE],
+        out_specs=[ANYWHERE, SMEM, SMEM],
         out_shape=[
-            jax.ShapeDtypeStruct((devices, rows, cols), jnp.bfloat16),
+            pltpu.HBM((devices, rows, cols), jnp.bfloat16),
             jax.ShapeDtypeStruct((devices,), jnp.int32),
             jax.ShapeDtypeStruct((mats,), jnp.int32),
+        ],
+        scratch_shapes=[
+            pltpu.SMEM((devices,), jnp.int32),
+            pltpu.SMEM((2 * HALVES * devices,), jnp.int32),
+            pltpu.SMEM((mats,), jnp.int32),
+            pltpu.VMEM(gradients.shape, gradients.dtype),
+            pltpu.VMEM(momentum.shape, momentum.dtype),
+            pltpu.VMEM((mats // CAP, rows, cols), jnp.bfloat16),
+            pltpu.SemaphoreType.DMA((2, mats // chunk)),
+            pltpu.SemaphoreType.DMA(()),
         ],
         compiler_params=PACK_PARAMS,
         cost_estimate=pl.CostEstimate(
@@ -165,8 +169,8 @@
 
         @pl.when(rank_ref[i] == 1)
         def _():
-            second_ref[owner] = nesterov
-            second_ref[other_ref[owner]] = nesterov
+            second_ref[order_place(owner, col_size)] = nesterov
+            second_ref[order_place(other_ref[owner], col_size)] = nesterov
 
         near = (owner % col_size) // width == col // width
         host = jnp.where(near, owner, other_ref[owner])
@@ -229,7 +233,7 @@
     total = 0.0
     for r in range(row_size):
         for c in range(col_size):
-            block = x_ref[r * col_size + c]
+            block = x_ref[order_place(r * col_size + c, col_size)]
             x_s[r * rows : (r + 1) * rows, c * cols : (c + 1) * cols] = block
             wide = block.astype(jnp.float32)
             total = total + sum_rows(wide * wide)
@@ -472,12 +476,13 @@
         for half in range(HALVES)
     ]
     first, other, rank = pack(gradients, momentum, owner_table, devices, col_size)
-    arrived_first = exchange(first, AXES)
+    order = sorted(range(devices), key=lambda d: order_place(d, col_size))
+    arrived_first = exchange(first, AXES, [order])
     new_momentum, second, places = update_momentum(
         gradients, momentum, owner_table, other, rank, col_size
     )
     arrived_first, second = lax.optimization_barrier((arrived_first, second))
-    arrived_second = exchange(second, AXES)
+    arrived_second = exchange(second, AXES, [order])
     owned, *back_first = orthogonalize(0, other, arrived_first, row_size, col_size)
     low = [back_first[0]] + [
         swap(back_first[k], k * col_size, devices) for k in range(1, LOW)

time: 109 us -> 112 us (1.028)
  waiting for transfers between devices: 52.8 us -> 58 us
  starting transfers between devices: 23.7 us -> 20.6 us
    all_to_all x3, waiting for transfers between devices: 39.8 us -> 45.1 us  [exchange(): lax.all_to_all(blocks, axes, split_axis=0, concat_axis=0, tiled=True, axi...]
    all_to_all x3, starting transfers between devices: 16.9 us -> 13.7 us  [exchange(): lax.all_to_all(blocks, axes, split_axis=0, concat_axis=0, tiled=True, axi...]
where the time goes in v17:
time: 112 us; the launch traced here: 111 us
  waiting for transfers between devices  58 us (52%)
  Pallas kernels  29.2 us (26%)
  starting transfers between devices  20.6 us (18%)
  local copies, waits for them, and re-layouts  2.51 us (2%)
    all_to_all x3, waiting for transfers between devices, exchange(): lax.all_to_all(blocks, axes, split_axis=0, concat_axis=0, tiled=True, axi...  45.1 us
    pallas_call x2, Pallas kernels, orthogonalize(): pl.pallas_call(functools.partial(ortho_kernel, row_size, col_size, slot),...  16.6 us
    all_to_all x3, starting transfers between devices, exchange(): lax.all_to_all(blocks, axes, split_axis=0, concat_axis=0, tiled=True, axi...  13.7 us
    ppermute x6, waiting for transfers between devices, swap(): return lax.ppermute(block, AXES, [(d, d ^ offset) for d in range(devices)])  12.9 us
    ppermute x6, starting transfers between devices, swap(): return lax.ppermute(block, AXES, [(d, d ^ offset) for d in range(devices)])  6.92 us
    pallas_call x1, Pallas kernels, pack(): pl.pallas_call(functools.partial(pack_kernel, chunk, col_size), in_specs=...  4.56 us
    pallas_call x1, Pallas kernels, update_momentum(): pl.pallas_call(functools.partial(momentum_kernel, chunk, col_size), grid_...  3.49 us
    unnamed x12, local copies, waits for them, and re-layouts  2.51 us
  transfers between devices with their start and end apart: 9, of which 5 were waited for; matrix products, arithmetic and copies ran while one was open for 0% of the time, Pallas kernels for 21%

profile of v17, /device:TPU:0, one launch (start us, length us, event | category | flops | bytes accessed | tf_op | source)
XLA Modules:
  0.0 111.1 jit_solution(9358472478189772475)
XLA Ops:
  0.6 4.6 %pack.1 = (bf16[32,88,256]{2,1,0:T(8,128)(2,1)}, s32[32]{0:T(128)}, s32[32]{0:T(128)}) custom-call(s32[32]{0:T(128)} %owner_ref.3, bf16[32,88,256]{2,1,0:T(8,128)(2,1)} %g_ref.3, f32[32,88,256]{2,1,0:T(8,128)} %m_ref.3), custom_call_target="tpu_custom_call" | custom-call | flops 2883584 | bytes 5767168 | tf_op jit(solution)/shard_map/pack/pallas_call | solution.py:123
  5.2 0.0 copy-start
  5.2 0.0 copy-start.3
  5.2 0.0 copy-start.4
  5.2 0.0 copy-start.5
  5.2 7.4 %all-to-all-start = ((bf16[32,88,256]{2,1,0:T(8,128)(2,1)}), bf16[32,88,256]{2,1,0:T(8,128)(2,1)}, u32[]{:S(2)}, u32[]{:S(2)}) async-start(bf16[32,88,256]{2,1,0:T(8,128)(2,1)} %get-tuple-element.34), calls=%async_computation | async-start | bytes 2883584 | tf_op jit(solution)/shard_map/all_to_all | solution.py:460
  12.7 0.0 copy-done
  12.7 0.0 copy-done.3
  12.7 0.0 copy-done.4
  12.7 0.0 copy-done.5
  12.7 0.0 copy-start.1
  12.7 1.4 %copy-done.1 = bf16[32,88,256]{2,1,0:T(8,128)(2,1)S(1)} copy-done((bf16[32,88,256]{2,1,0:T(8,128)(2,1)S(1)}, bf16[32,88,256]{2,1,0:T(8,128)(2,1)}, u32[]{:S(2)}) %copy-start.1) | copy-done | bytes 1441816
  14.1 3.5 %update_momentum.1 = (f32[32,88,256]{2,1,0:T(8,128)}, bf16[32,88,256]{2,1,0:T(8,128)(2,1)S(1)}, s32[64]{0:T(128)S(1)}) custom-call(s32[32]{0:T(128)S(1)} %copy-done.3, s32[32]{0:T(128)S(1)} %copy-done.4, s32[32]{0:T(128)S(1)} %copy-done.5, bf16[32,88,256]{2,1,0:T(8,128)(2,1)S(1)} %copy-done.1, f32[32,88,256]{2,1,0:T(8,128)S(1)} %copy-done), custom_call_target="tpu_custom_call" | custom-call | flops 2883584 | bytes 8650752 | tf_op jit(solution)/shard_map/update_momentum/pallas_call | solution.py:195
  17.6 0.0 copy-start.2
  17.6 1.1 %copy-done.2 = bf16[32,88,256]{2,1,0:T(8,128)(2,1)} copy-done((bf16[32,88,256]{2,1,0:T(8,128)(2,1)}, bf16[32,88,256]{2,1,0:T(8,128)(2,1)S(1)}, u32[]{:S(2)}) %copy-start.2) | copy-done | bytes 1441816
  18.7 30.0 %all-to-all-done.x_ref = bf16[32,88,256]{2,1,0:T(8,128)(2,1)} async-done(((bf16[32,88,256]{2,1,0:T(8,128)(2,1)}), bf16[32,88,256]{2,1,0:T(8,128)(2,1)}, u32[]{:S(2)}, u32[]{:S(2)}) %all-to-all-start) | async-done | bytes 1441824 | tf_op jit(solution)/shard_map/all_to_all | solution.py:460
  48.7 2.7 %all-to-all-start.1 = ((bf16[32,88,256]{2,1,0:T(8,128)(2,1)}), bf16[32,88,256]{2,1,0:T(8,128)(2,1)S(1)}, u32[]{:S(2)}, u32[]{:S(2)}) async-start(bf16[32,88,256]{2,1,0:T(8,128)(2,1)} %copy-done.2), calls=%async_computation.1 | async-start | bytes 2883584 | tf_op jit(solution)/shard_map/all_to_all | solution.py:460
  51.4 8.8 %orthogonalize.2 = (bf16[2,704,1024]{2,1,0:T(8,128)(2,1)}, bf16[4,88,256]{2,1,0:T(8,128)(2,1)S(1)}, bf16[4,88,256]{2,1,0:T(8,128)(2,1)S(1)}, bf16[4,88,256]{2,1,0:T(8,128)(2,1)S(1)}, bf16[4,88,256]{2,1,0:T(8,128)(2,1)S(1)}) custom-call(s32[32]{0:T(128)S(1)} %copy-done.4, bf16[32,88,256]{2,1,0:T(8,128)(2,1)} %all-to-all-done.x_ref), custom_call_target="tpu_custom_call" | custom-call | flops 6643777536 | bytes 4718592 | tf_op jit(solution)/shard_map/orthogonalize/pallas_call | solution.py:347
  60.1 0.2 collective-permute-start
  60.3 1.7 %collective-permute-start.1 = (bf16[4,88,256]{2,1,0:T(8,128)(2,1)S(1)}, bf16[4,88,256]{2,1,0:T(8,128)(2,1)S(1)}, u32[]{:S(2)}, u32[]{:S(2)}) collective-permute-start(bf16[4,88,256]{2,1,0:T(8,128)(2,1)S(1)} %get-tuple-element.39), channel_id=1, source_target_pairs={{0,8},{1,9},{2,10},{3,11},{4,12},{5,13},{6,14},{7,15},{8,0},{9,1},... | collective-permute-start | bytes 540680 | tf_op jit(solution)/shard_map/ppermute | solution.py:466
  62.0 0.1 collective-permute-start.2
  62.1 0.0 collective-permute-done.refs_1_
  62.1 9.0 %collective-permute-done.1.refs_2_ = bf16[4,88,256]{2,1,0:T(8,128)(2,1)S(1)} collective-permute-done((bf16[4,88,256]{2,1,0:T(8,128)(2,1)S(1)}, bf16[4,88,256]{2,1,0:T(8,128)(2,1)S(1)}, u32[]{:S(2)}, u32[]{:S(2)}) %collective-permute-start.1) | collective-permute-done | bytes 180256 | tf_op jit(solution)/shard_map/ppermute | solution.py:466
  71.1 3.9 %collective-permute-done.2.refs_3_ = bf16[4,88,256]{2,1,0:T(8,128)(2,1)S(1)} collective-permute-done((bf16[4,88,256]{2,1,0:T(8,128)(2,1)S(1)}, bf16[4,88,256]{2,1,0:T(8,128)(2,1)S(1)}, u32[]{:S(2)}, u32[]{:S(2)}) %collective-permute-start.2) | collective-permute-done | bytes 180256 | tf_op jit(solution)/shard_map/ppermute | solution.py:466
  75.0 0.8 restage.1
  75.8 3.5 %collective-permute-start.3 = (bf16[4,88,256]{2,1,0:T(8,128)(2,1)}, bf16[4,88,256]{2,1,0:T(8,128)(2,1)S(1)}, u32[]{:S(2)}, u32[]{:S(2)}) collective-permute-start(bf16[4,88,256]{2,1,0:T(8,128)(2,1)} %get-tuple-element.42), channel_id=1, source_target_pairs={{0,1},{1,0},{2,3},{3,2},{4,5},{5,4},{6,7},{7,6},{8,9},{9,8},{10,11... | collective-permute-start | bytes 540680 | tf_op jit(solution)/shard_map/ppermute | solution.py:466
  79.3 1.5 %collective-permute-start.4 = (bf16[4,88,256]{2,1,0:T(8,128)(2,1)}, bf16[4,88,256]{2,1,0:T(8,128)(2,1)S(1)}, u32[]{:S(2)}, u32[]{:S(2)}) collective-permute-start(bf16[4,88,256]{2,1,0:T(8,128)(2,1)} %get-tuple-element.43), channel_id=1, source_target_pairs={{0,16},{1,17},{2,18},{3,19},{4,20},{5,21},{6,22},{7,23},{8,24},{9,... | collective-permute-start | bytes 540680 | tf_op jit(solution)/shard_map/ppermute | solution.py:466
  80.8 0.0 collective-permute-start.5
  80.8 6.7 %all-to-all-done.1.x_ref = bf16[32,88,256]{2,1,0:T(8,128)(2,1)S(1)} async-done(((bf16[32,88,256]{2,1,0:T(8,128)(2,1)}), bf16[32,88,256]{2,1,0:T(8,128)(2,1)S(1)}, u32[]{:S(2)}, u32[]{:S(2)}) %all-to-all-start.1) | async-done | bytes 1441824 | tf_op jit(solution)/shard_map/all_to_all | solution.py:460
  87.5 7.8 %orthogonalize.3 = (bf16[704,1024]{1,0:T(8,128)(2,1)S(1)}, bf16[16,88,256]{2,1,0:T(8,128)(2,1)}) custom-call(s32[32]{0:T(128)S(1)} %copy-done.4, bf16[32,88,256]{2,1,0:T(8,128)(2,1)S(1)} %all-to-all-done.1.x_ref), custom_call_target="tpu_custom_call" | custom-call | flops 6643777536 | bytes 4718592 | tf_op jit(solution)/shard_map/orthogonalize/pallas_call | solution.py:347
  95.3 0.0 collective-permute-done.3.refs_1_
  95.3 0.0 collective-permute-done.4.refs_2_
  95.3 0.0 collective-permute-done.5.refs_3_
  95.3 3.6 %all-to-all-start.2 = ((bf16[16,88,256]{2,1,0:T(8,128)(2,1)}), bf16[16,88,256]{2,1,0:T(8,128)(2,1)S(1)}, u32[]{:S(2)}, u32[]{:S(2)}) async-start(bf16[16,88,256]{2,1,0:T(8,128)(2,1)} %get-tuple-element.48), calls=%async_computation.2 | async-start | bytes 1441792 | tf_op jit(solution)/shard_map/all_to_all | solution.py:460
  99.0 2.3 %store_early.1 = (bf16[2,704,1024]{2,1,0:T(8,128)(2,1)}, bf16[32,88,256]{2,1,0:T(8,128)(2,1)}) custom-call(s32[64]{0:T(128)S(1)} %get-tuple-element.33.list_ref, bf16[704,1024]{1,0:T(8,128)(2,1)S(1)} %get-tuple-element.49.whole_ref, bf16[2,704,1024]{2,1,0:T(8,128)(2,1)} %get-tuple-element.50.owned_in, ...), custom_call_target="tpu_custom_call", output_to_operand_aliasing={{0}: (2, {})} | custom-call | bytes 5767168 | tf_op jit(solution)/shard_map/store_early/pallas_call | solution.py:418
  101.3 8.4 %all-to-all-done.2.back_ref = bf16[16,88,256]{2,1,0:T(8,128)(2,1)S(1)} async-done(((bf16[16,88,256]{2,1,0:T(8,128)(2,1)}), bf16[16,88,256]{2,1,0:T(8,128)(2,1)S(1)}, u32[]{:S(2)}, u32[]{:S(2)}) %all-to-all-start.2) | async-done | bytes 720928 | tf_op jit(solution)/shard_map/all_to_all | solution.py:460
  109.7 1.4 %store_late.1 = bf16[32,88,256]{2,1,0:T(8,128)(2,1)} custom-call(s32[64]{0:T(128)S(1)} %get-tuple-element.33.list_ref, bf16[16,88,256]{2,1,0:T(8,128)(2,1)S(1)} %all-to-all-done.2.back_ref, bf16[32,88,256]{2,1,0:T(8,128)(2,1)} %get-tuple-element.55.update_in), custom_call_target="tpu_custom_call", output_to_operand_aliasing={{}: (2, {})} | custom-call | bytes 1441792 | tf_op jit(solution)/shard_map/store_late/pallas_call | solution.py:446
Async XLA Ops:
  5.2 7.5 %copy-start = (f32[32,88,256]{2,1,0:T(8,128)S(1)}, f32[32,88,256]{2,1,0:T(8,128)}, u32[]{:S(2)}) copy-start(f32[32,88,256]{2,1,0:T(8,128)} %m_ref.3) | copy-start | bytes 8650756
  5.2 7.5 %copy-start.3 = (s32[32]{0:T(128)S(1)}, s32[32]{0:T(128)}, u32[]{:S(2)}) copy-start(s32[32]{0:T(128)} %owner_ref.3) | copy-start | bytes 388
  5.2 7.5 %copy-start.4 = (s32[32]{0:T(128)S(1)}, s32[32]{0:T(128)}, u32[]{:S(2)}) copy-start(s32[32]{0:T(128)} %get-tuple-element.30.other_ref) | copy-start | bytes 388
  5.2 7.5 %copy-start.5 = (s32[32]{0:T(128)S(1)}, s32[32]{0:T(128)}, u32[]{:S(2)}) copy-start(s32[32]{0:T(128)} %get-tuple-element.31.rank_ref) | copy-start | bytes 388
  5.2 43.4 %all-to-all-start = ((bf16[32,88,256]{2,1,0:T(8,128)(2,1)}), bf16[32,88,256]{2,1,0:T(8,128)(2,1)}, u32[]{:S(2)}, u32[]{:S(2)}) async-start(bf16[32,88,256]{2,1,0:T(8,128)(2,1)} %get-tuple-element.34), calls=%async_computation | async-start | bytes 2883584 | tf_op jit(solution)/shard_map/all_to_all | solution.py:460
  12.7 1.4 %copy-start.1 = (bf16[32,88,256]{2,1,0:T(8,128)(2,1)S(1)}, bf16[32,88,256]{2,1,0:T(8,128)(2,1)}, u32[]{:S(2)}) copy-start(bf16[32,88,256]{2,1,0:T(8,128)(2,1)} %g_ref.3) | copy-start | bytes 4325380
  17.6 1.1 %copy-start.2 = (bf16[32,88,256]{2,1,0:T(8,128)(2,1)}, bf16[32,88,256]{2,1,0:T(8,128)(2,1)S(1)}, u32[]{:S(2)}) copy-start(bf16[32,88,256]{2,1,0:T(8,128)(2,1)S(1)} %get-tuple-element.45) | copy-start | bytes 4325380
  48.7 38.8 %all-to-all-start.1 = ((bf16[32,88,256]{2,1,0:T(8,128)(2,1)}), bf16[32,88,256]{2,1,0:T(8,128)(2,1)S(1)}, u32[]{:S(2)}, u32[]{:S(2)}) async-start(bf16[32,88,256]{2,1,0:T(8,128)(2,1)} %copy-done.2), calls=%async_computation.1 | async-start | bytes 2883584 | tf_op jit(solution)/shard_map/all_to_all | solution.py:460
  60.1 2.0 %collective-permute-start = (bf16[4,88,256]{2,1,0:T(8,128)(2,1)S(1)}, bf16[4,88,256]{2,1,0:T(8,128)(2,1)S(1)}, u32[]{:S(2)}, u32[]{:S(2)}) collective-permute-start(bf16[4,88,256]{2,1,0:T(8,128)(2,1)S(1)} %get-tuple-element.38), channel_id=1, source_target_pairs={{0,4},{1,5},{2,6},{3,7},{4,0},{5,1},{6,2},{7,3},{8,12},{9,13},{10,... | collective-permute-start | bytes 540680 | tf_op jit(solution)/shard_map/ppermute | solution.py:466
  60.3 10.7 %collective-permute-start.1 = (bf16[4,88,256]{2,1,0:T(8,128)(2,1)S(1)}, bf16[4,88,256]{2,1,0:T(8,128)(2,1)S(1)}, u32[]{:S(2)}, u32[]{:S(2)}) collective-permute-start(bf16[4,88,256]{2,1,0:T(8,128)(2,1)S(1)} %get-tuple-element.39), channel_id=1, source_target_pairs={{0,8},{1,9},{2,10},{3,11},{4,12},{5,13},{6,14},{7,15},{8,0},{9,1},... | collective-permute-start | bytes 540680 | tf_op jit(solution)/shard_map/ppermute | solution.py:466
  62.0 13.0 %collective-permute-start.2 = (bf16[4,88,256]{2,1,0:T(8,128)(2,1)S(1)}, bf16[4,88,256]{2,1,0:T(8,128)(2,1)S(1)}, u32[]{:S(2)}, u32[]{:S(2)}) collective-permute-start(bf16[4,88,256]{2,1,0:T(8,128)(2,1)S(1)} %get-tuple-element.40), channel_id=1, source_target_pairs={{0,12},{1,13},{2,14},{3,15},{4,8},{5,9},{6,10},{7,11},{8,4},{9,5},... | collective-permute-start | bytes 540680 | tf_op jit(solution)/shard_map/ppermute | solution.py:466
  75.8 19.5 %collective-permute-start.3 = (bf16[4,88,256]{2,1,0:T(8,128)(2,1)}, bf16[4,88,256]{2,1,0:T(8,128)(2,1)S(1)}, u32[]{:S(2)}, u32[]{:S(2)}) collective-permute-start(bf16[4,88,256]{2,1,0:T(8,128)(2,1)} %get-tuple-element.42), channel_id=1, source_target_pairs={{0,1},{1,0},{2,3},{3,2},{4,5},{5,4},{6,7},{7,6},{8,9},{9,8},{10,11... | collective-permute-start | bytes 540680 | tf_op jit(solution)/shard_map/ppermute | solution.py:466
  79.3 16.0 %collective-permute-start.4 = (bf16[4,88,256]{2,1,0:T(8,128)(2,1)}, bf16[4,88,256]{2,1,0:T(8,128)(2,1)S(1)}, u32[]{:S(2)}, u32[]{:S(2)}) collective-permute-start(bf16[4,88,256]{2,1,0:T(8,128)(2,1)} %get-tuple-element.43), channel_id=1, source_target_pairs={{0,16},{1,17},{2,18},{3,19},{4,20},{5,21},{6,22},{7,23},{8,24},{9,... | collective-permute-start | bytes 540680 | tf_op jit(solution)/shard_map/ppermute | solution.py:466
  80.8 14.6 %collective-permute-start.5 = (bf16[4,88,256]{2,1,0:T(8,128)(2,1)}, bf16[4,88,256]{2,1,0:T(8,128)(2,1)}, u32[]{:S(2)}, u32[]{:S(2)}) collective-permute-start(bf16[4,88,256]{2,1,0:T(8,128)(2,1)} %get-tuple-element.44), channel_id=1, source_target_pairs={{0,17},{1,16},{2,19},{3,18},{4,21},{5,20},{6,23},{7,22},{8,25},{9,... | collective-permute-start | bytes 540680 | tf_op jit(solution)/shard_map/ppermute | solution.py:466
  95.3 14.4 %all-to-all-start.2 = ((bf16[16,88,256]{2,1,0:T(8,128)(2,1)}), bf16[16,88,256]{2,1,0:T(8,128)(2,1)S(1)}, u32[]{:S(2)}, u32[]{:S(2)}) async-start(bf16[16,88,256]{2,1,0:T(8,128)(2,1)} %get-tuple-element.48), calls=%async_computation.2 | async-start | bytes 1441792 | tf_op jit(solution)/shard_map/all_to_all | solution.py:460

commit v18 on v16

--- a/solution.py
+++ b/solution.py
@@ -43,7 +43,7 @@
     return new, (grad + momentum_beta * new).astype(jnp.bfloat16)
 
 
-def make_plan(col_size, owner_ref, other_ref, rank_ref, count_ref, list_ref):
+def make_plan(col_size, owner_ref, other_ref, rank_ref, count_ref, list_ref, first_list):
     devices, mats = other_ref.shape[0], rank_ref.shape[0]
 
     def clear(d, _):
@@ -52,12 +52,13 @@
 
     lax.fori_loop(0, devices, clear, 0, unroll=8)
 
-    def rank_matrix(i, _):
+    def rank_matrix(i, found):
         owner = owner_ref[i]
         rank = count_ref[owner]
         rank_ref[i] = rank
         count_ref[owner] = rank + 1
-        return 0
+        first_list[found] = i
+        return found + 1 - rank
 
     lax.fori_loop(0, mats, rank_matrix, 0, unroll=8)
 
@@ -85,31 +86,27 @@
 
 def pack_kernel(
     chunk, col_size, owner_ref, g_ref, m_ref, first_ref, other_ref, rank_ref,
-    count_ref, list_ref, g_s, m_s, sems,
+    count_ref, list_ref, first_list, g_s, m_s, sems,
 ):
     mats = rank_ref.shape[0]
 
-    def loads(k):
+    loads = []
+    for k in range(mats // chunk):
         span = pl.ds(k * chunk, chunk)
-        return (
+        loads += [
             pltpu.make_async_copy(g_ref.at[span], g_s.at[span], sems.at[0, k]),
             pltpu.make_async_copy(m_ref.at[span], m_s.at[span], sems.at[1, k]),
-        )
-
-    for k in range(mats // chunk):
-        for load in loads(k):
-            load.start()
-    make_plan(col_size, owner_ref, other_ref, rank_ref, count_ref, list_ref)
-    for k in range(mats // chunk):
-        for load in loads(k):
-            load.wait()
-        for i in range(k * chunk, (k + 1) * chunk):
-
-            @pl.when(rank_ref[i] == 0)
-            def _():
-                nesterov = nesterov_of(g_s, m_s, i)[1]
-                first_ref[owner_ref[i]] = nesterov
-                first_ref[other_ref[owner_ref[i]]] = nesterov
+        ]
+    for load in loads:
+        load.start()
+    make_plan(col_size, owner_ref, other_ref, rank_ref, count_ref, list_ref, first_list)
+    for load in loads:
+        load.wait()
+    for k in range(mats // CAP):
+        i = first_list[k]
+        _, nesterov = nesterov_of(g_s, m_s, i)
+        first_ref[owner_ref[i]] = nesterov
+        first_ref[other_ref[owner_ref[i]]] = nesterov
 
 
 def pack(gradients, momentum, owner_table, devices, col_size):
@@ -125,6 +122,7 @@
             scratch_shapes=[
                 pltpu.SMEM((devices,), jnp.int32),
                 pltpu.SMEM((2 * HALVES * devices,), jnp.int32),
+                pltpu.SMEM((mats,), jnp.int32),
                 pltpu.VMEM(gradients.shape, gradients.dtype),
                 pltpu.VMEM(momentum.shape, momentum.dtype),
                 pltpu.SemaphoreType.DMA((2, mats // chunk)),
@@ -237,33 +235,39 @@
     return 1.0 / (jnp.sqrt(jnp.sum(total, keepdims=True)) + epsilon)
 
 
-def newton_schulz(height, tiles, inverse, x_s, y_s, gram_s, write):
-    padded, width = x_s.shape
-    tile = height // tiles
-    update_scale = 0.2 * math.sqrt(max(height, width))
+def update_scale(height, width):
+    return 0.2 * math.sqrt(max(height, width))
+
+
+def newton_schulz(height, inverse, x_s, y_s, gram_s, finish):
+    padded = x_s.shape[0]
+    tile = height // TILES
     for ref in (y_s, gram_s):
         ref[height:, :] = jnp.zeros((padded - height, ref.shape[1]), ref.dtype)
     for iteration in range(ITERS):
         src = x_s if iteration == 0 else y_s
-        for t in range(tiles):
+        for t in range(TILES):
             span = slice(t * tile, (t + 1) * tile)
             gram = matmul(src[span, :], src[...], 1)
             if iteration == 0:
                 gram = gram * (inverse * inverse)
             gram_s[span, :] = gram.astype(jnp.bfloat16)
-        for t in range(tiles):
+        for t in range(TILES):
             span = slice(t * tile, (t + 1) * tile)
             square = matmul(gram_s[span, :], gram_s[...], 0)
             mixing = coef_b * gram_s[span, :].astype(jnp.float32) + coef_c * square
-            combined = coef_a * src[span, :].astype(jnp.float32) + matmul(
-                mixing.astype(jnp.bfloat16), src[...], 0
-            )
-            if iteration == 0:
-                combined = combined * inverse
+            mixing = mixing.astype(jnp.bfloat16)
             if iteration + 1 < ITERS:
+                combined = combine(src, span, slice(None), mixing)
+                if iteration == 0:
+                    combined = combined * inverse
                 y_s[span, :] = combined.astype(jnp.bfloat16)
             else:
-                write(t, (update_scale * combined).astype(jnp.bfloat16))
+                finish(t, span, mixing)
+
+
+def combine(src, span, columns, mixing):
+    return coef_a * src[span, columns].astype(jnp.float32) + matmul(mixing, src[:, columns], 0)
 
 
 def stage_place(row_offset, col_offset, row_size, width):
@@ -276,48 +280,52 @@
     width = col_size // HALVES
     places = row_size * width
     height = rows * row_size
-    tiles = TILES
-    tile = height // tiles
+    tile = height // TILES
     if slot:
-        whole_ref, out_ref, x_s, y_s, gram_s, back_ref, sems = refs
+        y_s, mix_ref, out_ref, x_s, gram_s, back_ref, sems = refs
     else:
         owned_ref, low_refs = refs[0], refs[1 : 1 + LOW]
-        x_s, y_s, gram_s, back_ref, sems, whole_ref = refs[1 + LOW :]
+        x_s, gram_s, back_ref, sems, y_s, whole_ref = refs[1 + LOW :]
     row, col = lax.axis_index("dp"), lax.axis_index("owner")
     me = row * col_size + col
-    owns = other_ref[me] != me
-    low = col < width
     inverse = gather_blocks(x_ref, x_s, row_size, col_size)
+    scale = update_scale(height, cols * col_size)
 
     def copy_out(t):
         if slot:
-            span = pl.ds(t * (places // tiles), places // tiles)
+            span = pl.ds(t * (places // TILES), places // TILES)
             return pltpu.make_async_copy(back_ref.at[span], out_ref.at[span], sems.at[t])
         span = pl.ds(t * tile, tile)
         return pltpu.make_async_copy(whole_ref.at[span], owned_ref.at[slot, span], sems.at[t])
 
-    def write(t, result):
-        whole_ref[t * tile : (t + 1) * tile, :] = jnp.where(owns, result, jnp.zeros_like(result))
-        for j in range(row_size // tiles):
-            block = result[j * rows : (j + 1) * rows, :]
-            r = t * (row_size // tiles) + j
+    def finish(t, span, mixing):
+        if slot:
+            mix_ref[span, :] = mixing
+            near = pl.ds(pl.multiple_of(col // width * (width * cols), width * cols), width * cols)
+            result = (scale * combine(y_s, span, near, mixing)).astype(jnp.bfloat16)
+        else:
+            result = (scale * combine(y_s, span, slice(None), mixing)).astype(jnp.bfloat16)
+            owns = other_ref[me] != me
+            whole_ref[span, :] = jnp.where(owns, result, jnp.zeros_like(result))
+            half = width * cols
+            result = jnp.where(col < width, result[:, :half], result[:, half:])
+        for j in range(row_size // TILES):
+            r = t * (row_size // TILES) + j
             for c in range(width):
                 if slot:
                     place = r * width + c
                 else:
                     place = stage_place(r ^ row, c ^ (col % width), row_size, width)
-                back_ref[place] = jnp.where(
-                    low,
-                    block[:, c * cols : (c + 1) * cols],
-                    block[:, (c + width) * cols : (c + width + 1) * cols],
-                )
+                back_ref[place] = result[
+                    j * rows : (j + 1) * rows, c * cols : (c + 1) * cols
+                ]
         copy_out(t).start()
 
-    newton_schulz(height, tiles, inverse, x_s, y_s, gram_s, write)
+    newton_schulz(height, inverse, x_s, y_s, gram_s, finish)
     if not slot:
         for k in range(LOW):
             low_refs[k][...] = back_ref[k * places // LOW : (k + 1) * places // LOW]
-    for t in range(tiles):
+    for t in range(TILES):
         copy_out(t).wait()
 
 
@@ -328,18 +336,20 @@
     places = devices // HALVES
     scratch_shapes = [
         pltpu.VMEM((padded, width), jnp.bfloat16),
-        pltpu.VMEM((padded, width), jnp.bfloat16),
         pltpu.VMEM((padded, padded), jnp.bfloat16),
         pltpu.VMEM((places, rows, cols), jnp.bfloat16),
         pltpu.SemaphoreType.DMA((TILES,)),
     ]
     if slot:
-        out_specs = [VMEM, ANYWHERE]
-        out = [(height, width), (places, rows, cols)]
+        out_specs = [VMEM, VMEM, ANYWHERE]
+        out = [(padded, width), (height, padded), (places, rows, cols)]
     else:
         out_specs = [ANYWHERE] + [VMEM] * LOW
         out = [(CAP, height, width)] + [(places // LOW, rows, cols)] * LOW
-        scratch_shapes.append(pltpu.VMEM((height, width), jnp.bfloat16))
+        scratch_shapes += [
+            pltpu.VMEM((padded, width), jnp.bfloat16),
+            pltpu.VMEM((height, width), jnp.bfloat16),
+        ]
     return pl.pallas_call(
         functools.partial(ortho_kernel, row_size, col_size, slot),
         in_specs=[SMEM, VMEM],
@@ -398,22 +408,37 @@
     pltpu.make_async_copy(back_ref.at[span], update_ref.at[span], sem).wait()
 
 
-def early_kernel(list_ref, whole_ref, owned_in, *refs):
-    high_refs, (owned_ref, update_ref, back_s, own_sem, sem) = refs[:-5], refs[-5:]
-    own = pltpu.make_async_copy(whole_ref, owned_ref.at[CAP - 1], own_sem)
-    own.start()
+def early_kernel(col_size, list_ref, other_ref, y_ref, mix_ref, owned_in, *refs):
+    high_refs, (owned_ref, update_ref, back_s, whole_s, own_sems, sem) = refs[:-6], refs[-6:]
     for h, high_ref in enumerate(high_refs):
         back_s[h * LOW : (h + 1) * LOW] = high_ref[...]
     start_blocks(0, list_ref, back_s, update_ref, sem)
+    me = lax.axis_index("dp") * col_size + lax.axis_index("owner")
+    owns = other_ref[me] != me
+    height, width = whole_s.shape
+    tile = height // TILES
+    copies = []
+    for t in range(TILES):
+        span = slice(t * tile, (t + 1) * tile)
+        result = combine(y_ref, span, slice(None), mix_ref[span, :])
+        result = (update_scale(height, width) * result).astype(jnp.bfloat16)
+        whole_s[span, :] = jnp.where(owns, result, jnp.zeros_like(result))
+        rows = pl.ds(t * tile, tile)
+        copies.append(
+            pltpu.make_async_copy(whole_s.at[rows], owned_ref.at[CAP - 1, rows], own_sems.at[t])
+        )
+        copies[-1].start()
+    for copy in copies:
+        copy.wait()
     wait_blocks(back_s, update_ref, sem)
-    own.wait()
-
-
-def store_early(places, mats, matrix, owned, first):
+
+
+def store_early(places, other, current, mixing, owned, first, mats, col_size):
     _, rows, cols = first[0].shape
+    _, height, width = owned.shape
     return pl.pallas_call(
-        early_kernel,
-        in_specs=[SMEM, VMEM, ANYWHERE] + [VMEM] * len(first),
+        functools.partial(early_kernel, col_size),
+        in_specs=[SMEM, SMEM, VMEM, VMEM, ANYWHERE] + [VMEM] * len(first),
         out_specs=[ANYWHERE, ANYWHERE],
         out_shape=[
             jax.ShapeDtypeStruct(owned.shape, jnp.bfloat16),
@@ -421,16 +446,19 @@
         ],
         scratch_shapes=[
             pltpu.VMEM((LOW * len(first), rows, cols), jnp.bfloat16),
-            pltpu.SemaphoreType.DMA(()),
+            pltpu.VMEM((height, width), jnp.bfloat16),
+            pltpu.SemaphoreType.DMA((TILES,)),
             pltpu.SemaphoreType.DMA(()),
         ],
-        input_output_aliases={2: 0},
+        input_output_aliases={4: 0},
         compiler_params=PARAMS,
         cost_estimate=pl.CostEstimate(
-            flops=0, bytes_accessed=8 * mats * rows * cols, transcendentals=0
+            flops=2 * height * height * width,
+            bytes_accessed=8 * mats * rows * cols,
+            transcendentals=0,
         ),
         name="store_early",
-    )(places, matrix, owned, *first)
+    )(places, other, current, mixing, owned, *first)
 
 
 def late_kernel(list_ref, back_ref, update_in, update_ref, sem):
@@ -490,11 +518,11 @@
         for c in range(width)
         if r or c
     ]
-    matrix, back_second = orthogonalize(1, other, arrived_second, row_size, col_size)
+    current, mixing, back_second = orthogonalize(1, other, arrived_second, row_size, col_size)
     returned_first, back_second = lax.optimization_barrier((returned_first, back_second))
     returned_second = exchange(back_second, AXES, halves)
     owned, update = store_early(
-        places, owner_table.shape[0], matrix, owned, returned_first
+        places, other, current, mixing, owned, returned_first, owner_table.shape[0], col_size
     )
     update = store_late(places, returned_second, update)
     return (new_momentum, update, owned)

time: 109 us -> 111 us (1.018)
  local copies, waits for them, and re-layouts: 2.51 us -> 7.45 us
  waiting for transfers between devices: 52.8 us -> 48.9 us
    unnamed x12 -> x28, local copies, waits for them, and re-layouts: 2.51 us -> 7.45 us
    all_to_all x3, waiting for transfers between devices: 39.8 us -> 35.9 us  [exchange(): lax.all_to_all(blocks, axes, split_axis=0, concat_axis=0, tiled=True, axi...]
    pallas_call x1, Pallas kernels: 2.31 us -> 3.43 us  [store_early(): pl.pallas_call(functools.partial(early_kernel, col_size), in_specs=[SMEM,...]
where the time goes in v18:
time: 111 us; the launch traced here: 110 us
  waiting for transfers between devices  48.9 us (44%)
  Pallas kernels  29.2 us (26%)
  starting transfers between devices  24 us (22%)
  local copies, waits for them, and re-layouts  7.45 us (7%)
    all_to_all x3, waiting for transfers between devices, exchange(): lax.all_to_all(blocks, axes, split_axis=0, concat_axis=0, tiled=True, axi...  35.9 us
    all_to_all x3, starting transfers between devices, exchange(): lax.all_to_all(blocks, axes, split_axis=0, concat_axis=0, tiled=True, axi...  17.2 us
    pallas_call x2, Pallas kernels, orthogonalize(): pl.pallas_call(functools.partial(ortho_kernel, row_size, col_size, slot),...  16 us
    ppermute x6, waiting for transfers between devices, swap(): return lax.ppermute(block, AXES, [(d, d ^ offset) for d in range(devices)])  13 us
    unnamed x28, local copies, waits for them, and re-layouts  7.45 us
    ppermute x6, starting transfers between devices, swap(): return lax.ppermute(block, AXES, [(d, d ^ offset) for d in range(devices)])  6.84 us
    pallas_call x1, Pallas kernels, pack(): pl.pallas_call(functools.partial(pack_kernel, chunk, col_size), grid_spec...  4.33 us
    pallas_call x1, Pallas kernels, store_early(): pl.pallas_call(functools.partial(early_kernel, col_size), in_specs=[SMEM,...  3.43 us
  transfers between devices with their start and end apart: 9, of which 5 were waited for; matrix products, arithmetic and copies ran while one was open for 0% of the time, Pallas kernels for 21%

profile of v18, /device:TPU:0, one launch (start us, length us, event | category | flops | bytes accessed | tf_op | source)
XLA Modules:
  0.0 110.4 jit_solution(6816773109846420549)
XLA Ops:
  0.6 4.3 %pack.1 = (bf16[32,88,256]{2,1,0:T(8,128)(2,1)}, s32[32]{0:T(128)}, s32[32]{0:T(128)}) custom-call(s32[32]{0:T(128)} %owner_ref.3, bf16[32,88,256]{2,1,0:T(8,128)(2,1)} %g_ref.3, f32[32,88,256]{2,1,0:T(8,128)} %m_ref.3), custom_call_target="tpu_custom_call" | custom-call | flops 2883584 | bytes 5767168 | tf_op jit(solution)/shard_map/pack/pallas_call | solution.py:115
  5.0 0.0 copy-start
  5.0 0.0 copy-start.7
  5.0 0.0 copy-start.8
  5.0 0.0 copy-start.13
  5.0 7.4 %all-to-all-start = ((bf16[32,88,256]{2,1,0:T(8,128)(2,1)}), bf16[32,88,256]{2,1,0:T(8,128)(2,1)}, u32[]{:S(2)}, u32[]{:S(2)}) async-start(bf16[32,88,256]{2,1,0:T(8,128)(2,1)} %get-tuple-element.35), calls=%async_computation | async-start | bytes 2883584 | tf_op jit(solution)/shard_map/all_to_all | solution.py:484
  12.4 0.0 copy-done
  12.4 0.0 copy-done.7
  12.5 0.0 copy-done.8
  12.5 0.0 copy-done.13
  12.5 0.0 copy-start.1
  12.5 1.4 %copy-done.1 = bf16[32,88,256]{2,1,0:T(8,128)(2,1)S(1)} copy-done((bf16[32,88,256]{2,1,0:T(8,128)(2,1)S(1)}, bf16[32,88,256]{2,1,0:T(8,128)(2,1)}, u32[]{:S(2)}) %copy-start.1) | copy-done | bytes 1441816
  13.8 3.2 %update_momentum.1 = (f32[32,88,256]{2,1,0:T(8,128)}, bf16[32,88,256]{2,1,0:T(8,128)(2,1)S(1)}, s32[64]{0:T(128)S(1)}) custom-call(s32[32]{0:T(128)S(1)} %copy-done.7, s32[32]{0:T(128)S(1)} %copy-done.8, s32[32]{0:T(128)S(1)} %copy-done.13, bf16[32,88,256]{2,1,0:T(8,128)(2,1)S(1)} %copy-done.1, f32[32,88,256]{2,1,0:T(8,128)S(1)} %copy-done), custom_call_target="tpu_custom_call" | custom-call | flops 2883584 | bytes 8650752 | tf_op jit(solution)/shard_map/update_momentum/pallas_call | solution.py:189
  17.0 0.0 copy-start.2
  17.0 1.1 %copy-done.2 = bf16[32,88,256]{2,1,0:T(8,128)(2,1)} copy-done((bf16[32,88,256]{2,1,0:T(8,128)(2,1)}, bf16[32,88,256]{2,1,0:T(8,128)(2,1)S(1)}, u32[]{:S(2)}) %copy-start.2) | copy-done | bytes 1441816
  18.2 0.0 copy-start.10
  18.2 0.5 copy-done.10
  18.7 27.0 %all-to-all-done.x_ref = bf16[32,88,256]{2,1,0:T(8,128)(2,1)} async-done(((bf16[32,88,256]{2,1,0:T(8,128)(2,1)}), bf16[32,88,256]{2,1,0:T(8,128)(2,1)}, u32[]{:S(2)}, u32[]{:S(2)}) %all-to-all-start) | async-done | bytes 1441824 | tf_op jit(solution)/shard_map/all_to_all | solution.py:484
  45.6 4.6 %all-to-all-start.1 = ((bf16[32,88,256]{2,1,0:T(8,128)(2,1)}), bf16[32,88,256]{2,1,0:T(8,128)(2,1)S(1)}, u32[]{:S(2)}, u32[]{:S(2)}) async-start(bf16[32,88,256]{2,1,0:T(8,128)(2,1)} %copy-done.2), calls=%async_computation.1 | async-start | bytes 2883584 | tf_op jit(solution)/shard_map/all_to_all | solution.py:484
  50.2 8.8 %orthogonalize.2 = (bf16[2,704,1024]{2,1,0:T(8,128)(2,1)}, bf16[4,88,256]{2,1,0:T(8,128)(2,1)S(1)}, bf16[4,88,256]{2,1,0:T(8,128)(2,1)S(1)}, bf16[4,88,256]{2,1,0:T(8,128)(2,1)S(1)}, bf16[4,88,256]{2,1,0:T(8,128)(2,1)S(1)}) custom-call(s32[32]{0:T(128)S(1)} %copy-done.8, bf16[32,88,256]{2,1,0:T(8,128)(2,1)} %all-to-all-done.x_ref), custom_call_target="tpu_custom_call" | custom-call | flops 6643777536 | bytes 4718592 | tf_op jit(solution)/shard_map/orthogonalize/pallas_call | solution.py:353
  59.0 0.3 collective-permute-start
  59.3 1.7 %collective-permute-start.1 = (bf16[4,88,256]{2,1,0:T(8,128)(2,1)S(1)}, bf16[4,88,256]{2,1,0:T(8,128)(2,1)S(1)}, u32[]{:S(2)}, u32[]{:S(2)}) collective-permute-start(bf16[4,88,256]{2,1,0:T(8,128)(2,1)S(1)} %get-tuple-element.40), channel_id=1, source_target_pairs={{0,8},{1,9},{2,10},{3,11},{4,12},{5,13},{6,14},{7,15},{8,0},{9,1},... | collective-permute-start | bytes 540680 | tf_op jit(solution)/shard_map/ppermute | solution.py:490
  61.0 0.0 collective-permute-start.2
  61.0 0.0 collective-permute-done.refs_1_
  61.0 8.8 %collective-permute-done.1.refs_2_ = bf16[4,88,256]{2,1,0:T(8,128)(2,1)S(1)} collective-permute-done((bf16[4,88,256]{2,1,0:T(8,128)(2,1)S(1)}, bf16[4,88,256]{2,1,0:T(8,128)(2,1)S(1)}, u32[]{:S(2)}, u32[]{:S(2)}) %collective-permute-start.1) | collective-permute-done | bytes 180256 | tf_op jit(solution)/shard_map/ppermute | solution.py:490
  69.8 4.2 %collective-permute-done.2.refs_3_ = bf16[4,88,256]{2,1,0:T(8,128)(2,1)S(1)} collective-permute-done((bf16[4,88,256]{2,1,0:T(8,128)(2,1)S(1)}, bf16[4,88,256]{2,1,0:T(8,128)(2,1)S(1)}, u32[]{:S(2)}, u32[]{:S(2)}) %collective-permute-start.2) | collective-permute-done | bytes 180256 | tf_op jit(solution)/shard_map/ppermute | solution.py:490
  74.0 0.8 restage.1
  74.8 3.3 %collective-permute-start.3 = (bf16[4,88,256]{2,1,0:T(8,128)(2,1)}, bf16[4,88,256]{2,1,0:T(8,128)(2,1)S(1)}, u32[]{:S(2)}, u32[]{:S(2)}) collective-permute-start(bf16[4,88,256]{2,1,0:T(8,128)(2,1)} %get-tuple-element.43), channel_id=1, source_target_pairs={{0,1},{1,0},{2,3},{3,2},{4,5},{5,4},{6,7},{7,6},{8,9},{9,8},{10,11... | collective-permute-start | bytes 540680 | tf_op jit(solution)/shard_map/ppermute | solution.py:490
  78.2 1.5 %collective-permute-start.4 = (bf16[4,88,256]{2,1,0:T(8,128)(2,1)}, bf16[4,88,256]{2,1,0:T(8,128)(2,1)}, u32[]{:S(2)}, u32[]{:S(2)}) collective-permute-start(bf16[4,88,256]{2,1,0:T(8,128)(2,1)} %get-tuple-element.44), channel_id=1, source_target_pairs={{0,16},{1,17},{2,18},{3,19},{4,20},{5,21},{6,22},{7,23},{8,24},{9,... | collective-permute-start | bytes 540680 | tf_op jit(solution)/shard_map/ppermute | solution.py:490
  79.7 0.0 collective-permute-start.5
  79.7 3.8 %all-to-all-done.1.x_ref = bf16[32,88,256]{2,1,0:T(8,128)(2,1)S(1)} async-done(((bf16[32,88,256]{2,1,0:T(8,128)(2,1)}), bf16[32,88,256]{2,1,0:T(8,128)(2,1)S(1)}, u32[]{:S(2)}, u32[]{:S(2)}) %all-to-all-start.1) | async-done | bytes 1441824 | tf_op jit(solution)/shard_map/all_to_all | solution.py:484
  83.4 7.3 %orthogonalize.3 = (bf16[768,1024]{1,0:T(8,128)(2,1)S(1)}, bf16[704,768]{1,0:T(8,128)(2,1)S(1)}, bf16[16,88,256]{2,1,0:T(8,128)(2,1)}) custom-call(s32[32]{0:T(128)S(1)} %copy-done.8, bf16[32,88,256]{2,1,0:T(8,128)(2,1)S(1)} %all-to-all-done.1.x_ref), custom_call_target="tpu_custom_call" | custom-call | flops 6643777536 | bytes 4718592 | tf_op jit(solution)/shard_map/orthogonalize/pallas_call | solution.py:353
  90.7 0.0 copy-start.3
  90.7 1.0 copy-done.3
  91.7 0.0 collective-permute-done.3.refs_1_
  91.7 0.7 copy-done.5
  92.4 0.0 collective-permute-done.4.refs_2_
  92.4 0.0 collective-permute-done.5.refs_3_
  92.4 5.2 %all-to-all-start.2 = ((bf16[16,88,256]{2,1,0:T(8,128)(2,1)}), bf16[16,88,256]{2,1,0:T(8,128)(2,1)S(1)}, u32[]{:S(2)}, u32[]{:S(2)}) async-start(bf16[16,88,256]{2,1,0:T(8,128)(2,1)} %get-tuple-element.49), calls=%async_computation.2 | async-start | bytes 1441792 | tf_op jit(solution)/shard_map/all_to_all | solution.py:484
  97.6 0.0 copy-done.4
  97.6 0.0 copy-start.6
  97.6 0.9 copy-done.6
  98.5 0.7 copy-done.9
  99.2 0.6 copy-done.11
  99.8 3.4 %store_early.1 = (bf16[2,704,1024]{2,1,0:T(8,128)(2,1)}, bf16[32,88,256]{2,1,0:T(8,128)(2,1)}) custom-call(s32[64]{0:T(128)S(1)} %copy-done.11, s32[32]{0:T(128)S(1)} %copy-done.9, bf16[768,1024]{1,0:T(8,128)(2,1)S(1)} %get-tuple-element.50.y_ref, bf16[704,768]{1,0:T(8,128)(2,1)S(1)} %copy-done.4, ...), custom_call_target="tpu_custom_call", output_to_operand_aliasing={{0}: (4, {})} | custom-call | flops 1015021568 | bytes 5767168 | tf_op jit(solution)/shard_map/store_early/pallas_call | solution.py:439
  103.2 5.2 %all-to-all-done.2.back_ref = bf16[16,88,256]{2,1,0:T(8,128)(2,1)S(1)} async-done(((bf16[16,88,256]{2,1,0:T(8,128)(2,1)}), bf16[16,88,256]{2,1,0:T(8,128)(2,1)S(1)}, u32[]{:S(2)}, u32[]{:S(2)}) %all-to-all-start.2) | async-done | bytes 720928 | tf_op jit(solution)/shard_map/all_to_all | solution.py:484
  108.4 0.6 copy-done.12
  109.0 1.4 %store_late.1 = bf16[32,88,256]{2,1,0:T(8,128)(2,1)} custom-call(s32[64]{0:T(128)S(1)} %copy-done.12, bf16[16,88,256]{2,1,0:T(8,128)(2,1)S(1)} %all-to-all-done.2.back_ref, bf16[32,88,256]{2,1,0:T(8,128)(2,1)} %get-tuple-element.57.update_in), custom_call_target="tpu_custom_call", output_to_operand_aliasing={{}: (2, {})} | custom-call | bytes 1441792 | tf_op jit(solution)/shard_map/store_late/pallas_call | solution.py:470
  (5 shorter events, 0.0 us)
Async XLA Ops:
  5.0 7.5 %copy-start = (f32[32,88,256]{2,1,0:T(8,128)S(1)}, f32[32,88,256]{2,1,0:T(8,128)}, u32[]{:S(2)}) copy-start(f32[32,88,256]{2,1,0:T(8,128)} %m_ref.3) | copy-start | bytes 8650756
  5.0 7.5 %copy-start.7 = (s32[32]{0:T(128)S(1)}, s32[32]{0:T(128)}, u32[]{:S(2)}) copy-start(s32[32]{0:T(128)} %owner_ref.3) | copy-start | bytes 388
  5.0 7.5 %copy-start.8 = (s32[32]{0:T(128)S(1)}, s32[32]{0:T(128)}, u32[]{:S(2)}) copy-start(s32[32]{0:T(128)} %get-tuple-element.31.other_ref) | copy-start | bytes 388
  5.0 7.5 %copy-start.13 = (s32[32]{0:T(128)S(1)}, s32[32]{0:T(128)}, u32[]{:S(2)}) copy-start(s32[32]{0:T(128)} %get-tuple-element.32.rank_ref) | copy-start | bytes 388
  5.0 40.6 %all-to-all-start = ((bf16[32,88,256]{2,1,0:T(8,128)(2,1)}), bf16[32,88,256]{2,1,0:T(8,128)(2,1)}, u32[]{:S(2)}, u32[]{:S(2)}) async-start(bf16[32,88,256]{2,1,0:T(8,128)(2,1)} %get-tuple-element.35), calls=%async_computation | async-start | bytes 2883584 | tf_op jit(solution)/shard_map/all_to_all | solution.py:484
  12.5 1.4 %copy-start.1 = (bf16[32,88,256]{2,1,0:T(8,128)(2,1)S(1)}, bf16[32,88,256]{2,1,0:T(8,128)(2,1)}, u32[]{:S(2)}) copy-start(bf16[32,88,256]{2,1,0:T(8,128)(2,1)} %g_ref.3) | copy-start | bytes 4325380
  17.0 1.1 %copy-start.2 = (bf16[32,88,256]{2,1,0:T(8,128)(2,1)}, bf16[32,88,256]{2,1,0:T(8,128)(2,1)S(1)}, u32[]{:S(2)}) copy-start(bf16[32,88,256]{2,1,0:T(8,128)(2,1)S(1)} %get-tuple-element.46) | copy-start | bytes 4325380
  18.2 0.5 copy-start.10
  45.6 37.8 %all-to-all-start.1 = ((bf16[32,88,256]{2,1,0:T(8,128)(2,1)}), bf16[32,88,256]{2,1,0:T(8,128)(2,1)S(1)}, u32[]{:S(2)}, u32[]{:S(2)}) async-start(bf16[32,88,256]{2,1,0:T(8,128)(2,1)} %copy-done.2), calls=%async_computation.1 | async-start | bytes 2883584 | tf_op jit(solution)/shard_map/all_to_all | solution.py:484
  59.0 2.0 %collective-permute-start = (bf16[4,88,256]{2,1,0:T(8,128)(2,1)S(1)}, bf16[4,88,256]{2,1,0:T(8,128)(2,1)S(1)}, u32[]{:S(2)}, u32[]{:S(2)}) collective-permute-start(bf16[4,88,256]{2,1,0:T(8,128)(2,1)S(1)} %get-tuple-element.39), channel_id=1, source_target_pairs={{0,4},{1,5},{2,6},{3,7},{4,0},{5,1},{6,2},{7,3},{8,12},{9,13},{10,... | collective-permute-start | bytes 540680 | tf_op jit(solution)/shard_map/ppermute | solution.py:490
  59.3 10.5 %collective-permute-start.1 = (bf16[4,88,256]{2,1,0:T(8,128)(2,1)S(1)}, bf16[4,88,256]{2,1,0:T(8,128)(2,1)S(1)}, u32[]{:S(2)}, u32[]{:S(2)}) collective-permute-start(bf16[4,88,256]{2,1,0:T(8,128)(2,1)S(1)} %get-tuple-element.40), channel_id=1, source_target_pairs={{0,8},{1,9},{2,10},{3,11},{4,12},{5,13},{6,14},{7,15},{8,0},{9,1},... | collective-permute-start | bytes 540680 | tf_op jit(solution)/shard_map/ppermute | solution.py:490
  61.0 13.0 %collective-permute-start.2 = (bf16[4,88,256]{2,1,0:T(8,128)(2,1)S(1)}, bf16[4,88,256]{2,1,0:T(8,128)(2,1)S(1)}, u32[]{:S(2)}, u32[]{:S(2)}) collective-permute-start(bf16[4,88,256]{2,1,0:T(8,128)(2,1)S(1)} %get-tuple-element.41), channel_id=1, source_target_pairs={{0,12},{1,13},{2,14},{3,15},{4,8},{5,9},{6,10},{7,11},{8,4},{9,5},... | collective-permute-start | bytes 540680 | tf_op jit(solution)/shard_map/ppermute | solution.py:490
  74.8 16.9 %collective-permute-start.3 = (bf16[4,88,256]{2,1,0:T(8,128)(2,1)}, bf16[4,88,256]{2,1,0:T(8,128)(2,1)S(1)}, u32[]{:S(2)}, u32[]{:S(2)}) collective-permute-start(bf16[4,88,256]{2,1,0:T(8,128)(2,1)} %get-tuple-element.43), channel_id=1, source_target_pairs={{0,1},{1,0},{2,3},{3,2},{4,5},{5,4},{6,7},{7,6},{8,9},{9,8},{10,11... | collective-permute-start | bytes 540680 | tf_op jit(solution)/shard_map/ppermute | solution.py:490
  78.2 14.2 %collective-permute-start.4 = (bf16[4,88,256]{2,1,0:T(8,128)(2,1)}, bf16[4,88,256]{2,1,0:T(8,128)(2,1)}, u32[]{:S(2)}, u32[]{:S(2)}) collective-permute-start(bf16[4,88,256]{2,1,0:T(8,128)(2,1)} %get-tuple-element.44), channel_id=1, source_target_pairs={{0,16},{1,17},{2,18},{3,19},{4,20},{5,21},{6,22},{7,23},{8,24},{9,... | collective-permute-start | bytes 540680 | tf_op jit(solution)/shard_map/ppermute | solution.py:490
  79.7 12.7 %collective-permute-start.5 = (bf16[4,88,256]{2,1,0:T(8,128)(2,1)}, bf16[4,88,256]{2,1,0:T(8,128)(2,1)}, u32[]{:S(2)}, u32[]{:S(2)}) collective-permute-start(bf16[4,88,256]{2,1,0:T(8,128)(2,1)} %get-tuple-element.45), channel_id=1, source_target_pairs={{0,17},{1,16},{2,19},{3,18},{4,21},{5,20},{6,23},{7,22},{8,25},{9,... | collective-permute-start | bytes 540680 | tf_op jit(solution)/shard_map/ppermute | solution.py:490
  90.7 1.0 copy-start.3
  91.7 0.7 copy-start.5
  92.4 5.2 %copy-start.4 = (bf16[704,768]{1,0:T(8,128)(2,1)S(1)}, bf16[704,768]{1,0:T(8,128)(2,1)}, u32[]{:S(2)}) copy-start(bf16[704,768]{1,0:T(8,128)(2,1)} %copy-done.3) | copy-start | bytes 3244036
  92.4 16.0 %all-to-all-start.2 = ((bf16[16,88,256]{2,1,0:T(8,128)(2,1)}), bf16[16,88,256]{2,1,0:T(8,128)(2,1)S(1)}, u32[]{:S(2)}, u32[]{:S(2)}) async-start(bf16[16,88,256]{2,1,0:T(8,128)(2,1)} %get-tuple-element.49), calls=%async_computation.2 | async-start | bytes 1441792 | tf_op jit(solution)/shard_map/all_to_all | solution.py:484
  97.6 0.9 copy-start.6
  98.5 0.7 copy-start.9
  99.2 0.6 copy-start.11
  108.4 0.6 copy-start.12

commit v19 on v18

--- a/solution.py
+++ b/solution.py
@@ -43,7 +43,7 @@
     return new, (grad + momentum_beta * new).astype(jnp.bfloat16)
 
 
-def make_plan(col_size, owner_ref, other_ref, rank_ref, count_ref, list_ref, first_list):
+def make_plan(col_size, owner_ref, other_ref, rank_ref, count_ref, list_ref):
     devices, mats = other_ref.shape[0], rank_ref.shape[0]
 
     def clear(d, _):
@@ -52,13 +52,12 @@
 
     lax.fori_loop(0, devices, clear, 0, unroll=8)
 
-    def rank_matrix(i, found):
+    def rank_matrix(i, _):
         owner = owner_ref[i]
         rank = count_ref[owner]
         rank_ref[i] = rank
         count_ref[owner] = rank + 1
-        first_list[found] = i
-        return found + 1 - rank
+        return 0
 
     lax.fori_loop(0, mats, rank_matrix, 0, unroll=8)
 
@@ -86,27 +85,31 @@
 
 def pack_kernel(
     chunk, col_size, owner_ref, g_ref, m_ref, first_ref, other_ref, rank_ref,
-    count_ref, list_ref, first_list, g_s, m_s, sems,
+    count_ref, list_ref, g_s, m_s, sems,
 ):
     mats = rank_ref.shape[0]
 
-    loads = []
-    for k in range(mats // chunk):
+    def loads(k):
         span = pl.ds(k * chunk, chunk)
-        loads += [
+        return (
             pltpu.make_async_copy(g_ref.at[span], g_s.at[span], sems.at[0, k]),
             pltpu.make_async_copy(m_ref.at[span], m_s.at[span], sems.at[1, k]),
-        ]
-    for load in loads:
-        load.start()
-    make_plan(col_size, owner_ref, other_ref, rank_ref, count_ref, list_ref, first_list)
-    for load in loads:
-        load.wait()
-    for k in range(mats // CAP):
-        i = first_list[k]
-        _, nesterov = nesterov_of(g_s, m_s, i)
-        first_ref[owner_ref[i]] = nesterov
-        first_ref[other_ref[owner_ref[i]]] = nesterov
+        )
+
+    for k in range(mats // chunk):
+        for load in loads(k):
+            load.start()
+    make_plan(col_size, owner_ref, other_ref, rank_ref, count_ref, list_ref)
+    for k in range(mats // chunk):
+        for load in loads(k):
+            load.wait()
+        for i in range(k * chunk, (k + 1) * chunk):
+
+            @pl.when(rank_ref[i] == 0)
+            def _():
+                nesterov = nesterov_of(g_s, m_s, i)[1]
+                first_ref[owner_ref[i]] = nesterov
+                first_ref[other_ref[owner_ref[i]]] = nesterov
 
 
 def pack(gradients, momentum, owner_table, devices, col_size):
@@ -122,7 +125,6 @@
             scratch_shapes=[
                 pltpu.SMEM((devices,), jnp.int32),
                 pltpu.SMEM((2 * HALVES * devices,), jnp.int32),
-                pltpu.SMEM((mats,), jnp.int32),
                 pltpu.VMEM(gradients.shape, gradients.dtype),
                 pltpu.VMEM(momentum.shape, momentum.dtype),
                 pltpu.SemaphoreType.DMA((2, mats // chunk)),
@@ -355,9 +357,7 @@
         in_specs=[SMEM, VMEM],
         out_specs=out_specs,
         out_shape=[
-            pltpu.HBM(shape, jnp.bfloat16)
-            if spec is ANYWHERE
-            else jax.ShapeDtypeStruct(shape, jnp.bfloat16)
+            (pltpu.HBM if spec is ANYWHERE else pltpu.VMEM)(shape, jnp.bfloat16)
             for spec, shape in zip(out_specs, out)
         ],
         scratch_shapes=scratch_shapes,

time: 111 us -> 111 us (level)
  no operation moved by 1% of the time
where the time goes in v19:
time: 111 us; the launch traced here: 110 us
  waiting for transfers between devices  49 us (44%)
  Pallas kernels  29 us (26%)
  starting transfers between devices  24 us (22%)
  local copies, waits for them, and re-layouts  7.45 us (7%)
    all_to_all x3, waiting for transfers between devices, exchange(): lax.all_to_all(blocks, axes, split_axis=0, concat_axis=0, tiled=True, axi...  36 us
    all_to_all x3, starting transfers between devices, exchange(): lax.all_to_all(blocks, axes, split_axis=0, concat_axis=0, tiled=True, axi...  17.2 us
    pallas_call x2, Pallas kernels, orthogonalize(): pl.pallas_call(functools.partial(ortho_kernel, row_size, col_size, slot),...  16 us
    ppermute x6, waiting for transfers between devices, swap(): return lax.ppermute(block, AXES, [(d, d ^ offset) for d in range(devices)])  13 us
    unnamed x28, local copies, waits for them, and re-layouts  7.45 us
    ppermute x6, starting transfers between devices, swap(): return lax.ppermute(block, AXES, [(d, d ^ offset) for d in range(devices)])  6.8 us
    pallas_call x1, Pallas kernels, pack(): pl.pallas_call(functools.partial(pack_kernel, chunk, col_size), grid_spec...  4.04 us
    pallas_call x1, Pallas kernels, store_early(): pl.pallas_call(functools.partial(early_kernel, col_size), in_specs=[SMEM,...  3.43 us
  transfers between devices with their start and end apart: 9, of which 5 were waited for; matrix products, arithmetic and copies ran while one was open for 0% of the time, Pallas kernels for 21%

profile of v19, /device:TPU:0, one launch (start us, length us, event | category | flops | bytes accessed | tf_op | source)
XLA Modules:
  0.0 110.1 jit_solution(12576511459901722899)
XLA Ops:
  0.6 4.0 %pack.1 = (bf16[32,88,256]{2,1,0:T(8,128)(2,1)}, s32[32]{0:T(128)}, s32[32]{0:T(128)}) custom-call(s32[32]{0:T(128)} %owner_ref.3, bf16[32,88,256]{2,1,0:T(8,128)(2,1)} %g_ref.3, f32[32,88,256]{2,1,0:T(8,128)} %m_ref.3), custom_call_target="tpu_custom_call" | custom-call | flops 2883584 | bytes 5767168 | tf_op jit(solution)/shard_map/pack/pallas_call | solution.py:118
  4.7 0.0 copy-start
  4.7 0.0 copy-start.7
  4.7 0.0 copy-start.8
  4.7 0.0 copy-start.13
  4.7 7.4 %all-to-all-start = ((bf16[32,88,256]{2,1,0:T(8,128)(2,1)}), bf16[32,88,256]{2,1,0:T(8,128)(2,1)}, u32[]{:S(2)}, u32[]{:S(2)}) async-start(bf16[32,88,256]{2,1,0:T(8,128)(2,1)} %get-tuple-element.35), calls=%async_computation | async-start | bytes 2883584 | tf_op jit(solution)/shard_map/all_to_all | solution.py:484
  12.2 0.0 copy-done
  12.2 0.0 copy-done.7
  12.2 0.0 copy-done.8
  12.2 0.0 copy-done.13
  12.2 0.0 copy-start.1
  12.2 1.4 %copy-done.1 = bf16[32,88,256]{2,1,0:T(8,128)(2,1)S(1)} copy-done((bf16[32,88,256]{2,1,0:T(8,128)(2,1)S(1)}, bf16[32,88,256]{2,1,0:T(8,128)(2,1)}, u32[]{:S(2)}) %copy-start.1) | copy-done | bytes 1441816
  13.6 3.2 %update_momentum.1 = (f32[32,88,256]{2,1,0:T(8,128)}, bf16[32,88,256]{2,1,0:T(8,128)(2,1)S(1)}, s32[64]{0:T(128)S(1)}) custom-call(s32[32]{0:T(128)S(1)} %copy-done.7, s32[32]{0:T(128)S(1)} %copy-done.8, s32[32]{0:T(128)S(1)} %copy-done.13, bf16[32,88,256]{2,1,0:T(8,128)(2,1)S(1)} %copy-done.1, f32[32,88,256]{2,1,0:T(8,128)S(1)} %copy-done), custom_call_target="tpu_custom_call" | custom-call | flops 2883584 | bytes 8650752 | tf_op jit(solution)/shard_map/update_momentum/pallas_call | solution.py:191
  16.8 0.0 copy-start.2
  16.8 1.1 %copy-done.2 = bf16[32,88,256]{2,1,0:T(8,128)(2,1)} copy-done((bf16[32,88,256]{2,1,0:T(8,128)(2,1)}, bf16[32,88,256]{2,1,0:T(8,128)(2,1)S(1)}, u32[]{:S(2)}) %copy-start.2) | copy-done | bytes 1441816
  17.9 0.0 copy-start.10
  17.9 0.5 copy-done.10
  18.4 27.0 %all-to-all-done.x_ref = bf16[32,88,256]{2,1,0:T(8,128)(2,1)} async-done(((bf16[32,88,256]{2,1,0:T(8,128)(2,1)}), bf16[32,88,256]{2,1,0:T(8,128)(2,1)}, u32[]{:S(2)}, u32[]{:S(2)}) %all-to-all-start) | async-done | bytes 1441824 | tf_op jit(solution)/shard_map/all_to_all | solution.py:484
  45.4 4.6 %all-to-all-start.1 = ((bf16[32,88,256]{2,1,0:T(8,128)(2,1)}), bf16[32,88,256]{2,1,0:T(8,128)(2,1)S(1)}, u32[]{:S(2)}, u32[]{:S(2)}) async-start(bf16[32,88,256]{2,1,0:T(8,128)(2,1)} %copy-done.2), calls=%async_computation.1 | async-start | bytes 2883584 | tf_op jit(solution)/shard_map/all_to_all | solution.py:484
  49.9 8.8 %orthogonalize.2 = (bf16[2,704,1024]{2,1,0:T(8,128)(2,1)}, bf16[4,88,256]{2,1,0:T(8,128)(2,1)S(1)}, bf16[4,88,256]{2,1,0:T(8,128)(2,1)S(1)}, bf16[4,88,256]{2,1,0:T(8,128)(2,1)S(1)}, bf16[4,88,256]{2,1,0:T(8,128)(2,1)S(1)}) custom-call(s32[32]{0:T(128)S(1)} %copy-done.8, bf16[32,88,256]{2,1,0:T(8,128)(2,1)} %all-to-all-done.x_ref), custom_call_target="tpu_custom_call" | custom-call | flops 6643777536 | bytes 4718592 | tf_op jit(solution)/shard_map/orthogonalize/pallas_call | solution.py:355
  58.7 0.3 collective-permute-start
  59.0 1.7 %collective-permute-start.1 = (bf16[4,88,256]{2,1,0:T(8,128)(2,1)S(1)}, bf16[4,88,256]{2,1,0:T(8,128)(2,1)S(1)}, u32[]{:S(2)}, u32[]{:S(2)}) collective-permute-start(bf16[4,88,256]{2,1,0:T(8,128)(2,1)S(1)} %get-tuple-element.40), channel_id=1, source_target_pairs={{0,8},{1,9},{2,10},{3,11},{4,12},{5,13},{6,14},{7,15},{8,0},{9,1},... | collective-permute-start | bytes 540680 | tf_op jit(solution)/shard_map/ppermute | solution.py:490
  60.7 0.0 collective-permute-start.2
  60.7 0.0 collective-permute-done.refs_1_
  60.7 8.8 %collective-permute-done.1.refs_2_ = bf16[4,88,256]{2,1,0:T(8,128)(2,1)S(1)} collective-permute-done((bf16[4,88,256]{2,1,0:T(8,128)(2,1)S(1)}, bf16[4,88,256]{2,1,0:T(8,128)(2,1)S(1)}, u32[]{:S(2)}, u32[]{:S(2)}) %collective-permute-start.1) | collective-permute-done | bytes 180256 | tf_op jit(solution)/shard_map/ppermute | solution.py:490
  69.5 4.2 %collective-permute-done.2.refs_3_ = bf16[4,88,256]{2,1,0:T(8,128)(2,1)S(1)} collective-permute-done((bf16[4,88,256]{2,1,0:T(8,128)(2,1)S(1)}, bf16[4,88,256]{2,1,0:T(8,128)(2,1)S(1)}, u32[]{:S(2)}, u32[]{:S(2)}) %collective-permute-start.2) | collective-permute-done | bytes 180256 | tf_op jit(solution)/shard_map/ppermute | solution.py:490
  73.7 0.8 restage.1
  74.6 3.3 %collective-permute-start.3 = (bf16[4,88,256]{2,1,0:T(8,128)(2,1)}, bf16[4,88,256]{2,1,0:T(8,128)(2,1)S(1)}, u32[]{:S(2)}, u32[]{:S(2)}) collective-permute-start(bf16[4,88,256]{2,1,0:T(8,128)(2,1)} %get-tuple-element.43), channel_id=1, source_target_pairs={{0,1},{1,0},{2,3},{3,2},{4,5},{5,4},{6,7},{7,6},{8,9},{9,8},{10,11... | collective-permute-start | bytes 540680 | tf_op jit(solution)/shard_map/ppermute | solution.py:490
  77.9 1.5 %collective-permute-start.4 = (bf16[4,88,256]{2,1,0:T(8,128)(2,1)}, bf16[4,88,256]{2,1,0:T(8,128)(2,1)}, u32[]{:S(2)}, u32[]{:S(2)}) collective-permute-start(bf16[4,88,256]{2,1,0:T(8,128)(2,1)} %get-tuple-element.44), channel_id=1, source_target_pairs={{0,16},{1,17},{2,18},{3,19},{4,20},{5,21},{6,22},{7,23},{8,24},{9,... | collective-permute-start | bytes 540680 | tf_op jit(solution)/shard_map/ppermute | solution.py:490
  79.4 0.0 collective-permute-start.5
  79.4 3.8 %all-to-all-done.1.x_ref = bf16[32,88,256]{2,1,0:T(8,128)(2,1)S(1)} async-done(((bf16[32,88,256]{2,1,0:T(8,128)(2,1)}), bf16[32,88,256]{2,1,0:T(8,128)(2,1)S(1)}, u32[]{:S(2)}, u32[]{:S(2)}) %all-to-all-start.1) | async-done | bytes 1441824 | tf_op jit(solution)/shard_map/all_to_all | solution.py:484
  83.2 7.3 %orthogonalize.3 = (bf16[768,1024]{1,0:T(8,128)(2,1)S(1)}, bf16[704,768]{1,0:T(8,128)(2,1)S(1)}, bf16[16,88,256]{2,1,0:T(8,128)(2,1)}) custom-call(s32[32]{0:T(128)S(1)} %copy-done.8, bf16[32,88,256]{2,1,0:T(8,128)(2,1)S(1)} %all-to-all-done.1.x_ref), custom_call_target="tpu_custom_call" | custom-call | flops 6643777536 | bytes 4718592 | tf_op jit(solution)/shard_map/orthogonalize/pallas_call | solution.py:355
  90.4 0.0 copy-start.3
  90.4 1.0 copy-done.3
  91.4 0.0 collective-permute-done.3.refs_1_
  91.4 0.7 copy-done.5
  92.1 0.0 collective-permute-done.4.refs_2_
  92.1 0.0 collective-permute-done.5.refs_3_
  92.1 5.2 %all-to-all-start.2 = ((bf16[16,88,256]{2,1,0:T(8,128)(2,1)}), bf16[16,88,256]{2,1,0:T(8,128)(2,1)S(1)}, u32[]{:S(2)}, u32[]{:S(2)}) async-start(bf16[16,88,256]{2,1,0:T(8,128)(2,1)} %get-tuple-element.49), calls=%async_computation.2 | async-start | bytes 1441792 | tf_op jit(solution)/shard_map/all_to_all | solution.py:484
  97.3 0.0 copy-done.4
  97.3 0.0 copy-start.6
  97.3 0.9 copy-done.6
  98.2 0.7 copy-done.9
  98.9 0.6 copy-done.11
  99.5 3.4 %store_early.1 = (bf16[2,704,1024]{2,1,0:T(8,128)(2,1)}, bf16[32,88,256]{2,1,0:T(8,128)(2,1)}) custom-call(s32[64]{0:T(128)S(1)} %copy-done.11, s32[32]{0:T(128)S(1)} %copy-done.9, bf16[768,1024]{1,0:T(8,128)(2,1)S(1)} %get-tuple-element.50.y_ref, bf16[704,768]{1,0:T(8,128)(2,1)S(1)} %copy-done.4, ...), custom_call_target="tpu_custom_call", output_to_operand_aliasing={{0}: (4, {})} | custom-call | flops 1015021568 | bytes 5767168 | tf_op jit(solution)/shard_map/store_early/pallas_call | solution.py:439
  102.9 5.2 %all-to-all-done.2.back_ref = bf16[16,88,256]{2,1,0:T(8,128)(2,1)S(1)} async-done(((bf16[16,88,256]{2,1,0:T(8,128)(2,1)}), bf16[16,88,256]{2,1,0:T(8,128)(2,1)S(1)}, u32[]{:S(2)}, u32[]{:S(2)}) %all-to-all-start.2) | async-done | bytes 720928 | tf_op jit(solution)/shard_map/all_to_all | solution.py:484
  108.1 0.6 copy-done.12
  108.7 1.4 %store_late.1 = bf16[32,88,256]{2,1,0:T(8,128)(2,1)} custom-call(s32[64]{0:T(128)S(1)} %copy-done.12, bf16[16,88,256]{2,1,0:T(8,128)(2,1)S(1)} %all-to-all-done.2.back_ref, bf16[32,88,256]{2,1,0:T(8,128)(2,1)} %get-tuple-element.57.update_in), custom_call_target="tpu_custom_call", output_to_operand_aliasing={{}: (2, {})} | custom-call | bytes 1441792 | tf_op jit(solution)/shard_map/store_late/pallas_call | solution.py:470
  (5 shorter events, 0.0 us)
Async XLA Ops:
  4.7 7.5 %copy-start = (f32[32,88,256]{2,1,0:T(8,128)S(1)}, f32[32,88,256]{2,1,0:T(8,128)}, u32[]{:S(2)}) copy-start(f32[32,88,256]{2,1,0:T(8,128)} %m_ref.3) | copy-start | bytes 8650756
  4.7 7.5 %copy-start.7 = (s32[32]{0:T(128)S(1)}, s32[32]{0:T(128)}, u32[]{:S(2)}) copy-start(s32[32]{0:T(128)} %owner_ref.3) | copy-start | bytes 388
  4.7 7.5 %copy-start.8 = (s32[32]{0:T(128)S(1)}, s32[32]{0:T(128)}, u32[]{:S(2)}) copy-start(s32[32]{0:T(128)} %get-tuple-element.31.other_ref) | copy-start | bytes 388
  4.7 7.5 %copy-start.13 = (s32[32]{0:T(128)S(1)}, s32[32]{0:T(128)}, u32[]{:S(2)}) copy-start(s32[32]{0:T(128)} %get-tuple-element.32.rank_ref) | copy-start | bytes 388
  4.7 40.6 %all-to-all-start = ((bf16[32,88,256]{2,1,0:T(8,128)(2,1)}), bf16[32,88,256]{2,1,0:T(8,128)(2,1)}, u32[]{:S(2)}, u32[]{:S(2)}) async-start(bf16[32,88,256]{2,1,0:T(8,128)(2,1)} %get-tuple-element.35), calls=%async_computation | async-start | bytes 2883584 | tf_op jit(solution)/shard_map/all_to_all | solution.py:484
  12.2 1.4 %copy-start.1 = (bf16[32,88,256]{2,1,0:T(8,128)(2,1)S(1)}, bf16[32,88,256]{2,1,0:T(8,128)(2,1)}, u32[]{:S(2)}) copy-start(bf16[32,88,256]{2,1,0:T(8,128)(2,1)} %g_ref.3) | copy-start | bytes 4325380
  16.8 1.1 %copy-start.2 = (bf16[32,88,256]{2,1,0:T(8,128)(2,1)}, bf16[32,88,256]{2,1,0:T(8,128)(2,1)S(1)}, u32[]{:S(2)}) copy-start(bf16[32,88,256]{2,1,0:T(8,128)(2,1)S(1)} %get-tuple-element.46) | copy-start | bytes 4325380
  17.9 0.5 copy-start.10
  45.4 37.8 %all-to-all-start.1 = ((bf16[32,88,256]{2,1,0:T(8,128)(2,1)}), bf16[32,88,256]{2,1,0:T(8,128)(2,1)S(1)}, u32[]{:S(2)}, u32[]{:S(2)}) async-start(bf16[32,88,256]{2,1,0:T(8,128)(2,1)} %copy-done.2), calls=%async_computation.1 | async-start | bytes 2883584 | tf_op jit(solution)/shard_map/all_to_all | solution.py:484
  58.7 2.0 %collective-permute-start = (bf16[4,88,256]{2,1,0:T(8,128)(2,1)S(1)}, bf16[4,88,256]{2,1,0:T(8,128)(2,1)S(1)}, u32[]{:S(2)}, u32[]{:S(2)}) collective-permute-start(bf16[4,88,256]{2,1,0:T(8,128)(2,1)S(1)} %get-tuple-element.39), channel_id=1, source_target_pairs={{0,4},{1,5},{2,6},{3,7},{4,0},{5,1},{6,2},{7,3},{8,12},{9,13},{10,... | collective-permute-start | bytes 540680 | tf_op jit(solution)/shard_map/ppermute | solution.py:490
  59.0 10.4 %collective-permute-start.1 = (bf16[4,88,256]{2,1,0:T(8,128)(2,1)S(1)}, bf16[4,88,256]{2,1,0:T(8,128)(2,1)S(1)}, u32[]{:S(2)}, u32[]{:S(2)}) collective-permute-start(bf16[4,88,256]{2,1,0:T(8,128)(2,1)S(1)} %get-tuple-element.40), channel_id=1, source_target_pairs={{0,8},{1,9},{2,10},{3,11},{4,12},{5,13},{6,14},{7,15},{8,0},{9,1},... | collective-permute-start | bytes 540680 | tf_op jit(solution)/shard_map/ppermute | solution.py:490
  60.7 13.0 %collective-permute-start.2 = (bf16[4,88,256]{2,1,0:T(8,128)(2,1)S(1)}, bf16[4,88,256]{2,1,0:T(8,128)(2,1)S(1)}, u32[]{:S(2)}, u32[]{:S(2)}) collective-permute-start(bf16[4,88,256]{2,1,0:T(8,128)(2,1)S(1)} %get-tuple-element.41), channel_id=1, source_target_pairs={{0,12},{1,13},{2,14},{3,15},{4,8},{5,9},{6,10},{7,11},{8,4},{9,5},... | collective-permute-start | bytes 540680 | tf_op jit(solution)/shard_map/ppermute | solution.py:490
  74.6 16.8 %collective-permute-start.3 = (bf16[4,88,256]{2,1,0:T(8,128)(2,1)}, bf16[4,88,256]{2,1,0:T(8,128)(2,1)S(1)}, u32[]{:S(2)}, u32[]{:S(2)}) collective-permute-start(bf16[4,88,256]{2,1,0:T(8,128)(2,1)} %get-tuple-element.43), channel_id=1, source_target_pairs={{0,1},{1,0},{2,3},{3,2},{4,5},{5,4},{6,7},{7,6},{8,9},{9,8},{10,11... | collective-permute-start | bytes 540680 | tf_op jit(solution)/shard_map/ppermute | solution.py:490
  77.9 14.2 %collective-permute-start.4 = (bf16[4,88,256]{2,1,0:T(8,128)(2,1)}, bf16[4,88,256]{2,1,0:T(8,128)(2,1)}, u32[]{:S(2)}, u32[]{:S(2)}) collective-permute-start(bf16[4,88,256]{2,1,0:T(8,128)(2,1)} %get-tuple-element.44), channel_id=1, source_target_pairs={{0,16},{1,17},{2,18},{3,19},{4,20},{5,21},{6,22},{7,23},{8,24},{9,... | collective-permute-start | bytes 540680 | tf_op jit(solution)/shard_map/ppermute | solution.py:490
  79.4 12.7 %collective-permute-start.5 = (bf16[4,88,256]{2,1,0:T(8,128)(2,1)}, bf16[4,88,256]{2,1,0:T(8,128)(2,1)}, u32[]{:S(2)}, u32[]{:S(2)}) collective-permute-start(bf16[4,88,256]{2,1,0:T(8,128)(2,1)} %get-tuple-element.45), channel_id=1, source_target_pairs={{0,17},{1,16},{2,19},{3,18},{4,21},{5,20},{6,23},{7,22},{8,25},{9,... | collective-permute-start | bytes 540680 | tf_op jit(solution)/shard_map/ppermute | solution.py:490
  90.4 1.0 copy-start.3
  91.4 0.7 copy-start.5
  92.1 5.2 %copy-start.4 = (bf16[704,768]{1,0:T(8,128)(2,1)S(1)}, bf16[704,768]{1,0:T(8,128)(2,1)}, u32[]{:S(2)}) copy-start(bf16[704,768]{1,0:T(8,128)(2,1)} %copy-done.3) | copy-start | bytes 3244036
  92.1 16.0 %all-to-all-start.2 = ((bf16[16,88,256]{2,1,0:T(8,128)(2,1)}), bf16[16,88,256]{2,1,0:T(8,128)(2,1)S(1)}, u32[]{:S(2)}, u32[]{:S(2)}) async-start(bf16[16,88,256]{2,1,0:T(8,128)(2,1)} %get-tuple-element.49), calls=%async_computation.2 | async-start | bytes 1441792 | tf_op jit(solution)/shard_map/all_to_all | solution.py:484
  97.3 0.9 copy-start.6
  98.2 0.7 copy-start.9
  98.9 0.6 copy-start.11
  108.1 0.6 copy-start.12

commit v20 on v16

--- a/solution.py
+++ b/solution.py
@@ -237,33 +237,39 @@
     return 1.0 / (jnp.sqrt(jnp.sum(total, keepdims=True)) + epsilon)
 
 
-def newton_schulz(height, tiles, inverse, x_s, y_s, gram_s, write):
-    padded, width = x_s.shape
-    tile = height // tiles
-    update_scale = 0.2 * math.sqrt(max(height, width))
+def update_scale(height, width):
+    return 0.2 * math.sqrt(max(height, width))
+
+
+def newton_schulz(height, inverse, x_s, y_s, gram_s, finish):
+    padded = x_s.shape[0]
+    tile = height // TILES
     for ref in (y_s, gram_s):
         ref[height:, :] = jnp.zeros((padded - height, ref.shape[1]), ref.dtype)
     for iteration in range(ITERS):
         src = x_s if iteration == 0 else y_s
-        for t in range(tiles):
+        for t in range(TILES):
             span = slice(t * tile, (t + 1) * tile)
             gram = matmul(src[span, :], src[...], 1)
             if iteration == 0:
                 gram = gram * (inverse * inverse)
             gram_s[span, :] = gram.astype(jnp.bfloat16)
-        for t in range(tiles):
+        for t in range(TILES):
             span = slice(t * tile, (t + 1) * tile)
             square = matmul(gram_s[span, :], gram_s[...], 0)
             mixing = coef_b * gram_s[span, :].astype(jnp.float32) + coef_c * square
-            combined = coef_a * src[span, :].astype(jnp.float32) + matmul(
-                mixing.astype(jnp.bfloat16), src[...], 0
-            )
-            if iteration == 0:
-                combined = combined * inverse
+            mixing = mixing.astype(jnp.bfloat16)
             if iteration + 1 < ITERS:
+                combined = combine(src, span, slice(None), mixing)
+                if iteration == 0:
+                    combined = combined * inverse
                 y_s[span, :] = combined.astype(jnp.bfloat16)
             else:
-                write(t, (update_scale * combined).astype(jnp.bfloat16))
+                finish(t, span, mixing)
+
+
+def combine(src, span, columns, mixing):
+    return coef_a * src[span, columns].astype(jnp.float32) + matmul(mixing, src[:, columns], 0)
 
 
 def stage_place(row_offset, col_offset, row_size, width):
@@ -274,50 +280,64 @@
 def ortho_kernel(row_size, col_size, slot, other_ref, x_ref, *refs):
     _, rows, cols = x_ref.shape
     width = col_size // HALVES
+    half = width * cols
     places = row_size * width
     height = rows * row_size
-    tiles = TILES
-    tile = height // tiles
+    tile = height // TILES
     if slot:
-        whole_ref, out_ref, x_s, y_s, gram_s, back_ref, sems = refs
+        whole_ref, out_ref, x_s, y_s, gram_s, back_ref, sems, mix_s = refs
     else:
         owned_ref, low_refs = refs[0], refs[1 : 1 + LOW]
         x_s, y_s, gram_s, back_ref, sems, whole_ref = refs[1 + LOW :]
     row, col = lax.axis_index("dp"), lax.axis_index("owner")
     me = row * col_size + col
     owns = other_ref[me] != me
-    low = col < width
     inverse = gather_blocks(x_ref, x_s, row_size, col_size)
 
     def copy_out(t):
         if slot:
-            span = pl.ds(t * (places // tiles), places // tiles)
+            span = pl.ds(t * (places // TILES), places // TILES)
             return pltpu.make_async_copy(back_ref.at[span], out_ref.at[span], sems.at[t])
         span = pl.ds(t * tile, tile)
         return pltpu.make_async_copy(whole_ref.at[span], owned_ref.at[slot, span], sems.at[t])
 
-    def write(t, result):
-        whole_ref[t * tile : (t + 1) * tile, :] = jnp.where(owns, result, jnp.zeros_like(result))
-        for j in range(row_size // tiles):
-            block = result[j * rows : (j + 1) * rows, :]
-            r = t * (row_size // tiles) + j
+    def product(span, columns, mixing):
+        result = update_scale(height, cols * col_size) * combine(y_s, span, columns, mixing)
+        result = result.astype(jnp.bfloat16)
+        whole_ref[span, columns] = jnp.where(owns, result, jnp.zeros_like(result))
+        return result
+
+    def columns_of(number):
+        return pl.ds(pl.multiple_of(number * half, half), half)
+
+    def finish(t, span, mixing):
+        if slot:
+            mix_s[span, :] = mixing
+            result = product(span, columns_of(col // width), mixing)
+        else:
+            result = product(span, slice(None), mixing)
+            result = jnp.where(col < width, result[:, :half], result[:, half:])
+        for j in range(row_size // TILES):
+            r = t * (row_size // TILES) + j
             for c in range(width):
                 if slot:
                     place = r * width + c
                 else:
                     place = stage_place(r ^ row, c ^ (col % width), row_size, width)
-                back_ref[place] = jnp.where(
-                    low,
-                    block[:, c * cols : (c + 1) * cols],
-                    block[:, (c + width) * cols : (c + width + 1) * cols],
-                )
+                back_ref[place] = result[
+                    j * rows : (j + 1) * rows, c * cols : (c + 1) * cols
+                ]
         copy_out(t).start()
 
-    newton_schulz(height, tiles, inverse, x_s, y_s, gram_s, write)
-    if not slot:
+    newton_schulz(height, inverse, x_s, y_s, gram_s, finish)
+    if slot:
+        for t in range(TILES):
+            span = slice(t * tile, (t + 1) * tile)
+            product(span, columns_of(1 - col // width), mix_s[span, :])
+    else:
         for k in range(LOW):
             low_refs[k][...] = back_ref[k * places // LOW : (k + 1) * places // LOW]
-    for t in range(tiles):
+    for t in range(TILES):
         copy_out(t).wait()
 
 
@@ -334,6 +354,7 @@
         pltpu.SemaphoreType.DMA((TILES,)),
     ]
     if slot:
+        scratch_shapes.append(pltpu.VMEM((height, padded), jnp.bfloat16))
         out_specs = [VMEM, ANYWHERE]
         out = [(height, width), (places, rows, cols)]
     else:

time: 109 us -> 108 us (level)
  transfers between devices with their start and end apart: 9 -> 9, of which waited for: 5 -> 6; matrix products, arithmetic and copies ran while one was open for 0% -> 0% of each run, Pallas kernels for 21% -> 21%
where the time goes in v20:
time: 108 us
  waiting for transfers between devices  52.9 us (49%)
  Pallas kernels  27.9 us (26%)
  starting transfers between devices  23.7 us (22%)
  local copies, waits for them, and re-layouts  2.51 us (2%)
    all_to_all x3, waiting for transfers between devices, exchange(): lax.all_to_all(blocks, axes, split_axis=0, concat_axis=0, tiled=True, axi...  39.8 us
    all_to_all x3, starting transfers between devices, exchange(): lax.all_to_all(blocks, axes, split_axis=0, concat_axis=0, tiled=True, axi...  16.8 us
    pallas_call x2, Pallas kernels, orthogonalize(): pl.pallas_call(functools.partial(ortho_kernel, row_size, col_size, slot),...  16.1 us
    ppermute x6, waiting for transfers between devices, swap(): return lax.ppermute(block, AXES, [(d, d ^ offset) for d in range(devices)])  13.1 us
    ppermute x6, starting transfers between devices, swap(): return lax.ppermute(block, AXES, [(d, d ^ offset) for d in range(devices)])  6.81 us
    pallas_call x1, Pallas kernels, pack(): pl.pallas_call(functools.partial(pack_kernel, chunk, col_size), grid_spec...  4.04 us
    pallas_call x1, Pallas kernels, update_momentum(): pl.pallas_call(functools.partial(momentum_kernel, chunk, col_size), grid_...  3.21 us
    unnamed x12, local copies, waits for them, and re-layouts  2.51 us
  transfers between devices with their start and end apart: 9, of which 6 were waited for; matrix products, arithmetic and copies ran while one was open for 0% of the time, Pallas kernels for 21%

profile of v20, /device:TPU:0, one launch (start us, length us, event | category | flops | bytes accessed | tf_op | source)
XLA Modules:
  0.0 107.7 jit_solution(17044766066407388942)
XLA Ops:
  0.6 4.0 %pack.1 = (bf16[32,88,256]{2,1,0:T(8,128)(2,1)}, s32[32]{0:T(128)}, s32[32]{0:T(128)}) custom-call(s32[32]{0:T(128)} %owner_ref.3, bf16[32,88,256]{2,1,0:T(8,128)(2,1)} %g_ref.3, f32[32,88,256]{2,1,0:T(8,128)} %m_ref.3), custom_call_target="tpu_custom_call" | custom-call | flops 2883584 | bytes 5767168 | tf_op jit(solution)/shard_map/pack/pallas_call | solution.py:118
  4.7 0.0 copy-start
  4.7 0.0 copy-start.3
  4.7 0.0 copy-start.4
  4.7 0.0 copy-start.5
  4.7 7.4 %all-to-all-start = ((bf16[32,88,256]{2,1,0:T(8,128)(2,1)}), bf16[32,88,256]{2,1,0:T(8,128)(2,1)}, u32[]{:S(2)}, u32[]{:S(2)}) async-start(bf16[32,88,256]{2,1,0:T(8,128)(2,1)} %get-tuple-element.34), calls=%async_computation | async-start | bytes 2883584 | tf_op jit(solution)/shard_map/all_to_all | solution.py:477
  12.2 0.0 copy-done
  12.2 0.0 copy-done.3
  12.2 0.0 copy-done.4
  12.2 0.0 copy-done.5
  12.2 0.0 copy-start.1
  12.2 1.4 %copy-done.1 = bf16[32,88,256]{2,1,0:T(8,128)(2,1)S(1)} copy-done((bf16[32,88,256]{2,1,0:T(8,128)(2,1)S(1)}, bf16[32,88,256]{2,1,0:T(8,128)(2,1)}, u32[]{:S(2)}) %copy-start.1) | copy-done | bytes 1441816
  13.6 3.2 %update_momentum.1 = (f32[32,88,256]{2,1,0:T(8,128)}, bf16[32,88,256]{2,1,0:T(8,128)(2,1)S(1)}, s32[64]{0:T(128)S(1)}) custom-call(s32[32]{0:T(128)S(1)} %copy-done.3, s32[32]{0:T(128)S(1)} %copy-done.4, s32[32]{0:T(128)S(1)} %copy-done.5, bf16[32,88,256]{2,1,0:T(8,128)(2,1)S(1)} %copy-done.1, f32[32,88,256]{2,1,0:T(8,128)S(1)} %copy-done), custom_call_target="tpu_custom_call" | custom-call | flops 2883584 | bytes 8650752 | tf_op jit(solution)/shard_map/update_momentum/pallas_call | solution.py:191
  16.8 0.0 copy-start.2
  16.8 1.1 %copy-done.2 = bf16[32,88,256]{2,1,0:T(8,128)(2,1)} copy-done((bf16[32,88,256]{2,1,0:T(8,128)(2,1)}, bf16[32,88,256]{2,1,0:T(8,128)(2,1)S(1)}, u32[]{:S(2)}) %copy-start.2) | copy-done | bytes 1441816
  17.9 27.5 %all-to-all-done.x_ref = bf16[32,88,256]{2,1,0:T(8,128)(2,1)} async-done(((bf16[32,88,256]{2,1,0:T(8,128)(2,1)}), bf16[32,88,256]{2,1,0:T(8,128)(2,1)}, u32[]{:S(2)}, u32[]{:S(2)}) %all-to-all-start) | async-done | bytes 1441824 | tf_op jit(solution)/shard_map/all_to_all | solution.py:477
  45.4 4.6 %all-to-all-start.1 = ((bf16[32,88,256]{2,1,0:T(8,128)(2,1)}), bf16[32,88,256]{2,1,0:T(8,128)(2,1)S(1)}, u32[]{:S(2)}, u32[]{:S(2)}) async-start(bf16[32,88,256]{2,1,0:T(8,128)(2,1)} %copy-done.2), calls=%async_computation.1 | async-start | bytes 2883584 | tf_op jit(solution)/shard_map/all_to_all | solution.py:477
  49.9 8.8 %orthogonalize.2 = (bf16[2,704,1024]{2,1,0:T(8,128)(2,1)}, bf16[4,88,256]{2,1,0:T(8,128)(2,1)S(1)}, bf16[4,88,256]{2,1,0:T(8,128)(2,1)S(1)}, bf16[4,88,256]{2,1,0:T(8,128)(2,1)S(1)}, bf16[4,88,256]{2,1,0:T(8,128)(2,1)S(1)}) custom-call(s32[32]{0:T(128)S(1)} %copy-done.4, bf16[32,88,256]{2,1,0:T(8,128)(2,1)} %all-to-all-done.x_ref), custom_call_target="tpu_custom_call" | custom-call | flops 6643777536 | bytes 4718592 | tf_op jit(solution)/shard_map/orthogonalize/pallas_call | solution.py:364
  58.7 0.3 collective-permute-start
  59.0 1.7 %collective-permute-start.1 = (bf16[4,88,256]{2,1,0:T(8,128)(2,1)S(1)}, bf16[4,88,256]{2,1,0:T(8,128)(2,1)S(1)}, u32[]{:S(2)}, u32[]{:S(2)}) collective-permute-start(bf16[4,88,256]{2,1,0:T(8,128)(2,1)S(1)} %get-tuple-element.39), channel_id=1, source_target_pairs={{0,8},{1,9},{2,10},{3,11},{4,12},{5,13},{6,14},{7,15},{8,0},{9,1},... | collective-permute-start | bytes 540680 | tf_op jit(solution)/shard_map/ppermute | solution.py:483
  60.7 0.0 collective-permute-start.2
  60.7 0.0 collective-permute-done.refs_1_
  60.7 8.8 %collective-permute-done.1.refs_2_ = bf16[4,88,256]{2,1,0:T(8,128)(2,1)S(1)} collective-permute-done((bf16[4,88,256]{2,1,0:T(8,128)(2,1)S(1)}, bf16[4,88,256]{2,1,0:T(8,128)(2,1)S(1)}, u32[]{:S(2)}, u32[]{:S(2)}) %collective-permute-start.1) | collective-permute-done | bytes 180256 | tf_op jit(solution)/shard_map/ppermute | solution.py:483
  69.5 4.2 %collective-permute-done.2.refs_3_ = bf16[4,88,256]{2,1,0:T(8,128)(2,1)S(1)} collective-permute-done((bf16[4,88,256]{2,1,0:T(8,128)(2,1)S(1)}, bf16[4,88,256]{2,1,0:T(8,128)(2,1)S(1)}, u32[]{:S(2)}, u32[]{:S(2)}) %collective-permute-start.2) | collective-permute-done | bytes 180256 | tf_op jit(solution)/shard_map/ppermute | solution.py:483
  73.7 0.8 restage.1
  74.5 3.3 %collective-permute-start.3 = (bf16[4,88,256]{2,1,0:T(8,128)(2,1)}, bf16[4,88,256]{2,1,0:T(8,128)(2,1)S(1)}, u32[]{:S(2)}, u32[]{:S(2)}) collective-permute-start(bf16[4,88,256]{2,1,0:T(8,128)(2,1)} %get-tuple-element.42), channel_id=1, source_target_pairs={{0,1},{1,0},{2,3},{3,2},{4,5},{5,4},{6,7},{7,6},{8,9},{9,8},{10,11... | collective-permute-start | bytes 540680 | tf_op jit(solution)/shard_map/ppermute | solution.py:483
  77.9 1.5 %collective-permute-start.4 = (bf16[4,88,256]{2,1,0:T(8,128)(2,1)}, bf16[4,88,256]{2,1,0:T(8,128)(2,1)S(1)}, u32[]{:S(2)}, u32[]{:S(2)}) collective-permute-start(bf16[4,88,256]{2,1,0:T(8,128)(2,1)} %get-tuple-element.43), channel_id=1, source_target_pairs={{0,16},{1,17},{2,18},{3,19},{4,20},{5,21},{6,22},{7,23},{8,24},{9,... | collective-permute-start | bytes 540680 | tf_op jit(solution)/shard_map/ppermute | solution.py:483
  79.3 0.0 collective-permute-start.5
  79.4 3.8 %all-to-all-done.1.x_ref = bf16[32,88,256]{2,1,0:T(8,128)(2,1)S(1)} async-done(((bf16[32,88,256]{2,1,0:T(8,128)(2,1)}), bf16[32,88,256]{2,1,0:T(8,128)(2,1)S(1)}, u32[]{:S(2)}, u32[]{:S(2)}) %all-to-all-start.1) | async-done | bytes 1441824 | tf_op jit(solution)/shard_map/all_to_all | solution.py:477
  83.2 7.3 %orthogonalize.3 = (bf16[704,1024]{1,0:T(8,128)(2,1)S(1)}, bf16[16,88,256]{2,1,0:T(8,128)(2,1)}) custom-call(s32[32]{0:T(128)S(1)} %copy-done.4, bf16[32,88,256]{2,1,0:T(8,128)(2,1)S(1)} %all-to-all-done.1.x_ref), custom_call_target="tpu_custom_call" | custom-call | flops 6643777536 | bytes 4718592 | tf_op jit(solution)/shard_map/orthogonalize/pallas_call | solution.py:364
  90.5 0.0 collective-permute-done.3.refs_1_
  90.5 0.0 collective-permute-done.4.refs_2_
  90.5 0.1 collective-permute-done.5.refs_3_
  90.6 4.9 %all-to-all-start.2 = ((bf16[16,88,256]{2,1,0:T(8,128)(2,1)}), bf16[16,88,256]{2,1,0:T(8,128)(2,1)S(1)}, u32[]{:S(2)}, u32[]{:S(2)}) async-start(bf16[16,88,256]{2,1,0:T(8,128)(2,1)} %get-tuple-element.48), calls=%async_computation.2 | async-start | bytes 1441792 | tf_op jit(solution)/shard_map/all_to_all | solution.py:477
  95.5 2.3 %store_early.1 = (bf16[2,704,1024]{2,1,0:T(8,128)(2,1)}, bf16[32,88,256]{2,1,0:T(8,128)(2,1)}) custom-call(s32[64]{0:T(128)S(1)} %get-tuple-element.33.list_ref, bf16[704,1024]{1,0:T(8,128)(2,1)S(1)} %get-tuple-element.49.whole_ref, bf16[2,704,1024]{2,1,0:T(8,128)(2,1)} %get-tuple-element.50.owned_in, ...), custom_call_target="tpu_custom_call", output_to_operand_aliasing={{0}: (2, {})} | custom-call | bytes 5767168 | tf_op jit(solution)/shard_map/store_early/pallas_call | solution.py:435
  97.8 8.5 %all-to-all-done.2.back_ref = bf16[16,88,256]{2,1,0:T(8,128)(2,1)S(1)} async-done(((bf16[16,88,256]{2,1,0:T(8,128)(2,1)}), bf16[16,88,256]{2,1,0:T(8,128)(2,1)S(1)}, u32[]{:S(2)}, u32[]{:S(2)}) %all-to-all-start.2) | async-done | bytes 720928 | tf_op jit(solution)/shard_map/all_to_all | solution.py:477
  106.3 1.4 %store_late.1 = bf16[32,88,256]{2,1,0:T(8,128)(2,1)} custom-call(s32[64]{0:T(128)S(1)} %get-tuple-element.33.list_ref, bf16[16,88,256]{2,1,0:T(8,128)(2,1)S(1)} %all-to-all-done.2.back_ref, bf16[32,88,256]{2,1,0:T(8,128)(2,1)} %get-tuple-element.55.update_in), custom_call_target="tpu_custom_call", output_to_operand_aliasing={{}: (2, {})} | custom-call | bytes 1441792 | tf_op jit(solution)/shard_map/store_late/pallas_call | solution.py:463
Async XLA Ops:
  4.7 7.5 %copy-start = (f32[32,88,256]{2,1,0:T(8,128)S(1)}, f32[32,88,256]{2,1,0:T(8,128)}, u32[]{:S(2)}) copy-start(f32[32,88,256]{2,1,0:T(8,128)} %m_ref.3) | copy-start | bytes 8650756
  4.7 7.5 %copy-start.3 = (s32[32]{0:T(128)S(1)}, s32[32]{0:T(128)}, u32[]{:S(2)}) copy-start(s32[32]{0:T(128)} %owner_ref.3) | copy-start | bytes 388
  4.7 7.5 %copy-start.4 = (s32[32]{0:T(128)S(1)}, s32[32]{0:T(128)}, u32[]{:S(2)}) copy-start(s32[32]{0:T(128)} %get-tuple-element.30.other_ref) | copy-start | bytes 388
  4.7 7.5 %copy-start.5 = (s32[32]{0:T(128)S(1)}, s32[32]{0:T(128)}, u32[]{:S(2)}) copy-start(s32[32]{0:T(128)} %get-tuple-element.31.rank_ref) | copy-start | bytes 388
  4.7 40.6 %all-to-all-start = ((bf16[32,88,256]{2,1,0:T(8,128)(2,1)}), bf16[32,88,256]{2,1,0:T(8,128)(2,1)}, u32[]{:S(2)}, u32[]{:S(2)}) async-start(bf16[32,88,256]{2,1,0:T(8,128)(2,1)} %get-tuple-element.34), calls=%async_computation | async-start | bytes 2883584 | tf_op jit(solution)/shard_map/all_to_all | solution.py:477
  12.2 1.4 %copy-start.1 = (bf16[32,88,256]{2,1,0:T(8,128)(2,1)S(1)}, bf16[32,88,256]{2,1,0:T(8,128)(2,1)}, u32[]{:S(2)}) copy-start(bf16[32,88,256]{2,1,0:T(8,128)(2,1)} %g_ref.3) | copy-start | bytes 4325380
  16.8 1.1 %copy-start.2 = (bf16[32,88,256]{2,1,0:T(8,128)(2,1)}, bf16[32,88,256]{2,1,0:T(8,128)(2,1)S(1)}, u32[]{:S(2)}) copy-start(bf16[32,88,256]{2,1,0:T(8,128)(2,1)S(1)} %get-tuple-element.45) | copy-start | bytes 4325380
  45.4 37.8 %all-to-all-start.1 = ((bf16[32,88,256]{2,1,0:T(8,128)(2,1)}), bf16[32,88,256]{2,1,0:T(8,128)(2,1)S(1)}, u32[]{:S(2)}, u32[]{:S(2)}) async-start(bf16[32,88,256]{2,1,0:T(8,128)(2,1)} %copy-done.2), calls=%async_computation.1 | async-start | bytes 2883584 | tf_op jit(solution)/shard_map/all_to_all | solution.py:477
  58.7 2.0 %collective-permute-start = (bf16[4,88,256]{2,1,0:T(8,128)(2,1)S(1)}, bf16[4,88,256]{2,1,0:T(8,128)(2,1)S(1)}, u32[]{:S(2)}, u32[]{:S(2)}) collective-permute-start(bf16[4,88,256]{2,1,0:T(8,128)(2,1)S(1)} %get-tuple-element.38), channel_id=1, source_target_pairs={{0,4},{1,5},{2,6},{3,7},{4,0},{5,1},{6,2},{7,3},{8,12},{9,13},{10,... | collective-permute-start | bytes 540680 | tf_op jit(solution)/shard_map/ppermute | solution.py:483
  59.0 10.5 %collective-permute-start.1 = (bf16[4,88,256]{2,1,0:T(8,128)(2,1)S(1)}, bf16[4,88,256]{2,1,0:T(8,128)(2,1)S(1)}, u32[]{:S(2)}, u32[]{:S(2)}) collective-permute-start(bf16[4,88,256]{2,1,0:T(8,128)(2,1)S(1)} %get-tuple-element.39), channel_id=1, source_target_pairs={{0,8},{1,9},{2,10},{3,11},{4,12},{5,13},{6,14},{7,15},{8,0},{9,1},... | collective-permute-start | bytes 540680 | tf_op jit(solution)/shard_map/ppermute | solution.py:483
  60.7 13.0 %collective-permute-start.2 = (bf16[4,88,256]{2,1,0:T(8,128)(2,1)S(1)}, bf16[4,88,256]{2,1,0:T(8,128)(2,1)S(1)}, u32[]{:S(2)}, u32[]{:S(2)}) collective-permute-start(bf16[4,88,256]{2,1,0:T(8,128)(2,1)S(1)} %get-tuple-element.40), channel_id=1, source_target_pairs={{0,12},{1,13},{2,14},{3,15},{4,8},{5,9},{6,10},{7,11},{8,4},{9,5},... | collective-permute-start | bytes 540680 | tf_op jit(solution)/shard_map/ppermute | solution.py:483
  74.5 15.9 %collective-permute-start.3 = (bf16[4,88,256]{2,1,0:T(8,128)(2,1)}, bf16[4,88,256]{2,1,0:T(8,128)(2,1)S(1)}, u32[]{:S(2)}, u32[]{:S(2)}) collective-permute-start(bf16[4,88,256]{2,1,0:T(8,128)(2,1)} %get-tuple-element.42), channel_id=1, source_target_pairs={{0,1},{1,0},{2,3},{3,2},{4,5},{5,4},{6,7},{7,6},{8,9},{9,8},{10,11... | collective-permute-start | bytes 540680 | tf_op jit(solution)/shard_map/ppermute | solution.py:483
  77.9 12.6 %collective-permute-start.4 = (bf16[4,88,256]{2,1,0:T(8,128)(2,1)}, bf16[4,88,256]{2,1,0:T(8,128)(2,1)S(1)}, u32[]{:S(2)}, u32[]{:S(2)}) collective-permute-start(bf16[4,88,256]{2,1,0:T(8,128)(2,1)} %get-tuple-element.43), channel_id=1, source_target_pairs={{0,16},{1,17},{2,18},{3,19},{4,20},{5,21},{6,22},{7,23},{8,24},{9,... | collective-permute-start | bytes 540680 | tf_op jit(solution)/shard_map/ppermute | solution.py:483
  79.3 11.2 %collective-permute-start.5 = (bf16[4,88,256]{2,1,0:T(8,128)(2,1)}, bf16[4,88,256]{2,1,0:T(8,128)(2,1)}, u32[]{:S(2)}, u32[]{:S(2)}) collective-permute-start(bf16[4,88,256]{2,1,0:T(8,128)(2,1)} %get-tuple-element.44), channel_id=1, source_target_pairs={{0,17},{1,16},{2,19},{3,18},{4,21},{5,20},{6,23},{7,22},{8,25},{9,... | collective-permute-start | bytes 540680 | tf_op jit(solution)/shard_map/ppermute | solution.py:483
  90.6 15.7 %all-to-all-start.2 = ((bf16[16,88,256]{2,1,0:T(8,128)(2,1)}), bf16[16,88,256]{2,1,0:T(8,128)(2,1)S(1)}, u32[]{:S(2)}, u32[]{:S(2)}) async-start(bf16[16,88,256]{2,1,0:T(8,128)(2,1)} %get-tuple-element.48), calls=%async_computation.2 | async-start | bytes 1441792 | tf_op jit(solution)/shard_map/all_to_all | solution.py:477

commit v21 on v20

--- a/solution.py
+++ b/solution.py
@@ -41,6 +41,11 @@
     grad = grad_ref[j].astype(jnp.float32)
     new = momentum_beta * momentum_ref[j] + grad
     return new, (grad + momentum_beta * new).astype(jnp.bfloat16)
+
+
+def order_place(d, col_size):
+    row, col = d // col_size, d % col_size
+    return row // 2 * (2 * col_size) + col * 2 + row % 2
 
 
 def make_plan(col_size, owner_ref, other_ref, rank_ref, count_ref, list_ref):
@@ -108,8 +113,8 @@
             @pl.when(rank_ref[i] == 0)
             def _():
                 nesterov = nesterov_of(g_s, m_s, i)[1]
-                first_ref[owner_ref[i]] = nesterov
-                first_ref[other_ref[owner_ref[i]]] = nesterov
+                first_ref[order_place(owner_ref[i], col_size)] = nesterov
+                first_ref[order_place(other_ref[owner_ref[i]], col_size)] = nesterov
 
 
 def pack(gradients, momentum, owner_table, devices, col_size):
@@ -165,8 +170,8 @@
 
         @pl.when(rank_ref[i] == 1)
         def _():
-            second_ref[owner] = nesterov
-            second_ref[other_ref[owner]] = nesterov
+            second_ref[order_place(owner, col_size)] = nesterov
+            second_ref[order_place(other_ref[owner], col_size)] = nesterov
 
         near = (owner % col_size) // width == col // width
         host = jnp.where(near, owner, other_ref[owner])
@@ -229,7 +234,7 @@
     total = 0.0
     for r in range(row_size):
         for c in range(col_size):
-            block = x_ref[r * col_size + c]
+            block = x_ref[order_place(r * col_size + c, col_size)]
             x_s[r * rows : (r + 1) * rows, c * cols : (c + 1) * cols] = block
             wide = block.astype(jnp.float32)
             total = total + sum_rows(wide * wide)
@@ -493,12 +498,13 @@
         for half in range(HALVES)
     ]
     first, other, rank = pack(gradients, momentum, owner_table, devices, col_size)
-    arrived_first = exchange(first, AXES)
+    order = sorted(range(devices), key=lambda d: order_place(d, col_size))
+    arrived_first = exchange(first, AXES, [order])
     new_momentum, second, places = update_momentum(
         gradients, momentum, owner_table, other, rank, col_size
     )
     arrived_first, second = lax.optimization_barrier((arrived_first, second))
-    arrived_second = exchange(second, AXES)
+    arrived_second = exchange(second, AXES, [order])
     owned, *back_first = orthogonalize(0, other, arrived_first, row_size, col_size)
     low = [back_first[0]] + [
         swap(back_first[k], k * col_size, devices) for k in range(1, LOW)

time: 108 us -> 111 us (1.028)
  waiting for transfers between devices: 52.9 us -> 57.5 us
  starting transfers between devices: 23.7 us -> 21.1 us
    all_to_all x3, waiting for transfers between devices: 39.8 us -> 45.1 us  [exchange(): lax.all_to_all(blocks, axes, split_axis=0, concat_axis=0, tiled=True, axi...]
    all_to_all x3, starting transfers between devices: 16.8 us -> 13.9 us  [exchange(): lax.all_to_all(blocks, axes, split_axis=0, concat_axis=0, tiled=True, axi...]
  transfers between devices with their start and end apart: 9 -> 9, of which waited for: 6 -> 5; matrix products, arithmetic and copies ran while one was open for 0% -> 0% of each run, Pallas kernels for 21% -> 21%
where the time goes in v21:
time: 111 us; the launch traced here: 110 us
  waiting for transfers between devices  57.5 us (52%)
  Pallas kernels  28.2 us (25%)
  starting transfers between devices  21.1 us (19%)
  local copies, waits for them, and re-layouts  2.51 us (2%)
    all_to_all x3, waiting for transfers between devices, exchange(): lax.all_to_all(blocks, axes, split_axis=0, concat_axis=0, tiled=True, axi...  45.1 us
    pallas_call x2, Pallas kernels, orthogonalize(): pl.pallas_call(functools.partial(ortho_kernel, row_size, col_size, slot),...  16.1 us
    all_to_all x3, starting transfers between devices, exchange(): lax.all_to_all(blocks, axes, split_axis=0, concat_axis=0, tiled=True, axi...  13.9 us
    ppermute x6, waiting for transfers between devices, swap(): return lax.ppermute(block, AXES, [(d, d ^ offset) for d in range(devices)])  12.5 us
    ppermute x6, starting transfers between devices, swap(): return lax.ppermute(block, AXES, [(d, d ^ offset) for d in range(devices)])  7.22 us
    pallas_call x1, Pallas kernels, pack(): pl.pallas_call(functools.partial(pack_kernel, chunk, col_size), grid_spec...  4.04 us
    pallas_call x1, Pallas kernels, update_momentum(): pl.pallas_call(functools.partial(momentum_kernel, chunk, col_size), grid_...  3.58 us
    unnamed x12, local copies, waits for them, and re-layouts  2.51 us
  transfers between devices with their start and end apart: 9, of which 5 were waited for; matrix products, arithmetic and copies ran while one was open for 0% of the time, Pallas kernels for 21%

profile of v21, /device:TPU:0, one launch (start us, length us, event | category | flops | bytes accessed | tf_op | source)
XLA Modules:
  0.0 110.3 jit_solution(571484211838047680)
XLA Ops:
  0.6 4.0 %pack.1 = (bf16[32,88,256]{2,1,0:T(8,128)(2,1)}, s32[32]{0:T(128)}, s32[32]{0:T(128)}) custom-call(s32[32]{0:T(128)} %owner_ref.3, bf16[32,88,256]{2,1,0:T(8,128)(2,1)} %g_ref.3, f32[32,88,256]{2,1,0:T(8,128)} %m_ref.3), custom_call_target="tpu_custom_call" | custom-call | flops 2883584 | bytes 5767168 | tf_op jit(solution)/shard_map/pack/pallas_call | solution.py:123
  4.7 0.0 copy-start
  4.7 0.0 copy-start.3
  4.7 0.0 copy-start.4
  4.7 0.0 copy-start.5
  4.7 7.4 %all-to-all-start = ((bf16[32,88,256]{2,1,0:T(8,128)(2,1)}), bf16[32,88,256]{2,1,0:T(8,128)(2,1)}, u32[]{:S(2)}, u32[]{:S(2)}) async-start(bf16[32,88,256]{2,1,0:T(8,128)(2,1)} %get-tuple-element.34), calls=%async_computation | async-start | bytes 2883584 | tf_op jit(solution)/shard_map/all_to_all | solution.py:482
  12.2 0.0 copy-done
  12.2 0.0 copy-done.3
  12.2 0.0 copy-done.4
  12.2 0.0 copy-done.5
  12.2 0.0 copy-start.1
  12.2 1.4 %copy-done.1 = bf16[32,88,256]{2,1,0:T(8,128)(2,1)S(1)} copy-done((bf16[32,88,256]{2,1,0:T(8,128)(2,1)S(1)}, bf16[32,88,256]{2,1,0:T(8,128)(2,1)}, u32[]{:S(2)}) %copy-start.1) | copy-done | bytes 1441816
  13.6 3.6 %update_momentum.1 = (f32[32,88,256]{2,1,0:T(8,128)}, bf16[32,88,256]{2,1,0:T(8,128)(2,1)S(1)}, s32[64]{0:T(128)S(1)}) custom-call(s32[32]{0:T(128)S(1)} %copy-done.3, s32[32]{0:T(128)S(1)} %copy-done.4, s32[32]{0:T(128)S(1)} %copy-done.5, bf16[32,88,256]{2,1,0:T(8,128)(2,1)S(1)} %copy-done.1, f32[32,88,256]{2,1,0:T(8,128)S(1)} %copy-done), custom_call_target="tpu_custom_call" | custom-call | flops 2883584 | bytes 8650752 | tf_op jit(solution)/shard_map/update_momentum/pallas_call | solution.py:196
  17.1 0.0 copy-start.2
  17.1 1.1 %copy-done.2 = bf16[32,88,256]{2,1,0:T(8,128)(2,1)} copy-done((bf16[32,88,256]{2,1,0:T(8,128)(2,1)}, bf16[32,88,256]{2,1,0:T(8,128)(2,1)S(1)}, u32[]{:S(2)}) %copy-start.2) | copy-done | bytes 1441816
  18.3 29.9 %all-to-all-done.x_ref = bf16[32,88,256]{2,1,0:T(8,128)(2,1)} async-done(((bf16[32,88,256]{2,1,0:T(8,128)(2,1)}), bf16[32,88,256]{2,1,0:T(8,128)(2,1)}, u32[]{:S(2)}, u32[]{:S(2)}) %all-to-all-start) | async-done | bytes 1441824 | tf_op jit(solution)/shard_map/all_to_all | solution.py:482
  48.2 2.9 %all-to-all-start.1 = ((bf16[32,88,256]{2,1,0:T(8,128)(2,1)}), bf16[32,88,256]{2,1,0:T(8,128)(2,1)S(1)}, u32[]{:S(2)}, u32[]{:S(2)}) async-start(bf16[32,88,256]{2,1,0:T(8,128)(2,1)} %copy-done.2), calls=%async_computation.1 | async-start | bytes 2883584 | tf_op jit(solution)/shard_map/all_to_all | solution.py:482
  51.1 8.8 %orthogonalize.2 = (bf16[2,704,1024]{2,1,0:T(8,128)(2,1)}, bf16[4,88,256]{2,1,0:T(8,128)(2,1)S(1)}, bf16[4,88,256]{2,1,0:T(8,128)(2,1)S(1)}, bf16[4,88,256]{2,1,0:T(8,128)(2,1)S(1)}, bf16[4,88,256]{2,1,0:T(8,128)(2,1)S(1)}) custom-call(s32[32]{0:T(128)S(1)} %copy-done.4, bf16[32,88,256]{2,1,0:T(8,128)(2,1)} %all-to-all-done.x_ref), custom_call_target="tpu_custom_call" | custom-call | flops 6643777536 | bytes 4718592 | tf_op jit(solution)/shard_map/orthogonalize/pallas_call | solution.py:369
  59.8 0.2 collective-permute-start
  60.0 1.7 %collective-permute-start.1 = (bf16[4,88,256]{2,1,0:T(8,128)(2,1)S(1)}, bf16[4,88,256]{2,1,0:T(8,128)(2,1)S(1)}, u32[]{:S(2)}, u32[]{:S(2)}) collective-permute-start(bf16[4,88,256]{2,1,0:T(8,128)(2,1)S(1)} %get-tuple-element.39), channel_id=1, source_target_pairs={{0,8},{1,9},{2,10},{3,11},{4,12},{5,13},{6,14},{7,15},{8,0},{9,1},... | collective-permute-start | bytes 540680 | tf_op jit(solution)/shard_map/ppermute | solution.py:488
  61.7 0.1 collective-permute-start.2
  61.8 0.0 collective-permute-done.refs_1_
  61.8 8.1 %collective-permute-done.1.refs_2_ = bf16[4,88,256]{2,1,0:T(8,128)(2,1)S(1)} collective-permute-done((bf16[4,88,256]{2,1,0:T(8,128)(2,1)S(1)}, bf16[4,88,256]{2,1,0:T(8,128)(2,1)S(1)}, u32[]{:S(2)}, u32[]{:S(2)}) %collective-permute-start.1) | collective-permute-done | bytes 180256 | tf_op jit(solution)/shard_map/ppermute | solution.py:488
  69.9 4.4 %collective-permute-done.2.refs_3_ = bf16[4,88,256]{2,1,0:T(8,128)(2,1)S(1)} collective-permute-done((bf16[4,88,256]{2,1,0:T(8,128)(2,1)S(1)}, bf16[4,88,256]{2,1,0:T(8,128)(2,1)S(1)}, u32[]{:S(2)}, u32[]{:S(2)}) %collective-permute-start.2) | collective-permute-done | bytes 180256 | tf_op jit(solution)/shard_map/ppermute | solution.py:488
  74.3 0.8 restage.1
  75.1 3.8 %collective-permute-start.3 = (bf16[4,88,256]{2,1,0:T(8,128)(2,1)}, bf16[4,88,256]{2,1,0:T(8,128)(2,1)S(1)}, u32[]{:S(2)}, u32[]{:S(2)}) collective-permute-start(bf16[4,88,256]{2,1,0:T(8,128)(2,1)} %get-tuple-element.42), channel_id=1, source_target_pairs={{0,1},{1,0},{2,3},{3,2},{4,5},{5,4},{6,7},{7,6},{8,9},{9,8},{10,11... | collective-permute-start | bytes 540680 | tf_op jit(solution)/shard_map/ppermute | solution.py:488
  78.8 1.5 %collective-permute-start.4 = (bf16[4,88,256]{2,1,0:T(8,128)(2,1)}, bf16[4,88,256]{2,1,0:T(8,128)(2,1)S(1)}, u32[]{:S(2)}, u32[]{:S(2)}) collective-permute-start(bf16[4,88,256]{2,1,0:T(8,128)(2,1)} %get-tuple-element.43), channel_id=1, source_target_pairs={{0,16},{1,17},{2,18},{3,19},{4,20},{5,21},{6,22},{7,23},{8,24},{9,... | collective-permute-start | bytes 540680 | tf_op jit(solution)/shard_map/ppermute | solution.py:488
  80.3 0.0 collective-permute-start.5
  80.4 6.7 %all-to-all-done.1.x_ref = bf16[32,88,256]{2,1,0:T(8,128)(2,1)S(1)} async-done(((bf16[32,88,256]{2,1,0:T(8,128)(2,1)}), bf16[32,88,256]{2,1,0:T(8,128)(2,1)S(1)}, u32[]{:S(2)}, u32[]{:S(2)}) %all-to-all-start.1) | async-done | bytes 1441824 | tf_op jit(solution)/shard_map/all_to_all | solution.py:482
  87.1 7.3 %orthogonalize.3 = (bf16[704,1024]{1,0:T(8,128)(2,1)S(1)}, bf16[16,88,256]{2,1,0:T(8,128)(2,1)}) custom-call(s32[32]{0:T(128)S(1)} %copy-done.4, bf16[32,88,256]{2,1,0:T(8,128)(2,1)S(1)} %all-to-all-done.1.x_ref), custom_call_target="tpu_custom_call" | custom-call | flops 6643777536 | bytes 4718592 | tf_op jit(solution)/shard_map/orthogonalize/pallas_call | solution.py:369
  94.4 0.0 collective-permute-done.3.refs_1_
  94.4 0.0 collective-permute-done.4.refs_2_
  94.4 0.0 collective-permute-done.5.refs_3_
  94.4 3.6 %all-to-all-start.2 = ((bf16[16,88,256]{2,1,0:T(8,128)(2,1)}), bf16[16,88,256]{2,1,0:T(8,128)(2,1)S(1)}, u32[]{:S(2)}, u32[]{:S(2)}) async-start(bf16[16,88,256]{2,1,0:T(8,128)(2,1)} %get-tuple-element.48), calls=%async_computation.2 | async-start | bytes 1441792 | tf_op jit(solution)/shard_map/all_to_all | solution.py:482
  98.0 2.3 %store_early.1 = (bf16[2,704,1024]{2,1,0:T(8,128)(2,1)}, bf16[32,88,256]{2,1,0:T(8,128)(2,1)}) custom-call(s32[64]{0:T(128)S(1)} %get-tuple-element.33.list_ref, bf16[704,1024]{1,0:T(8,128)(2,1)S(1)} %get-tuple-element.49.whole_ref, bf16[2,704,1024]{2,1,0:T(8,128)(2,1)} %get-tuple-element.50.owned_in, ...), custom_call_target="tpu_custom_call", output_to_operand_aliasing={{0}: (2, {})} | custom-call | bytes 5767168 | tf_op jit(solution)/shard_map/store_early/pallas_call | solution.py:440
  100.3 8.4 %all-to-all-done.2.back_ref = bf16[16,88,256]{2,1,0:T(8,128)(2,1)S(1)} async-done(((bf16[16,88,256]{2,1,0:T(8,128)(2,1)}), bf16[16,88,256]{2,1,0:T(8,128)(2,1)S(1)}, u32[]{:S(2)}, u32[]{:S(2)}) %all-to-all-start.2) | async-done | bytes 720928 | tf_op jit(solution)/shard_map/all_to_all | solution.py:482
  108.8 1.4 %store_late.1 = bf16[32,88,256]{2,1,0:T(8,128)(2,1)} custom-call(s32[64]{0:T(128)S(1)} %get-tuple-element.33.list_ref, bf16[16,88,256]{2,1,0:T(8,128)(2,1)S(1)} %all-to-all-done.2.back_ref, bf16[32,88,256]{2,1,0:T(8,128)(2,1)} %get-tuple-element.55.update_in), custom_call_target="tpu_custom_call", output_to_operand_aliasing={{}: (2, {})} | custom-call | bytes 1441792 | tf_op jit(solution)/shard_map/store_late/pallas_call | solution.py:468
Async XLA Ops:
  4.7 7.5 %copy-start = (f32[32,88,256]{2,1,0:T(8,128)S(1)}, f32[32,88,256]{2,1,0:T(8,128)}, u32[]{:S(2)}) copy-start(f32[32,88,256]{2,1,0:T(8,128)} %m_ref.3) | copy-start | bytes 8650756
  4.7 7.5 %copy-start.3 = (s32[32]{0:T(128)S(1)}, s32[32]{0:T(128)}, u32[]{:S(2)}) copy-start(s32[32]{0:T(128)} %owner_ref.3) | copy-start | bytes 388
  4.7 7.5 %copy-start.4 = (s32[32]{0:T(128)S(1)}, s32[32]{0:T(128)}, u32[]{:S(2)}) copy-start(s32[32]{0:T(128)} %get-tuple-element.30.other_ref) | copy-start | bytes 388
  4.7 7.5 %copy-start.5 = (s32[32]{0:T(128)S(1)}, s32[32]{0:T(128)}, u32[]{:S(2)}) copy-start(s32[32]{0:T(128)} %get-tuple-element.31.rank_ref) | copy-start | bytes 388
  4.7 43.5 %all-to-all-start = ((bf16[32,88,256]{2,1,0:T(8,128)(2,1)}), bf16[32,88,256]{2,1,0:T(8,128)(2,1)}, u32[]{:S(2)}, u32[]{:S(2)}) async-start(bf16[32,88,256]{2,1,0:T(8,128)(2,1)} %get-tuple-element.34), calls=%async_computation | async-start | bytes 2883584 | tf_op jit(solution)/shard_map/all_to_all | solution.py:482
  12.2 1.4 %copy-start.1 = (bf16[32,88,256]{2,1,0:T(8,128)(2,1)S(1)}, bf16[32,88,256]{2,1,0:T(8,128)(2,1)}, u32[]{:S(2)}) copy-start(bf16[32,88,256]{2,1,0:T(8,128)(2,1)} %g_ref.3) | copy-start | bytes 4325380
  17.1 1.1 %copy-start.2 = (bf16[32,88,256]{2,1,0:T(8,128)(2,1)}, bf16[32,88,256]{2,1,0:T(8,128)(2,1)S(1)}, u32[]{:S(2)}) copy-start(bf16[32,88,256]{2,1,0:T(8,128)(2,1)S(1)} %get-tuple-element.45) | copy-start | bytes 4325380
  48.2 38.9 %all-to-all-start.1 = ((bf16[32,88,256]{2,1,0:T(8,128)(2,1)}), bf16[32,88,256]{2,1,0:T(8,128)(2,1)S(1)}, u32[]{:S(2)}, u32[]{:S(2)}) async-start(bf16[32,88,256]{2,1,0:T(8,128)(2,1)} %copy-done.2), calls=%async_computation.1 | async-start | bytes 2883584 | tf_op jit(solution)/shard_map/all_to_all | solution.py:482
  59.8 2.0 %collective-permute-start = (bf16[4,88,256]{2,1,0:T(8,128)(2,1)S(1)}, bf16[4,88,256]{2,1,0:T(8,128)(2,1)S(1)}, u32[]{:S(2)}, u32[]{:S(2)}) collective-permute-start(bf16[4,88,256]{2,1,0:T(8,128)(2,1)S(1)} %get-tuple-element.38), channel_id=1, source_target_pairs={{0,4},{1,5},{2,6},{3,7},{4,0},{5,1},{6,2},{7,3},{8,12},{9,13},{10,... | collective-permute-start | bytes 540680 | tf_op jit(solution)/shard_map/ppermute | solution.py:488
  60.0 9.9 %collective-permute-start.1 = (bf16[4,88,256]{2,1,0:T(8,128)(2,1)S(1)}, bf16[4,88,256]{2,1,0:T(8,128)(2,1)S(1)}, u32[]{:S(2)}, u32[]{:S(2)}) collective-permute-start(bf16[4,88,256]{2,1,0:T(8,128)(2,1)S(1)} %get-tuple-element.39), channel_id=1, source_target_pairs={{0,8},{1,9},{2,10},{3,11},{4,12},{5,13},{6,14},{7,15},{8,0},{9,1},... | collective-permute-start | bytes 540680 | tf_op jit(solution)/shard_map/ppermute | solution.py:488
  61.7 12.6 %collective-permute-start.2 = (bf16[4,88,256]{2,1,0:T(8,128)(2,1)S(1)}, bf16[4,88,256]{2,1,0:T(8,128)(2,1)S(1)}, u32[]{:S(2)}, u32[]{:S(2)}) collective-permute-start(bf16[4,88,256]{2,1,0:T(8,128)(2,1)S(1)} %get-tuple-element.40), channel_id=1, source_target_pairs={{0,12},{1,13},{2,14},{3,15},{4,8},{5,9},{6,10},{7,11},{8,4},{9,5},... | collective-permute-start | bytes 540680 | tf_op jit(solution)/shard_map/ppermute | solution.py:488
  75.1 19.3 %collective-permute-start.3 = (bf16[4,88,256]{2,1,0:T(8,128)(2,1)}, bf16[4,88,256]{2,1,0:T(8,128)(2,1)S(1)}, u32[]{:S(2)}, u32[]{:S(2)}) collective-permute-start(bf16[4,88,256]{2,1,0:T(8,128)(2,1)} %get-tuple-element.42), channel_id=1, source_target_pairs={{0,1},{1,0},{2,3},{3,2},{4,5},{5,4},{6,7},{7,6},{8,9},{9,8},{10,11... | collective-permute-start | bytes 540680 | tf_op jit(solution)/shard_map/ppermute | solution.py:488
  78.8 15.5 %collective-permute-start.4 = (bf16[4,88,256]{2,1,0:T(8,128)(2,1)}, bf16[4,88,256]{2,1,0:T(8,128)(2,1)S(1)}, u32[]{:S(2)}, u32[]{:S(2)}) collective-permute-start(bf16[4,88,256]{2,1,0:T(8,128)(2,1)} %get-tuple-element.43), channel_id=1, source_target_pairs={{0,16},{1,17},{2,18},{3,19},{4,20},{5,21},{6,22},{7,23},{8,24},{9,... | collective-permute-start | bytes 540680 | tf_op jit(solution)/shard_map/ppermute | solution.py:488
  80.3 14.0 %collective-permute-start.5 = (bf16[4,88,256]{2,1,0:T(8,128)(2,1)}, bf16[4,88,256]{2,1,0:T(8,128)(2,1)}, u32[]{:S(2)}, u32[]{:S(2)}) collective-permute-start(bf16[4,88,256]{2,1,0:T(8,128)(2,1)} %get-tuple-element.44), channel_id=1, source_target_pairs={{0,17},{1,16},{2,19},{3,18},{4,21},{5,20},{6,23},{7,22},{8,25},{9,... | collective-permute-start | bytes 540680 | tf_op jit(solution)/shard_map/ppermute | solution.py:488
  94.4 14.4 %all-to-all-start.2 = ((bf16[16,88,256]{2,1,0:T(8,128)(2,1)}), bf16[16,88,256]{2,1,0:T(8,128)(2,1)S(1)}, u32[]{:S(2)}, u32[]{:S(2)}) async-start(bf16[16,88,256]{2,1,0:T(8,128)(2,1)} %get-tuple-element.48), calls=%async_computation.2 | async-start | bytes 1441792 | tf_op jit(solution)/shard_map/all_to_all | solution.py:482

commit v22 on v20

--- a/solution.py
+++ b/solution.py
@@ -11,7 +11,7 @@
 ITERS = 2
 CAP = 2
 HALVES = 2
-TILES = 2
+TILES = 4
 LOW = 4
 
 coef_a = 3.4445

time: 108 us -> 110 us (1.019)
  Pallas kernels: 27.9 us -> 31.4 us
    pallas_call x2, Pallas kernels: 16.1 us -> 19.6 us  [orthogonalize(): pl.pallas_call(functools.partial(ortho_kernel, row_size, col_size, slot),...]
  transfers between devices with their start and end apart: 9 -> 9, of which waited for: 6 -> 5; matrix products, arithmetic and copies ran while one was open for 0% -> 0% of each run, Pallas kernels for 21% -> 24%
where the time goes in v22:
time: 110 us
  waiting for transfers between devices  51.9 us (47%)
  Pallas kernels  31.4 us (29%)
  starting transfers between devices  22.9 us (21%)
  local copies, waits for them, and re-layouts  2.51 us (2%)
    all_to_all x3, waiting for transfers between devices, exchange(): lax.all_to_all(blocks, axes, split_axis=0, concat_axis=0, tiled=True, axi...  39 us
    pallas_call x2, Pallas kernels, orthogonalize(): pl.pallas_call(functools.partial(ortho_kernel, row_size, col_size, slot),...  19.6 us
    all_to_all x3, starting transfers between devices, exchange(): lax.all_to_all(blocks, axes, split_axis=0, concat_axis=0, tiled=True, axi...  16.9 us
    ppermute x6, waiting for transfers between devices, swap(): return lax.ppermute(block, AXES, [(d, d ^ offset) for d in range(devices)])  12.9 us
    ppermute x6, starting transfers between devices, swap(): return lax.ppermute(block, AXES, [(d, d ^ offset) for d in range(devices)])  6.02 us
    pallas_call x1, Pallas kernels, pack(): pl.pallas_call(functools.partial(pack_kernel, chunk, col_size), grid_spec...  4.04 us
    pallas_call x1, Pallas kernels, update_momentum(): pl.pallas_call(functools.partial(momentum_kernel, chunk, col_size), grid_...  3.21 us
    unnamed x12, local copies, waits for them, and re-layouts  2.51 us
  transfers between devices with their start and end apart: 9, of which 5 were waited for; matrix products, arithmetic and copies ran while one was open for 0% of the time, Pallas kernels for 24%

profile of v22, /device:TPU:0, one launch (start us, length us, event | category | flops | bytes accessed | tf_op | source)
XLA Modules:
  0.0 109.5 jit_solution(12008965421224035227)
XLA Ops:
  0.6 4.0 %pack.1 = (bf16[32,88,256]{2,1,0:T(8,128)(2,1)}, s32[32]{0:T(128)}, s32[32]{0:T(128)}) custom-call(s32[32]{0:T(128)} %owner_ref.3, bf16[32,88,256]{2,1,0:T(8,128)(2,1)} %g_ref.3, f32[32,88,256]{2,1,0:T(8,128)} %m_ref.3), custom_call_target="tpu_custom_call" | custom-call | flops 2883584 | bytes 5767168 | tf_op jit(solution)/shard_map/pack/pallas_call | solution.py:118
  4.7 0.0 copy-start
  4.7 0.0 copy-start.3
  4.7 0.0 copy-start.4
  4.7 0.0 copy-start.5
  4.7 7.4 %all-to-all-start = ((bf16[32,88,256]{2,1,0:T(8,128)(2,1)}), bf16[32,88,256]{2,1,0:T(8,128)(2,1)}, u32[]{:S(2)}, u32[]{:S(2)}) async-start(bf16[32,88,256]{2,1,0:T(8,128)(2,1)} %get-tuple-element.34), calls=%async_computation | async-start | bytes 2883584 | tf_op jit(solution)/shard_map/all_to_all | solution.py:477
  12.2 0.0 copy-done
  12.2 0.0 copy-done.3
  12.2 0.0 copy-done.4
  12.2 0.0 copy-done.5
  12.2 0.0 copy-start.1
  12.2 1.4 %copy-done.1 = bf16[32,88,256]{2,1,0:T(8,128)(2,1)S(1)} copy-done((bf16[32,88,256]{2,1,0:T(8,128)(2,1)S(1)}, bf16[32,88,256]{2,1,0:T(8,128)(2,1)}, u32[]{:S(2)}) %copy-start.1) | copy-done | bytes 1441816
  13.6 3.2 %update_momentum.1 = (f32[32,88,256]{2,1,0:T(8,128)}, bf16[32,88,256]{2,1,0:T(8,128)(2,1)S(1)}, s32[64]{0:T(128)S(1)}) custom-call(s32[32]{0:T(128)S(1)} %copy-done.3, s32[32]{0:T(128)S(1)} %copy-done.4, s32[32]{0:T(128)S(1)} %copy-done.5, bf16[32,88,256]{2,1,0:T(8,128)(2,1)S(1)} %copy-done.1, f32[32,88,256]{2,1,0:T(8,128)S(1)} %copy-done), custom_call_target="tpu_custom_call" | custom-call | flops 2883584 | bytes 8650752 | tf_op jit(solution)/shard_map/update_momentum/pallas_call | solution.py:191
  16.8 0.0 copy-start.2
  16.8 1.1 %copy-done.2 = bf16[32,88,256]{2,1,0:T(8,128)(2,1)} copy-done((bf16[32,88,256]{2,1,0:T(8,128)(2,1)}, bf16[32,88,256]{2,1,0:T(8,128)(2,1)S(1)}, u32[]{:S(2)}) %copy-start.2) | copy-done | bytes 1441816
  17.9 27.5 %all-to-all-done.x_ref = bf16[32,88,256]{2,1,0:T(8,128)(2,1)} async-done(((bf16[32,88,256]{2,1,0:T(8,128)(2,1)}), bf16[32,88,256]{2,1,0:T(8,128)(2,1)}, u32[]{:S(2)}, u32[]{:S(2)}) %all-to-all-start) | async-done | bytes 1441824 | tf_op jit(solution)/shard_map/all_to_all | solution.py:477
  45.4 4.6 %all-to-all-start.1 = ((bf16[32,88,256]{2,1,0:T(8,128)(2,1)}), bf16[32,88,256]{2,1,0:T(8,128)(2,1)S(1)}, u32[]{:S(2)}, u32[]{:S(2)}) async-start(bf16[32,88,256]{2,1,0:T(8,128)(2,1)} %copy-done.2), calls=%async_computation.1 | async-start | bytes 2883584 | tf_op jit(solution)/shard_map/all_to_all | solution.py:477
  49.9 10.5 %orthogonalize.2 = (bf16[2,704,1024]{2,1,0:T(8,128)(2,1)}, bf16[4,88,256]{2,1,0:T(8,128)(2,1)S(1)}, bf16[4,88,256]{2,1,0:T(8,128)(2,1)S(1)}, bf16[4,88,256]{2,1,0:T(8,128)(2,1)S(1)}, bf16[4,88,256]{2,1,0:T(8,128)(2,1)S(1)}) custom-call(s32[32]{0:T(128)S(1)} %copy-done.4, bf16[32,88,256]{2,1,0:T(8,128)(2,1)} %all-to-all-done.x_ref), custom_call_target="tpu_custom_call" | custom-call | flops 6643777536 | bytes 4718592 | tf_op jit(solution)/shard_map/orthogonalize/pallas_call | solution.py:364
  60.5 0.3 collective-permute-start
  60.8 1.7 %collective-permute-start.1 = (bf16[4,88,256]{2,1,0:T(8,128)(2,1)S(1)}, bf16[4,88,256]{2,1,0:T(8,128)(2,1)S(1)}, u32[]{:S(2)}, u32[]{:S(2)}) collective-permute-start(bf16[4,88,256]{2,1,0:T(8,128)(2,1)S(1)} %get-tuple-element.39), channel_id=1, source_target_pairs={{0,8},{1,9},{2,10},{3,11},{4,12},{5,13},{6,14},{7,15},{8,0},{9,1},... | collective-permute-start | bytes 540680 | tf_op jit(solution)/shard_map/ppermute | solution.py:483
  62.5 0.0 collective-permute-start.2
  62.5 0.0 collective-permute-done.refs_1_
  62.5 7.8 %collective-permute-done.1.refs_2_ = bf16[4,88,256]{2,1,0:T(8,128)(2,1)S(1)} collective-permute-done((bf16[4,88,256]{2,1,0:T(8,128)(2,1)S(1)}, bf16[4,88,256]{2,1,0:T(8,128)(2,1)S(1)}, u32[]{:S(2)}, u32[]{:S(2)}) %collective-permute-start.1) | collective-permute-done | bytes 180256 | tf_op jit(solution)/shard_map/ppermute | solution.py:483
  70.3 5.0 %collective-permute-done.2.refs_3_ = bf16[4,88,256]{2,1,0:T(8,128)(2,1)S(1)} collective-permute-done((bf16[4,88,256]{2,1,0:T(8,128)(2,1)S(1)}, bf16[4,88,256]{2,1,0:T(8,128)(2,1)S(1)}, u32[]{:S(2)}, u32[]{:S(2)}) %collective-permute-start.2) | collective-permute-done | bytes 180256 | tf_op jit(solution)/shard_map/ppermute | solution.py:483
  75.3 0.8 restage.1
  76.1 2.6 %collective-permute-start.3 = (bf16[4,88,256]{2,1,0:T(8,128)(2,1)}, bf16[4,88,256]{2,1,0:T(8,128)(2,1)S(1)}, u32[]{:S(2)}, u32[]{:S(2)}) collective-permute-start(bf16[4,88,256]{2,1,0:T(8,128)(2,1)} %get-tuple-element.42), channel_id=1, source_target_pairs={{0,1},{1,0},{2,3},{3,2},{4,5},{5,4},{6,7},{7,6},{8,9},{9,8},{10,11... | collective-permute-start | bytes 540680 | tf_op jit(solution)/shard_map/ppermute | solution.py:483
  78.7 1.5 %collective-permute-start.4 = (bf16[4,88,256]{2,1,0:T(8,128)(2,1)}, bf16[4,88,256]{2,1,0:T(8,128)(2,1)S(1)}, u32[]{:S(2)}, u32[]{:S(2)}) collective-permute-start(bf16[4,88,256]{2,1,0:T(8,128)(2,1)} %get-tuple-element.43), channel_id=1, source_target_pairs={{0,16},{1,17},{2,18},{3,19},{4,20},{5,21},{6,22},{7,23},{8,24},{9,... | collective-permute-start | bytes 540680 | tf_op jit(solution)/shard_map/ppermute | solution.py:483
  80.1 0.0 collective-permute-start.5
  80.2 3.0 %all-to-all-done.1.x_ref = bf16[32,88,256]{2,1,0:T(8,128)(2,1)S(1)} async-done(((bf16[32,88,256]{2,1,0:T(8,128)(2,1)}), bf16[32,88,256]{2,1,0:T(8,128)(2,1)S(1)}, u32[]{:S(2)}, u32[]{:S(2)}) %all-to-all-start.1) | async-done | bytes 1441824 | tf_op jit(solution)/shard_map/all_to_all | solution.py:477
  83.2 9.1 %orthogonalize.3 = (bf16[704,1024]{1,0:T(8,128)(2,1)S(1)}, bf16[16,88,256]{2,1,0:T(8,128)(2,1)}) custom-call(s32[32]{0:T(128)S(1)} %copy-done.4, bf16[32,88,256]{2,1,0:T(8,128)(2,1)S(1)} %all-to-all-done.1.x_ref), custom_call_target="tpu_custom_call" | custom-call | flops 6643777536 | bytes 4718592 | tf_op jit(solution)/shard_map/orthogonalize/pallas_call | solution.py:364
  92.3 0.0 collective-permute-done.3.refs_1_
  92.3 0.0 collective-permute-done.4.refs_2_
  92.3 0.0 collective-permute-done.5.refs_3_
  92.3 4.9 %all-to-all-start.2 = ((bf16[16,88,256]{2,1,0:T(8,128)(2,1)}), bf16[16,88,256]{2,1,0:T(8,128)(2,1)S(1)}, u32[]{:S(2)}, u32[]{:S(2)}) async-start(bf16[16,88,256]{2,1,0:T(8,128)(2,1)} %get-tuple-element.48), calls=%async_computation.2 | async-start | bytes 1441792 | tf_op jit(solution)/shard_map/all_to_all | solution.py:477
  97.3 2.3 %store_early.1 = (bf16[2,704,1024]{2,1,0:T(8,128)(2,1)}, bf16[32,88,256]{2,1,0:T(8,128)(2,1)}) custom-call(s32[64]{0:T(128)S(1)} %get-tuple-element.33.list_ref, bf16[704,1024]{1,0:T(8,128)(2,1)S(1)} %get-tuple-element.49.whole_ref, bf16[2,704,1024]{2,1,0:T(8,128)(2,1)} %get-tuple-element.50.owned_in, ...), custom_call_target="tpu_custom_call", output_to_operand_aliasing={{0}: (2, {})} | custom-call | bytes 5767168 | tf_op jit(solution)/shard_map/store_early/pallas_call | solution.py:435
  99.6 8.5 %all-to-all-done.2.back_ref = bf16[16,88,256]{2,1,0:T(8,128)(2,1)S(1)} async-done(((bf16[16,88,256]{2,1,0:T(8,128)(2,1)}), bf16[16,88,256]{2,1,0:T(8,128)(2,1)S(1)}, u32[]{:S(2)}, u32[]{:S(2)}) %all-to-all-start.2) | async-done | bytes 720928 | tf_op jit(solution)/shard_map/all_to_all | solution.py:477
  108.1 1.4 %store_late.1 = bf16[32,88,256]{2,1,0:T(8,128)(2,1)} custom-call(s32[64]{0:T(128)S(1)} %get-tuple-element.33.list_ref, bf16[16,88,256]{2,1,0:T(8,128)(2,1)S(1)} %all-to-all-done.2.back_ref, bf16[32,88,256]{2,1,0:T(8,128)(2,1)} %get-tuple-element.55.update_in), custom_call_target="tpu_custom_call", output_to_operand_aliasing={{}: (2, {})} | custom-call | bytes 1441792 | tf_op jit(solution)/shard_map/store_late/pallas_call | solution.py:463
Async XLA Ops:
  4.7 7.5 %copy-start = (f32[32,88,256]{2,1,0:T(8,128)S(1)}, f32[32,88,256]{2,1,0:T(8,128)}, u32[]{:S(2)}) copy-start(f32[32,88,256]{2,1,0:T(8,128)} %m_ref.3) | copy-start | bytes 8650756
  4.7 7.5 %copy-start.3 = (s32[32]{0:T(128)S(1)}, s32[32]{0:T(128)}, u32[]{:S(2)}) copy-start(s32[32]{0:T(128)} %owner_ref.3) | copy-start | bytes 388
  4.7 7.5 %copy-start.4 = (s32[32]{0:T(128)S(1)}, s32[32]{0:T(128)}, u32[]{:S(2)}) copy-start(s32[32]{0:T(128)} %get-tuple-element.30.other_ref) | copy-start | bytes 388
  4.7 7.5 %copy-start.5 = (s32[32]{0:T(128)S(1)}, s32[32]{0:T(128)}, u32[]{:S(2)}) copy-start(s32[32]{0:T(128)} %get-tuple-element.31.rank_ref) | copy-start | bytes 388
  4.7 40.6 %all-to-all-start = ((bf16[32,88,256]{2,1,0:T(8,128)(2,1)}), bf16[32,88,256]{2,1,0:T(8,128)(2,1)}, u32[]{:S(2)}, u32[]{:S(2)}) async-start(bf16[32,88,256]{2,1,0:T(8,128)(2,1)} %get-tuple-element.34), calls=%async_computation | async-start | bytes 2883584 | tf_op jit(solution)/shard_map/all_to_all | solution.py:477
  12.2 1.4 %copy-start.1 = (bf16[32,88,256]{2,1,0:T(8,128)(2,1)S(1)}, bf16[32,88,256]{2,1,0:T(8,128)(2,1)}, u32[]{:S(2)}) copy-start(bf16[32,88,256]{2,1,0:T(8,128)(2,1)} %g_ref.3) | copy-start | bytes 4325380
  16.8 1.1 %copy-start.2 = (bf16[32,88,256]{2,1,0:T(8,128)(2,1)}, bf16[32,88,256]{2,1,0:T(8,128)(2,1)S(1)}, u32[]{:S(2)}) copy-start(bf16[32,88,256]{2,1,0:T(8,128)(2,1)S(1)} %get-tuple-element.45) | copy-start | bytes 4325380
  45.4 37.8 %all-to-all-start.1 = ((bf16[32,88,256]{2,1,0:T(8,128)(2,1)}), bf16[32,88,256]{2,1,0:T(8,128)(2,1)S(1)}, u32[]{:S(2)}, u32[]{:S(2)}) async-start(bf16[32,88,256]{2,1,0:T(8,128)(2,1)} %copy-done.2), calls=%async_computation.1 | async-start | bytes 2883584 | tf_op jit(solution)/shard_map/all_to_all | solution.py:477
  60.5 2.0 %collective-permute-start = (bf16[4,88,256]{2,1,0:T(8,128)(2,1)S(1)}, bf16[4,88,256]{2,1,0:T(8,128)(2,1)S(1)}, u32[]{:S(2)}, u32[]{:S(2)}) collective-permute-start(bf16[4,88,256]{2,1,0:T(8,128)(2,1)S(1)} %get-tuple-element.38), channel_id=1, source_target_pairs={{0,4},{1,5},{2,6},{3,7},{4,0},{5,1},{6,2},{7,3},{8,12},{9,13},{10,... | collective-permute-start | bytes 540680 | tf_op jit(solution)/shard_map/ppermute | solution.py:483
  60.8 9.5 %collective-permute-start.1 = (bf16[4,88,256]{2,1,0:T(8,128)(2,1)S(1)}, bf16[4,88,256]{2,1,0:T(8,128)(2,1)S(1)}, u32[]{:S(2)}, u32[]{:S(2)}) collective-permute-start(bf16[4,88,256]{2,1,0:T(8,128)(2,1)S(1)} %get-tuple-element.39), channel_id=1, source_target_pairs={{0,8},{1,9},{2,10},{3,11},{4,12},{5,13},{6,14},{7,15},{8,0},{9,1},... | collective-permute-start | bytes 540680 | tf_op jit(solution)/shard_map/ppermute | solution.py:483
  62.5 12.8 %collective-permute-start.2 = (bf16[4,88,256]{2,1,0:T(8,128)(2,1)S(1)}, bf16[4,88,256]{2,1,0:T(8,128)(2,1)S(1)}, u32[]{:S(2)}, u32[]{:S(2)}) collective-permute-start(bf16[4,88,256]{2,1,0:T(8,128)(2,1)S(1)} %get-tuple-element.40), channel_id=1, source_target_pairs={{0,12},{1,13},{2,14},{3,15},{4,8},{5,9},{6,10},{7,11},{8,4},{9,5},... | collective-permute-start | bytes 540680 | tf_op jit(solution)/shard_map/ppermute | solution.py:483
  76.1 16.2 %collective-permute-start.3 = (bf16[4,88,256]{2,1,0:T(8,128)(2,1)}, bf16[4,88,256]{2,1,0:T(8,128)(2,1)S(1)}, u32[]{:S(2)}, u32[]{:S(2)}) collective-permute-start(bf16[4,88,256]{2,1,0:T(8,128)(2,1)} %get-tuple-element.42), channel_id=1, source_target_pairs={{0,1},{1,0},{2,3},{3,2},{4,5},{5,4},{6,7},{7,6},{8,9},{9,8},{10,11... | collective-permute-start | bytes 540680 | tf_op jit(solution)/shard_map/ppermute | solution.py:483
  78.7 13.6 %collective-permute-start.4 = (bf16[4,88,256]{2,1,0:T(8,128)(2,1)}, bf16[4,88,256]{2,1,0:T(8,128)(2,1)S(1)}, u32[]{:S(2)}, u32[]{:S(2)}) collective-permute-start(bf16[4,88,256]{2,1,0:T(8,128)(2,1)} %get-tuple-element.43), channel_id=1, source_target_pairs={{0,16},{1,17},{2,18},{3,19},{4,20},{5,21},{6,22},{7,23},{8,24},{9,... | collective-permute-start | bytes 540680 | tf_op jit(solution)/shard_map/ppermute | solution.py:483
  80.1 12.2 %collective-permute-start.5 = (bf16[4,88,256]{2,1,0:T(8,128)(2,1)}, bf16[4,88,256]{2,1,0:T(8,128)(2,1)}, u32[]{:S(2)}, u32[]{:S(2)}) collective-permute-start(bf16[4,88,256]{2,1,0:T(8,128)(2,1)} %get-tuple-element.44), channel_id=1, source_target_pairs={{0,17},{1,16},{2,19},{3,18},{4,21},{5,20},{6,23},{7,22},{8,25},{9,... | collective-permute-start | bytes 540680 | tf_op jit(solution)/shard_map/ppermute | solution.py:483
  92.3 15.8 %all-to-all-start.2 = ((bf16[16,88,256]{2,1,0:T(8,128)(2,1)}), bf16[16,88,256]{2,1,0:T(8,128)(2,1)S(1)}, u32[]{:S(2)}, u32[]{:S(2)}) async-start(bf16[16,88,256]{2,1,0:T(8,128)(2,1)} %get-tuple-element.48), calls=%async_computation.2 | async-start | bytes 1441792 | tf_op jit(solution)/shard_map/all_to_all | solution.py:477

commit v23 on v20

--- a/solution.py
+++ b/solution.py
@@ -248,12 +248,10 @@
         ref[height:, :] = jnp.zeros((padded - height, ref.shape[1]), ref.dtype)
     for iteration in range(ITERS):
         src = x_s if iteration == 0 else y_s
-        for t in range(TILES):
-            span = slice(t * tile, (t + 1) * tile)
-            gram = matmul(src[span, :], src[...], 1)
-            if iteration == 0:
-                gram = gram * (inverse * inverse)
-            gram_s[span, :] = gram.astype(jnp.bfloat16)
+        gram = matmul(src[:height, :], src[...], 1)
+        if iteration == 0:
+            gram = gram * (inverse * inverse)
+        gram_s[:height, :] = gram.astype(jnp.bfloat16)
         for t in range(TILES):
             span = slice(t * tile, (t + 1) * tile)
             square = matmul(gram_s[span, :], gram_s[...], 0)

time: 108 us -> 109 us (level)
  Pallas kernels: 27.9 us -> 29.4 us
    pallas_call x2, Pallas kernels: 16.1 us -> 17.7 us  [orthogonalize(): pl.pallas_call(functools.partial(ortho_kernel, row_size, col_size, slot),...]
    all_to_all x3, waiting for transfers between devices: 39.8 us -> 38.7 us  [exchange(): lax.all_to_all(blocks, axes, split_axis=0, concat_axis=0, tiled=True, axi...]
  transfers between devices with their start and end apart: 9 -> 9, of which waited for: 6 -> 5; matrix products, arithmetic and copies ran while one was open for 0% -> 0% of each run, Pallas kernels for 21% -> 22%
where the time goes in v23:
time: 109 us; the launch traced here: 108 us
  waiting for transfers between devices  52.1 us (48%)
  Pallas kernels  29.4 us (27%)
  starting transfers between devices  23.7 us (22%)
  local copies, waits for them, and re-layouts  2.51 us (2%)
    all_to_all x3, waiting for transfers between devices, exchange(): lax.all_to_all(blocks, axes, split_axis=0, concat_axis=0, tiled=True, axi...  38.7 us
    pallas_call x2, Pallas kernels, orthogonalize(): pl.pallas_call(functools.partial(ortho_kernel, row_size, col_size, slot),...  17.7 us
    all_to_all x3, starting transfers between devices, exchange(): lax.all_to_all(blocks, axes, split_axis=0, concat_axis=0, tiled=True, axi...  16.9 us
    ppermute x6, waiting for transfers between devices, swap(): return lax.ppermute(block, AXES, [(d, d ^ offset) for d in range(devices)])  13.3 us
    ppermute x6, starting transfers between devices, swap(): return lax.ppermute(block, AXES, [(d, d ^ offset) for d in range(devices)])  6.77 us
    pallas_call x1, Pallas kernels, pack(): pl.pallas_call(functools.partial(pack_kernel, chunk, col_size), grid_spec...  4.04 us
    pallas_call x1, Pallas kernels, update_momentum(): pl.pallas_call(functools.partial(momentum_kernel, chunk, col_size), grid_...  3.21 us
    unnamed x12, local copies, waits for them, and re-layouts  2.51 us
  transfers between devices with their start and end apart: 9, of which 5 were waited for; matrix products, arithmetic and copies ran while one was open for 0% of the time, Pallas kernels for 22%

profile of v23, /device:TPU:0, one launch (start us, length us, event | category | flops | bytes accessed | tf_op | source)
XLA Modules:
  0.0 108.5 jit_solution(17318578986346002148)
XLA Ops:
  0.6 4.0 %pack.1 = (bf16[32,88,256]{2,1,0:T(8,128)(2,1)}, s32[32]{0:T(128)}, s32[32]{0:T(128)}) custom-call(s32[32]{0:T(128)} %owner_ref.3, bf16[32,88,256]{2,1,0:T(8,128)(2,1)} %g_ref.3, f32[32,88,256]{2,1,0:T(8,128)} %m_ref.3), custom_call_target="tpu_custom_call" | custom-call | flops 2883584 | bytes 5767168 | tf_op jit(solution)/shard_map/pack/pallas_call | solution.py:118
  4.7 0.0 copy-start
  4.7 0.0 copy-start.3
  4.7 0.0 copy-start.4
  4.7 0.0 copy-start.5
  4.7 7.4 %all-to-all-start = ((bf16[32,88,256]{2,1,0:T(8,128)(2,1)}), bf16[32,88,256]{2,1,0:T(8,128)(2,1)}, u32[]{:S(2)}, u32[]{:S(2)}) async-start(bf16[32,88,256]{2,1,0:T(8,128)(2,1)} %get-tuple-element.34), calls=%async_computation | async-start | bytes 2883584 | tf_op jit(solution)/shard_map/all_to_all | solution.py:475
  12.2 0.0 copy-done
  12.2 0.0 copy-done.3
  12.2 0.0 copy-done.4
  12.2 0.0 copy-done.5
  12.2 0.0 copy-start.1
  12.2 1.4 %copy-done.1 = bf16[32,88,256]{2,1,0:T(8,128)(2,1)S(1)} copy-done((bf16[32,88,256]{2,1,0:T(8,128)(2,1)S(1)}, bf16[32,88,256]{2,1,0:T(8,128)(2,1)}, u32[]{:S(2)}) %copy-start.1) | copy-done | bytes 1441816
  13.6 3.2 %update_momentum.1 = (f32[32,88,256]{2,1,0:T(8,128)}, bf16[32,88,256]{2,1,0:T(8,128)(2,1)S(1)}, s32[64]{0:T(128)S(1)}) custom-call(s32[32]{0:T(128)S(1)} %copy-done.3, s32[32]{0:T(128)S(1)} %copy-done.4, s32[32]{0:T(128)S(1)} %copy-done.5, bf16[32,88,256]{2,1,0:T(8,128)(2,1)S(1)} %copy-done.1, f32[32,88,256]{2,1,0:T(8,128)S(1)} %copy-done), custom_call_target="tpu_custom_call" | custom-call | flops 2883584 | bytes 8650752 | tf_op jit(solution)/shard_map/update_momentum/pallas_call | solution.py:191
  16.8 0.0 copy-start.2
  16.8 1.1 %copy-done.2 = bf16[32,88,256]{2,1,0:T(8,128)(2,1)} copy-done((bf16[32,88,256]{2,1,0:T(8,128)(2,1)}, bf16[32,88,256]{2,1,0:T(8,128)(2,1)S(1)}, u32[]{:S(2)}) %copy-start.2) | copy-done | bytes 1441816
  17.9 27.5 %all-to-all-done.x_ref = bf16[32,88,256]{2,1,0:T(8,128)(2,1)} async-done(((bf16[32,88,256]{2,1,0:T(8,128)(2,1)}), bf16[32,88,256]{2,1,0:T(8,128)(2,1)}, u32[]{:S(2)}, u32[]{:S(2)}) %all-to-all-start) | async-done | bytes 1441824 | tf_op jit(solution)/shard_map/all_to_all | solution.py:475
  45.4 4.6 %all-to-all-start.1 = ((bf16[32,88,256]{2,1,0:T(8,128)(2,1)}), bf16[32,88,256]{2,1,0:T(8,128)(2,1)S(1)}, u32[]{:S(2)}, u32[]{:S(2)}) async-start(bf16[32,88,256]{2,1,0:T(8,128)(2,1)} %copy-done.2), calls=%async_computation.1 | async-start | bytes 2883584 | tf_op jit(solution)/shard_map/all_to_all | solution.py:475
  49.9 9.6 %orthogonalize.2 = (bf16[2,704,1024]{2,1,0:T(8,128)(2,1)}, bf16[4,88,256]{2,1,0:T(8,128)(2,1)S(1)}, bf16[4,88,256]{2,1,0:T(8,128)(2,1)S(1)}, bf16[4,88,256]{2,1,0:T(8,128)(2,1)S(1)}, bf16[4,88,256]{2,1,0:T(8,128)(2,1)S(1)}) custom-call(s32[32]{0:T(128)S(1)} %copy-done.4, bf16[32,88,256]{2,1,0:T(8,128)(2,1)} %all-to-all-done.x_ref), custom_call_target="tpu_custom_call" | custom-call | flops 6643777536 | bytes 4718592 | tf_op jit(solution)/shard_map/orthogonalize/pallas_call | solution.py:362
  59.5 0.3 collective-permute-start
  59.8 1.7 %collective-permute-start.1 = (bf16[4,88,256]{2,1,0:T(8,128)(2,1)S(1)}, bf16[4,88,256]{2,1,0:T(8,128)(2,1)S(1)}, u32[]{:S(2)}, u32[]{:S(2)}) collective-permute-start(bf16[4,88,256]{2,1,0:T(8,128)(2,1)S(1)} %get-tuple-element.39), channel_id=1, source_target_pairs={{0,8},{1,9},{2,10},{3,11},{4,12},{5,13},{6,14},{7,15},{8,0},{9,1},... | collective-permute-start | bytes 540680 | tf_op jit(solution)/shard_map/ppermute | solution.py:481
  61.5 0.0 collective-permute-start.2
  61.5 0.0 collective-permute-done.refs_1_
  61.5 8.5 %collective-permute-done.1.refs_2_ = bf16[4,88,256]{2,1,0:T(8,128)(2,1)S(1)} collective-permute-done((bf16[4,88,256]{2,1,0:T(8,128)(2,1)S(1)}, bf16[4,88,256]{2,1,0:T(8,128)(2,1)S(1)}, u32[]{:S(2)}, u32[]{:S(2)}) %collective-permute-start.1) | collective-permute-done | bytes 180256 | tf_op jit(solution)/shard_map/ppermute | solution.py:481
  70.0 4.8 %collective-permute-done.2.refs_3_ = bf16[4,88,256]{2,1,0:T(8,128)(2,1)S(1)} collective-permute-done((bf16[4,88,256]{2,1,0:T(8,128)(2,1)S(1)}, bf16[4,88,256]{2,1,0:T(8,128)(2,1)S(1)}, u32[]{:S(2)}, u32[]{:S(2)}) %collective-permute-start.2) | collective-permute-done | bytes 180256 | tf_op jit(solution)/shard_map/ppermute | solution.py:481
  74.9 0.8 restage.1
  75.7 3.3 %collective-permute-start.3 = (bf16[4,88,256]{2,1,0:T(8,128)(2,1)}, bf16[4,88,256]{2,1,0:T(8,128)(2,1)S(1)}, u32[]{:S(2)}, u32[]{:S(2)}) collective-permute-start(bf16[4,88,256]{2,1,0:T(8,128)(2,1)} %get-tuple-element.42), channel_id=1, source_target_pairs={{0,1},{1,0},{2,3},{3,2},{4,5},{5,4},{6,7},{7,6},{8,9},{9,8},{10,11... | collective-permute-start | bytes 540680 | tf_op jit(solution)/shard_map/ppermute | solution.py:481
  79.0 1.5 %collective-permute-start.4 = (bf16[4,88,256]{2,1,0:T(8,128)(2,1)}, bf16[4,88,256]{2,1,0:T(8,128)(2,1)S(1)}, u32[]{:S(2)}, u32[]{:S(2)}) collective-permute-start(bf16[4,88,256]{2,1,0:T(8,128)(2,1)} %get-tuple-element.43), channel_id=1, source_target_pairs={{0,16},{1,17},{2,18},{3,19},{4,20},{5,21},{6,22},{7,23},{8,24},{9,... | collective-permute-start | bytes 540680 | tf_op jit(solution)/shard_map/ppermute | solution.py:481
  80.4 0.0 collective-permute-start.5
  80.4 2.7 %all-to-all-done.1.x_ref = bf16[32,88,256]{2,1,0:T(8,128)(2,1)S(1)} async-done(((bf16[32,88,256]{2,1,0:T(8,128)(2,1)}), bf16[32,88,256]{2,1,0:T(8,128)(2,1)S(1)}, u32[]{:S(2)}, u32[]{:S(2)}) %all-to-all-start.1) | async-done | bytes 1441824 | tf_op jit(solution)/shard_map/all_to_all | solution.py:475
  83.2 8.1 %orthogonalize.3 = (bf16[704,1024]{1,0:T(8,128)(2,1)S(1)}, bf16[16,88,256]{2,1,0:T(8,128)(2,1)}) custom-call(s32[32]{0:T(128)S(1)} %copy-done.4, bf16[32,88,256]{2,1,0:T(8,128)(2,1)S(1)} %all-to-all-done.1.x_ref), custom_call_target="tpu_custom_call" | custom-call | flops 6643777536 | bytes 4718592 | tf_op jit(solution)/shard_map/orthogonalize/pallas_call | solution.py:362
  91.2 0.0 collective-permute-done.3.refs_1_
  91.3 0.0 collective-permute-done.4.refs_2_
  91.3 0.0 collective-permute-done.5.refs_3_
  91.3 4.9 %all-to-all-start.2 = ((bf16[16,88,256]{2,1,0:T(8,128)(2,1)}), bf16[16,88,256]{2,1,0:T(8,128)(2,1)S(1)}, u32[]{:S(2)}, u32[]{:S(2)}) async-start(bf16[16,88,256]{2,1,0:T(8,128)(2,1)} %get-tuple-element.48), calls=%async_computation.2 | async-start | bytes 1441792 | tf_op jit(solution)/shard_map/all_to_all | solution.py:475
  96.2 2.3 %store_early.1 = (bf16[2,704,1024]{2,1,0:T(8,128)(2,1)}, bf16[32,88,256]{2,1,0:T(8,128)(2,1)}) custom-call(s32[64]{0:T(128)S(1)} %get-tuple-element.33.list_ref, bf16[704,1024]{1,0:T(8,128)(2,1)S(1)} %get-tuple-element.49.whole_ref, bf16[2,704,1024]{2,1,0:T(8,128)(2,1)} %get-tuple-element.50.owned_in, ...), custom_call_target="tpu_custom_call", output_to_operand_aliasing={{0}: (2, {})} | custom-call | bytes 5767168 | tf_op jit(solution)/shard_map/store_early/pallas_call | solution.py:433
  98.6 8.5 %all-to-all-done.2.back_ref = bf16[16,88,256]{2,1,0:T(8,128)(2,1)S(1)} async-done(((bf16[16,88,256]{2,1,0:T(8,128)(2,1)}), bf16[16,88,256]{2,1,0:T(8,128)(2,1)S(1)}, u32[]{:S(2)}, u32[]{:S(2)}) %all-to-all-start.2) | async-done | bytes 720928 | tf_op jit(solution)/shard_map/all_to_all | solution.py:475
  107.1 1.4 %store_late.1 = bf16[32,88,256]{2,1,0:T(8,128)(2,1)} custom-call(s32[64]{0:T(128)S(1)} %get-tuple-element.33.list_ref, bf16[16,88,256]{2,1,0:T(8,128)(2,1)S(1)} %all-to-all-done.2.back_ref, bf16[32,88,256]{2,1,0:T(8,128)(2,1)} %get-tuple-element.55.update_in), custom_call_target="tpu_custom_call", output_to_operand_aliasing={{}: (2, {})} | custom-call | bytes 1441792 | tf_op jit(solution)/shard_map/store_late/pallas_call | solution.py:461
Async XLA Ops:
  4.7 7.5 %copy-start = (f32[32,88,256]{2,1,0:T(8,128)S(1)}, f32[32,88,256]{2,1,0:T(8,128)}, u32[]{:S(2)}) copy-start(f32[32,88,256]{2,1,0:T(8,128)} %m_ref.3) | copy-start | bytes 8650756
  4.7 7.5 %copy-start.3 = (s32[32]{0:T(128)S(1)}, s32[32]{0:T(128)}, u32[]{:S(2)}) copy-start(s32[32]{0:T(128)} %owner_ref.3) | copy-start | bytes 388
  4.7 7.5 %copy-start.4 = (s32[32]{0:T(128)S(1)}, s32[32]{0:T(128)}, u32[]{:S(2)}) copy-start(s32[32]{0:T(128)} %get-tuple-element.30.other_ref) | copy-start | bytes 388
  4.7 7.5 %copy-start.5 = (s32[32]{0:T(128)S(1)}, s32[32]{0:T(128)}, u32[]{:S(2)}) copy-start(s32[32]{0:T(128)} %get-tuple-element.31.rank_ref) | copy-start | bytes 388
  4.7 40.6 %all-to-all-start = ((bf16[32,88,256]{2,1,0:T(8,128)(2,1)}), bf16[32,88,256]{2,1,0:T(8,128)(2,1)}, u32[]{:S(2)}, u32[]{:S(2)}) async-start(bf16[32,88,256]{2,1,0:T(8,128)(2,1)} %get-tuple-element.34), calls=%async_computation | async-start | bytes 2883584 | tf_op jit(solution)/shard_map/all_to_all | solution.py:475
  12.2 1.4 %copy-start.1 = (bf16[32,88,256]{2,1,0:T(8,128)(2,1)S(1)}, bf16[32,88,256]{2,1,0:T(8,128)(2,1)}, u32[]{:S(2)}) copy-start(bf16[32,88,256]{2,1,0:T(8,128)(2,1)} %g_ref.3) | copy-start | bytes 4325380
  16.8 1.1 %copy-start.2 = (bf16[32,88,256]{2,1,0:T(8,128)(2,1)}, bf16[32,88,256]{2,1,0:T(8,128)(2,1)S(1)}, u32[]{:S(2)}) copy-start(bf16[32,88,256]{2,1,0:T(8,128)(2,1)S(1)} %get-tuple-element.45) | copy-start | bytes 4325380
  45.4 37.8 %all-to-all-start.1 = ((bf16[32,88,256]{2,1,0:T(8,128)(2,1)}), bf16[32,88,256]{2,1,0:T(8,128)(2,1)S(1)}, u32[]{:S(2)}, u32[]{:S(2)}) async-start(bf16[32,88,256]{2,1,0:T(8,128)(2,1)} %copy-done.2), calls=%async_computation.1 | async-start | bytes 2883584 | tf_op jit(solution)/shard_map/all_to_all | solution.py:475
  59.5 2.0 %collective-permute-start = (bf16[4,88,256]{2,1,0:T(8,128)(2,1)S(1)}, bf16[4,88,256]{2,1,0:T(8,128)(2,1)S(1)}, u32[]{:S(2)}, u32[]{:S(2)}) collective-permute-start(bf16[4,88,256]{2,1,0:T(8,128)(2,1)S(1)} %get-tuple-element.38), channel_id=1, source_target_pairs={{0,4},{1,5},{2,6},{3,7},{4,0},{5,1},{6,2},{7,3},{8,12},{9,13},{10,... | collective-permute-start | bytes 540680 | tf_op jit(solution)/shard_map/ppermute | solution.py:481
  59.8 10.2 %collective-permute-start.1 = (bf16[4,88,256]{2,1,0:T(8,128)(2,1)S(1)}, bf16[4,88,256]{2,1,0:T(8,128)(2,1)S(1)}, u32[]{:S(2)}, u32[]{:S(2)}) collective-permute-start(bf16[4,88,256]{2,1,0:T(8,128)(2,1)S(1)} %get-tuple-element.39), channel_id=1, source_target_pairs={{0,8},{1,9},{2,10},{3,11},{4,12},{5,13},{6,14},{7,15},{8,0},{9,1},... | collective-permute-start | bytes 540680 | tf_op jit(solution)/shard_map/ppermute | solution.py:481
  61.5 13.3 %collective-permute-start.2 = (bf16[4,88,256]{2,1,0:T(8,128)(2,1)S(1)}, bf16[4,88,256]{2,1,0:T(8,128)(2,1)S(1)}, u32[]{:S(2)}, u32[]{:S(2)}) collective-permute-start(bf16[4,88,256]{2,1,0:T(8,128)(2,1)S(1)} %get-tuple-element.40), channel_id=1, source_target_pairs={{0,12},{1,13},{2,14},{3,15},{4,8},{5,9},{6,10},{7,11},{8,4},{9,5},... | collective-permute-start | bytes 540680 | tf_op jit(solution)/shard_map/ppermute | solution.py:481
  75.7 15.6 %collective-permute-start.3 = (bf16[4,88,256]{2,1,0:T(8,128)(2,1)}, bf16[4,88,256]{2,1,0:T(8,128)(2,1)S(1)}, u32[]{:S(2)}, u32[]{:S(2)}) collective-permute-start(bf16[4,88,256]{2,1,0:T(8,128)(2,1)} %get-tuple-element.42), channel_id=1, source_target_pairs={{0,1},{1,0},{2,3},{3,2},{4,5},{5,4},{6,7},{7,6},{8,9},{9,8},{10,11... | collective-permute-start | bytes 540680 | tf_op jit(solution)/shard_map/ppermute | solution.py:481
  79.0 12.3 %collective-permute-start.4 = (bf16[4,88,256]{2,1,0:T(8,128)(2,1)}, bf16[4,88,256]{2,1,0:T(8,128)(2,1)S(1)}, u32[]{:S(2)}, u32[]{:S(2)}) collective-permute-start(bf16[4,88,256]{2,1,0:T(8,128)(2,1)} %get-tuple-element.43), channel_id=1, source_target_pairs={{0,16},{1,17},{2,18},{3,19},{4,20},{5,21},{6,22},{7,23},{8,24},{9,... | collective-permute-start | bytes 540680 | tf_op jit(solution)/shard_map/ppermute | solution.py:481
  80.4 10.8 %collective-permute-start.5 = (bf16[4,88,256]{2,1,0:T(8,128)(2,1)}, bf16[4,88,256]{2,1,0:T(8,128)(2,1)}, u32[]{:S(2)}, u32[]{:S(2)}) collective-permute-start(bf16[4,88,256]{2,1,0:T(8,128)(2,1)} %get-tuple-element.44), channel_id=1, source_target_pairs={{0,17},{1,16},{2,19},{3,18},{4,21},{5,20},{6,23},{7,22},{8,25},{9,... | collective-permute-start | bytes 540680 | tf_op jit(solution)/shard_map/ppermute | solution.py:481
  91.3 15.8 %all-to-all-start.2 = ((bf16[16,88,256]{2,1,0:T(8,128)(2,1)}), bf16[16,88,256]{2,1,0:T(8,128)(2,1)S(1)}, u32[]{:S(2)}, u32[]{:S(2)}) async-start(bf16[16,88,256]{2,1,0:T(8,128)(2,1)} %get-tuple-element.48), calls=%async_computation.2 | async-start | bytes 1441792 | tf_op jit(solution)/shard_map/all_to_all | solution.py:475

commit v24 on v23

--- a/solution.py
+++ b/solution.py
@@ -12,6 +12,7 @@
 CAP = 2
 HALVES = 2
 TILES = 2
+COLUMNS = 256
 LOW = 4
 
 coef_a = 3.4445
@@ -241,29 +242,33 @@
     return 0.2 * math.sqrt(max(height, width))
 
 
-def newton_schulz(height, inverse, x_s, y_s, gram_s, finish):
+def newton_schulz(height, inverse, x_s, y_s, gram_s, mix_s, finish):
     padded = x_s.shape[0]
     tile = height // TILES
     for ref in (y_s, gram_s):
         ref[height:, :] = jnp.zeros((padded - height, ref.shape[1]), ref.dtype)
     for iteration in range(ITERS):
         src = x_s if iteration == 0 else y_s
-        gram = matmul(src[:height, :], src[...], 1)
-        if iteration == 0:
-            gram = gram * (inverse * inverse)
-        gram_s[:height, :] = gram.astype(jnp.bfloat16)
+        for c in range(0, padded, COLUMNS):
+            columns = slice(c, c + COLUMNS)
+            gram = matmul(src[:height, :], src[columns, :], 1)
+            if iteration == 0:
+                gram = gram * (inverse * inverse)
+            gram_s[:height, columns] = gram.astype(jnp.bfloat16)
+        for c in range(0, padded, COLUMNS):
+            columns = slice(c, c + COLUMNS)
+            square = matmul(gram_s[:height, :], gram_s[:, columns], 0)
+            mixing = coef_b * gram_s[:height, columns].astype(jnp.float32) + coef_c * square
+            mix_s[:, columns] = mixing.astype(jnp.bfloat16)
         for t in range(TILES):
             span = slice(t * tile, (t + 1) * tile)
-            square = matmul(gram_s[span, :], gram_s[...], 0)
-            mixing = coef_b * gram_s[span, :].astype(jnp.float32) + coef_c * square
-            mixing = mixing.astype(jnp.bfloat16)
             if iteration + 1 < ITERS:
-                combined = combine(src, span, slice(None), mixing)
+                combined = combine(src, span, slice(None), mix_s[span, :])
                 if iteration == 0:
                     combined = combined * inverse
                 y_s[span, :] = combined.astype(jnp.bfloat16)
             else:
-                finish(t, span, mixing)
+                finish(t, span, mix_s[span, :])
 
 
 def combine(src, span, columns, mixing):
@@ -286,7 +291,7 @@
         whole_ref, out_ref, x_s, y_s, gram_s, back_ref, sems, mix_s = refs
     else:
         owned_ref, low_refs = refs[0], refs[1 : 1 + LOW]
-        x_s, y_s, gram_s, back_ref, sems, whole_ref = refs[1 + LOW :]
+        x_s, y_s, gram_s, back_ref, sems, mix_s, whole_ref = refs[1 + LOW :]
     row, col = lax.axis_index("dp"), lax.axis_index("owner")
     me = row * col_size + col
     owns = other_ref[me] != me
@@ -310,7 +315,6 @@
 
     def finish(t, span, mixing):
         if slot:
-            mix_s[span, :] = mixing
             result = product(span, columns_of(col // width), mixing)
         else:
             result = product(span, slice(None), mixing)
@@ -327,7 +331,7 @@
                 ]
         copy_out(t).start()
 
-    newton_schulz(height, inverse, x_s, y_s, gram_s, finish)
+    newton_schulz(height, inverse, x_s, y_s, gram_s, mix_s, finish)
     if slot:
         for t in range(TILES):
             span = slice(t * tile, (t + 1) * tile)
@@ -350,9 +354,9 @@
         pltpu.VMEM((padded, padded), jnp.bfloat16),
         pltpu.VMEM((places, rows, cols), jnp.bfloat16),
         pltpu.SemaphoreType.DMA((TILES,)),
+        pltpu.VMEM((height, padded), jnp.bfloat16),
     ]
     if slot:
-        scratch_shapes.append(pltpu.VMEM((height, padded), jnp.bfloat16))
         out_specs = [VMEM, ANYWHERE]
         out = [(height, width), (places, rows, cols)]
     else:

time: 109 us -> 108 us (level)
  transfers between devices with their start and end apart: 9 -> 9, of which waited for: 5 -> 5; matrix products, arithmetic and copies ran while one was open for 0% -> 0% of each run, Pallas kernels for 22% -> 21%
where the time goes in v24:
time: 108 us
  waiting for transfers between devices  52.5 us (49%)
  Pallas kernels  28.4 us (26%)
  starting transfers between devices  23.8 us (22%)
  local copies, waits for them, and re-layouts  2.51 us (2%)
    all_to_all x3, waiting for transfers between devices, exchange(): lax.all_to_all(blocks, axes, split_axis=0, concat_axis=0, tiled=True, axi...  39.5 us
    all_to_all x3, starting transfers between devices, exchange(): lax.all_to_all(blocks, axes, split_axis=0, concat_axis=0, tiled=True, axi...  16.9 us
    pallas_call x2, Pallas kernels, orthogonalize(): pl.pallas_call(functools.partial(ortho_kernel, row_size, col_size, slot),...  16.6 us
    ppermute x6, waiting for transfers between devices, swap(): return lax.ppermute(block, AXES, [(d, d ^ offset) for d in range(devices)])  13 us
    ppermute x6, starting transfers between devices, swap(): return lax.ppermute(block, AXES, [(d, d ^ offset) for d in range(devices)])  6.86 us
    pallas_call x1, Pallas kernels, pack(): pl.pallas_call(functools.partial(pack_kernel, chunk, col_size), grid_spec...  4.04 us
    pallas_call x1, Pallas kernels, update_momentum(): pl.pallas_call(functools.partial(momentum_kernel, chunk, col_size), grid_...  3.21 us
    unnamed x12, local copies, waits for them, and re-layouts  2.51 us
  transfers between devices with their start and end apart: 9, of which 5 were waited for; matrix products, arithmetic and copies ran while one was open for 0% of the time, Pallas kernels for 21%

profile of v24, /device:TPU:0, one launch (start us, length us, event | category | flops | bytes accessed | tf_op | source)
XLA Modules:
  0.0 108.0 jit_solution(8325227366833855487)
XLA Ops:
  0.6 4.0 %pack.1 = (bf16[32,88,256]{2,1,0:T(8,128)(2,1)}, s32[32]{0:T(128)}, s32[32]{0:T(128)}) custom-call(s32[32]{0:T(128)} %owner_ref.3, bf16[32,88,256]{2,1,0:T(8,128)(2,1)} %g_ref.3, f32[32,88,256]{2,1,0:T(8,128)} %m_ref.3), custom_call_target="tpu_custom_call" | custom-call | flops 2883584 | bytes 5767168 | tf_op jit(solution)/shard_map/pack/pallas_call | solution.py:119
  4.7 0.0 copy-start
  4.7 0.0 copy-start.3
  4.7 0.0 copy-start.4
  4.7 0.0 copy-start.5
  4.7 7.4 %all-to-all-start = ((bf16[32,88,256]{2,1,0:T(8,128)(2,1)}), bf16[32,88,256]{2,1,0:T(8,128)(2,1)}, u32[]{:S(2)}, u32[]{:S(2)}) async-start(bf16[32,88,256]{2,1,0:T(8,128)(2,1)} %get-tuple-element.34), calls=%async_computation | async-start | bytes 2883584 | tf_op jit(solution)/shard_map/all_to_all | solution.py:479
  12.2 0.0 copy-done
  12.2 0.0 copy-done.3
  12.2 0.0 copy-done.4
  12.2 0.0 copy-done.5
  12.2 0.0 copy-start.1
  12.2 1.4 %copy-done.1 = bf16[32,88,256]{2,1,0:T(8,128)(2,1)S(1)} copy-done((bf16[32,88,256]{2,1,0:T(8,128)(2,1)S(1)}, bf16[32,88,256]{2,1,0:T(8,128)(2,1)}, u32[]{:S(2)}) %copy-start.1) | copy-done | bytes 1441816
  13.6 3.2 %update_momentum.1 = (f32[32,88,256]{2,1,0:T(8,128)}, bf16[32,88,256]{2,1,0:T(8,128)(2,1)S(1)}, s32[64]{0:T(128)S(1)}) custom-call(s32[32]{0:T(128)S(1)} %copy-done.3, s32[32]{0:T(128)S(1)} %copy-done.4, s32[32]{0:T(128)S(1)} %copy-done.5, bf16[32,88,256]{2,1,0:T(8,128)(2,1)S(1)} %copy-done.1, f32[32,88,256]{2,1,0:T(8,128)S(1)} %copy-done), custom_call_target="tpu_custom_call" | custom-call | flops 2883584 | bytes 8650752 | tf_op jit(solution)/shard_map/update_momentum/pallas_call | solution.py:192
  16.8 0.0 copy-start.2
  16.8 1.1 %copy-done.2 = bf16[32,88,256]{2,1,0:T(8,128)(2,1)} copy-done((bf16[32,88,256]{2,1,0:T(8,128)(2,1)}, bf16[32,88,256]{2,1,0:T(8,128)(2,1)S(1)}, u32[]{:S(2)}) %copy-start.2) | copy-done | bytes 1441816
  17.9 27.5 %all-to-all-done.x_ref = bf16[32,88,256]{2,1,0:T(8,128)(2,1)} async-done(((bf16[32,88,256]{2,1,0:T(8,128)(2,1)}), bf16[32,88,256]{2,1,0:T(8,128)(2,1)}, u32[]{:S(2)}, u32[]{:S(2)}) %all-to-all-start) | async-done | bytes 1441824 | tf_op jit(solution)/shard_map/all_to_all | solution.py:479
  45.4 4.6 %all-to-all-start.1 = ((bf16[32,88,256]{2,1,0:T(8,128)(2,1)}), bf16[32,88,256]{2,1,0:T(8,128)(2,1)S(1)}, u32[]{:S(2)}, u32[]{:S(2)}) async-start(bf16[32,88,256]{2,1,0:T(8,128)(2,1)} %copy-done.2), calls=%async_computation.1 | async-start | bytes 2883584 | tf_op jit(solution)/shard_map/all_to_all | solution.py:479
  49.9 9.1 %orthogonalize.2 = (bf16[2,704,1024]{2,1,0:T(8,128)(2,1)}, bf16[4,88,256]{2,1,0:T(8,128)(2,1)S(1)}, bf16[4,88,256]{2,1,0:T(8,128)(2,1)S(1)}, bf16[4,88,256]{2,1,0:T(8,128)(2,1)S(1)}, bf16[4,88,256]{2,1,0:T(8,128)(2,1)S(1)}) custom-call(s32[32]{0:T(128)S(1)} %copy-done.4, bf16[32,88,256]{2,1,0:T(8,128)(2,1)} %all-to-all-done.x_ref), custom_call_target="tpu_custom_call" | custom-call | flops 6643777536 | bytes 4718592 | tf_op jit(solution)/shard_map/orthogonalize/pallas_call | solution.py:366
  59.0 0.3 collective-permute-start
  59.3 1.7 %collective-permute-start.1 = (bf16[4,88,256]{2,1,0:T(8,128)(2,1)S(1)}, bf16[4,88,256]{2,1,0:T(8,128)(2,1)S(1)}, u32[]{:S(2)}, u32[]{:S(2)}) collective-permute-start(bf16[4,88,256]{2,1,0:T(8,128)(2,1)S(1)} %get-tuple-element.39), channel_id=1, source_target_pairs={{0,8},{1,9},{2,10},{3,11},{4,12},{5,13},{6,14},{7,15},{8,0},{9,1},... | collective-permute-start | bytes 540680 | tf_op jit(solution)/shard_map/ppermute | solution.py:485
  61.0 0.0 collective-permute-start.2
  61.0 0.0 collective-permute-done.refs_1_
  61.0 8.8 %collective-permute-done.1.refs_2_ = bf16[4,88,256]{2,1,0:T(8,128)(2,1)S(1)} collective-permute-done((bf16[4,88,256]{2,1,0:T(8,128)(2,1)S(1)}, bf16[4,88,256]{2,1,0:T(8,128)(2,1)S(1)}, u32[]{:S(2)}, u32[]{:S(2)}) %collective-permute-start.1) | collective-permute-done | bytes 180256 | tf_op jit(solution)/shard_map/ppermute | solution.py:485
  69.8 4.2 %collective-permute-done.2.refs_3_ = bf16[4,88,256]{2,1,0:T(8,128)(2,1)S(1)} collective-permute-done((bf16[4,88,256]{2,1,0:T(8,128)(2,1)S(1)}, bf16[4,88,256]{2,1,0:T(8,128)(2,1)S(1)}, u32[]{:S(2)}, u32[]{:S(2)}) %collective-permute-start.2) | collective-permute-done | bytes 180256 | tf_op jit(solution)/shard_map/ppermute | solution.py:485
  74.0 0.8 restage.1
  74.8 3.4 %collective-permute-start.3 = (bf16[4,88,256]{2,1,0:T(8,128)(2,1)}, bf16[4,88,256]{2,1,0:T(8,128)(2,1)S(1)}, u32[]{:S(2)}, u32[]{:S(2)}) collective-permute-start(bf16[4,88,256]{2,1,0:T(8,128)(2,1)} %get-tuple-element.42), channel_id=1, source_target_pairs={{0,1},{1,0},{2,3},{3,2},{4,5},{5,4},{6,7},{7,6},{8,9},{9,8},{10,11... | collective-permute-start | bytes 540680 | tf_op jit(solution)/shard_map/ppermute | solution.py:485
  78.2 1.4 %collective-permute-start.4 = (bf16[4,88,256]{2,1,0:T(8,128)(2,1)}, bf16[4,88,256]{2,1,0:T(8,128)(2,1)S(1)}, u32[]{:S(2)}, u32[]{:S(2)}) collective-permute-start(bf16[4,88,256]{2,1,0:T(8,128)(2,1)} %get-tuple-element.43), channel_id=1, source_target_pairs={{0,16},{1,17},{2,18},{3,19},{4,20},{5,21},{6,22},{7,23},{8,24},{9,... | collective-permute-start | bytes 540680 | tf_op jit(solution)/shard_map/ppermute | solution.py:485
  79.6 0.1 collective-permute-start.5
  79.7 3.5 %all-to-all-done.1.x_ref = bf16[32,88,256]{2,1,0:T(8,128)(2,1)S(1)} async-done(((bf16[32,88,256]{2,1,0:T(8,128)(2,1)}), bf16[32,88,256]{2,1,0:T(8,128)(2,1)S(1)}, u32[]{:S(2)}, u32[]{:S(2)}) %all-to-all-start.1) | async-done | bytes 1441824 | tf_op jit(solution)/shard_map/all_to_all | solution.py:479
  83.2 7.6 %orthogonalize.3 = (bf16[704,1024]{1,0:T(8,128)(2,1)S(1)}, bf16[16,88,256]{2,1,0:T(8,128)(2,1)}) custom-call(s32[32]{0:T(128)S(1)} %copy-done.4, bf16[32,88,256]{2,1,0:T(8,128)(2,1)S(1)} %all-to-all-done.1.x_ref), custom_call_target="tpu_custom_call" | custom-call | flops 6643777536 | bytes 4718592 | tf_op jit(solution)/shard_map/orthogonalize/pallas_call | solution.py:366
  90.8 0.0 collective-permute-done.3.refs_1_
  90.8 0.0 collective-permute-done.4.refs_2_
  90.8 0.0 collective-permute-done.5.refs_3_
  90.8 4.9 %all-to-all-start.2 = ((bf16[16,88,256]{2,1,0:T(8,128)(2,1)}), bf16[16,88,256]{2,1,0:T(8,128)(2,1)S(1)}, u32[]{:S(2)}, u32[]{:S(2)}) async-start(bf16[16,88,256]{2,1,0:T(8,128)(2,1)} %get-tuple-element.48), calls=%async_computation.2 | async-start | bytes 1441792 | tf_op jit(solution)/shard_map/all_to_all | solution.py:479
  95.7 2.3 %store_early.1 = (bf16[2,704,1024]{2,1,0:T(8,128)(2,1)}, bf16[32,88,256]{2,1,0:T(8,128)(2,1)}) custom-call(s32[64]{0:T(128)S(1)} %get-tuple-element.33.list_ref, bf16[704,1024]{1,0:T(8,128)(2,1)S(1)} %get-tuple-element.49.whole_ref, bf16[2,704,1024]{2,1,0:T(8,128)(2,1)} %get-tuple-element.50.owned_in, ...), custom_call_target="tpu_custom_call", output_to_operand_aliasing={{0}: (2, {})} | custom-call | bytes 5767168 | tf_op jit(solution)/shard_map/store_early/pallas_call | solution.py:437
  98.1 8.5 %all-to-all-done.2.back_ref = bf16[16,88,256]{2,1,0:T(8,128)(2,1)S(1)} async-done(((bf16[16,88,256]{2,1,0:T(8,128)(2,1)}), bf16[16,88,256]{2,1,0:T(8,128)(2,1)S(1)}, u32[]{:S(2)}, u32[]{:S(2)}) %all-to-all-start.2) | async-done | bytes 720928 | tf_op jit(solution)/shard_map/all_to_all | solution.py:479
  106.6 1.4 %store_late.1 = bf16[32,88,256]{2,1,0:T(8,128)(2,1)} custom-call(s32[64]{0:T(128)S(1)} %get-tuple-element.33.list_ref, bf16[16,88,256]{2,1,0:T(8,128)(2,1)S(1)} %all-to-all-done.2.back_ref, bf16[32,88,256]{2,1,0:T(8,128)(2,1)} %get-tuple-element.55.update_in), custom_call_target="tpu_custom_call", output_to_operand_aliasing={{}: (2, {})} | custom-call | bytes 1441792 | tf_op jit(solution)/shard_map/store_late/pallas_call | solution.py:465
Async XLA Ops:
  4.7 7.5 %copy-start = (f32[32,88,256]{2,1,0:T(8,128)S(1)}, f32[32,88,256]{2,1,0:T(8,128)}, u32[]{:S(2)}) copy-start(f32[32,88,256]{2,1,0:T(8,128)} %m_ref.3) | copy-start | bytes 8650756
  4.7 7.5 %copy-start.3 = (s32[32]{0:T(128)S(1)}, s32[32]{0:T(128)}, u32[]{:S(2)}) copy-start(s32[32]{0:T(128)} %owner_ref.3) | copy-start | bytes 388
  4.7 7.5 %copy-start.4 = (s32[32]{0:T(128)S(1)}, s32[32]{0:T(128)}, u32[]{:S(2)}) copy-start(s32[32]{0:T(128)} %get-tuple-element.30.other_ref) | copy-start | bytes 388
  4.7 7.5 %copy-start.5 = (s32[32]{0:T(128)S(1)}, s32[32]{0:T(128)}, u32[]{:S(2)}) copy-start(s32[32]{0:T(128)} %get-tuple-element.31.rank_ref) | copy-start | bytes 388
  4.7 40.6 %all-to-all-start = ((bf16[32,88,256]{2,1,0:T(8,128)(2,1)}), bf16[32,88,256]{2,1,0:T(8,128)(2,1)}, u32[]{:S(2)}, u32[]{:S(2)}) async-start(bf16[32,88,256]{2,1,0:T(8,128)(2,1)} %get-tuple-element.34), calls=%async_computation | async-start | bytes 2883584 | tf_op jit(solution)/shard_map/all_to_all | solution.py:479
  12.2 1.4 %copy-start.1 = (bf16[32,88,256]{2,1,0:T(8,128)(2,1)S(1)}, bf16[32,88,256]{2,1,0:T(8,128)(2,1)}, u32[]{:S(2)}) copy-start(bf16[32,88,256]{2,1,0:T(8,128)(2,1)} %g_ref.3) | copy-start | bytes 4325380
  16.8 1.1 %copy-start.2 = (bf16[32,88,256]{2,1,0:T(8,128)(2,1)}, bf16[32,88,256]{2,1,0:T(8,128)(2,1)S(1)}, u32[]{:S(2)}) copy-start(bf16[32,88,256]{2,1,0:T(8,128)(2,1)S(1)} %get-tuple-element.45) | copy-start | bytes 4325380
  45.4 37.8 %all-to-all-start.1 = ((bf16[32,88,256]{2,1,0:T(8,128)(2,1)}), bf16[32,88,256]{2,1,0:T(8,128)(2,1)S(1)}, u32[]{:S(2)}, u32[]{:S(2)}) async-start(bf16[32,88,256]{2,1,0:T(8,128)(2,1)} %copy-done.2), calls=%async_computation.1 | async-start | bytes 2883584 | tf_op jit(solution)/shard_map/all_to_all | solution.py:479
  59.0 2.0 %collective-permute-start = (bf16[4,88,256]{2,1,0:T(8,128)(2,1)S(1)}, bf16[4,88,256]{2,1,0:T(8,128)(2,1)S(1)}, u32[]{:S(2)}, u32[]{:S(2)}) collective-permute-start(bf16[4,88,256]{2,1,0:T(8,128)(2,1)S(1)} %get-tuple-element.38), channel_id=1, source_target_pairs={{0,4},{1,5},{2,6},{3,7},{4,0},{5,1},{6,2},{7,3},{8,12},{9,13},{10,... | collective-permute-start | bytes 540680 | tf_op jit(solution)/shard_map/ppermute | solution.py:485
  59.3 10.5 %collective-permute-start.1 = (bf16[4,88,256]{2,1,0:T(8,128)(2,1)S(1)}, bf16[4,88,256]{2,1,0:T(8,128)(2,1)S(1)}, u32[]{:S(2)}, u32[]{:S(2)}) collective-permute-start(bf16[4,88,256]{2,1,0:T(8,128)(2,1)S(1)} %get-tuple-element.39), channel_id=1, source_target_pairs={{0,8},{1,9},{2,10},{3,11},{4,12},{5,13},{6,14},{7,15},{8,0},{9,1},... | collective-permute-start | bytes 540680 | tf_op jit(solution)/shard_map/ppermute | solution.py:485
  61.0 13.0 %collective-permute-start.2 = (bf16[4,88,256]{2,1,0:T(8,128)(2,1)S(1)}, bf16[4,88,256]{2,1,0:T(8,128)(2,1)S(1)}, u32[]{:S(2)}, u32[]{:S(2)}) collective-permute-start(bf16[4,88,256]{2,1,0:T(8,128)(2,1)S(1)} %get-tuple-element.40), channel_id=1, source_target_pairs={{0,12},{1,13},{2,14},{3,15},{4,8},{5,9},{6,10},{7,11},{8,4},{9,5},... | collective-permute-start | bytes 540680 | tf_op jit(solution)/shard_map/ppermute | solution.py:485
  74.8 15.9 %collective-permute-start.3 = (bf16[4,88,256]{2,1,0:T(8,128)(2,1)}, bf16[4,88,256]{2,1,0:T(8,128)(2,1)S(1)}, u32[]{:S(2)}, u32[]{:S(2)}) collective-permute-start(bf16[4,88,256]{2,1,0:T(8,128)(2,1)} %get-tuple-element.42), channel_id=1, source_target_pairs={{0,1},{1,0},{2,3},{3,2},{4,5},{5,4},{6,7},{7,6},{8,9},{9,8},{10,11... | collective-permute-start | bytes 540680 | tf_op jit(solution)/shard_map/ppermute | solution.py:485
  78.2 12.6 %collective-permute-start.4 = (bf16[4,88,256]{2,1,0:T(8,128)(2,1)}, bf16[4,88,256]{2,1,0:T(8,128)(2,1)S(1)}, u32[]{:S(2)}, u32[]{:S(2)}) collective-permute-start(bf16[4,88,256]{2,1,0:T(8,128)(2,1)} %get-tuple-element.43), channel_id=1, source_target_pairs={{0,16},{1,17},{2,18},{3,19},{4,20},{5,21},{6,22},{7,23},{8,24},{9,... | collective-permute-start | bytes 540680 | tf_op jit(solution)/shard_map/ppermute | solution.py:485
  79.6 11.2 %collective-permute-start.5 = (bf16[4,88,256]{2,1,0:T(8,128)(2,1)}, bf16[4,88,256]{2,1,0:T(8,128)(2,1)}, u32[]{:S(2)}, u32[]{:S(2)}) collective-permute-start(bf16[4,88,256]{2,1,0:T(8,128)(2,1)} %get-tuple-element.44), channel_id=1, source_target_pairs={{0,17},{1,16},{2,19},{3,18},{4,21},{5,20},{6,23},{7,22},{8,25},{9,... | collective-permute-start | bytes 540680 | tf_op jit(solution)/shard_map/ppermute | solution.py:485
  90.8 15.8 %all-to-all-start.2 = ((bf16[16,88,256]{2,1,0:T(8,128)(2,1)}), bf16[16,88,256]{2,1,0:T(8,128)(2,1)S(1)}, u32[]{:S(2)}, u32[]{:S(2)}) async-start(bf16[16,88,256]{2,1,0:T(8,128)(2,1)} %get-tuple-element.48), calls=%async_computation.2 | async-start | bytes 1441792 | tf_op jit(solution)/shard_map/all_to_all | solution.py:479

commit v25 on v20

--- a/solution.py
+++ b/solution.py
@@ -84,8 +84,8 @@
 
 
 def pack_kernel(
-    chunk, col_size, owner_ref, g_ref, m_ref, first_ref, other_ref, rank_ref,
-    count_ref, list_ref, g_s, m_s, sems,
+    chunk, col_size, owner_ref, g_ref, m_ref, out_ref, other_ref, rank_ref,
+    count_ref, list_ref, g_s, m_s, sems, first_ref, out_sems,
 ):
     mats = rank_ref.shape[0]
 
@@ -110,6 +110,19 @@
                 nesterov = nesterov_of(g_s, m_s, i)[1]
                 first_ref[owner_ref[i]] = nesterov
                 first_ref[other_ref[owner_ref[i]]] = nesterov
+
+    stores = []
+    parts = out_sems.shape[0]
+    part = first_ref.shape[0] // parts
+    for k in range(parts):
+        span = pl.ds(k * part, part)
+        stores.append(
+            pltpu.make_async_copy(first_ref.at[span], out_ref.at[span], out_sems.at[k])
+        )
+    for store in stores:
+        store.start()
+    for store in stores:
+        store.wait()
 
 
 def pack(gradients, momentum, owner_table, devices, col_size):
@@ -121,17 +134,19 @@
             num_scalar_prefetch=1,
             grid=(1,),
             in_specs=[ANYWHERE, ANYWHERE],
-            out_specs=[whole((devices, rows, cols)), SMEM, SMEM],
+            out_specs=[ANYWHERE, SMEM, SMEM],
             scratch_shapes=[
                 pltpu.SMEM((devices,), jnp.int32),
                 pltpu.SMEM((2 * HALVES * devices,), jnp.int32),
                 pltpu.VMEM(gradients.shape, gradients.dtype),
                 pltpu.VMEM(momentum.shape, momentum.dtype),
                 pltpu.SemaphoreType.DMA((2, mats // chunk)),
+                pltpu.VMEM((devices, rows, cols), jnp.bfloat16),
+                pltpu.SemaphoreType.DMA((8,)),
             ],
         ),
         out_shape=[
-            jax.ShapeDtypeStruct((devices, rows, cols), jnp.bfloat16),
+            pltpu.HBM((devices, rows, cols), jnp.bfloat16),
             jax.ShapeDtypeStruct((devices,), jnp.int32),
             jax.ShapeDtypeStruct((mats,), jnp.int32),
         ],

time: 108 us -> 109 us (level)
  no operation moved by 1% of the time
where the time goes in v25:
time: 109 us; the launch traced here: 108 us
  waiting for transfers between devices  52.9 us (49%)
  Pallas kernels  28.4 us (26%)
  starting transfers between devices  23.7 us (22%)
  local copies, waits for them, and re-layouts  2.51 us (2%)
    all_to_all x3, waiting for transfers between devices, exchange(): lax.all_to_all(blocks, axes, split_axis=0, concat_axis=0, tiled=True, axi...  39.8 us
    all_to_all x3, starting transfers between devices, exchange(): lax.all_to_all(blocks, axes, split_axis=0, concat_axis=0, tiled=True, axi...  16.8 us
    pallas_call x2, Pallas kernels, orthogonalize(): pl.pallas_call(functools.partial(ortho_kernel, row_size, col_size, slot),...  16.1 us
    ppermute x6, waiting for transfers between devices, swap(): return lax.ppermute(block, AXES, [(d, d ^ offset) for d in range(devices)])  13.1 us
    ppermute x6, starting transfers between devices, swap(): return lax.ppermute(block, AXES, [(d, d ^ offset) for d in range(devices)])  6.83 us
    pallas_call x1, Pallas kernels, pack(): pl.pallas_call(functools.partial(pack_kernel, chunk, col_size), grid_spec...  4.61 us
    pallas_call x1, Pallas kernels, update_momentum(): pl.pallas_call(functools.partial(momentum_kernel, chunk, col_size), grid_...  3.21 us
    unnamed x12, local copies, waits for them, and re-layouts  2.51 us
  transfers between devices with their start and end apart: 9, of which 6 were waited for; matrix products, arithmetic and copies ran while one was open for 0% of the time, Pallas kernels for 21%

profile of v25, /device:TPU:0, one launch (start us, length us, event | category | flops | bytes accessed | tf_op | source)
XLA Modules:
  0.0 108.3 jit_solution(7582988511471232747)
XLA Ops:
  0.6 4.6 %pack.1 = (bf16[32,88,256]{2,1,0:T(8,128)(2,1)}, s32[32]{0:T(128)}, s32[32]{0:T(128)}) custom-call(s32[32]{0:T(128)} %owner_ref.3, bf16[32,88,256]{2,1,0:T(8,128)(2,1)} %g_ref.3, f32[32,88,256]{2,1,0:T(8,128)} %m_ref.3), custom_call_target="tpu_custom_call" | custom-call | flops 2883584 | bytes 5767168 | tf_op jit(solution)/shard_map/pack/pallas_call | solution.py:131
  5.2 0.0 copy-start
  5.3 0.0 copy-start.3
  5.3 0.0 copy-start.4
  5.3 0.0 copy-start.5
  5.3 7.4 %all-to-all-start = ((bf16[32,88,256]{2,1,0:T(8,128)(2,1)}), bf16[32,88,256]{2,1,0:T(8,128)(2,1)}, u32[]{:S(2)}, u32[]{:S(2)}) async-start(bf16[32,88,256]{2,1,0:T(8,128)(2,1)} %get-tuple-element.34), calls=%async_computation | async-start | bytes 2883584 | tf_op jit(solution)/shard_map/all_to_all | solution.py:492
  12.7 0.0 copy-done
  12.7 0.0 copy-done.3
  12.7 0.0 copy-done.4
  12.8 0.0 copy-done.5
  12.8 0.0 copy-start.1
  12.8 1.4 %copy-done.1 = bf16[32,88,256]{2,1,0:T(8,128)(2,1)S(1)} copy-done((bf16[32,88,256]{2,1,0:T(8,128)(2,1)S(1)}, bf16[32,88,256]{2,1,0:T(8,128)(2,1)}, u32[]{:S(2)}) %copy-start.1) | copy-done | bytes 1441816
  14.1 3.2 %update_momentum.1 = (f32[32,88,256]{2,1,0:T(8,128)}, bf16[32,88,256]{2,1,0:T(8,128)(2,1)S(1)}, s32[64]{0:T(128)S(1)}) custom-call(s32[32]{0:T(128)S(1)} %copy-done.3, s32[32]{0:T(128)S(1)} %copy-done.4, s32[32]{0:T(128)S(1)} %copy-done.5, bf16[32,88,256]{2,1,0:T(8,128)(2,1)S(1)} %copy-done.1, f32[32,88,256]{2,1,0:T(8,128)S(1)} %copy-done), custom_call_target="tpu_custom_call" | custom-call | flops 2883584 | bytes 8650752 | tf_op jit(solution)/shard_map/update_momentum/pallas_call | solution.py:206
  17.3 0.0 copy-start.2
  17.3 1.1 %copy-done.2 = bf16[32,88,256]{2,1,0:T(8,128)(2,1)} copy-done((bf16[32,88,256]{2,1,0:T(8,128)(2,1)}, bf16[32,88,256]{2,1,0:T(8,128)(2,1)S(1)}, u32[]{:S(2)}) %copy-start.2) | copy-done | bytes 1441816
  18.5 27.5 %all-to-all-done.x_ref = bf16[32,88,256]{2,1,0:T(8,128)(2,1)} async-done(((bf16[32,88,256]{2,1,0:T(8,128)(2,1)}), bf16[32,88,256]{2,1,0:T(8,128)(2,1)}, u32[]{:S(2)}, u32[]{:S(2)}) %all-to-all-start) | async-done | bytes 1441824 | tf_op jit(solution)/shard_map/all_to_all | solution.py:492
  45.9 4.6 %all-to-all-start.1 = ((bf16[32,88,256]{2,1,0:T(8,128)(2,1)}), bf16[32,88,256]{2,1,0:T(8,128)(2,1)S(1)}, u32[]{:S(2)}, u32[]{:S(2)}) async-start(bf16[32,88,256]{2,1,0:T(8,128)(2,1)} %copy-done.2), calls=%async_computation.1 | async-start | bytes 2883584 | tf_op jit(solution)/shard_map/all_to_all | solution.py:492
  50.5 8.8 %orthogonalize.2 = (bf16[2,704,1024]{2,1,0:T(8,128)(2,1)}, bf16[4,88,256]{2,1,0:T(8,128)(2,1)S(1)}, bf16[4,88,256]{2,1,0:T(8,128)(2,1)S(1)}, bf16[4,88,256]{2,1,0:T(8,128)(2,1)S(1)}, bf16[4,88,256]{2,1,0:T(8,128)(2,1)S(1)}) custom-call(s32[32]{0:T(128)S(1)} %copy-done.4, bf16[32,88,256]{2,1,0:T(8,128)(2,1)} %all-to-all-done.x_ref), custom_call_target="tpu_custom_call" | custom-call | flops 6643777536 | bytes 4718592 | tf_op jit(solution)/shard_map/orthogonalize/pallas_call | solution.py:379
  59.3 0.3 collective-permute-start
  59.6 1.7 %collective-permute-start.1 = (bf16[4,88,256]{2,1,0:T(8,128)(2,1)S(1)}, bf16[4,88,256]{2,1,0:T(8,128)(2,1)S(1)}, u32[]{:S(2)}, u32[]{:S(2)}) collective-permute-start(bf16[4,88,256]{2,1,0:T(8,128)(2,1)S(1)} %get-tuple-element.39), channel_id=1, source_target_pairs={{0,8},{1,9},{2,10},{3,11},{4,12},{5,13},{6,14},{7,15},{8,0},{9,1},... | collective-permute-start | bytes 540680 | tf_op jit(solution)/shard_map/ppermute | solution.py:498
  61.3 0.0 collective-permute-start.2
  61.3 0.0 collective-permute-done.refs_1_
  61.3 8.8 %collective-permute-done.1.refs_2_ = bf16[4,88,256]{2,1,0:T(8,128)(2,1)S(1)} collective-permute-done((bf16[4,88,256]{2,1,0:T(8,128)(2,1)S(1)}, bf16[4,88,256]{2,1,0:T(8,128)(2,1)S(1)}, u32[]{:S(2)}, u32[]{:S(2)}) %collective-permute-start.1) | collective-permute-done | bytes 180256 | tf_op jit(solution)/shard_map/ppermute | solution.py:498
  70.1 4.2 %collective-permute-done.2.refs_3_ = bf16[4,88,256]{2,1,0:T(8,128)(2,1)S(1)} collective-permute-done((bf16[4,88,256]{2,1,0:T(8,128)(2,1)S(1)}, bf16[4,88,256]{2,1,0:T(8,128)(2,1)S(1)}, u32[]{:S(2)}, u32[]{:S(2)}) %collective-permute-start.2) | collective-permute-done | bytes 180256 | tf_op jit(solution)/shard_map/ppermute | solution.py:498
  74.3 0.8 restage.1
  75.1 3.4 %collective-permute-start.3 = (bf16[4,88,256]{2,1,0:T(8,128)(2,1)}, bf16[4,88,256]{2,1,0:T(8,128)(2,1)S(1)}, u32[]{:S(2)}, u32[]{:S(2)}) collective-permute-start(bf16[4,88,256]{2,1,0:T(8,128)(2,1)} %get-tuple-element.42), channel_id=1, source_target_pairs={{0,1},{1,0},{2,3},{3,2},{4,5},{5,4},{6,7},{7,6},{8,9},{9,8},{10,11... | collective-permute-start | bytes 540680 | tf_op jit(solution)/shard_map/ppermute | solution.py:498
  78.5 1.5 %collective-permute-start.4 = (bf16[4,88,256]{2,1,0:T(8,128)(2,1)}, bf16[4,88,256]{2,1,0:T(8,128)(2,1)S(1)}, u32[]{:S(2)}, u32[]{:S(2)}) collective-permute-start(bf16[4,88,256]{2,1,0:T(8,128)(2,1)} %get-tuple-element.43), channel_id=1, source_target_pairs={{0,16},{1,17},{2,18},{3,19},{4,20},{5,21},{6,22},{7,23},{8,24},{9,... | collective-permute-start | bytes 540680 | tf_op jit(solution)/shard_map/ppermute | solution.py:498
  79.9 0.0 collective-permute-start.5
  79.9 3.8 %all-to-all-done.1.x_ref = bf16[32,88,256]{2,1,0:T(8,128)(2,1)S(1)} async-done(((bf16[32,88,256]{2,1,0:T(8,128)(2,1)}), bf16[32,88,256]{2,1,0:T(8,128)(2,1)S(1)}, u32[]{:S(2)}, u32[]{:S(2)}) %all-to-all-start.1) | async-done | bytes 1441824 | tf_op jit(solution)/shard_map/all_to_all | solution.py:492
  83.7 7.3 %orthogonalize.3 = (bf16[704,1024]{1,0:T(8,128)(2,1)S(1)}, bf16[16,88,256]{2,1,0:T(8,128)(2,1)}) custom-call(s32[32]{0:T(128)S(1)} %copy-done.4, bf16[32,88,256]{2,1,0:T(8,128)(2,1)S(1)} %all-to-all-done.1.x_ref), custom_call_target="tpu_custom_call" | custom-call | flops 6643777536 | bytes 4718592 | tf_op jit(solution)/shard_map/orthogonalize/pallas_call | solution.py:379
  91.0 0.0 collective-permute-done.3.refs_1_
  91.0 0.0 collective-permute-done.4.refs_2_
  91.1 0.1 collective-permute-done.5.refs_3_
  91.1 4.9 %all-to-all-start.2 = ((bf16[16,88,256]{2,1,0:T(8,128)(2,1)}), bf16[16,88,256]{2,1,0:T(8,128)(2,1)S(1)}, u32[]{:S(2)}, u32[]{:S(2)}) async-start(bf16[16,88,256]{2,1,0:T(8,128)(2,1)} %get-tuple-element.48), calls=%async_computation.2 | async-start | bytes 1441792 | tf_op jit(solution)/shard_map/all_to_all | solution.py:492
  96.0 2.3 %store_early.1 = (bf16[2,704,1024]{2,1,0:T(8,128)(2,1)}, bf16[32,88,256]{2,1,0:T(8,128)(2,1)}) custom-call(s32[64]{0:T(128)S(1)} %get-tuple-element.33.list_ref, bf16[704,1024]{1,0:T(8,128)(2,1)S(1)} %get-tuple-element.49.whole_ref, bf16[2,704,1024]{2,1,0:T(8,128)(2,1)} %get-tuple-element.50.owned_in, ...), custom_call_target="tpu_custom_call", output_to_operand_aliasing={{0}: (2, {})} | custom-call | bytes 5767168 | tf_op jit(solution)/shard_map/store_early/pallas_call | solution.py:450
  98.3 8.5 %all-to-all-done.2.back_ref = bf16[16,88,256]{2,1,0:T(8,128)(2,1)S(1)} async-done(((bf16[16,88,256]{2,1,0:T(8,128)(2,1)}), bf16[16,88,256]{2,1,0:T(8,128)(2,1)S(1)}, u32[]{:S(2)}, u32[]{:S(2)}) %all-to-all-start.2) | async-done | bytes 720928 | tf_op jit(solution)/shard_map/all_to_all | solution.py:492
  106.9 1.4 %store_late.1 = bf16[32,88,256]{2,1,0:T(8,128)(2,1)} custom-call(s32[64]{0:T(128)S(1)} %get-tuple-element.33.list_ref, bf16[16,88,256]{2,1,0:T(8,128)(2,1)S(1)} %all-to-all-done.2.back_ref, bf16[32,88,256]{2,1,0:T(8,128)(2,1)} %get-tuple-element.55.update_in), custom_call_target="tpu_custom_call", output_to_operand_aliasing={{}: (2, {})} | custom-call | bytes 1441792 | tf_op jit(solution)/shard_map/store_late/pallas_call | solution.py:478
Async XLA Ops:
  5.2 7.5 %copy-start = (f32[32,88,256]{2,1,0:T(8,128)S(1)}, f32[32,88,256]{2,1,0:T(8,128)}, u32[]{:S(2)}) copy-start(f32[32,88,256]{2,1,0:T(8,128)} %m_ref.3) | copy-start | bytes 8650756
  5.3 7.5 %copy-start.3 = (s32[32]{0:T(128)S(1)}, s32[32]{0:T(128)}, u32[]{:S(2)}) copy-start(s32[32]{0:T(128)} %owner_ref.3) | copy-start | bytes 388
  5.3 7.5 %copy-start.4 = (s32[32]{0:T(128)S(1)}, s32[32]{0:T(128)}, u32[]{:S(2)}) copy-start(s32[32]{0:T(128)} %get-tuple-element.30.other_ref) | copy-start | bytes 388
  5.3 7.5 %copy-start.5 = (s32[32]{0:T(128)S(1)}, s32[32]{0:T(128)}, u32[]{:S(2)}) copy-start(s32[32]{0:T(128)} %get-tuple-element.31.rank_ref) | copy-start | bytes 388
  5.3 40.6 %all-to-all-start = ((bf16[32,88,256]{2,1,0:T(8,128)(2,1)}), bf16[32,88,256]{2,1,0:T(8,128)(2,1)}, u32[]{:S(2)}, u32[]{:S(2)}) async-start(bf16[32,88,256]{2,1,0:T(8,128)(2,1)} %get-tuple-element.34), calls=%async_computation | async-start | bytes 2883584 | tf_op jit(solution)/shard_map/all_to_all | solution.py:492
  12.8 1.4 %copy-start.1 = (bf16[32,88,256]{2,1,0:T(8,128)(2,1)S(1)}, bf16[32,88,256]{2,1,0:T(8,128)(2,1)}, u32[]{:S(2)}) copy-start(bf16[32,88,256]{2,1,0:T(8,128)(2,1)} %g_ref.3) | copy-start | bytes 4325380
  17.3 1.1 %copy-start.2 = (bf16[32,88,256]{2,1,0:T(8,128)(2,1)}, bf16[32,88,256]{2,1,0:T(8,128)(2,1)S(1)}, u32[]{:S(2)}) copy-start(bf16[32,88,256]{2,1,0:T(8,128)(2,1)S(1)} %get-tuple-element.45) | copy-start | bytes 4325380
  45.9 37.8 %all-to-all-start.1 = ((bf16[32,88,256]{2,1,0:T(8,128)(2,1)}), bf16[32,88,256]{2,1,0:T(8,128)(2,1)S(1)}, u32[]{:S(2)}, u32[]{:S(2)}) async-start(bf16[32,88,256]{2,1,0:T(8,128)(2,1)} %copy-done.2), calls=%async_computation.1 | async-start | bytes 2883584 | tf_op jit(solution)/shard_map/all_to_all | solution.py:492
  59.3 2.0 %collective-permute-start = (bf16[4,88,256]{2,1,0:T(8,128)(2,1)S(1)}, bf16[4,88,256]{2,1,0:T(8,128)(2,1)S(1)}, u32[]{:S(2)}, u32[]{:S(2)}) collective-permute-start(bf16[4,88,256]{2,1,0:T(8,128)(2,1)S(1)} %get-tuple-element.38), channel_id=1, source_target_pairs={{0,4},{1,5},{2,6},{3,7},{4,0},{5,1},{6,2},{7,3},{8,12},{9,13},{10,... | collective-permute-start | bytes 540680 | tf_op jit(solution)/shard_map/ppermute | solution.py:498
  59.6 10.5 %collective-permute-start.1 = (bf16[4,88,256]{2,1,0:T(8,128)(2,1)S(1)}, bf16[4,88,256]{2,1,0:T(8,128)(2,1)S(1)}, u32[]{:S(2)}, u32[]{:S(2)}) collective-permute-start(bf16[4,88,256]{2,1,0:T(8,128)(2,1)S(1)} %get-tuple-element.39), channel_id=1, source_target_pairs={{0,8},{1,9},{2,10},{3,11},{4,12},{5,13},{6,14},{7,15},{8,0},{9,1},... | collective-permute-start | bytes 540680 | tf_op jit(solution)/shard_map/ppermute | solution.py:498
  61.3 13.0 %collective-permute-start.2 = (bf16[4,88,256]{2,1,0:T(8,128)(2,1)S(1)}, bf16[4,88,256]{2,1,0:T(8,128)(2,1)S(1)}, u32[]{:S(2)}, u32[]{:S(2)}) collective-permute-start(bf16[4,88,256]{2,1,0:T(8,128)(2,1)S(1)} %get-tuple-element.40), channel_id=1, source_target_pairs={{0,12},{1,13},{2,14},{3,15},{4,8},{5,9},{6,10},{7,11},{8,4},{9,5},... | collective-permute-start | bytes 540680 | tf_op jit(solution)/shard_map/ppermute | solution.py:498
  75.1 15.9 %collective-permute-start.3 = (bf16[4,88,256]{2,1,0:T(8,128)(2,1)}, bf16[4,88,256]{2,1,0:T(8,128)(2,1)S(1)}, u32[]{:S(2)}, u32[]{:S(2)}) collective-permute-start(bf16[4,88,256]{2,1,0:T(8,128)(2,1)} %get-tuple-element.42), channel_id=1, source_target_pairs={{0,1},{1,0},{2,3},{3,2},{4,5},{5,4},{6,7},{7,6},{8,9},{9,8},{10,11... | collective-permute-start | bytes 540680 | tf_op jit(solution)/shard_map/ppermute | solution.py:498
  78.5 12.6 %collective-permute-start.4 = (bf16[4,88,256]{2,1,0:T(8,128)(2,1)}, bf16[4,88,256]{2,1,0:T(8,128)(2,1)S(1)}, u32[]{:S(2)}, u32[]{:S(2)}) collective-permute-start(bf16[4,88,256]{2,1,0:T(8,128)(2,1)} %get-tuple-element.43), channel_id=1, source_target_pairs={{0,16},{1,17},{2,18},{3,19},{4,20},{5,21},{6,22},{7,23},{8,24},{9,... | collective-permute-start | bytes 540680 | tf_op jit(solution)/shard_map/ppermute | solution.py:498
  79.9 11.2 %collective-permute-start.5 = (bf16[4,88,256]{2,1,0:T(8,128)(2,1)}, bf16[4,88,256]{2,1,0:T(8,128)(2,1)}, u32[]{:S(2)}, u32[]{:S(2)}) collective-permute-start(bf16[4,88,256]{2,1,0:T(8,128)(2,1)} %get-tuple-element.44), channel_id=1, source_target_pairs={{0,17},{1,16},{2,19},{3,18},{4,21},{5,20},{6,23},{7,22},{8,25},{9,... | collective-permute-start | bytes 540680 | tf_op jit(solution)/shard_map/ppermute | solution.py:498
  91.1 15.7 %all-to-all-start.2 = ((bf16[16,88,256]{2,1,0:T(8,128)(2,1)}), bf16[16,88,256]{2,1,0:T(8,128)(2,1)S(1)}, u32[]{:S(2)}, u32[]{:S(2)}) async-start(bf16[16,88,256]{2,1,0:T(8,128)(2,1)} %get-tuple-element.48), calls=%async_computation.2 | async-start | bytes 1441792 | tf_op jit(solution)/shard_map/all_to_all | solution.py:492

commit v26 on v20

--- a/solution.py
+++ b/solution.py
@@ -114,7 +114,7 @@
 
 def pack(gradients, momentum, owner_table, devices, col_size):
     mats, rows, cols = gradients.shape
-    chunk = 8
+    chunk = 16
     return pl.pallas_call(
         functools.partial(pack_kernel, chunk, col_size),
         grid_spec=pltpu.PrefetchScalarGridSpec(

time: 108 us -> 108 us (level)
  no operation moved by 1% of the time
where the time goes in v26:
time: 108 us
  waiting for transfers between devices  52.9 us (49%)
  Pallas kernels  27.9 us (26%)
  starting transfers between devices  23.7 us (22%)
  local copies, waits for them, and re-layouts  2.51 us (2%)
    all_to_all x3, waiting for transfers between devices, exchange(): lax.all_to_all(blocks, axes, split_axis=0, concat_axis=0, tiled=True, axi...  39.8 us
    all_to_all x3, starting transfers between devices, exchange(): lax.all_to_all(blocks, axes, split_axis=0, concat_axis=0, tiled=True, axi...  16.8 us
    pallas_call x2, Pallas kernels, orthogonalize(): pl.pallas_call(functools.partial(ortho_kernel, row_size, col_size, slot),...  16.1 us
    ppermute x6, waiting for transfers between devices, swap(): return lax.ppermute(block, AXES, [(d, d ^ offset) for d in range(devices)])  13.1 us
    ppermute x6, starting transfers between devices, swap(): return lax.ppermute(block, AXES, [(d, d ^ offset) for d in range(devices)])  6.83 us
    pallas_call x1, Pallas kernels, pack(): pl.pallas_call(functools.partial(pack_kernel, chunk, col_size), grid_spec...  4.05 us
    pallas_call x1, Pallas kernels, update_momentum(): pl.pallas_call(functools.partial(momentum_kernel, chunk, col_size), grid_...  3.21 us
    unnamed x12, local copies, waits for them, and re-layouts  2.51 us
  transfers between devices with their start and end apart: 9, of which 6 were waited for; matrix products, arithmetic and copies ran while one was open for 0% of the time, Pallas kernels for 21%

profile of v26, /device:TPU:0, one launch (start us, length us, event | category | flops | bytes accessed | tf_op | source)
XLA Modules:
  0.0 107.7 jit_solution(11340853861185355162)
XLA Ops:
  0.6 4.0 %pack.1 = (bf16[32,88,256]{2,1,0:T(8,128)(2,1)}, s32[32]{0:T(128)}, s32[32]{0:T(128)}) custom-call(s32[32]{0:T(128)} %owner_ref.3, bf16[32,88,256]{2,1,0:T(8,128)(2,1)} %g_ref.3, f32[32,88,256]{2,1,0:T(8,128)} %m_ref.3), custom_call_target="tpu_custom_call" | custom-call | flops 2883584 | bytes 5767168 | tf_op jit(solution)/shard_map/pack/pallas_call | solution.py:118
  4.7 0.0 copy-start
  4.7 0.0 copy-start.3
  4.7 0.0 copy-start.4
  4.7 0.0 copy-start.5
  4.7 7.4 %all-to-all-start = ((bf16[32,88,256]{2,1,0:T(8,128)(2,1)}), bf16[32,88,256]{2,1,0:T(8,128)(2,1)}, u32[]{:S(2)}, u32[]{:S(2)}) async-start(bf16[32,88,256]{2,1,0:T(8,128)(2,1)} %get-tuple-element.34), calls=%async_computation | async-start | bytes 2883584 | tf_op jit(solution)/shard_map/all_to_all | solution.py:477
  12.2 0.0 copy-done
  12.2 0.0 copy-done.3
  12.2 0.0 copy-done.4
  12.2 0.0 copy-done.5
  12.2 0.0 copy-start.1
  12.2 1.4 %copy-done.1 = bf16[32,88,256]{2,1,0:T(8,128)(2,1)S(1)} copy-done((bf16[32,88,256]{2,1,0:T(8,128)(2,1)S(1)}, bf16[32,88,256]{2,1,0:T(8,128)(2,1)}, u32[]{:S(2)}) %copy-start.1) | copy-done | bytes 1441816
  13.6 3.2 %update_momentum.1 = (f32[32,88,256]{2,1,0:T(8,128)}, bf16[32,88,256]{2,1,0:T(8,128)(2,1)S(1)}, s32[64]{0:T(128)S(1)}) custom-call(s32[32]{0:T(128)S(1)} %copy-done.3, s32[32]{0:T(128)S(1)} %copy-done.4, s32[32]{0:T(128)S(1)} %copy-done.5, bf16[32,88,256]{2,1,0:T(8,128)(2,1)S(1)} %copy-done.1, f32[32,88,256]{2,1,0:T(8,128)S(1)} %copy-done), custom_call_target="tpu_custom_call" | custom-call | flops 2883584 | bytes 8650752 | tf_op jit(solution)/shard_map/update_momentum/pallas_call | solution.py:191
  16.8 0.0 copy-start.2
  16.8 1.1 %copy-done.2 = bf16[32,88,256]{2,1,0:T(8,128)(2,1)} copy-done((bf16[32,88,256]{2,1,0:T(8,128)(2,1)}, bf16[32,88,256]{2,1,0:T(8,128)(2,1)S(1)}, u32[]{:S(2)}) %copy-start.2) | copy-done | bytes 1441816
  17.9 27.5 %all-to-all-done.x_ref = bf16[32,88,256]{2,1,0:T(8,128)(2,1)} async-done(((bf16[32,88,256]{2,1,0:T(8,128)(2,1)}), bf16[32,88,256]{2,1,0:T(8,128)(2,1)}, u32[]{:S(2)}, u32[]{:S(2)}) %all-to-all-start) | async-done | bytes 1441824 | tf_op jit(solution)/shard_map/all_to_all | solution.py:477
  45.4 4.6 %all-to-all-start.1 = ((bf16[32,88,256]{2,1,0:T(8,128)(2,1)}), bf16[32,88,256]{2,1,0:T(8,128)(2,1)S(1)}, u32[]{:S(2)}, u32[]{:S(2)}) async-start(bf16[32,88,256]{2,1,0:T(8,128)(2,1)} %copy-done.2), calls=%async_computation.1 | async-start | bytes 2883584 | tf_op jit(solution)/shard_map/all_to_all | solution.py:477
  49.9 8.8 %orthogonalize.2 = (bf16[2,704,1024]{2,1,0:T(8,128)(2,1)}, bf16[4,88,256]{2,1,0:T(8,128)(2,1)S(1)}, bf16[4,88,256]{2,1,0:T(8,128)(2,1)S(1)}, bf16[4,88,256]{2,1,0:T(8,128)(2,1)S(1)}, bf16[4,88,256]{2,1,0:T(8,128)(2,1)S(1)}) custom-call(s32[32]{0:T(128)S(1)} %copy-done.4, bf16[32,88,256]{2,1,0:T(8,128)(2,1)} %all-to-all-done.x_ref), custom_call_target="tpu_custom_call" | custom-call | flops 6643777536 | bytes 4718592 | tf_op jit(solution)/shard_map/orthogonalize/pallas_call | solution.py:364
  58.7 0.3 collective-permute-start
  59.1 1.7 %collective-permute-start.1 = (bf16[4,88,256]{2,1,0:T(8,128)(2,1)S(1)}, bf16[4,88,256]{2,1,0:T(8,128)(2,1)S(1)}, u32[]{:S(2)}, u32[]{:S(2)}) collective-permute-start(bf16[4,88,256]{2,1,0:T(8,128)(2,1)S(1)} %get-tuple-element.39), channel_id=1, source_target_pairs={{0,8},{1,9},{2,10},{3,11},{4,12},{5,13},{6,14},{7,15},{8,0},{9,1},... | collective-permute-start | bytes 540680 | tf_op jit(solution)/shard_map/ppermute | solution.py:483
  60.7 0.0 collective-permute-start.2
  60.7 0.0 collective-permute-done.refs_1_
  60.7 8.8 %collective-permute-done.1.refs_2_ = bf16[4,88,256]{2,1,0:T(8,128)(2,1)S(1)} collective-permute-done((bf16[4,88,256]{2,1,0:T(8,128)(2,1)S(1)}, bf16[4,88,256]{2,1,0:T(8,128)(2,1)S(1)}, u32[]{:S(2)}, u32[]{:S(2)}) %collective-permute-start.1) | collective-permute-done | bytes 180256 | tf_op jit(solution)/shard_map/ppermute | solution.py:483
  69.5 4.2 %collective-permute-done.2.refs_3_ = bf16[4,88,256]{2,1,0:T(8,128)(2,1)S(1)} collective-permute-done((bf16[4,88,256]{2,1,0:T(8,128)(2,1)S(1)}, bf16[4,88,256]{2,1,0:T(8,128)(2,1)S(1)}, u32[]{:S(2)}, u32[]{:S(2)}) %collective-permute-start.2) | collective-permute-done | bytes 180256 | tf_op jit(solution)/shard_map/ppermute | solution.py:483
  73.7 0.8 restage.1
  74.5 3.4 %collective-permute-start.3 = (bf16[4,88,256]{2,1,0:T(8,128)(2,1)}, bf16[4,88,256]{2,1,0:T(8,128)(2,1)S(1)}, u32[]{:S(2)}, u32[]{:S(2)}) collective-permute-start(bf16[4,88,256]{2,1,0:T(8,128)(2,1)} %get-tuple-element.42), channel_id=1, source_target_pairs={{0,1},{1,0},{2,3},{3,2},{4,5},{5,4},{6,7},{7,6},{8,9},{9,8},{10,11... | collective-permute-start | bytes 540680 | tf_op jit(solution)/shard_map/ppermute | solution.py:483
  77.9 1.5 %collective-permute-start.4 = (bf16[4,88,256]{2,1,0:T(8,128)(2,1)}, bf16[4,88,256]{2,1,0:T(8,128)(2,1)S(1)}, u32[]{:S(2)}, u32[]{:S(2)}) collective-permute-start(bf16[4,88,256]{2,1,0:T(8,128)(2,1)} %get-tuple-element.43), channel_id=1, source_target_pairs={{0,16},{1,17},{2,18},{3,19},{4,20},{5,21},{6,22},{7,23},{8,24},{9,... | collective-permute-start | bytes 540680 | tf_op jit(solution)/shard_map/ppermute | solution.py:483
  79.4 0.0 collective-permute-start.5
  79.4 3.8 %all-to-all-done.1.x_ref = bf16[32,88,256]{2,1,0:T(8,128)(2,1)S(1)} async-done(((bf16[32,88,256]{2,1,0:T(8,128)(2,1)}), bf16[32,88,256]{2,1,0:T(8,128)(2,1)S(1)}, u32[]{:S(2)}, u32[]{:S(2)}) %all-to-all-start.1) | async-done | bytes 1441824 | tf_op jit(solution)/shard_map/all_to_all | solution.py:477
  83.2 7.3 %orthogonalize.3 = (bf16[704,1024]{1,0:T(8,128)(2,1)S(1)}, bf16[16,88,256]{2,1,0:T(8,128)(2,1)}) custom-call(s32[32]{0:T(128)S(1)} %copy-done.4, bf16[32,88,256]{2,1,0:T(8,128)(2,1)S(1)} %all-to-all-done.1.x_ref), custom_call_target="tpu_custom_call" | custom-call | flops 6643777536 | bytes 4718592 | tf_op jit(solution)/shard_map/orthogonalize/pallas_call | solution.py:364
  90.5 0.0 collective-permute-done.3.refs_1_
  90.5 0.0 collective-permute-done.4.refs_2_
  90.5 0.1 collective-permute-done.5.refs_3_
  90.6 4.9 %all-to-all-start.2 = ((bf16[16,88,256]{2,1,0:T(8,128)(2,1)}), bf16[16,88,256]{2,1,0:T(8,128)(2,1)S(1)}, u32[]{:S(2)}, u32[]{:S(2)}) async-start(bf16[16,88,256]{2,1,0:T(8,128)(2,1)} %get-tuple-element.48), calls=%async_computation.2 | async-start | bytes 1441792 | tf_op jit(solution)/shard_map/all_to_all | solution.py:477
  95.5 2.3 %store_early.1 = (bf16[2,704,1024]{2,1,0:T(8,128)(2,1)}, bf16[32,88,256]{2,1,0:T(8,128)(2,1)}) custom-call(s32[64]{0:T(128)S(1)} %get-tuple-element.33.list_ref, bf16[704,1024]{1,0:T(8,128)(2,1)S(1)} %get-tuple-element.49.whole_ref, bf16[2,704,1024]{2,1,0:T(8,128)(2,1)} %get-tuple-element.50.owned_in, ...), custom_call_target="tpu_custom_call", output_to_operand_aliasing={{0}: (2, {})} | custom-call | bytes 5767168 | tf_op jit(solution)/shard_map/store_early/pallas_call | solution.py:435
  97.8 8.5 %all-to-all-done.2.back_ref = bf16[16,88,256]{2,1,0:T(8,128)(2,1)S(1)} async-done(((bf16[16,88,256]{2,1,0:T(8,128)(2,1)}), bf16[16,88,256]{2,1,0:T(8,128)(2,1)S(1)}, u32[]{:S(2)}, u32[]{:S(2)}) %all-to-all-start.2) | async-done | bytes 720928 | tf_op jit(solution)/shard_map/all_to_all | solution.py:477
  106.3 1.4 %store_late.1 = bf16[32,88,256]{2,1,0:T(8,128)(2,1)} custom-call(s32[64]{0:T(128)S(1)} %get-tuple-element.33.list_ref, bf16[16,88,256]{2,1,0:T(8,128)(2,1)S(1)} %all-to-all-done.2.back_ref, bf16[32,88,256]{2,1,0:T(8,128)(2,1)} %get-tuple-element.55.update_in), custom_call_target="tpu_custom_call", output_to_operand_aliasing={{}: (2, {})} | custom-call | bytes 1441792 | tf_op jit(solution)/shard_map/store_late/pallas_call | solution.py:463
Async XLA Ops:
  4.7 7.5 %copy-start = (f32[32,88,256]{2,1,0:T(8,128)S(1)}, f32[32,88,256]{2,1,0:T(8,128)}, u32[]{:S(2)}) copy-start(f32[32,88,256]{2,1,0:T(8,128)} %m_ref.3) | copy-start | bytes 8650756
  4.7 7.5 %copy-start.3 = (s32[32]{0:T(128)S(1)}, s32[32]{0:T(128)}, u32[]{:S(2)}) copy-start(s32[32]{0:T(128)} %owner_ref.3) | copy-start | bytes 388
  4.7 7.5 %copy-start.4 = (s32[32]{0:T(128)S(1)}, s32[32]{0:T(128)}, u32[]{:S(2)}) copy-start(s32[32]{0:T(128)} %get-tuple-element.30.other_ref) | copy-start | bytes 388
  4.7 7.5 %copy-start.5 = (s32[32]{0:T(128)S(1)}, s32[32]{0:T(128)}, u32[]{:S(2)}) copy-start(s32[32]{0:T(128)} %get-tuple-element.31.rank_ref) | copy-start | bytes 388
  4.7 40.6 %all-to-all-start = ((bf16[32,88,256]{2,1,0:T(8,128)(2,1)}), bf16[32,88,256]{2,1,0:T(8,128)(2,1)}, u32[]{:S(2)}, u32[]{:S(2)}) async-start(bf16[32,88,256]{2,1,0:T(8,128)(2,1)} %get-tuple-element.34), calls=%async_computation | async-start | bytes 2883584 | tf_op jit(solution)/shard_map/all_to_all | solution.py:477
  12.2 1.4 %copy-start.1 = (bf16[32,88,256]{2,1,0:T(8,128)(2,1)S(1)}, bf16[32,88,256]{2,1,0:T(8,128)(2,1)}, u32[]{:S(2)}) copy-start(bf16[32,88,256]{2,1,0:T(8,128)(2,1)} %g_ref.3) | copy-start | bytes 4325380
  16.8 1.1 %copy-start.2 = (bf16[32,88,256]{2,1,0:T(8,128)(2,1)}, bf16[32,88,256]{2,1,0:T(8,128)(2,1)S(1)}, u32[]{:S(2)}) copy-start(bf16[32,88,256]{2,1,0:T(8,128)(2,1)S(1)} %get-tuple-element.45) | copy-start | bytes 4325380
  45.4 37.8 %all-to-all-start.1 = ((bf16[32,88,256]{2,1,0:T(8,128)(2,1)}), bf16[32,88,256]{2,1,0:T(8,128)(2,1)S(1)}, u32[]{:S(2)}, u32[]{:S(2)}) async-start(bf16[32,88,256]{2,1,0:T(8,128)(2,1)} %copy-done.2), calls=%async_computation.1 | async-start | bytes 2883584 | tf_op jit(solution)/shard_map/all_to_all | solution.py:477
  58.7 2.0 %collective-permute-start = (bf16[4,88,256]{2,1,0:T(8,128)(2,1)S(1)}, bf16[4,88,256]{2,1,0:T(8,128)(2,1)S(1)}, u32[]{:S(2)}, u32[]{:S(2)}) collective-permute-start(bf16[4,88,256]{2,1,0:T(8,128)(2,1)S(1)} %get-tuple-element.38), channel_id=1, source_target_pairs={{0,4},{1,5},{2,6},{3,7},{4,0},{5,1},{6,2},{7,3},{8,12},{9,13},{10,... | collective-permute-start | bytes 540680 | tf_op jit(solution)/shard_map/ppermute | solution.py:483
  59.1 10.5 %collective-permute-start.1 = (bf16[4,88,256]{2,1,0:T(8,128)(2,1)S(1)}, bf16[4,88,256]{2,1,0:T(8,128)(2,1)S(1)}, u32[]{:S(2)}, u32[]{:S(2)}) collective-permute-start(bf16[4,88,256]{2,1,0:T(8,128)(2,1)S(1)} %get-tuple-element.39), channel_id=1, source_target_pairs={{0,8},{1,9},{2,10},{3,11},{4,12},{5,13},{6,14},{7,15},{8,0},{9,1},... | collective-permute-start | bytes 540680 | tf_op jit(solution)/shard_map/ppermute | solution.py:483
  60.7 13.0 %collective-permute-start.2 = (bf16[4,88,256]{2,1,0:T(8,128)(2,1)S(1)}, bf16[4,88,256]{2,1,0:T(8,128)(2,1)S(1)}, u32[]{:S(2)}, u32[]{:S(2)}) collective-permute-start(bf16[4,88,256]{2,1,0:T(8,128)(2,1)S(1)} %get-tuple-element.40), channel_id=1, source_target_pairs={{0,12},{1,13},{2,14},{3,15},{4,8},{5,9},{6,10},{7,11},{8,4},{9,5},... | collective-permute-start | bytes 540680 | tf_op jit(solution)/shard_map/ppermute | solution.py:483
  74.5 15.9 %collective-permute-start.3 = (bf16[4,88,256]{2,1,0:T(8,128)(2,1)}, bf16[4,88,256]{2,1,0:T(8,128)(2,1)S(1)}, u32[]{:S(2)}, u32[]{:S(2)}) collective-permute-start(bf16[4,88,256]{2,1,0:T(8,128)(2,1)} %get-tuple-element.42), channel_id=1, source_target_pairs={{0,1},{1,0},{2,3},{3,2},{4,5},{5,4},{6,7},{7,6},{8,9},{9,8},{10,11... | collective-permute-start | bytes 540680 | tf_op jit(solution)/shard_map/ppermute | solution.py:483
  77.9 12.6 %collective-permute-start.4 = (bf16[4,88,256]{2,1,0:T(8,128)(2,1)}, bf16[4,88,256]{2,1,0:T(8,128)(2,1)S(1)}, u32[]{:S(2)}, u32[]{:S(2)}) collective-permute-start(bf16[4,88,256]{2,1,0:T(8,128)(2,1)} %get-tuple-element.43), channel_id=1, source_target_pairs={{0,16},{1,17},{2,18},{3,19},{4,20},{5,21},{6,22},{7,23},{8,24},{9,... | collective-permute-start | bytes 540680 | tf_op jit(solution)/shard_map/ppermute | solution.py:483
  79.4 11.2 %collective-permute-start.5 = (bf16[4,88,256]{2,1,0:T(8,128)(2,1)}, bf16[4,88,256]{2,1,0:T(8,128)(2,1)}, u32[]{:S(2)}, u32[]{:S(2)}) collective-permute-start(bf16[4,88,256]{2,1,0:T(8,128)(2,1)} %get-tuple-element.44), channel_id=1, source_target_pairs={{0,17},{1,16},{2,19},{3,18},{4,21},{5,20},{6,23},{7,22},{8,25},{9,... | collective-permute-start | bytes 540680 | tf_op jit(solution)/shard_map/ppermute | solution.py:483
  90.6 15.7 %all-to-all-start.2 = ((bf16[16,88,256]{2,1,0:T(8,128)(2,1)}), bf16[16,88,256]{2,1,0:T(8,128)(2,1)S(1)}, u32[]{:S(2)}, u32[]{:S(2)}) async-start(bf16[16,88,256]{2,1,0:T(8,128)(2,1)} %get-tuple-element.48), calls=%async_computation.2 | async-start | bytes 1441792 | tf_op jit(solution)/shard_map/all_to_all | solution.py:477

commit v27 on v26

--- a/solution.py
+++ b/solution.py
@@ -50,7 +50,7 @@
         count_ref[d] = 0
         return 0
 
-    lax.fori_loop(0, devices, clear, 0, unroll=8)
+    lax.fori_loop(0, devices, clear, 0, unroll=32)
 
     def rank_matrix(i, _):
         owner = owner_ref[i]
@@ -59,7 +59,7 @@
         count_ref[owner] = rank + 1
         return 0
 
-    lax.fori_loop(0, mats, rank_matrix, 0, unroll=8)
+    lax.fori_loop(0, mats, rank_matrix, 0, unroll=32)
 
     def list_device(d, found):
         owns = jnp.minimum(count_ref[d], 1)
@@ -71,7 +71,7 @@
         list_ref[row * devices + place] = d
         return tuple(n + jnp.where(row == k, 1, 0) for k, n in enumerate(found))
 
-    found = lax.fori_loop(0, devices, list_device, (0,) * (2 * HALVES), unroll=8)
+    found = lax.fori_loop(0, devices, list_device, (0,) * (2 * HALVES), unroll=32)
     for half in range(HALVES):
 
         def pair(k, _):

time: 108 us -> 108 us (level)
  no operation moved by 1% of the time
where the time goes in v27:
time: 108 us
  waiting for transfers between devices  52.9 us (49%)
  Pallas kernels  27.9 us (26%)
  starting transfers between devices  23.7 us (22%)
  local copies, waits for them, and re-layouts  2.51 us (2%)
    all_to_all x3, waiting for transfers between devices, exchange(): lax.all_to_all(blocks, axes, split_axis=0, concat_axis=0, tiled=True, axi...  39.8 us
    all_to_all x3, starting transfers between devices, exchange(): lax.all_to_all(blocks, axes, split_axis=0, concat_axis=0, tiled=True, axi...  16.8 us
    pallas_call x2, Pallas kernels, orthogonalize(): pl.pallas_call(functools.partial(ortho_kernel, row_size, col_size, slot),...  16.1 us
    ppermute x6, waiting for transfers between devices, swap(): return lax.ppermute(block, AXES, [(d, d ^ offset) for d in range(devices)])  13.1 us
    ppermute x6, starting transfers between devices, swap(): return lax.ppermute(block, AXES, [(d, d ^ offset) for d in range(devices)])  6.83 us
    pallas_call x1, Pallas kernels, pack(): pl.pallas_call(functools.partial(pack_kernel, chunk, col_size), grid_spec...  4.05 us
    pallas_call x1, Pallas kernels, update_momentum(): pl.pallas_call(functools.partial(momentum_kernel, chunk, col_size), grid_...  3.21 us
    unnamed x12, local copies, waits for them, and re-layouts  2.51 us
  transfers between devices with their start and end apart: 9, of which 6 were waited for; matrix products, arithmetic and copies ran while one was open for 0% of the time, Pallas kernels for 21%

profile of v27, /device:TPU:0, one launch (start us, length us, event | category | flops | bytes accessed | tf_op | source)
XLA Modules:
  0.0 107.7 jit_solution(18382826564864825887)
XLA Ops:
  0.6 4.0 %pack.1 = (bf16[32,88,256]{2,1,0:T(8,128)(2,1)}, s32[32]{0:T(128)}, s32[32]{0:T(128)}) custom-call(s32[32]{0:T(128)} %owner_ref.3, bf16[32,88,256]{2,1,0:T(8,128)(2,1)} %g_ref.3, f32[32,88,256]{2,1,0:T(8,128)} %m_ref.3), custom_call_target="tpu_custom_call" | custom-call | flops 2883584 | bytes 5767168 | tf_op jit(solution)/shard_map/pack/pallas_call | solution.py:118
  4.7 0.0 copy-start
  4.7 0.0 copy-start.3
  4.7 0.0 copy-start.4
  4.7 0.0 copy-start.5
  4.7 7.4 %all-to-all-start = ((bf16[32,88,256]{2,1,0:T(8,128)(2,1)}), bf16[32,88,256]{2,1,0:T(8,128)(2,1)}, u32[]{:S(2)}, u32[]{:S(2)}) async-start(bf16[32,88,256]{2,1,0:T(8,128)(2,1)} %get-tuple-element.34), calls=%async_computation | async-start | bytes 2883584 | tf_op jit(solution)/shard_map/all_to_all | solution.py:477
  12.2 0.0 copy-done
  12.2 0.0 copy-done.3
  12.2 0.0 copy-done.4
  12.2 0.0 copy-done.5
  12.2 0.0 copy-start.1
  12.2 1.4 %copy-done.1 = bf16[32,88,256]{2,1,0:T(8,128)(2,1)S(1)} copy-done((bf16[32,88,256]{2,1,0:T(8,128)(2,1)S(1)}, bf16[32,88,256]{2,1,0:T(8,128)(2,1)}, u32[]{:S(2)}) %copy-start.1) | copy-done | bytes 1441816
  13.6 3.2 %update_momentum.1 = (f32[32,88,256]{2,1,0:T(8,128)}, bf16[32,88,256]{2,1,0:T(8,128)(2,1)S(1)}, s32[64]{0:T(128)S(1)}) custom-call(s32[32]{0:T(128)S(1)} %copy-done.3, s32[32]{0:T(128)S(1)} %copy-done.4, s32[32]{0:T(128)S(1)} %copy-done.5, bf16[32,88,256]{2,1,0:T(8,128)(2,1)S(1)} %copy-done.1, f32[32,88,256]{2,1,0:T(8,128)S(1)} %copy-done), custom_call_target="tpu_custom_call" | custom-call | flops 2883584 | bytes 8650752 | tf_op jit(solution)/shard_map/update_momentum/pallas_call | solution.py:191
  16.8 0.0 copy-start.2
  16.8 1.1 %copy-done.2 = bf16[32,88,256]{2,1,0:T(8,128)(2,1)} copy-done((bf16[32,88,256]{2,1,0:T(8,128)(2,1)}, bf16[32,88,256]{2,1,0:T(8,128)(2,1)S(1)}, u32[]{:S(2)}) %copy-start.2) | copy-done | bytes 1441816
  17.9 27.5 %all-to-all-done.x_ref = bf16[32,88,256]{2,1,0:T(8,128)(2,1)} async-done(((bf16[32,88,256]{2,1,0:T(8,128)(2,1)}), bf16[32,88,256]{2,1,0:T(8,128)(2,1)}, u32[]{:S(2)}, u32[]{:S(2)}) %all-to-all-start) | async-done | bytes 1441824 | tf_op jit(solution)/shard_map/all_to_all | solution.py:477
  45.4 4.6 %all-to-all-start.1 = ((bf16[32,88,256]{2,1,0:T(8,128)(2,1)}), bf16[32,88,256]{2,1,0:T(8,128)(2,1)S(1)}, u32[]{:S(2)}, u32[]{:S(2)}) async-start(bf16[32,88,256]{2,1,0:T(8,128)(2,1)} %copy-done.2), calls=%async_computation.1 | async-start | bytes 2883584 | tf_op jit(solution)/shard_map/all_to_all | solution.py:477
  49.9 8.8 %orthogonalize.2 = (bf16[2,704,1024]{2,1,0:T(8,128)(2,1)}, bf16[4,88,256]{2,1,0:T(8,128)(2,1)S(1)}, bf16[4,88,256]{2,1,0:T(8,128)(2,1)S(1)}, bf16[4,88,256]{2,1,0:T(8,128)(2,1)S(1)}, bf16[4,88,256]{2,1,0:T(8,128)(2,1)S(1)}) custom-call(s32[32]{0:T(128)S(1)} %copy-done.4, bf16[32,88,256]{2,1,0:T(8,128)(2,1)} %all-to-all-done.x_ref), custom_call_target="tpu_custom_call" | custom-call | flops 6643777536 | bytes 4718592 | tf_op jit(solution)/shard_map/orthogonalize/pallas_call | solution.py:364
  58.7 0.3 collective-permute-start
  59.1 1.7 %collective-permute-start.1 = (bf16[4,88,256]{2,1,0:T(8,128)(2,1)S(1)}, bf16[4,88,256]{2,1,0:T(8,128)(2,1)S(1)}, u32[]{:S(2)}, u32[]{:S(2)}) collective-permute-start(bf16[4,88,256]{2,1,0:T(8,128)(2,1)S(1)} %get-tuple-element.39), channel_id=1, source_target_pairs={{0,8},{1,9},{2,10},{3,11},{4,12},{5,13},{6,14},{7,15},{8,0},{9,1},... | collective-permute-start | bytes 540680 | tf_op jit(solution)/shard_map/ppermute | solution.py:483
  60.7 0.0 collective-permute-start.2
  60.7 0.0 collective-permute-done.refs_1_
  60.7 8.8 %collective-permute-done.1.refs_2_ = bf16[4,88,256]{2,1,0:T(8,128)(2,1)S(1)} collective-permute-done((bf16[4,88,256]{2,1,0:T(8,128)(2,1)S(1)}, bf16[4,88,256]{2,1,0:T(8,128)(2,1)S(1)}, u32[]{:S(2)}, u32[]{:S(2)}) %collective-permute-start.1) | collective-permute-done | bytes 180256 | tf_op jit(solution)/shard_map/ppermute | solution.py:483
  69.5 4.2 %collective-permute-done.2.refs_3_ = bf16[4,88,256]{2,1,0:T(8,128)(2,1)S(1)} collective-permute-done((bf16[4,88,256]{2,1,0:T(8,128)(2,1)S(1)}, bf16[4,88,256]{2,1,0:T(8,128)(2,1)S(1)}, u32[]{:S(2)}, u32[]{:S(2)}) %collective-permute-start.2) | collective-permute-done | bytes 180256 | tf_op jit(solution)/shard_map/ppermute | solution.py:483
  73.7 0.8 restage.1
  74.5 3.4 %collective-permute-start.3 = (bf16[4,88,256]{2,1,0:T(8,128)(2,1)}, bf16[4,88,256]{2,1,0:T(8,128)(2,1)S(1)}, u32[]{:S(2)}, u32[]{:S(2)}) collective-permute-start(bf16[4,88,256]{2,1,0:T(8,128)(2,1)} %get-tuple-element.42), channel_id=1, source_target_pairs={{0,1},{1,0},{2,3},{3,2},{4,5},{5,4},{6,7},{7,6},{8,9},{9,8},{10,11... | collective-permute-start | bytes 540680 | tf_op jit(solution)/shard_map/ppermute | solution.py:483
  77.9 1.5 %collective-permute-start.4 = (bf16[4,88,256]{2,1,0:T(8,128)(2,1)}, bf16[4,88,256]{2,1,0:T(8,128)(2,1)S(1)}, u32[]{:S(2)}, u32[]{:S(2)}) collective-permute-start(bf16[4,88,256]{2,1,0:T(8,128)(2,1)} %get-tuple-element.43), channel_id=1, source_target_pairs={{0,16},{1,17},{2,18},{3,19},{4,20},{5,21},{6,22},{7,23},{8,24},{9,... | collective-permute-start | bytes 540680 | tf_op jit(solution)/shard_map/ppermute | solution.py:483
  79.4 0.0 collective-permute-start.5
  79.4 3.8 %all-to-all-done.1.x_ref = bf16[32,88,256]{2,1,0:T(8,128)(2,1)S(1)} async-done(((bf16[32,88,256]{2,1,0:T(8,128)(2,1)}), bf16[32,88,256]{2,1,0:T(8,128)(2,1)S(1)}, u32[]{:S(2)}, u32[]{:S(2)}) %all-to-all-start.1) | async-done | bytes 1441824 | tf_op jit(solution)/shard_map/all_to_all | solution.py:477
  83.2 7.3 %orthogonalize.3 = (bf16[704,1024]{1,0:T(8,128)(2,1)S(1)}, bf16[16,88,256]{2,1,0:T(8,128)(2,1)}) custom-call(s32[32]{0:T(128)S(1)} %copy-done.4, bf16[32,88,256]{2,1,0:T(8,128)(2,1)S(1)} %all-to-all-done.1.x_ref), custom_call_target="tpu_custom_call" | custom-call | flops 6643777536 | bytes 4718592 | tf_op jit(solution)/shard_map/orthogonalize/pallas_call | solution.py:364
  90.5 0.0 collective-permute-done.3.refs_1_
  90.5 0.0 collective-permute-done.4.refs_2_
  90.5 0.1 collective-permute-done.5.refs_3_
  90.6 4.9 %all-to-all-start.2 = ((bf16[16,88,256]{2,1,0:T(8,128)(2,1)}), bf16[16,88,256]{2,1,0:T(8,128)(2,1)S(1)}, u32[]{:S(2)}, u32[]{:S(2)}) async-start(bf16[16,88,256]{2,1,0:T(8,128)(2,1)} %get-tuple-element.48), calls=%async_computation.2 | async-start | bytes 1441792 | tf_op jit(solution)/shard_map/all_to_all | solution.py:477
  95.5 2.3 %store_early.1 = (bf16[2,704,1024]{2,1,0:T(8,128)(2,1)}, bf16[32,88,256]{2,1,0:T(8,128)(2,1)}) custom-call(s32[64]{0:T(128)S(1)} %get-tuple-element.33.list_ref, bf16[704,1024]{1,0:T(8,128)(2,1)S(1)} %get-tuple-element.49.whole_ref, bf16[2,704,1024]{2,1,0:T(8,128)(2,1)} %get-tuple-element.50.owned_in, ...), custom_call_target="tpu_custom_call", output_to_operand_aliasing={{0}: (2, {})} | custom-call | bytes 5767168 | tf_op jit(solution)/shard_map/store_early/pallas_call | solution.py:435
  97.8 8.5 %all-to-all-done.2.back_ref = bf16[16,88,256]{2,1,0:T(8,128)(2,1)S(1)} async-done(((bf16[16,88,256]{2,1,0:T(8,128)(2,1)}), bf16[16,88,256]{2,1,0:T(8,128)(2,1)S(1)}, u32[]{:S(2)}, u32[]{:S(2)}) %all-to-all-start.2) | async-done | bytes 720928 | tf_op jit(solution)/shard_map/all_to_all | solution.py:477
  106.3 1.4 %store_late.1 = bf16[32,88,256]{2,1,0:T(8,128)(2,1)} custom-call(s32[64]{0:T(128)S(1)} %get-tuple-element.33.list_ref, bf16[16,88,256]{2,1,0:T(8,128)(2,1)S(1)} %all-to-all-done.2.back_ref, bf16[32,88,256]{2,1,0:T(8,128)(2,1)} %get-tuple-element.55.update_in), custom_call_target="tpu_custom_call", output_to_operand_aliasing={{}: (2, {})} | custom-call | bytes 1441792 | tf_op jit(solution)/shard_map/store_late/pallas_call | solution.py:463
Async XLA Ops:
  4.7 7.5 %copy-start = (f32[32,88,256]{2,1,0:T(8,128)S(1)}, f32[32,88,256]{2,1,0:T(8,128)}, u32[]{:S(2)}) copy-start(f32[32,88,256]{2,1,0:T(8,128)} %m_ref.3) | copy-start | bytes 8650756
  4.7 7.5 %copy-start.3 = (s32[32]{0:T(128)S(1)}, s32[32]{0:T(128)}, u32[]{:S(2)}) copy-start(s32[32]{0:T(128)} %owner_ref.3) | copy-start | bytes 388
  4.7 7.5 %copy-start.4 = (s32[32]{0:T(128)S(1)}, s32[32]{0:T(128)}, u32[]{:S(2)}) copy-start(s32[32]{0:T(128)} %get-tuple-element.30.other_ref) | copy-start | bytes 388
  4.7 7.5 %copy-start.5 = (s32[32]{0:T(128)S(1)}, s32[32]{0:T(128)}, u32[]{:S(2)}) copy-start(s32[32]{0:T(128)} %get-tuple-element.31.rank_ref) | copy-start | bytes 388
  4.7 40.6 %all-to-all-start = ((bf16[32,88,256]{2,1,0:T(8,128)(2,1)}), bf16[32,88,256]{2,1,0:T(8,128)(2,1)}, u32[]{:S(2)}, u32[]{:S(2)}) async-start(bf16[32,88,256]{2,1,0:T(8,128)(2,1)} %get-tuple-element.34), calls=%async_computation | async-start | bytes 2883584 | tf_op jit(solution)/shard_map/all_to_all | solution.py:477
  12.2 1.4 %copy-start.1 = (bf16[32,88,256]{2,1,0:T(8,128)(2,1)S(1)}, bf16[32,88,256]{2,1,0:T(8,128)(2,1)}, u32[]{:S(2)}) copy-start(bf16[32,88,256]{2,1,0:T(8,128)(2,1)} %g_ref.3) | copy-start | bytes 4325380
  16.8 1.1 %copy-start.2 = (bf16[32,88,256]{2,1,0:T(8,128)(2,1)}, bf16[32,88,256]{2,1,0:T(8,128)(2,1)S(1)}, u32[]{:S(2)}) copy-start(bf16[32,88,256]{2,1,0:T(8,128)(2,1)S(1)} %get-tuple-element.45) | copy-start | bytes 4325380
  45.4 37.8 %all-to-all-start.1 = ((bf16[32,88,256]{2,1,0:T(8,128)(2,1)}), bf16[32,88,256]{2,1,0:T(8,128)(2,1)S(1)}, u32[]{:S(2)}, u32[]{:S(2)}) async-start(bf16[32,88,256]{2,1,0:T(8,128)(2,1)} %copy-done.2), calls=%async_computation.1 | async-start | bytes 2883584 | tf_op jit(solution)/shard_map/all_to_all | solution.py:477
  58.7 2.0 %collective-permute-start = (bf16[4,88,256]{2,1,0:T(8,128)(2,1)S(1)}, bf16[4,88,256]{2,1,0:T(8,128)(2,1)S(1)}, u32[]{:S(2)}, u32[]{:S(2)}) collective-permute-start(bf16[4,88,256]{2,1,0:T(8,128)(2,1)S(1)} %get-tuple-element.38), channel_id=1, source_target_pairs={{0,4},{1,5},{2,6},{3,7},{4,0},{5,1},{6,2},{7,3},{8,12},{9,13},{10,... | collective-permute-start | bytes 540680 | tf_op jit(solution)/shard_map/ppermute | solution.py:483
  59.1 10.5 %collective-permute-start.1 = (bf16[4,88,256]{2,1,0:T(8,128)(2,1)S(1)}, bf16[4,88,256]{2,1,0:T(8,128)(2,1)S(1)}, u32[]{:S(2)}, u32[]{:S(2)}) collective-permute-start(bf16[4,88,256]{2,1,0:T(8,128)(2,1)S(1)} %get-tuple-element.39), channel_id=1, source_target_pairs={{0,8},{1,9},{2,10},{3,11},{4,12},{5,13},{6,14},{7,15},{8,0},{9,1},... | collective-permute-start | bytes 540680 | tf_op jit(solution)/shard_map/ppermute | solution.py:483
  60.7 13.0 %collective-permute-start.2 = (bf16[4,88,256]{2,1,0:T(8,128)(2,1)S(1)}, bf16[4,88,256]{2,1,0:T(8,128)(2,1)S(1)}, u32[]{:S(2)}, u32[]{:S(2)}) collective-permute-start(bf16[4,88,256]{2,1,0:T(8,128)(2,1)S(1)} %get-tuple-element.40), channel_id=1, source_target_pairs={{0,12},{1,13},{2,14},{3,15},{4,8},{5,9},{6,10},{7,11},{8,4},{9,5},... | collective-permute-start | bytes 540680 | tf_op jit(solution)/shard_map/ppermute | solution.py:483
  74.5 15.9 %collective-permute-start.3 = (bf16[4,88,256]{2,1,0:T(8,128)(2,1)}, bf16[4,88,256]{2,1,0:T(8,128)(2,1)S(1)}, u32[]{:S(2)}, u32[]{:S(2)}) collective-permute-start(bf16[4,88,256]{2,1,0:T(8,128)(2,1)} %get-tuple-element.42), channel_id=1, source_target_pairs={{0,1},{1,0},{2,3},{3,2},{4,5},{5,4},{6,7},{7,6},{8,9},{9,8},{10,11... | collective-permute-start | bytes 540680 | tf_op jit(solution)/shard_map/ppermute | solution.py:483
  77.9 12.6 %collective-permute-start.4 = (bf16[4,88,256]{2,1,0:T(8,128)(2,1)}, bf16[4,88,256]{2,1,0:T(8,128)(2,1)S(1)}, u32[]{:S(2)}, u32[]{:S(2)}) collective-permute-start(bf16[4,88,256]{2,1,0:T(8,128)(2,1)} %get-tuple-element.43), channel_id=1, source_target_pairs={{0,16},{1,17},{2,18},{3,19},{4,20},{5,21},{6,22},{7,23},{8,24},{9,... | collective-permute-start | bytes 540680 | tf_op jit(solution)/shard_map/ppermute | solution.py:483
  79.4 11.2 %collective-permute-start.5 = (bf16[4,88,256]{2,1,0:T(8,128)(2,1)}, bf16[4,88,256]{2,1,0:T(8,128)(2,1)}, u32[]{:S(2)}, u32[]{:S(2)}) collective-permute-start(bf16[4,88,256]{2,1,0:T(8,128)(2,1)} %get-tuple-element.44), channel_id=1, source_target_pairs={{0,17},{1,16},{2,19},{3,18},{4,21},{5,20},{6,23},{7,22},{8,25},{9,... | collective-permute-start | bytes 540680 | tf_op jit(solution)/shard_map/ppermute | solution.py:483
  90.6 15.7 %all-to-all-start.2 = ((bf16[16,88,256]{2,1,0:T(8,128)(2,1)}), bf16[16,88,256]{2,1,0:T(8,128)(2,1)S(1)}, u32[]{:S(2)}, u32[]{:S(2)}) async-start(bf16[16,88,256]{2,1,0:T(8,128)(2,1)} %get-tuple-element.48), calls=%async_computation.2 | async-start | bytes 1441792 | tf_op jit(solution)/shard_map/all_to_all | solution.py:477
